TPU v7x, 512 devices: a whole 4x8x8 slice. The times are simulated.
512 devices in a mesh: gx: 16 (over x, y_hi), gy: 8 (over z), gz: 4 (over y_lo, core).
Axes of the slice: x: 4, y: 8 (y_hi: 4, y_lo: 2; y = y_hi * 2 + y_lo), z: 8, core: 2. Of those that a mesh axis runs over, the one named last changes fastest.
Arguments:
- displacement: float32 [3, 128, 128, 512], P(None, 'gx', 'gy', 'gz'), may hold values from -6 to 6
- previous: float32 [3, 128, 128, 512], P(None, 'gx', 'gy', 'gz'), may hold values from -6 to 6
- courant: float32 [128, 128, 512], P('gx', 'gy', 'gz'), may hold values from 0.02 to 0.2
- damping: float32 [128, 128, 512], P('gx', 'gy', 'gz'), may hold values from 0 to 0.3
- send_cells: int32 [256, 8, 128], P('gx', 'gy'), may hold values from 0 to 127
- building_slot: int32 [524288], P(('gx', 'gy', 'gz')), may hold values from 0 to 2047
- building_class: int32 [524288], P(('gx', 'gy', 'gz')), may hold values from 0 to 7
- city: int32 [524288], P(('gx', 'gy', 'gz')), may hold values from 0 to 15
- mode_count: int32 [8], replicated, may hold values from 1 to 8
- modal_filter: bfloat16 [64, 24], replicated, may hold values from -1.25 to 1.25
- amplify: float32 [16], replicated, may hold values from 0.5 to 3
- median: float32 [16, 8], replicated, may hold values from 0 to 1.5
- spread: float32 [16, 8], replicated, may hold values from 0.2 to 0.8
Outputs:
- final_field: float32 [3, 128, 128, 512], P(None, 'gx', 'gy', 'gz')
- probability: float32 [16, 524288], P(None, ('gx', 'gy', 'gz'))
All inputs are finite; a program needn't handle non-finite values.
Results may differ from a plain program's by a relative error of at most 0.00079.
Values may be sent and summed in bfloat16 or wider, within the bound.
No kernel may reach another device: no remote copies, remote signals or barrier semaphores. Data moves between devices by JAX's collectives and lax.ppermute only.
A program may use at most 64 MiB of HBM per device.

v0:
```python
import jax
import jax.numpy as jnp
from jax import lax
from jax.sharding import PartitionSpec as P

STEPS = 8
CLASSES = 8
MODES = 8
CITIES = 16


def extended_2(block, sides, width):
    for axis, dim in sides:
        count = lax.axis_size(axis)
        forward = [(i, i + 1) for i in range(count - 1)]
        backward = [(target, source) for source, target in forward]
        low = lax.ppermute(
            lax.slice_in_dim(block, block.shape[dim] - width, None, axis=dim), axis, forward
        )
        high = lax.ppermute(lax.slice_in_dim(block, 0, width, axis=dim), axis, backward)
        block = jnp.concatenate([low, block, high], axis=dim)
    return block


def from_root(value, axis, source):
    kept = jnp.where(lax.axis_index(axis) == source, value, 0).astype(value.dtype)
    return lax.psum(kept, axis)


def window(extended, axis_dim, offset):
    starts = [0, 2, 2, 2]
    limits = [
        extended.shape[0],
        extended.shape[1] - 2,
        extended.shape[2] - 2,
        extended.shape[3] - 2,
    ]
    starts[axis_dim] = starts[axis_dim] + offset
    limits[axis_dim] = limits[axis_dim] + offset
    return lax.slice(extended, starts, limits)


def advance(extended, prev_core, rate_core, damp_core):
    core = extended[:, 2:-2, 2:-2, 2:-2]
    laplace = -7.5 * core
    for axis_dim in (1, 2, 3):
        for offset, weight in (
            (-2, -1.0 / 12.0),
            (-1, 4.0 / 3.0),
            (1, 4.0 / 3.0),
            (2, -1.0 / 12.0),
        ):
            laplace = laplace + weight * window(extended, axis_dim, offset)
    return (2.0 * core - (1.0 - damp_core) * prev_core + rate_core * laplace) / (1.0 + damp_core)


def body(
    displacement,
    previous,
    courant,
    damping,
    send_cells,
    building_slot,
    building_class,
    city,
    mode_count,
    modal_filter,
    amplify,
    median,
    spread,
):
    size_x, size_y, size_z = courant.shape
    field = displacement
    earlier = previous
    records = []
    for step_index in range(STEPS):
        extended = extended_2(field, (("gx", 1), ("gy", 2), ("gz", 3)), 2)
        fresh = advance(extended, earlier, courant, damping)
        records.append(fresh[:, :, :, 0])
        earlier = field
        field = fresh
    record = jnp.stack(records).reshape(3 * STEPS, size_x * size_y).astype(jnp.bfloat16)
    outgoing = jnp.take(record, send_cells.reshape(-1), axis=1)
    received = lax.all_to_all(outgoing, "gx", split_axis=1, concat_axis=1, tiled=True)
    received = from_root(received, "gz", 0)
    motion = jnp.take(received, building_slot, axis=1)
    count = motion.shape[1]
    modal = jnp.dot(modal_filter, motion, preferred_element_type=jnp.float32)
    squared = (modal * modal).reshape(CLASSES, MODES, count)
    mode_mask = (jnp.arange(MODES)[None, :] < mode_count[:, None]).astype(jnp.float32)
    per_class = jnp.sum(squared * mode_mask[:, :, None], axis=1)
    onehot = (building_class[None, :] == jnp.arange(CLASSES)[:, None]).astype(jnp.float32)
    energy = jnp.sum(onehot * per_class, axis=0)
    city_hot = (city[None, :] == jnp.arange(CITIES)[:, None]).astype(jnp.float32)
    amp_each = jnp.sum(city_hot * amplify[:, None], axis=0)
    logdemand = jnp.log(amp_each) + 0.5 * jnp.log1p(energy)
    med_each = jnp.dot(median, onehot, precision=lax.Precision.HIGHEST)
    spread_each = jnp.dot(spread, onehot, precision=lax.Precision.HIGHEST)
    probability = jax.nn.sigmoid((logdemand[None, :] - med_each) / spread_each)
    return (field, probability)


def solution(mesh):
    placed = (
        P(None, "gx", "gy", "gz"),
        P(None, "gx", "gy", "gz"),
        P("gx", "gy", "gz"),
        P("gx", "gy", "gz"),
        P("gx", "gy", None),
        P(("gx", "gy", "gz")),
        P(("gx", "gy", "gz")),
        P(("gx", "gy", "gz")),
        P(),
        P(),
        P(),
        P(),
        P(),
    )
    return jax.shard_map(
        body,
        mesh=mesh,
        in_specs=placed,
        out_specs=(P(None, "gx", "gy", "gz"), P(None, ("gx", "gy", "gz"))),
        check_vma=False,
    )
```

profile of v0, /device:TPU:1, one launch (start us, length us, event | category | flops | bytes accessed | tf_op | source)
XLA Modules:
  0.0 361.6 jit_solution(12004309218185235125)
XLA Ops:
  8.1 5.0 %collective-permute-start = (f32[3,2,16,128]{3,2,1,0:T(8,128)S(1)}, f32[3,2,16,128]{3,2,1,0:T(8,128)S(1)}, u32[]{:S(2)}, u32[]{:S(2)}) collective-permute-start(f32[3,2,16,128]{3,2,1,0:T(8,128)S(1)} %get-tuple-element.58), channel_id=1, source_target_pairs={{0,32},{32,64},{64,96},{96,128},{128,160},{160,192},{192,224},{224... | collective-permute-start | bytes 147464 | tf_op jit(solution)/shard_map/ppermute | solution.py:17
  14.5 6.0 %collective-permute-done.1 = f32[3,2,16,128]{3,2,1,0:T(8,128)S(1)} collective-permute-done((f32[3,2,16,128]{3,2,1,0:T(8,128)S(1)}, f32[3,2,16,128]{3,2,1,0:T(8,128)S(1)}, u32[]{:S(2)}, u32[]{:S(2)}) %collective-permute-start.1) | collective-permute-done | bytes 49184 | tf_op jit(solution)/shard_map/ppermute | solution.py:20
  30.2 4.7 %collective-permute-start.4 = (f32[3,12,20,2]{3,2,1,0:T(8,128)S(1)}, f32[3,12,20,2]{3,2,1,0:T(8,128)S(1)}, u32[]{:S(2)}, u32[]{:S(2)}) collective-permute-start(f32[3,12,20,2]{3,2,1,0:T(8,128)S(1)} %get-tuple-element.22), channel_id=1, source_target_pairs={{0,1},{1,2},{2,3},{4,5},{5,6},{6,7},{8,9},{9,10},{10,11},{12,13},{... | collective-permute-start | bytes 17288 | tf_op jit(solution)/shard_map/ppermute | solution.py:17
  40.2 4.5 %collective-permute-done.5 = f32[3,12,20,2]{3,2,1,0:T(8,128)S(1)} collective-permute-done((f32[3,12,20,2]{3,2,1,0:T(8,128)S(1)}, f32[3,12,20,2]{3,2,1,0:T(8,128)S(1)}, u32[]{:S(2)}, u32[]{:S(2)}) %collective-permute-start.5) | collective-permute-done | bytes 5792 | tf_op jit(solution)/shard_map/ppermute | solution.py:20
  45.3 5.6 %collective-permute-start.6 = (f32[3,2,16,128]{3,2,1,0:T(8,128)S(1)}, f32[3,2,16,128]{3,2,1,0:T(8,128)S(1)}, u32[]{:S(2)}, u32[]{:S(2)}) collective-permute-start(f32[3,2,16,128]{3,2,1,0:T(8,128)S(1)} %get-tuple-element.52), channel_id=1, source_target_pairs={{0,32},{32,64},{64,96},{96,128},{128,160},{160,192},{192,224},{224... | collective-permute-start | bytes 147464 | tf_op jit(solution)/shard_map/ppermute | solution.py:17
  52.3 4.9 %collective-permute-done.7 = f32[3,2,16,128]{3,2,1,0:T(8,128)S(1)} collective-permute-done((f32[3,2,16,128]{3,2,1,0:T(8,128)S(1)}, f32[3,2,16,128]{3,2,1,0:T(8,128)S(1)}, u32[]{:S(2)}, u32[]{:S(2)}) %collective-permute-start.7) | collective-permute-done | bytes 49184 | tf_op jit(solution)/shard_map/ppermute | solution.py:20
  62.6 5.2 %collective-permute-done.9 = f32[3,12,2,128]{3,2,1,0:T(2,128)S(1)} collective-permute-done((f32[3,12,2,128]{3,2,1,0:T(2,128)S(1)}, f32[3,12,2,128]{3,2,1,0:T(2,128)S(1)}, u32[]{:S(2)}, u32[]{:S(2)}) %collective-permute-start.9) | collective-permute-done | bytes 36896 | tf_op jit(solution)/shard_map/ppermute | solution.py:20
  77.2 4.4 %collective-permute-done.11 = f32[3,12,20,2]{3,2,1,0:T(8,128)S(1)} collective-permute-done((f32[3,12,20,2]{3,2,1,0:T(8,128)S(1)}, f32[3,12,20,2]{3,2,1,0:T(8,128)S(1)}, u32[]{:S(2)}, u32[]{:S(2)}) %collective-permute-start.11) | collective-permute-done | bytes 5792 | tf_op jit(solution)/shard_map/ppermute | solution.py:20
  86.4 4.9 %collective-permute-done.13 = f32[3,2,16,128]{3,2,1,0:T(8,128)S(1)} collective-permute-done((f32[3,2,16,128]{3,2,1,0:T(8,128)S(1)}, f32[3,2,16,128]{3,2,1,0:T(8,128)S(1)}, u32[]{:S(2)}, u32[]{:S(2)}) %collective-permute-start.13) | collective-permute-done | bytes 49184 | tf_op jit(solution)/shard_map/ppermute | solution.py:20
  91.4 4.9 %collective-permute-start.14 = (f32[3,12,2,128]{3,2,1,0:T(2,128)S(1)}, f32[3,12,2,128]{3,2,1,0:T(2,128)S(1)}, u32[]{:S(2)}, u32[]{:S(2)}) collective-permute-start(f32[3,12,2,128]{3,2,1,0:T(2,128)S(1)} %get-tuple-element.34), channel_id=1, source_target_pairs={{0,4},{4,8},{8,12},{12,16},{16,20},{20,24},{24,28},{1,5},{5,9},{9,... | collective-permute-start | bytes 110600 | tf_op jit(solution)/shard_map/ppermute | solution.py:17
  110.6 4.4 %collective-permute-done.17 = f32[3,12,20,2]{3,2,1,0:T(8,128)S(1)} collective-permute-done((f32[3,12,20,2]{3,2,1,0:T(8,128)S(1)}, f32[3,12,20,2]{3,2,1,0:T(8,128)S(1)}, u32[]{:S(2)}, u32[]{:S(2)}) %collective-permute-start.17) | collective-permute-done | bytes 5792 | tf_op jit(solution)/shard_map/ppermute | solution.py:20
  115.6 5.0 %collective-permute-start.18 = (f32[3,2,16,128]{3,2,1,0:T(8,128)S(1)}, f32[3,2,16,128]{3,2,1,0:T(8,128)S(1)}, u32[]{:S(2)}, u32[]{:S(2)}) collective-permute-start(f32[3,2,16,128]{3,2,1,0:T(8,128)S(1)} %get-tuple-element.48), channel_id=1, source_target_pairs={{0,32},{32,64},{64,96},{96,128},{128,160},{160,192},{192,224},{224... | collective-permute-start | bytes 147464 | tf_op jit(solution)/shard_map/ppermute | solution.py:17
  122.0 4.9 %collective-permute-done.19 = f32[3,2,16,128]{3,2,1,0:T(8,128)S(1)} collective-permute-done((f32[3,2,16,128]{3,2,1,0:T(8,128)S(1)}, f32[3,2,16,128]{3,2,1,0:T(8,128)S(1)}, u32[]{:S(2)}, u32[]{:S(2)}) %collective-permute-start.19) | collective-permute-done | bytes 49184 | tf_op jit(solution)/shard_map/ppermute | solution.py:20
  135.6 4.2 %collective-permute-start.22 = (f32[3,12,20,2]{3,2,1,0:T(8,128)S(1)}, f32[3,12,20,2]{3,2,1,0:T(8,128)S(1)}, u32[]{:S(2)}, u32[]{:S(2)}) collective-permute-start(f32[3,12,20,2]{3,2,1,0:T(8,128)S(1)} %get-tuple-element.16), channel_id=1, source_target_pairs={{0,1},{1,2},{2,3},{4,5},{5,6},{6,7},{8,9},{9,10},{10,11},{12,13},{... | collective-permute-start | bytes 17288 | tf_op jit(solution)/shard_map/ppermute | solution.py:17
  145.0 4.4 %collective-permute-done.23 = f32[3,12,20,2]{3,2,1,0:T(8,128)S(1)} collective-permute-done((f32[3,12,20,2]{3,2,1,0:T(8,128)S(1)}, f32[3,12,20,2]{3,2,1,0:T(8,128)S(1)}, u32[]{:S(2)}, u32[]{:S(2)}) %collective-permute-start.23) | collective-permute-done | bytes 5792 | tf_op jit(solution)/shard_map/ppermute | solution.py:20
  149.9 4.3 %collective-permute-start.24 = (f32[3,2,16,128]{3,2,1,0:T(8,128)S(1)}, f32[3,2,16,128]{3,2,1,0:T(8,128)S(1)}, u32[]{:S(2)}, u32[]{:S(2)}) collective-permute-start(f32[3,2,16,128]{3,2,1,0:T(8,128)S(1)} %get-tuple-element.46), channel_id=1, source_target_pairs={{0,32},{32,64},{64,96},{96,128},{128,160},{160,192},{192,224},{224... | collective-permute-start | bytes 147464 | tf_op jit(solution)/shard_map/ppermute | solution.py:17
  155.7 5.0 %collective-permute-done.25 = f32[3,2,16,128]{3,2,1,0:T(8,128)S(1)} collective-permute-done((f32[3,2,16,128]{3,2,1,0:T(8,128)S(1)}, f32[3,2,16,128]{3,2,1,0:T(8,128)S(1)}, u32[]{:S(2)}, u32[]{:S(2)}) %collective-permute-start.25) | collective-permute-done | bytes 49184 | tf_op jit(solution)/shard_map/ppermute | solution.py:20
  178.0 4.4 %collective-permute-done.29 = f32[3,12,20,2]{3,2,1,0:T(8,128)S(1)} collective-permute-done((f32[3,12,20,2]{3,2,1,0:T(8,128)S(1)}, f32[3,12,20,2]{3,2,1,0:T(8,128)S(1)}, u32[]{:S(2)}, u32[]{:S(2)}) %collective-permute-start.29) | collective-permute-done | bytes 5792 | tf_op jit(solution)/shard_map/ppermute | solution.py:20
  183.0 6.0 %collective-permute-start.30 = (f32[3,2,16,128]{3,2,1,0:T(8,128)S(1)}, f32[3,2,16,128]{3,2,1,0:T(8,128)S(1)}, u32[]{:S(2)}, u32[]{:S(2)}) collective-permute-start(f32[3,2,16,128]{3,2,1,0:T(8,128)S(1)} %get-tuple-element.44), channel_id=1, source_target_pairs={{0,32},{32,64},{64,96},{96,128},{128,160},{160,192},{192,224},{224... | collective-permute-start | bytes 147464 | tf_op jit(solution)/shard_map/ppermute | solution.py:17
  190.3 4.9 %collective-permute-done.31 = f32[3,2,16,128]{3,2,1,0:T(8,128)S(1)} collective-permute-done((f32[3,2,16,128]{3,2,1,0:T(8,128)S(1)}, f32[3,2,16,128]{3,2,1,0:T(8,128)S(1)}, u32[]{:S(2)}, u32[]{:S(2)}) %collective-permute-start.31) | collective-permute-done | bytes 49184 | tf_op jit(solution)/shard_map/ppermute | solution.py:20
  203.4 4.2 %collective-permute-start.34 = (f32[3,12,20,2]{3,2,1,0:T(8,128)S(1)}, f32[3,12,20,2]{3,2,1,0:T(8,128)S(1)}, u32[]{:S(2)}, u32[]{:S(2)}) collective-permute-start(f32[3,12,20,2]{3,2,1,0:T(8,128)S(1)} %get-tuple-element.12), channel_id=1, source_target_pairs={{0,1},{1,2},{2,3},{4,5},{5,6},{6,7},{8,9},{9,10},{10,11},{12,13},{... | collective-permute-start | bytes 17288 | tf_op jit(solution)/shard_map/ppermute | solution.py:17
  212.8 4.4 %collective-permute-done.35 = f32[3,12,20,2]{3,2,1,0:T(8,128)S(1)} collective-permute-done((f32[3,12,20,2]{3,2,1,0:T(8,128)S(1)}, f32[3,12,20,2]{3,2,1,0:T(8,128)S(1)}, u32[]{:S(2)}, u32[]{:S(2)}) %collective-permute-start.35) | collective-permute-done | bytes 5792 | tf_op jit(solution)/shard_map/ppermute | solution.py:20
  223.0 4.8 %collective-permute-done.37 = f32[3,2,16,128]{3,2,1,0:T(8,128)S(1)} collective-permute-done((f32[3,2,16,128]{3,2,1,0:T(8,128)S(1)}, f32[3,2,16,128]{3,2,1,0:T(8,128)S(1)}, u32[]{:S(2)}, u32[]{:S(2)}) %collective-permute-start.37) | collective-permute-done | bytes 49184 | tf_op jit(solution)/shard_map/ppermute | solution.py:20
  235.9 4.2 %collective-permute-start.40 = (f32[3,12,20,2]{3,2,1,0:T(8,128)S(1)}, f32[3,12,20,2]{3,2,1,0:T(8,128)S(1)}, u32[]{:S(2)}, u32[]{:S(2)}) collective-permute-start(f32[3,12,20,2]{3,2,1,0:T(8,128)S(1)} %get-tuple-element.10), channel_id=1, source_target_pairs={{0,1},{1,2},{2,3},{4,5},{5,6},{6,7},{8,9},{9,10},{10,11},{12,13},{... | collective-permute-start | bytes 17288 | tf_op jit(solution)/shard_map/ppermute | solution.py:17
  245.3 4.4 %collective-permute-done.41 = f32[3,12,20,2]{3,2,1,0:T(8,128)S(1)} collective-permute-done((f32[3,12,20,2]{3,2,1,0:T(8,128)S(1)}, f32[3,12,20,2]{3,2,1,0:T(8,128)S(1)}, u32[]{:S(2)}, u32[]{:S(2)}) %collective-permute-start.41) | collective-permute-done | bytes 5792 | tf_op jit(solution)/shard_map/ppermute | solution.py:20
  255.4 4.9 %collective-permute-done.43 = f32[3,2,16,128]{3,2,1,0:T(8,128)S(1)} collective-permute-done((f32[3,2,16,128]{3,2,1,0:T(8,128)S(1)}, f32[3,2,16,128]{3,2,1,0:T(8,128)S(1)}, u32[]{:S(2)}, u32[]{:S(2)}) %collective-permute-start.43) | collective-permute-done | bytes 49184 | tf_op jit(solution)/shard_map/ppermute | solution.py:20
  268.2 4.2 %collective-permute-start.46 = (f32[3,12,20,2]{3,2,1,0:T(8,128)S(1)}, f32[3,12,20,2]{3,2,1,0:T(8,128)S(1)}, u32[]{:S(2)}, u32[]{:S(2)}) collective-permute-start(f32[3,12,20,2]{3,2,1,0:T(8,128)S(1)} %get-tuple-element.8), channel_id=1, source_target_pairs={{0,1},{1,2},{2,3},{4,5},{5,6},{6,7},{8,9},{9,10},{10,11},{12,13},{... | collective-permute-start | bytes 17288 | tf_op jit(solution)/shard_map/ppermute | solution.py:17
  277.6 4.4 %collective-permute-done.47 = f32[3,12,20,2]{3,2,1,0:T(8,128)S(1)} collective-permute-done((f32[3,12,20,2]{3,2,1,0:T(8,128)S(1)}, f32[3,12,20,2]{3,2,1,0:T(8,128)S(1)}, u32[]{:S(2)}, u32[]{:S(2)}) %collective-permute-start.47) | collective-permute-done | bytes 5792 | tf_op jit(solution)/shard_map/ppermute | solution.py:20
  283.0 6.2 %gather_fusion = bf16[2048,24]{1,0:T(8,128)(2,1)S(1)} fusion(bf16[24,128]{0,1:T(8,128)(2,1)S(1)} %copy.1328, s32[2048]{0:T(1024)S(1)} %broadcast_clamp_fusion), kind=kCustom, calls=%fused_computation | custom fusion | bytes 204800 | tf_op jit(solution)/shard_map/jit(_take)/gather | solution.py:83
  290.0 7.1 %all-to-all-start = ((bf16[24,16,128]{2,0,1:T(8,128)(2,1)}), bf16[24,16,128]{2,0,1:T(8,128)(2,1)S(1)}, u32[]{:S(2)}, u32[]{:S(2)}) async-start(bf16[24,16,128]{2,0,1:T(8,128)(2,1)} %broadcast_select_fusion), calls=%async_computation | async-start | bytes 196608 | tf_op jit(solution)/shard_map/all_to_all | solution.py:84
  297.3 9.1 %all-to-all-done = bf16[24,16,128]{2,0,1:T(8,128)(2,1)S(1)} async-done(((bf16[24,16,128]{2,0,1:T(8,128)(2,1)}), bf16[24,16,128]{2,0,1:T(8,128)(2,1)S(1)}, u32[]{:S(2)}, u32[]{:S(2)}) %all-to-all-start) | async-done | bytes 98336 | tf_op jit(solution)/shard_map/all_to_all | solution.py:84
  308.2 39.6 %all-reduce.2.cloned.1.call-done = bf16[24,2048]{0,1:T(8,128)(2,1)} async-done(((bf16[24,2048]{0,1:T(8,128)(2,1)}), bf16[24,2048]{0,1:T(8,128)(2,1)}) %all-reduce.2.cloned.1.call-update) | async-done | bytes 98320 | tf_op jit(solution)/shard_map/psum | solution.py:27
  (177 shorter events, 151.2 us)
Async XLA Ops:
  8.1 6.3 %collective-permute-start = (f32[3,2,16,128]{3,2,1,0:T(8,128)S(1)}, f32[3,2,16,128]{3,2,1,0:T(8,128)S(1)}, u32[]{:S(2)}, u32[]{:S(2)}) collective-permute-start(f32[3,2,16,128]{3,2,1,0:T(8,128)S(1)} %get-tuple-element.58), channel_id=1, source_target_pairs={{0,32},{32,64},{64,96},{96,128},{128,160},{160,192},{192,224},{224... | collective-permute-start | bytes 147464 | tf_op jit(solution)/shard_map/ppermute | solution.py:17
  13.1 7.4 %collective-permute-start.1 = (f32[3,2,16,128]{3,2,1,0:T(8,128)S(1)}, f32[3,2,16,128]{3,2,1,0:T(8,128)S(1)}, u32[]{:S(2)}, u32[]{:S(2)}) collective-permute-start(f32[3,2,16,128]{3,2,1,0:T(8,128)S(1)} %get-tuple-element.57), channel_id=1, source_target_pairs={{32,0},{64,32},{96,64},{128,96},{160,128},{192,160},{224,192},{256... | collective-permute-start | bytes 147464 | tf_op jit(solution)/shard_map/ppermute | solution.py:20
  30.2 10.0 %collective-permute-start.4 = (f32[3,12,20,2]{3,2,1,0:T(8,128)S(1)}, f32[3,12,20,2]{3,2,1,0:T(8,128)S(1)}, u32[]{:S(2)}, u32[]{:S(2)}) collective-permute-start(f32[3,12,20,2]{3,2,1,0:T(8,128)S(1)} %get-tuple-element.22), channel_id=1, source_target_pairs={{0,1},{1,2},{2,3},{4,5},{5,6},{6,7},{8,9},{9,10},{10,11},{12,13},{... | collective-permute-start | bytes 17288 | tf_op jit(solution)/shard_map/ppermute | solution.py:17
  35.0 9.8 %collective-permute-start.5 = (f32[3,12,20,2]{3,2,1,0:T(8,128)S(1)}, f32[3,12,20,2]{3,2,1,0:T(8,128)S(1)}, u32[]{:S(2)}, u32[]{:S(2)}) collective-permute-start(f32[3,12,20,2]{3,2,1,0:T(8,128)S(1)} %get-tuple-element.23), channel_id=1, source_target_pairs={{1,0},{2,1},{3,2},{5,4},{6,5},{7,6},{9,8},{10,9},{11,10},{13,12},{... | collective-permute-start | bytes 17288 | tf_op jit(solution)/shard_map/ppermute | solution.py:20
  45.3 7.0 %collective-permute-start.6 = (f32[3,2,16,128]{3,2,1,0:T(8,128)S(1)}, f32[3,2,16,128]{3,2,1,0:T(8,128)S(1)}, u32[]{:S(2)}, u32[]{:S(2)}) collective-permute-start(f32[3,2,16,128]{3,2,1,0:T(8,128)S(1)} %get-tuple-element.52), channel_id=1, source_target_pairs={{0,32},{32,64},{64,96},{96,128},{128,160},{160,192},{192,224},{224... | collective-permute-start | bytes 147464 | tf_op jit(solution)/shard_map/ppermute | solution.py:17
  51.0 6.3 %collective-permute-start.7 = (f32[3,2,16,128]{3,2,1,0:T(8,128)S(1)}, f32[3,2,16,128]{3,2,1,0:T(8,128)S(1)}, u32[]{:S(2)}, u32[]{:S(2)}) collective-permute-start(f32[3,2,16,128]{3,2,1,0:T(8,128)S(1)} %get-tuple-element.53), channel_id=1, source_target_pairs={{32,0},{64,32},{96,64},{128,96},{160,128},{192,160},{224,192},{256... | collective-permute-start | bytes 147464 | tf_op jit(solution)/shard_map/ppermute | solution.py:20
  61.3 6.6 %collective-permute-start.9 = (f32[3,12,2,128]{3,2,1,0:T(2,128)S(1)}, f32[3,12,2,128]{3,2,1,0:T(2,128)S(1)}, u32[]{:S(2)}, u32[]{:S(2)}) collective-permute-start(f32[3,12,2,128]{3,2,1,0:T(2,128)S(1)} %get-tuple-element.37), channel_id=1, source_target_pairs={{4,0},{8,4},{12,8},{16,12},{20,16},{24,20},{28,24},{5,1},{9,5},{13... | collective-permute-start | bytes 110600 | tf_op jit(solution)/shard_map/ppermute | solution.py:20
  68.1 9.1 %collective-permute-start.10 = (f32[3,12,20,2]{3,2,1,0:T(8,128)S(1)}, f32[3,12,20,2]{3,2,1,0:T(8,128)S(1)}, u32[]{:S(2)}, u32[]{:S(2)}) collective-permute-start(f32[3,12,20,2]{3,2,1,0:T(8,128)S(1)} %get-tuple-element.20), channel_id=1, source_target_pairs={{0,1},{1,2},{2,3},{4,5},{5,6},{6,7},{8,9},{9,10},{10,11},{12,13},{... | collective-permute-start | bytes 17288 | tf_op jit(solution)/shard_map/ppermute | solution.py:17
  72.0 9.6 %collective-permute-start.11 = (f32[3,12,20,2]{3,2,1,0:T(8,128)S(1)}, f32[3,12,20,2]{3,2,1,0:T(8,128)S(1)}, u32[]{:S(2)}, u32[]{:S(2)}) collective-permute-start(f32[3,12,20,2]{3,2,1,0:T(8,128)S(1)} %get-tuple-element.21), channel_id=1, source_target_pairs={{1,0},{2,1},{3,2},{5,4},{6,5},{7,6},{9,8},{10,9},{11,10},{13,12},{... | collective-permute-start | bytes 17288 | tf_op jit(solution)/shard_map/ppermute | solution.py:20
  85.1 6.3 %collective-permute-start.13 = (f32[3,2,16,128]{3,2,1,0:T(8,128)S(1)}, f32[3,2,16,128]{3,2,1,0:T(8,128)S(1)}, u32[]{:S(2)}, u32[]{:S(2)}) collective-permute-start(f32[3,2,16,128]{3,2,1,0:T(8,128)S(1)} %get-tuple-element.51), channel_id=1, source_target_pairs={{32,0},{64,32},{96,64},{128,96},{160,128},{192,160},{224,192},{256... | collective-permute-start | bytes 147464 | tf_op jit(solution)/shard_map/ppermute | solution.py:20
  91.4 6.2 %collective-permute-start.14 = (f32[3,12,2,128]{3,2,1,0:T(2,128)S(1)}, f32[3,12,2,128]{3,2,1,0:T(2,128)S(1)}, u32[]{:S(2)}, u32[]{:S(2)}) collective-permute-start(f32[3,12,2,128]{3,2,1,0:T(2,128)S(1)} %get-tuple-element.34), channel_id=1, source_target_pairs={{0,4},{4,8},{8,12},{12,16},{16,20},{20,24},{24,28},{1,5},{5,9},{9,... | collective-permute-start | bytes 110600 | tf_op jit(solution)/shard_map/ppermute | solution.py:17
  101.5 9.1 %collective-permute-start.16 = (f32[3,12,20,2]{3,2,1,0:T(8,128)S(1)}, f32[3,12,20,2]{3,2,1,0:T(8,128)S(1)}, u32[]{:S(2)}, u32[]{:S(2)}) collective-permute-start(f32[3,12,20,2]{3,2,1,0:T(8,128)S(1)} %get-tuple-element.18), channel_id=1, source_target_pairs={{0,1},{1,2},{2,3},{4,5},{5,6},{6,7},{8,9},{9,10},{10,11},{12,13},{... | collective-permute-start | bytes 17288 | tf_op jit(solution)/shard_map/ppermute | solution.py:17
  105.4 9.6 %collective-permute-start.17 = (f32[3,12,20,2]{3,2,1,0:T(8,128)S(1)}, f32[3,12,20,2]{3,2,1,0:T(8,128)S(1)}, u32[]{:S(2)}, u32[]{:S(2)}) collective-permute-start(f32[3,12,20,2]{3,2,1,0:T(8,128)S(1)} %get-tuple-element.19), channel_id=1, source_target_pairs={{1,0},{2,1},{3,2},{5,4},{6,5},{7,6},{9,8},{10,9},{11,10},{13,12},{... | collective-permute-start | bytes 17288 | tf_op jit(solution)/shard_map/ppermute | solution.py:20
  115.6 6.4 %collective-permute-start.18 = (f32[3,2,16,128]{3,2,1,0:T(8,128)S(1)}, f32[3,2,16,128]{3,2,1,0:T(8,128)S(1)}, u32[]{:S(2)}, u32[]{:S(2)}) collective-permute-start(f32[3,2,16,128]{3,2,1,0:T(8,128)S(1)} %get-tuple-element.48), channel_id=1, source_target_pairs={{0,32},{32,64},{64,96},{96,128},{128,160},{160,192},{192,224},{224... | collective-permute-start | bytes 147464 | tf_op jit(solution)/shard_map/ppermute | solution.py:17
  120.6 6.3 %collective-permute-start.19 = (f32[3,2,16,128]{3,2,1,0:T(8,128)S(1)}, f32[3,2,16,128]{3,2,1,0:T(8,128)S(1)}, u32[]{:S(2)}, u32[]{:S(2)}) collective-permute-start(f32[3,2,16,128]{3,2,1,0:T(8,128)S(1)} %get-tuple-element.49), channel_id=1, source_target_pairs={{32,0},{64,32},{96,64},{128,96},{160,128},{192,160},{224,192},{256... | collective-permute-start | bytes 147464 | tf_op jit(solution)/shard_map/ppermute | solution.py:20
  135.6 9.4 %collective-permute-start.22 = (f32[3,12,20,2]{3,2,1,0:T(8,128)S(1)}, f32[3,12,20,2]{3,2,1,0:T(8,128)S(1)}, u32[]{:S(2)}, u32[]{:S(2)}) collective-permute-start(f32[3,12,20,2]{3,2,1,0:T(8,128)S(1)} %get-tuple-element.16), channel_id=1, source_target_pairs={{0,1},{1,2},{2,3},{4,5},{5,6},{6,7},{8,9},{9,10},{10,11},{12,13},{... | collective-permute-start | bytes 17288 | tf_op jit(solution)/shard_map/ppermute | solution.py:17
  139.7 9.6 %collective-permute-start.23 = (f32[3,12,20,2]{3,2,1,0:T(8,128)S(1)}, f32[3,12,20,2]{3,2,1,0:T(8,128)S(1)}, u32[]{:S(2)}, u32[]{:S(2)}) collective-permute-start(f32[3,12,20,2]{3,2,1,0:T(8,128)S(1)} %get-tuple-element.17), channel_id=1, source_target_pairs={{1,0},{2,1},{3,2},{5,4},{6,5},{7,6},{9,8},{10,9},{11,10},{13,12},{... | collective-permute-start | bytes 17288 | tf_op jit(solution)/shard_map/ppermute | solution.py:20
  154.2 6.4 %collective-permute-start.25 = (f32[3,2,16,128]{3,2,1,0:T(8,128)S(1)}, f32[3,2,16,128]{3,2,1,0:T(8,128)S(1)}, u32[]{:S(2)}, u32[]{:S(2)}) collective-permute-start(f32[3,2,16,128]{3,2,1,0:T(8,128)S(1)} %get-tuple-element.47), channel_id=1, source_target_pairs={{32,0},{64,32},{96,64},{128,96},{160,128},{192,160},{224,192},{256... | collective-permute-start | bytes 147464 | tf_op jit(solution)/shard_map/ppermute | solution.py:20
  168.8 9.2 %collective-permute-start.28 = (f32[3,12,20,2]{3,2,1,0:T(8,128)S(1)}, f32[3,12,20,2]{3,2,1,0:T(8,128)S(1)}, u32[]{:S(2)}, u32[]{:S(2)}) collective-permute-start(f32[3,12,20,2]{3,2,1,0:T(8,128)S(1)} %get-tuple-element.14), channel_id=1, source_target_pairs={{0,1},{1,2},{2,3},{4,5},{5,6},{6,7},{8,9},{9,10},{10,11},{12,13},{... | collective-permute-start | bytes 17288 | tf_op jit(solution)/shard_map/ppermute | solution.py:17
  172.8 9.6 %collective-permute-start.29 = (f32[3,12,20,2]{3,2,1,0:T(8,128)S(1)}, f32[3,12,20,2]{3,2,1,0:T(8,128)S(1)}, u32[]{:S(2)}, u32[]{:S(2)}) collective-permute-start(f32[3,12,20,2]{3,2,1,0:T(8,128)S(1)} %get-tuple-element.15), channel_id=1, source_target_pairs={{1,0},{2,1},{3,2},{5,4},{6,5},{7,6},{9,8},{10,9},{11,10},{13,12},{... | collective-permute-start | bytes 17288 | tf_op jit(solution)/shard_map/ppermute | solution.py:20
  183.0 7.3 %collective-permute-start.30 = (f32[3,2,16,128]{3,2,1,0:T(8,128)S(1)}, f32[3,2,16,128]{3,2,1,0:T(8,128)S(1)}, u32[]{:S(2)}, u32[]{:S(2)}) collective-permute-start(f32[3,2,16,128]{3,2,1,0:T(8,128)S(1)} %get-tuple-element.44), channel_id=1, source_target_pairs={{0,32},{32,64},{64,96},{96,128},{128,160},{160,192},{192,224},{224... | collective-permute-start | bytes 147464 | tf_op jit(solution)/shard_map/ppermute | solution.py:17
  189.0 6.3 %collective-permute-start.31 = (f32[3,2,16,128]{3,2,1,0:T(8,128)S(1)}, f32[3,2,16,128]{3,2,1,0:T(8,128)S(1)}, u32[]{:S(2)}, u32[]{:S(2)}) collective-permute-start(f32[3,2,16,128]{3,2,1,0:T(8,128)S(1)} %get-tuple-element.45), channel_id=1, source_target_pairs={{32,0},{64,32},{96,64},{128,96},{160,128},{192,160},{224,192},{256... | collective-permute-start | bytes 147464 | tf_op jit(solution)/shard_map/ppermute | solution.py:20
  203.4 9.4 %collective-permute-start.34 = (f32[3,12,20,2]{3,2,1,0:T(8,128)S(1)}, f32[3,12,20,2]{3,2,1,0:T(8,128)S(1)}, u32[]{:S(2)}, u32[]{:S(2)}) collective-permute-start(f32[3,12,20,2]{3,2,1,0:T(8,128)S(1)} %get-tuple-element.12), channel_id=1, source_target_pairs={{0,1},{1,2},{2,3},{4,5},{5,6},{6,7},{8,9},{9,10},{10,11},{12,13},{... | collective-permute-start | bytes 17288 | tf_op jit(solution)/shard_map/ppermute | solution.py:17
  207.5 9.6 %collective-permute-start.35 = (f32[3,12,20,2]{3,2,1,0:T(8,128)S(1)}, f32[3,12,20,2]{3,2,1,0:T(8,128)S(1)}, u32[]{:S(2)}, u32[]{:S(2)}) collective-permute-start(f32[3,12,20,2]{3,2,1,0:T(8,128)S(1)} %get-tuple-element.13), channel_id=1, source_target_pairs={{1,0},{2,1},{3,2},{5,4},{6,5},{7,6},{9,8},{10,9},{11,10},{13,12},{... | collective-permute-start | bytes 17288 | tf_op jit(solution)/shard_map/ppermute | solution.py:20
  221.6 6.3 %collective-permute-start.37 = (f32[3,2,16,128]{3,2,1,0:T(8,128)S(1)}, f32[3,2,16,128]{3,2,1,0:T(8,128)S(1)}, u32[]{:S(2)}, u32[]{:S(2)}) collective-permute-start(f32[3,2,16,128]{3,2,1,0:T(8,128)S(1)} %get-tuple-element.43), channel_id=1, source_target_pairs={{32,0},{64,32},{96,64},{128,96},{160,128},{192,160},{224,192},{256... | collective-permute-start | bytes 147464 | tf_op jit(solution)/shard_map/ppermute | solution.py:20
  235.9 9.4 %collective-permute-start.40 = (f32[3,12,20,2]{3,2,1,0:T(8,128)S(1)}, f32[3,12,20,2]{3,2,1,0:T(8,128)S(1)}, u32[]{:S(2)}, u32[]{:S(2)}) collective-permute-start(f32[3,12,20,2]{3,2,1,0:T(8,128)S(1)} %get-tuple-element.10), channel_id=1, source_target_pairs={{0,1},{1,2},{2,3},{4,5},{5,6},{6,7},{8,9},{9,10},{10,11},{12,13},{... | collective-permute-start | bytes 17288 | tf_op jit(solution)/shard_map/ppermute | solution.py:17
  240.1 9.6 %collective-permute-start.41 = (f32[3,12,20,2]{3,2,1,0:T(8,128)S(1)}, f32[3,12,20,2]{3,2,1,0:T(8,128)S(1)}, u32[]{:S(2)}, u32[]{:S(2)}) collective-permute-start(f32[3,12,20,2]{3,2,1,0:T(8,128)S(1)} %get-tuple-element.11), channel_id=1, source_target_pairs={{1,0},{2,1},{3,2},{5,4},{6,5},{7,6},{9,8},{10,9},{11,10},{13,12},{... | collective-permute-start | bytes 17288 | tf_op jit(solution)/shard_map/ppermute | solution.py:20
  254.1 6.3 %collective-permute-start.43 = (f32[3,2,16,128]{3,2,1,0:T(8,128)S(1)}, f32[3,2,16,128]{3,2,1,0:T(8,128)S(1)}, u32[]{:S(2)}, u32[]{:S(2)}) collective-permute-start(f32[3,2,16,128]{3,2,1,0:T(8,128)S(1)} %get-tuple-element.41), channel_id=1, source_target_pairs={{32,0},{64,32},{96,64},{128,96},{160,128},{192,160},{224,192},{256... | collective-permute-start | bytes 147464 | tf_op jit(solution)/shard_map/ppermute | solution.py:20
  268.2 9.4 %collective-permute-start.46 = (f32[3,12,20,2]{3,2,1,0:T(8,128)S(1)}, f32[3,12,20,2]{3,2,1,0:T(8,128)S(1)}, u32[]{:S(2)}, u32[]{:S(2)}) collective-permute-start(f32[3,12,20,2]{3,2,1,0:T(8,128)S(1)} %get-tuple-element.8), channel_id=1, source_target_pairs={{0,1},{1,2},{2,3},{4,5},{5,6},{6,7},{8,9},{9,10},{10,11},{12,13},{... | collective-permute-start | bytes 17288 | tf_op jit(solution)/shard_map/ppermute | solution.py:17
  272.4 9.6 %collective-permute-start.47 = (f32[3,12,20,2]{3,2,1,0:T(8,128)S(1)}, f32[3,12,20,2]{3,2,1,0:T(8,128)S(1)}, u32[]{:S(2)}, u32[]{:S(2)}) collective-permute-start(f32[3,12,20,2]{3,2,1,0:T(8,128)S(1)} %get-tuple-element.9), channel_id=1, source_target_pairs={{1,0},{2,1},{3,2},{5,4},{6,5},{7,6},{9,8},{10,9},{11,10},{13,12},{... | collective-permute-start | bytes 17288 | tf_op jit(solution)/shard_map/ppermute | solution.py:20
  290.0 16.4 %all-to-all-start = ((bf16[24,16,128]{2,0,1:T(8,128)(2,1)}), bf16[24,16,128]{2,0,1:T(8,128)(2,1)S(1)}, u32[]{:S(2)}, u32[]{:S(2)}) async-start(bf16[24,16,128]{2,0,1:T(8,128)(2,1)} %broadcast_select_fusion), calls=%async_computation | async-start | bytes 196608 | tf_op jit(solution)/shard_map/all_to_all | solution.py:84
  297.1 50.7 %all-reduce.2.cloned.1.call-start = ((), (), s32[]{:S(2)}) async-start(), calls=%async_computation.1 | async-start | bytes 1048576 | tf_op jit(solution)/shard_map/psum | solution.py:27
  (32 other events, 500.2 us)
Sparse Core Ops, SparseCore 0:
  307.6 40.1 all-reduce.1
where the time goes:
time: 363 us; the launch traced here: 362 us
  waiting for transfers between devices  180 us (50%)
  starting transfers between devices  142 us (39%)
  local copies, waits for them, and re-layouts  17.4 us (5%)
  between operations  15 us (4%)
  other arithmetic  6.11 us (2%)
    ppermute x24, waiting for transfers between devices, extended_2(): lax.ppermute(lax.slice_in_dim(block, 0, width, axis=dim), axis, backward)  105 us
    ppermute x24, starting transfers between devices, extended_2(): lax.ppermute(lax.slice_in_dim(block, block.shape[dim] - width, None, axis...  98.3 us
    psum x1, waiting for transfers between devices, from_root(): return lax.psum(kept, axis)  39.6 us
    ppermute x24, starting transfers between devices, extended_2(): lax.ppermute(lax.slice_in_dim(block, 0, width, axis=dim), axis, backward)  36.3 us
    ppermute x24, waiting for transfers between devices, extended_2(): lax.ppermute(lax.slice_in_dim(block, block.shape[dim] - width, None, axis...  25.7 us
    all_to_all x1, waiting for transfers between devices, body(): lax.all_to_all(outgoing, 'gx', split_axis=1, concat_axis=1, tiled=True)  9.13 us
  transfers between devices with their start and end apart: 50, of which 34 were waited for; matrix products, arithmetic and copies ran while one was open for 0% of the time, Pallas kernels for 0%

commit v1 on v0

v1 whole, which is shorter than its diff:
```python
import functools

import jax
import jax.numpy as jnp
from jax import lax
from jax.experimental import pallas as pl
from jax.experimental.pallas import tpu as pltpu
from jax.sharding import PartitionSpec as P

STEPS = 8
HALF = 4
DEEP = 2 * HALF
CLASSES = 8
MODES = 8
F32 = jnp.float32
VMEM_LIMIT = 48 * 1024 * 1024

XU, XP, XH = 8, 6, 7
YU, YP, YH = 22, 18, 20


def lane_of():
    return lax.broadcasted_iota(jnp.int32, (8, 128), 1)


def pack_faces(values, lane):
    packed = pltpu.roll(values[0], 8, 1)
    for at in range(1, len(values)):
        packed = jnp.where(lane // 16 == at, pltpu.roll(values[at], (16 * at + 8) % 128, 1), packed)
    return packed


def pack_kernel(u_ref, p_ref, c_ref, d_ref, out_ref):
    lane = lane_of()

    def plane(x, carry):
        for row in (0, 8):
            rows = pl.ds(row, 8)
            values = [u_ref[k, x, rows, :] for k in range(3)] + [p_ref[k, x, rows, :] for k in range(3)]
            values += [c_ref[x, rows, :], d_ref[x, rows, :]]
            out_ref[x, rows, :] = pack_faces(values, lane)
        return carry

    lax.fori_loop(0, 8, plane, 0)


def x_message_kernel(coefficients, *refs):
    if coefficients:
        low_ref, high_ref, u_ref, p_ref, c_ref, d_ref, halo_ref, up_ref, down_ref = refs
    else:
        low_ref, high_ref, u_ref, p_ref, halo_ref, up_ref, down_ref = refs
    lane = lax.broadcasted_iota(jnp.int32, (8, 16, 128), 2)
    halo = jnp.where(lane % 16 < 8, low_ref[...], high_ref[...])
    halo_ref[...] = halo
    at = 0
    for k in range(3):
        up_ref[at : at + 8] = u_ref[k]
        down_ref[at : at + 8] = u_ref[k]
        at += XU
    parts = [p_ref.at[k] for k in range(3)] + ([c_ref, d_ref] if coefficients else [])
    for part in parts:
        up_ref[at : at + XP] = part[8 - XP : 8]
        down_ref[at : at + XP] = part[0:XP]
        at += XP
    up_ref[at : at + XH] = halo[8 - XH : 8]
    down_ref[at : at + XH] = halo[0:XH]


def y_message_kernel(coefficients, *refs):
    if coefficients:
        u_ref, p_ref, c_ref, d_ref, halo_ref, low_ref, high_ref, up_ref, down_ref = refs
    else:
        u_ref, p_ref, halo_ref, low_ref, high_ref, up_ref, down_ref = refs
    parts = [(u_ref.at[k], XU, YU) for k in range(3)] + [(p_ref.at[k], XP, YP) for k in range(3)]
    if coefficients:
        parts += [(c_ref, XP, YP), (d_ref, XP, YP)]
    parts += [(halo_ref, XH, YH)]
    x_at = y_at = 0
    for own, x_planes, y_planes in parts:
        side = (y_planes - 8) // 2
        for out_ref, rows in ((up_ref, slice(8, 16)), (down_ref, slice(0, 8))):
            out_ref[y_at : y_at + side] = low_ref[x_at + x_planes - side : x_at + x_planes, rows, :]
            out_ref[y_at + side : y_at + side + 8] = own[:, rows, :]
            out_ref[y_at + side + 8 : y_at + y_planes] = high_ref[x_at : x_at + side, rows, :]
        x_at += x_planes
        y_at += y_planes


def fill(target, own, x_low, x_high, y_low, y_high, x_at, x_planes, y_at, y_planes):
    target[8 - x_planes : 8, 16:32, :] = x_low[x_at : x_at + x_planes]
    target[8:16, 16:32, :] = own[...]
    target[16 : 16 + x_planes, 16:32, :] = x_high[x_at : x_at + x_planes]
    side = (y_planes - 8) // 2
    target[8 - side : 16 + side, 8:16, :] = y_low[y_at : y_at + y_planes]
    target[8 - side : 16 + side, 32:40, :] = y_high[y_at : y_at + y_planes]


def steps_kernel(first, *refs):
    if first:
        (u_in, p_in, c_in, d_in, halo_in, x_low, x_high, y_low, y_high) = refs[:9]
        (u_out, p_out, face_out, seen_out, a_out, e_out, ha_out, he_out) = refs[9:17]
        u_ref, p_ref, hu_ref, hp_ref, c_ref, d_ref = refs[17:]
        a_ref, e_ref, ha_ref, he_ref = a_out, e_out, ha_out, he_out
    else:
        (u_in, p_in, halo_in, x_low, x_high, y_low, y_high, seen_in, a_ref, e_ref, ha_ref, he_ref) = refs[:12]
        (cells_in, filter_in, count_in) = refs[12:15]
        (u_out, table_out) = refs[15:17]
        u_ref, p_ref, hu_ref, hp_ref, seen_out = refs[17:]
    lane = lane_of()
    low1, low2 = lane == 0, lane < 2
    high1, high2 = lane == 127, lane >= 126
    inner = lane % 16
    up1, up2 = inner == 8, (inner == 8) | (inner == 9)
    down1, down2 = inner == 7, (inner == 7) | (inner == 6)

    x_at = y_at = 0
    for k in range(3):
        fill(u_ref.at[k], u_in.at[k], x_low, x_high, y_low, y_high, x_at, XU, y_at, YU)
        x_at, y_at = x_at + XU, y_at + YU
    for k in range(3):
        fill(p_ref.at[k], p_in.at[k], x_low, x_high, y_low, y_high, x_at, XP, y_at, YP)
        x_at, y_at = x_at + XP, y_at + YP
    if first:
        for target, own in ((c_ref, c_in), (d_ref, d_in)):
            fill(target, own, x_low, x_high, y_low, y_high, x_at, XP, y_at, YP)
            x_at, y_at = x_at + XP, y_at + YP
    fill(hu_ref, halo_in, x_low, x_high, y_low, y_high, x_at, XH, y_at, YH)

    def prepare(x, carry):
        for tile in range(4):
            rows = pl.ds(8 + 8 * tile, 8)
            held = pl.ds(8 * tile, 8)
            halo = hu_ref[x, rows, :]
            hp_ref[x, rows, :] = pltpu.roll(halo, 128 - 48, 1)
            if first:
                share = 1.0 / (1.0 + d_ref[x, rows, :])
                a_ref[x, held, :] = 2.0 * share
                e_ref[x, held, :] = c_ref[x, rows, :] * share * (1.0 / 12.0)
                share = 1.0 / (1.0 + pltpu.roll(halo, 128 - 16, 1))
                for target, value in ((ha_ref, 2.0 * share), (he_ref, halo * share * (1.0 / 12.0))):
                    spread = jnp.where(lane < 16, pltpu.roll(value, 32, 1), pltpu.roll(value, 48, 1))
                    target[x, held, :] = jnp.where(lane < 32, spread, pltpu.roll(value, 64, 1))
        return carry

    lax.fori_loop(2, 22, prepare, 0)

    def update(src, dst, hsrc, hdst, x, tile, with_halo):
        row = 8 + 8 * tile
        rows = pl.ds(row, 8)
        halo = hsrc[x, rows, :]
        a_each = a_ref[x, pl.ds(8 * tile, 8), :]
        e_each = e_ref[x, pl.ds(8 * tile, 8), :]
        centres, fresh = [], []
        for k in range(3):
            v = src[k, x, rows, :]
            beyond = pltpu.roll(halo, (128 - 16 * k - 8) % 128, 1)
            near = pltpu.roll(jnp.where(low1, beyond, v), 127, 1) + pltpu.roll(jnp.where(high1, beyond, v), 1, 1)
            far = pltpu.roll(jnp.where(low2, beyond, v), 126, 1) + pltpu.roll(jnp.where(high2, beyond, v), 2, 1)
            near += (src[k, x - 1, rows, :] + src[k, x + 1, rows, :]) + (
                src[k, x, pl.ds(row - 1, 8), :] + src[k, x, pl.ds(row + 1, 8), :]
            )
            far += (src[k, x - 2, rows, :] + src[k, x + 2, rows, :]) + (
                src[k, x, pl.ds(row - 2, 8), :] + src[k, x, pl.ds(row + 2, 8), :]
            )
            laplace = 16.0 * near - far - 90.0 * v
            old = dst[k, x, rows, :]
            new = old + a_each * (v - old) + e_each * laplace
            dst[k, x, rows, :] = new
            centres.append(v)
            fresh.append(new)
        if with_halo:
            edge = pack_faces(centres, lane)
            near = pltpu.roll(jnp.where(up1, edge, halo), 127, 1) + pltpu.roll(jnp.where(down1, edge, halo), 1, 1)
            far = pltpu.roll(jnp.where(up2, edge, halo), 126, 1) + pltpu.roll(jnp.where(down2, edge, halo), 2, 1)
            near += (hsrc[x - 1, rows, :] + hsrc[x + 1, rows, :]) + (
                hsrc[x, pl.ds(row - 1, 8), :] + hsrc[x, pl.ds(row + 1, 8), :]
            )
            far += (hsrc[x - 2, rows, :] + hsrc[x + 2, rows, :]) + (
                hsrc[x, pl.ds(row - 2, 8), :] + hsrc[x, pl.ds(row + 2, 8), :]
            )
            laplace = 16.0 * near - far - 90.0 * halo
            old = hdst[x, rows, :]
            held = pl.ds(8 * tile, 8)
            hdst[x, rows, :] = old + ha_ref[x, held, :] * (halo - old) + he_ref[x, held, :] * laplace
        return fresh

    def see(x, tile, fresh, step):
        rows = pl.ds(8 * (tile - 1), 8)
        seen = seen_out[x - 8, rows, :]
        for k in range(3):
            seen = jnp.where(lane == 3 * step + k, jnp.broadcast_to(fresh[k][:, 0:1], (8, 128)), seen)
        seen_out[x - 8, rows, :] = seen

    if first:
        seen_out[...] = jnp.zeros((8, 16, 128), F32)
    else:
        seen_out[...] = seen_in[...]
    begin = 0 if first else HALF
    buffers = [(u_ref, hu_ref), (p_ref, hp_ref)]
    for step in range(HALF - 1):
        (src, hsrc), (dst, hdst) = buffers[step % 2], buffers[(step + 1) % 2]

        def outer(x, carry, src=src, dst=dst, hsrc=hsrc, hdst=hdst):
            for tile in range(4):
                update(src, dst, hsrc, hdst, x, tile, True)
            return carry

        def own(x, carry, src=src, dst=dst, hsrc=hsrc, hdst=hdst, step=step):
            for tile in range(4):
                fresh = update(src, dst, hsrc, hdst, x, tile, True)
                if tile in (1, 2):
                    see(x, tile, fresh, begin + step)
            return carry

        lax.fori_loop(2 * step + 2, 8, outer, 0)
        lax.fori_loop(8, 16, own, 0)
        lax.fori_loop(16, 22 - 2 * step, outer, 0)

    (src, hsrc), (dst, hdst) = buffers[1], buffers[0]

    def last(x, carry):
        for tile in (1, 2):
            fresh = update(src, dst, hsrc, hdst, x, tile, False)
            see(x, tile, fresh, begin + HALF - 1)
            rows = pl.ds(8 * (tile - 1), 8)
            for k in range(3):
                u_out[k, x - 8, rows, :] = fresh[k]
            if first:
                before = [src[k, x, pl.ds(8 + 8 * tile, 8), :] for k in range(3)]
                for k in range(3):
                    p_out[k, x - 8, rows, :] = before[k]
                face_out[x - 8, rows, :] = pack_faces(fresh + before, lane)
        return carry

    lax.fori_loop(8, 16, last, 0)

    if not first:
        motion = seen_out[...].reshape(128, 128).astype(jnp.bfloat16)
        modal = lax.dot_general(filter_in[...], motion, (((1,), (1,)), ((), ())), preferred_element_type=F32)
        modes = lax.broadcasted_iota(jnp.int32, (MODES, 128), 0)
        energies = []
        for kind in range(CLASSES):
            part = modal[MODES * kind : MODES * (kind + 1), :]
            part = jnp.where(modes < count_in[kind], part * part, 0.0)
            energies.append(jnp.sum(part, axis=0, keepdims=True))
        demand = 0.5 * jnp.log1p(jnp.concatenate(energies, axis=0))
        for owner in range(table_out.shape[0]):
            cells = jnp.broadcast_to(cells_in[owner : owner + 1, :], (CLASSES, 128))
            chosen = jnp.take_along_axis(demand, cells, axis=1)
            for level in range(table_out.shape[1]):
                table_out[owner, level] = chosen


def fragility_kernel(table_ref, slot_ref, kind_ref, city_ref, amplify_ref, median_ref, spread_ref, out_ref):
    sources = table_ref.shape[0]
    slot, kind, city = slot_ref[...], kind_ref[...], city_ref[...]
    column = slot % 128
    key = (slot // 128) * CLASSES + kind
    demand = jnp.zeros((8, 128), F32)
    for source in range(sources):
        for each in range(CLASSES):
            row = jnp.broadcast_to(table_ref[source, each : each + 1, :], (8, 128))
            found = jnp.take_along_axis(row, column, axis=1)
            demand = jnp.where(key == source * CLASSES + each, found, demand)
    gain = jnp.log(jnp.broadcast_to(amplify_ref[...], (8, 128)))
    demand = demand + jnp.take_along_axis(gain, city, axis=1)
    for group in range(8):
        level = jnp.broadcast_to(demand[group : group + 1, :], (8, 128))
        index = jnp.broadcast_to(kind[group : group + 1, :], (8, 128))
        for half in (0, 8):
            middle = jnp.take_along_axis(median_ref[half : half + 8, :], index, axis=1)
            width = jnp.take_along_axis(spread_ref[half : half + 8, :], index, axis=1)
            out_ref[half : half + 8, 128 * group : 128 * group + 128] = jax.nn.sigmoid((level - middle) / width)


VM = pl.BlockSpec(memory_space=pltpu.VMEM)
SM = pl.BlockSpec(memory_space=pltpu.SMEM)


def call(kernel, name, shapes, args, specs=None, scratch=()):
    out = [jax.ShapeDtypeStruct(s, F32) for s in shapes]
    return pl.pallas_call(
        kernel,
        out_shape=out,
        in_specs=specs or [VM] * len(args),
        out_specs=[VM] * len(out),
        scratch_shapes=list(scratch),
        compiler_params=pltpu.CompilerParams(vmem_limit_bytes=VMEM_LIMIT),
        name=name,
    )(*args)


def both_ways(to_up, to_down, axis):
    count = lax.axis_size(axis)
    forward = [(i, i + 1) for i in range(count - 1)]
    backward = [(i + 1, i) for i in range(count - 1)]
    return lax.ppermute(to_up, axis, forward), lax.ppermute(to_down, axis, backward)


def exchange(u, p, faces, coefficients):
    extra = list(coefficients)
    has = bool(extra)
    z_low, z_high = both_ways(faces, faces, "gz")
    planes = 3 * XU + (3 + len(extra)) * XP + XH
    halo, up, down = call(
        functools.partial(x_message_kernel, has),
        "x_message",
        [(8, 16, 128), (planes, 16, 128), (planes, 16, 128)],
        [z_low, z_high, u, p] + extra,
    )
    x_low, x_high = both_ways(up, down, "gx")
    planes = 3 * YU + (3 + len(extra)) * YP + YH
    up, down = call(
        functools.partial(y_message_kernel, has),
        "y_message",
        [(planes, 8, 128), (planes, 8, 128)],
        [u, p] + extra + [halo, x_low, x_high],
    )
    y_low, y_high = both_ways(up, down, "gy")
    return halo, x_low, x_high, y_low, y_high


def body(
    displacement,
    previous,
    courant,
    damping,
    send_cells,
    building_slot,
    building_class,
    city,
    mode_count,
    modal_filter,
    amplify,
    median,
    spread,
):
    own = (3, 8, 16, 128)
    plane = (8, 16, 128)
    wide = [pltpu.VMEM((3, 24, 48, 128), F32)] * 2 + [pltpu.VMEM((24, 48, 128), F32)] * 2

    (faces,) = call(pack_kernel, "faces", [plane], [displacement, previous, courant, damping])
    received = exchange(displacement, previous, faces, (courant, damping))
    u, p, faces, seen, *coefficients = call(
        functools.partial(steps_kernel, True),
        "steps_first",
        [own, own, plane, plane] + [(24, 32, 128)] * 4,
        [displacement, previous, courant, damping, *received],
        scratch=wide + [pltpu.VMEM((24, 48, 128), F32)] * 2,
    )
    received = exchange(u, p, faces, ())
    owners, levels = lax.axis_size("gx"), lax.axis_size("gz")
    filters = jnp.pad(modal_filter, ((0, 0), (0, 128 - 3 * STEPS)))
    args = [u, p, *received, seen, *coefficients, send_cells.reshape(owners, 128), filters, mode_count]
    field, table = call(
        functools.partial(steps_kernel, False),
        "steps_second",
        [own, (owners, levels, CLASSES, 128)],
        args,
        specs=[VM] * (len(args) - 1) + [SM],
        scratch=wide + [pltpu.VMEM(plane, F32)],
    )
    table = table.reshape(owners * levels, CLASSES, 128)
    table = lax.all_to_all(table, ("gx", "gz"), split_axis=0, concat_axis=0, tiled=True)
    table = table.reshape(owners, levels, CLASSES, 128)[:, 0]
    (probability,) = call(
        fragility_kernel,
        "fragility",
        [(16, 1024)],
        [
            table,
            building_slot.reshape(8, 128),
            building_class.reshape(8, 128),
            city.reshape(8, 128),
            jnp.pad(amplify, (0, 112), constant_values=1.0).reshape(1, 128),
            jnp.pad(median, ((0, 0), (0, 120))),
            jnp.pad(spread, ((0, 0), (0, 120)), constant_values=1.0),
        ],
    )
    return (field, probability)


def solution(mesh):
    placed = (
        P(None, "gx", "gy", "gz"),
        P(None, "gx", "gy", "gz"),
        P("gx", "gy", "gz"),
        P("gx", "gy", "gz"),
        P("gx", "gy", None),
        P(("gx", "gy", "gz")),
        P(("gx", "gy", "gz")),
        P(("gx", "gy", "gz")),
        P(),
        P(),
        P(),
        P(),
        P(),
    )
    return jax.shard_map(
        body,
        mesh=mesh,
        in_specs=placed,
        out_specs=(P(None, "gx", "gy", "gz"), P(None, ("gx", "gy", "gz"))),
        check_vma=False,
    )
```

time: 363 us -> 180 us (0.50)
  starting transfers between devices: 142 us -> 43.7 us
  waiting for transfers between devices: 180 us -> 89 us
  Pallas kernels: 0 us -> 36.1 us
  between operations: 15 us -> 0.88 us
  local copies, waits for them, and re-layouts: 17.4 us -> 9.8 us
  other arithmetic: 6.11 us -> 0 us
    ppermute x48 -> x12, starting transfers between devices: 135 us -> 35.9 us  [the longest x6 22.7 us: both_ways(): lax.ppermute(to_up, axis, forward)]
    ppermute x48 -> x12, waiting for transfers between devices: 131 us -> 78.4 us  [the longest x6 50.7 us: both_ways(): lax.ppermute(to_up, axis, forward)]
    psum x1 -> x0, waiting for transfers between devices: 39.6 us -> none  [from_root(): return lax.psum(kept, axis)]
    pallas_call x0 -> x8, Pallas kernels: none -> 36.1 us  [call(): pl.pallas_call(kernel, out_shape=out, in_specs=specs or [VM] * len(args),...]
    gather x3 -> x0, local copies, waits for them, and re-layouts: 10.4 us -> none  [the longest x2 6.4 us: body(): outgoing = jnp.take(record, send_cells.reshape(-1), axis=1)]
    unnamed x36 -> x43, local copies, waits for them, and re-layouts: 2.18 us -> 9.77 us
    div x8 -> x0, other arithmetic: 4.47 us -> none  [advance(): (2.0 * core - (1.0 - damp_core) * prev_core + rate_core * laplace) / (1.0...]
  transfers between devices with their start and end apart: 50 -> 13, of which waited for: 34 -> 11; matrix products, arithmetic and copies ran while one was open for 0% -> 0% of each run, Pallas kernels for 0% -> 0%
where the time goes in v1:
time: 180 us; the launch traced here: 179 us
  waiting for transfers between devices  89 us (49%)
  starting transfers between devices  43.7 us (24%)
  Pallas kernels  36.1 us (20%)
  local copies, waits for them, and re-layouts  9.8 us (5%)
    ppermute x6, waiting for transfers between devices, both_ways(): lax.ppermute(to_up, axis, forward)  50.7 us
    pallas_call x8, Pallas kernels, call(): pl.pallas_call(kernel, out_shape=out, in_specs=specs or [VM] * len(args),...  36.1 us
    ppermute x6, waiting for transfers between devices, both_ways(): lax.ppermute(to_down, axis, backward)  27.7 us
    ppermute x6, starting transfers between devices, both_ways(): lax.ppermute(to_up, axis, forward)  22.7 us
    ppermute x6, starting transfers between devices, both_ways(): lax.ppermute(to_down, axis, backward)  13.2 us
    all_to_all x1, waiting for transfers between devices, body(): lax.all_to_all(table, ('gx', 'gz'), split_axis=0, concat_axis=0, tiled=True)  10.6 us
    unnamed x43, local copies, waits for them, and re-layouts  9.77 us
    all_to_all x1, starting transfers between devices, body(): lax.all_to_all(table, ('gx', 'gz'), split_axis=0, concat_axis=0, tiled=True)  7.86 us
  transfers between devices with their start and end apart: 13, of which 11 were waited for; matrix products, arithmetic and copies ran while one was open for 0% of the time, Pallas kernels for 0%

profile of v1, /device:TPU:1, one launch (start us, length us, event | category | flops | bytes accessed | tf_op | source)
XLA Modules:
  0.0 179.5 jit_solution(15239470995720119655)
XLA Ops:
  0.6 0.9 copy-done
  1.6 0.9 copy-done.1
  4.8 4.6 %collective-permute-start = (f32[8,16,128]{2,1,0:T(8,128)S(1)}, f32[8,16,128]{2,1,0:T(8,128)S(1)}, u32[]{:S(2)}, u32[]{:S(2)}) collective-permute-start(f32[8,16,128]{2,1,0:T(8,128)S(1)} %faces.1), channel_id=1, source_target_pairs={{0,1},{1,2},{2,3},{4,5},{5,6},{6,7},{8,9},{9,10},{10,11},{12,13},{... | collective-permute-start | bytes 196616 | tf_op jit(solution)/shard_map/ppermute | solution.py:297
  9.4 5.5 %collective-permute-start.1 = (f32[8,16,128]{2,1,0:T(8,128)S(1)}, f32[8,16,128]{2,1,0:T(8,128)S(1)}, u32[]{:S(2)}, u32[]{:S(2)}) collective-permute-start(f32[8,16,128]{2,1,0:T(8,128)S(1)} %faces.1), channel_id=1, source_target_pairs={{1,0},{2,1},{3,2},{5,4},{6,5},{7,6},{9,8},{10,9},{11,10},{13,12},{... | collective-permute-start | bytes 196616 | tf_op jit(solution)/shard_map/ppermute | solution.py:297
  14.9 0.9 collective-permute-done.1.refs_1_
  15.9 3.5 %collective-permute-start.2 = (f32[61,16,128]{2,1,0:T(8,128)S(1)}, f32[61,16,128]{2,1,0:T(8,128)S(1)}, u32[]{:S(2)}, u32[]{:S(2)}) collective-permute-start(f32[61,16,128]{2,1,0:T(8,128)S(1)} %get-tuple-element.23), channel_id=1, source_target_pairs={{0,32},{32,64},{64,96},{96,128},{128,160},{160,192},{192,224},{224... | collective-permute-start | bytes 1499144 | tf_op jit(solution)/shard_map/ppermute | solution.py:297
  19.3 1.3 collective-permute-start.3
  20.6 18.8 %collective-permute-done.2.refs_5_ = f32[61,16,128]{2,1,0:T(8,128)S(1)} collective-permute-done((f32[61,16,128]{2,1,0:T(8,128)S(1)}, f32[61,16,128]{2,1,0:T(8,128)S(1)}, u32[]{:S(2)}, u32[]{:S(2)}) %collective-permute-start.2) | collective-permute-done | bytes 499744 | tf_op jit(solution)/shard_map/ppermute | solution.py:297
  39.5 4.0 %collective-permute-done.3.refs_6_ = f32[61,16,128]{2,1,0:T(8,128)S(1)} collective-permute-done((f32[61,16,128]{2,1,0:T(8,128)S(1)}, f32[61,16,128]{2,1,0:T(8,128)S(1)}, u32[]{:S(2)}, u32[]{:S(2)}) %collective-permute-start.3) | collective-permute-done | bytes 499744 | tf_op jit(solution)/shard_map/ppermute | solution.py:297
  43.6 4.0 %collective-permute-start.4 = (f32[176,8,128]{2,1,0:T(8,128)S(1)}, f32[176,8,128]{2,1,0:T(8,128)S(1)}, u32[]{:S(2)}, u32[]{:S(2)}) collective-permute-start(f32[176,8,128]{2,1,0:T(8,128)S(1)} %get-tuple-element.25), channel_id=1, source_target_pairs={{0,4},{4,8},{8,12},{12,16},{16,20},{20,24},{24,28},{1,5},{5,9},{9,... | collective-permute-start | bytes 2162696 | tf_op jit(solution)/shard_map/ppermute | solution.py:297
  47.6 1.3 collective-permute-start.5
  48.9 13.8 %collective-permute-done.4.refs_7_ = f32[176,8,128]{2,1,0:T(8,128)S(1)} collective-permute-done((f32[176,8,128]{2,1,0:T(8,128)S(1)}, f32[176,8,128]{2,1,0:T(8,128)S(1)}, u32[]{:S(2)}, u32[]{:S(2)}) %collective-permute-start.4) | collective-permute-done | bytes 720928 | tf_op jit(solution)/shard_map/ppermute | solution.py:297
  62.7 4.8 %collective-permute-done.5.refs_8_ = f32[176,8,128]{2,1,0:T(8,128)S(1)} collective-permute-done((f32[176,8,128]{2,1,0:T(8,128)S(1)}, f32[176,8,128]{2,1,0:T(8,128)S(1)}, u32[]{:S(2)}, u32[]{:S(2)}) %collective-permute-start.5) | collective-permute-done | bytes 720928 | tf_op jit(solution)/shard_map/ppermute | solution.py:297
  67.4 17.0 %steps_first.1 = (f32[3,8,16,128]{3,2,1,0:T(8,128)S(1)}, f32[3,8,16,128]{3,2,1,0:T(8,128)S(1)}, f32[8,16,128]{2,1,0:T(8,128)S(1)}, f32[8,16,128]{2,1,0:T(8,128)S...) custom-call(f32[3,8,16,128]{3,2,1,0:T(8,128)S(1)} %copy-done, ...), custom_call_target="tpu_custom_call" | custom-call | tf_op jit(solution)/shard_map/steps_first/pallas_call | solution.py:282
  84.4 1.9 %collective-permute-start.6 = (f32[8,16,128]{2,1,0:T(8,128)S(1)}, f32[8,16,128]{2,1,0:T(8,128)S(1)}, u32[]{:S(2)}, u32[]{:S(2)}) collective-permute-start(f32[8,16,128]{2,1,0:T(8,128)S(1)} %get-tuple-element.29), channel_id=1, source_target_pairs={{0,1},{1,2},{2,3},{4,5},{5,6},{6,7},{8,9},{9,10},{10,11},{12,13},{... | collective-permute-start | bytes 196616 | tf_op jit(solution)/shard_map/ppermute | solution.py:297
  86.4 2.5 %collective-permute-start.7 = (f32[8,16,128]{2,1,0:T(8,128)S(1)}, f32[8,16,128]{2,1,0:T(8,128)S(1)}, u32[]{:S(2)}, u32[]{:S(2)}) collective-permute-start(f32[8,16,128]{2,1,0:T(8,128)S(1)} %get-tuple-element.29), channel_id=1, source_target_pairs={{1,0},{2,1},{3,2},{5,4},{6,5},{7,6},{9,8},{10,9},{11,10},{13,12},{... | collective-permute-start | bytes 196616 | tf_op jit(solution)/shard_map/ppermute | solution.py:297
  88.9 3.1 %collective-permute-done.7.refs_1_ = f32[8,16,128]{2,1,0:T(8,128)S(1)} collective-permute-done((f32[8,16,128]{2,1,0:T(8,128)S(1)}, f32[8,16,128]{2,1,0:T(8,128)S(1)}, u32[]{:S(2)}, u32[]{:S(2)}) %collective-permute-start.7) | collective-permute-done | bytes 65568 | tf_op jit(solution)/shard_map/ppermute | solution.py:297
  92.0 4.7 %collective-permute-start.8 = (f32[49,16,128]{2,1,0:T(8,128)S(1)}, f32[49,16,128]{2,1,0:T(8,128)S(1)}, u32[]{:S(2)}, u32[]{:S(2)}) collective-permute-start(f32[49,16,128]{2,1,0:T(8,128)S(1)} %get-tuple-element.31), channel_id=1, source_target_pairs={{0,32},{32,64},{64,96},{96,128},{128,160},{160,192},{192,224},{224... | collective-permute-start | bytes 1204232 | tf_op jit(solution)/shard_map/ppermute | solution.py:297
  96.7 1.3 collective-permute-start.9
  98.0 6.5 %collective-permute-done.8.refs_3_ = f32[49,16,128]{2,1,0:T(8,128)S(1)} collective-permute-done((f32[49,16,128]{2,1,0:T(8,128)S(1)}, f32[49,16,128]{2,1,0:T(8,128)S(1)}, u32[]{:S(2)}, u32[]{:S(2)}) %collective-permute-start.8) | collective-permute-done | bytes 401440 | tf_op jit(solution)/shard_map/ppermute | solution.py:297
  104.5 9.2 %collective-permute-done.9.refs_4_ = f32[49,16,128]{2,1,0:T(8,128)S(1)} collective-permute-done((f32[49,16,128]{2,1,0:T(8,128)S(1)}, f32[49,16,128]{2,1,0:T(8,128)S(1)}, u32[]{:S(2)}, u32[]{:S(2)}) %collective-permute-start.9) | collective-permute-done | bytes 401440 | tf_op jit(solution)/shard_map/ppermute | solution.py:297
  113.7 1.1 y_message.3
  114.8 4.0 %collective-permute-start.10 = (f32[140,8,128]{2,1,0:T(8,128)}, f32[140,8,128]{2,1,0:T(8,128)S(1)}, u32[]{:S(2)}, u32[]{:S(2)}) collective-permute-start(f32[140,8,128]{2,1,0:T(8,128)} %get-tuple-element.33), channel_id=1, source_target_pairs={{0,4},{4,8},{8,12},{12,16},{16,20},{20,24},{24,28},{1,5},{5,9},{9,... | collective-permute-start | bytes 1720328 | tf_op jit(solution)/shard_map/ppermute | solution.py:297
  118.8 1.3 collective-permute-start.11
  120.3 11.6 %collective-permute-done.10.refs_5_ = f32[140,8,128]{2,1,0:T(8,128)S(1)} collective-permute-done((f32[140,8,128]{2,1,0:T(8,128)}, f32[140,8,128]{2,1,0:T(8,128)S(1)}, u32[]{:S(2)}, u32[]{:S(2)}) %collective-permute-start.10) | collective-permute-done | bytes 573472 | tf_op jit(solution)/shard_map/ppermute | solution.py:297
  131.9 5.9 %collective-permute-done.11.refs_6_ = f32[140,8,128]{2,1,0:T(8,128)S(1)} collective-permute-done((f32[140,8,128]{2,1,0:T(8,128)}, f32[140,8,128]{2,1,0:T(8,128)S(1)}, u32[]{:S(2)}, u32[]{:S(2)}) %collective-permute-start.11) | collective-permute-done | bytes 573472 | tf_op jit(solution)/shard_map/ppermute | solution.py:297
  138.4 1.0 copy-done.5
  139.4 0.8 copy-done.7
  141.1 16.2 %steps_second.1 = (f32[3,8,16,128]{3,2,1,0:T(8,128)}, f32[16,4,8,128]{3,2,1,0:T(8,128)S(1)}) custom-call(f32[3,8,16,128]{3,2,1,0:T(8,128)S(1)} %get-tuple-element.27.refs_2_.refs_0_, f32[3,8,16,128]{3,2,1,0:T(8,128)S(1)} %get-tuple-element.28.refs_3_.refs_1_, f32[8,16,128]{2,1,0:T(8,128)S(1)} %copy-done.7, ...), custom_call_target="tpu_custom_call" | custom-call | tf_op jit(solution)/shard_map/steps_second/pallas_call | solution.py:282
  157.9 7.9 %all-to-all-start = ((f32[64,8,128]{2,1,0:T(8,128)}), f32[64,8,128]{2,1,0:T(8,128)S(1)}, u32[]{:S(2)}, u32[]{:S(2)}) async-start(f32[64,8,128]{2,1,0:T(8,128)} %bitcast.12), calls=%async_computation | async-start | bytes 524288 | tf_op jit(solution)/shard_map/all_to_all | solution.py:364
  167.2 10.6 %all-to-all-done = f32[64,8,128]{2,1,0:T(8,128)S(1)} async-done(((f32[64,8,128]{2,1,0:T(8,128)}), f32[64,8,128]{2,1,0:T(8,128)S(1)}, u32[]{:S(2)}, u32[]{:S(2)}) %all-to-all-start) | async-done | bytes 262176 | tf_op jit(solution)/shard_map/all_to_all | solution.py:364
  178.5 0.9 fragility.1
  (50 shorter events, 7.0 us)
Async XLA Ops:
  0.6 0.9 copy-start
  1.6 0.9 copy-start.1
  2.5 0.8 copy-start.2
  3.3 0.8 copy-start.3
  4.8 10.1 %collective-permute-start = (f32[8,16,128]{2,1,0:T(8,128)S(1)}, f32[8,16,128]{2,1,0:T(8,128)S(1)}, u32[]{:S(2)}, u32[]{:S(2)}) collective-permute-start(f32[8,16,128]{2,1,0:T(8,128)S(1)} %faces.1), channel_id=1, source_target_pairs={{0,1},{1,2},{2,3},{4,5},{5,6},{6,7},{8,9},{9,10},{10,11},{12,13},{... | collective-permute-start | bytes 196616 | tf_op jit(solution)/shard_map/ppermute | solution.py:297
  9.4 6.4 %collective-permute-start.1 = (f32[8,16,128]{2,1,0:T(8,128)S(1)}, f32[8,16,128]{2,1,0:T(8,128)S(1)}, u32[]{:S(2)}, u32[]{:S(2)}) collective-permute-start(f32[8,16,128]{2,1,0:T(8,128)S(1)} %faces.1), channel_id=1, source_target_pairs={{1,0},{2,1},{3,2},{5,4},{6,5},{7,6},{9,8},{10,9},{11,10},{13,12},{... | collective-permute-start | bytes 196616 | tf_op jit(solution)/shard_map/ppermute | solution.py:297
  15.9 23.6 %collective-permute-start.2 = (f32[61,16,128]{2,1,0:T(8,128)S(1)}, f32[61,16,128]{2,1,0:T(8,128)S(1)}, u32[]{:S(2)}, u32[]{:S(2)}) collective-permute-start(f32[61,16,128]{2,1,0:T(8,128)S(1)} %get-tuple-element.23), channel_id=1, source_target_pairs={{0,32},{32,64},{64,96},{96,128},{128,160},{160,192},{192,224},{224... | collective-permute-start | bytes 1499144 | tf_op jit(solution)/shard_map/ppermute | solution.py:297
  19.3 24.1 %collective-permute-start.3 = (f32[61,16,128]{2,1,0:T(8,128)S(1)}, f32[61,16,128]{2,1,0:T(8,128)S(1)}, u32[]{:S(2)}, u32[]{:S(2)}) collective-permute-start(f32[61,16,128]{2,1,0:T(8,128)S(1)} %get-tuple-element.24), channel_id=1, source_target_pairs={{32,0},{64,32},{96,64},{128,96},{160,128},{192,160},{224,192},{256... | collective-permute-start | bytes 1499144 | tf_op jit(solution)/shard_map/ppermute | solution.py:297
  43.6 19.1 %collective-permute-start.4 = (f32[176,8,128]{2,1,0:T(8,128)S(1)}, f32[176,8,128]{2,1,0:T(8,128)S(1)}, u32[]{:S(2)}, u32[]{:S(2)}) collective-permute-start(f32[176,8,128]{2,1,0:T(8,128)S(1)} %get-tuple-element.25), channel_id=1, source_target_pairs={{0,4},{4,8},{8,12},{12,16},{16,20},{20,24},{24,28},{1,5},{5,9},{9,... | collective-permute-start | bytes 2162696 | tf_op jit(solution)/shard_map/ppermute | solution.py:297
  47.6 19.8 %collective-permute-start.5 = (f32[176,8,128]{2,1,0:T(8,128)S(1)}, f32[176,8,128]{2,1,0:T(8,128)S(1)}, u32[]{:S(2)}, u32[]{:S(2)}) collective-permute-start(f32[176,8,128]{2,1,0:T(8,128)S(1)} %get-tuple-element.26), channel_id=1, source_target_pairs={{4,0},{8,4},{12,8},{16,12},{20,16},{24,20},{28,24},{5,1},{9,5},{13... | collective-permute-start | bytes 2162696 | tf_op jit(solution)/shard_map/ppermute | solution.py:297
  84.4 7.6 %copy-start.9 = (f32[8,16,128]{2,1,0:T(8,128)}, f32[8,16,128]{2,1,0:T(8,128)S(1)}, u32[]{:S(2)}) copy-start(f32[8,16,128]{2,1,0:T(8,128)S(1)} %get-tuple-element.35.refs_7_) | copy-start | bytes 196612
  84.4 30.4 %copy-start.4 = (f32[24,32,128]{2,1,0:T(8,128)}, f32[24,32,128]{2,1,0:T(8,128)S(1)}, u32[]{:S(2)}) copy-start(f32[24,32,128]{2,1,0:T(8,128)S(1)} %get-tuple-element.39.refs_11_) | copy-start | bytes 1179652
  84.4 4.4 %collective-permute-start.6 = (f32[8,16,128]{2,1,0:T(8,128)S(1)}, f32[8,16,128]{2,1,0:T(8,128)S(1)}, u32[]{:S(2)}, u32[]{:S(2)}) collective-permute-start(f32[8,16,128]{2,1,0:T(8,128)S(1)} %get-tuple-element.29), channel_id=1, source_target_pairs={{0,1},{1,2},{2,3},{4,5},{5,6},{6,7},{8,9},{9,10},{10,11},{12,13},{... | collective-permute-start | bytes 196616 | tf_op jit(solution)/shard_map/ppermute | solution.py:297
  86.4 5.6 %collective-permute-start.7 = (f32[8,16,128]{2,1,0:T(8,128)S(1)}, f32[8,16,128]{2,1,0:T(8,128)S(1)}, u32[]{:S(2)}, u32[]{:S(2)}) collective-permute-start(f32[8,16,128]{2,1,0:T(8,128)S(1)} %get-tuple-element.29), channel_id=1, source_target_pairs={{1,0},{2,1},{3,2},{5,4},{6,5},{7,6},{9,8},{10,9},{11,10},{13,12},{... | collective-permute-start | bytes 196616 | tf_op jit(solution)/shard_map/ppermute | solution.py:297
  92.0 22.8 %copy-start.6 = (f32[8,16,128]{2,1,0:T(8,128)}, f32[8,16,128]{2,1,0:T(8,128)S(1)}, u32[]{:S(2)}) copy-start(f32[8,16,128]{2,1,0:T(8,128)S(1)} %get-tuple-element.30.refs_2_) | copy-start | bytes 196612
  92.0 12.5 %collective-permute-start.8 = (f32[49,16,128]{2,1,0:T(8,128)S(1)}, f32[49,16,128]{2,1,0:T(8,128)S(1)}, u32[]{:S(2)}, u32[]{:S(2)}) collective-permute-start(f32[49,16,128]{2,1,0:T(8,128)S(1)} %get-tuple-element.31), channel_id=1, source_target_pairs={{0,32},{32,64},{64,96},{96,128},{128,160},{160,192},{192,224},{224... | collective-permute-start | bytes 1204232 | tf_op jit(solution)/shard_map/ppermute | solution.py:297
  96.7 17.0 %collective-permute-start.9 = (f32[49,16,128]{2,1,0:T(8,128)S(1)}, f32[49,16,128]{2,1,0:T(8,128)S(1)}, u32[]{:S(2)}, u32[]{:S(2)}) collective-permute-start(f32[49,16,128]{2,1,0:T(8,128)S(1)} %get-tuple-element.32), channel_id=1, source_target_pairs={{32,0},{64,32},{96,64},{128,96},{160,128},{192,160},{224,192},{256... | collective-permute-start | bytes 1204232 | tf_op jit(solution)/shard_map/ppermute | solution.py:297
  113.7 6.4 %copy-start.16 = (bf16[64,24]{0,1:T(8,128)(2,1)S(1)}, bf16[64,24]{0,1:T(8,128)(2,1)}, u32[]{:S(2)}) copy-start(bf16[64,24]{0,1:T(8,128)(2,1)} %param.22) | copy-start | bytes 9220
  114.8 17.0 %collective-permute-start.10 = (f32[140,8,128]{2,1,0:T(8,128)}, f32[140,8,128]{2,1,0:T(8,128)S(1)}, u32[]{:S(2)}, u32[]{:S(2)}) collective-permute-start(f32[140,8,128]{2,1,0:T(8,128)} %get-tuple-element.33), channel_id=1, source_target_pairs={{0,4},{4,8},{8,12},{12,16},{16,20},{20,24},{24,28},{1,5},{5,9},{9,... | collective-permute-start | bytes 1720328 | tf_op jit(solution)/shard_map/ppermute | solution.py:297
  118.8 18.9 %collective-permute-start.11 = (f32[140,8,128]{2,1,0:T(8,128)}, f32[140,8,128]{2,1,0:T(8,128)S(1)}, u32[]{:S(2)}, u32[]{:S(2)}) collective-permute-start(f32[140,8,128]{2,1,0:T(8,128)} %get-tuple-element.34), channel_id=1, source_target_pairs={{4,0},{8,4},{12,8},{16,12},{20,16},{24,20},{28,24},{5,1},{9,5},{13... | collective-permute-start | bytes 1720328 | tf_op jit(solution)/shard_map/ppermute | solution.py:297
  120.3 17.5 %copy-start.11 = (s32[16,1,128]{2,1,0:T(1,128)S(1)}, s32[16,1,128]{2,1,0:T(1,128)}, u32[]{:S(2)}) copy-start(s32[16,1,128]{2,1,0:T(1,128)} %param.17) | copy-start | bytes 24580
  137.7 0.7 copy-start.15
  138.4 1.0 copy-start.5
  139.4 0.8 copy-start.7
  140.2 0.8 copy-start.10
  157.2 0.7 copy-start.8
  157.9 7.9 %copy-start.17 = (f32[16,8]{0,1:T(8,128)S(1)}, f32[16,8]{0,1:T(8,128)}, u32[]{:S(2)}) copy-start(f32[16,8]{0,1:T(8,128)} %param.24) | copy-start | bytes 1540
  157.9 19.9 %all-to-all-start = ((f32[64,8,128]{2,1,0:T(8,128)}), f32[64,8,128]{2,1,0:T(8,128)S(1)}, u32[]{:S(2)}, u32[]{:S(2)}) async-start(f32[64,8,128]{2,1,0:T(8,128)} %bitcast.12), calls=%async_computation | async-start | bytes 524288 | tf_op jit(solution)/shard_map/all_to_all | solution.py:364
  165.8 0.7 copy-start.18
  177.8 0.7 copy-start.13
  177.8 0.7 copy-start.14
  177.8 0.7 copy-start.12
  (1 other events, 0.7 us)

commit v2 on v1

--- a/solution.py
+++ b/solution.py
@@ -13,7 +13,7 @@
 CLASSES = 8
 MODES = 8
 F32 = jnp.float32
-VMEM_LIMIT = 48 * 1024 * 1024
+VMEM_LIMIT = 24 * 1024 * 1024
 
 XU, XP, XH = 8, 6, 7
 YU, YP, YH = 22, 18, 20
@@ -30,15 +30,26 @@
     return packed
 
 
-def pack_kernel(u_ref, p_ref, c_ref, d_ref, out_ref):
+def start_kernel(u_in, p_in, c_in, d_in, u_ref, p_ref, a_ref, e_ref, face_ref, c_ref, d_ref, sems):
+    copies = [pltpu.make_async_copy(c_in, c_ref, sems.at[0]), pltpu.make_async_copy(d_in, d_ref, sems.at[1])]
+    for k in range(3):
+        copies.append(pltpu.make_async_copy(u_in.at[k], u_ref.at[k], sems.at[2 + k]))
+        copies.append(pltpu.make_async_copy(p_in.at[k], p_ref.at[k], sems.at[5 + k]))
+    for copy in copies:
+        copy.start()
+    for copy in copies:
+        copy.wait()
     lane = lane_of()
 
     def plane(x, carry):
         for row in (0, 8):
             rows = pl.ds(row, 8)
+            share = 1.0 / (1.0 + d_ref[x, rows, :])
             values = [u_ref[k, x, rows, :] for k in range(3)] + [p_ref[k, x, rows, :] for k in range(3)]
-            values += [c_ref[x, rows, :], d_ref[x, rows, :]]
-            out_ref[x, rows, :] = pack_faces(values, lane)
+            values += [2.0 * share, c_ref[x, rows, :] * share * (1.0 / 12.0)]
+            a_ref[x, rows, :] = values[6]
+            e_ref[x, rows, :] = values[7]
+            face_ref[x, rows, :] = pack_faces(values, lane)
         return carry
 
     lax.fori_loop(0, 8, plane, 0)
@@ -86,26 +97,43 @@
         y_at += y_planes
 
 
-def fill(target, own, x_low, x_high, y_low, y_high, x_at, x_planes, y_at, y_planes):
-    target[8 - x_planes : 8, 16:32, :] = x_low[x_at : x_at + x_planes]
-    target[8:16, 16:32, :] = own[...]
-    target[16 : 16 + x_planes, 16:32, :] = x_high[x_at : x_at + x_planes]
-    side = (y_planes - 8) // 2
-    target[8 - side : 16 + side, 8:16, :] = y_low[y_at : y_at + y_planes]
-    target[8 - side : 16 + side, 32:40, :] = y_high[y_at : y_at + y_planes]
+def fill(parts, x_low, x_high, y_low, y_high, x_at, x_planes, y_at, y_planes):
+    count = len(parts)
+
+    def own(i, carry):
+        for (target, row), block in parts:
+            target[8 + i, row + 8 : row + 24, :] = block[i]
+        return carry
+
+    def x_side(i, carry):
+        for at, ((target, row), _) in enumerate(parts):
+            target[8 - x_planes + i, row + 8 : row + 24, :] = x_low[x_at + at * x_planes + i]
+            target[16 + i, row + 8 : row + 24, :] = x_high[x_at + at * x_planes + i]
+        return carry
+
+    def y_side(i, carry):
+        side = (y_planes - 8) // 2
+        for at, ((target, row), _) in enumerate(parts):
+            target[8 - side + i, row : row + 8, :] = y_low[y_at + at * y_planes + i]
+            target[8 - side + i, row + 24 : row + 32, :] = y_high[y_at + at * y_planes + i]
+        return carry
+
+    lax.fori_loop(0, 8, own, 0)
+    lax.fori_loop(0, x_planes, x_side, 0)
+    lax.fori_loop(0, y_planes, y_side, 0)
+    return x_at + count * x_planes, y_at + count * y_planes
 
 
 def steps_kernel(first, *refs):
     if first:
-        (u_in, p_in, c_in, d_in, halo_in, x_low, x_high, y_low, y_high) = refs[:9]
-        (u_out, p_out, face_out, seen_out, a_out, e_out, ha_out, he_out) = refs[9:17]
-        u_ref, p_ref, hu_ref, hp_ref, c_ref, d_ref = refs[17:]
-        a_ref, e_ref, ha_ref, he_ref = a_out, e_out, ha_out, he_out
+        (u_in, p_in, a_in, e_in, halo_in, x_low, x_high, y_low, y_high) = refs[:9]
+        (u_out, p_out, face_out, seen_out, a_ref, e_ref, ha_ref, he_ref) = refs[9:17]
+        state_ref, edge_ref = refs[17:]
     else:
         (u_in, p_in, halo_in, x_low, x_high, y_low, y_high, seen_in, a_ref, e_ref, ha_ref, he_ref) = refs[:12]
         (cells_in, filter_in, count_in) = refs[12:15]
         (u_out, table_out) = refs[15:17]
-        u_ref, p_ref, hu_ref, hp_ref, seen_out = refs[17:]
+        state_ref, edge_ref, seen_out = refs[17:]
     lane = lane_of()
     low1, low2 = lane == 0, lane < 2
     high1, high2 = lane == 127, lane >= 126
@@ -113,126 +141,106 @@
     up1, up2 = inner == 8, (inner == 8) | (inner == 9)
     down1, down2 = inner == 7, (inner == 7) | (inner == 6)
 
-    x_at = y_at = 0
-    for k in range(3):
-        fill(u_ref.at[k], u_in.at[k], x_low, x_high, y_low, y_high, x_at, XU, y_at, YU)
-        x_at, y_at = x_at + XU, y_at + YU
-    for k in range(3):
-        fill(p_ref.at[k], p_in.at[k], x_low, x_high, y_low, y_high, x_at, XP, y_at, YP)
-        x_at, y_at = x_at + XP, y_at + YP
+    sides = (x_low, x_high, y_low, y_high)
+    x_at, y_at = fill([((state_ref.at[0, k], 8), u_in.at[k]) for k in range(3)], *sides, 0, XU, 0, YU)
+    parts = [((state_ref.at[1, k], 8), p_in.at[k]) for k in range(3)]
     if first:
-        for target, own in ((c_ref, c_in), (d_ref, d_in)):
-            fill(target, own, x_low, x_high, y_low, y_high, x_at, XP, y_at, YP)
-            x_at, y_at = x_at + XP, y_at + YP
-    fill(hu_ref, halo_in, x_low, x_high, y_low, y_high, x_at, XH, y_at, YH)
+        parts += [((a_ref, 0), a_in), ((e_ref, 0), e_in)]
+    x_at, y_at = fill(parts, *sides, x_at, XP, y_at, YP)
+    fill([((state_ref.at[0, 3], 8), halo_in)], *sides, x_at, XH, y_at, YH)
 
     def prepare(x, carry):
         for tile in range(4):
             rows = pl.ds(8 + 8 * tile, 8)
             held = pl.ds(8 * tile, 8)
-            halo = hu_ref[x, rows, :]
-            hp_ref[x, rows, :] = pltpu.roll(halo, 128 - 48, 1)
+            halo = state_ref[0, 3, x, rows, :]
+            state_ref[1, 3, x, rows, :] = pltpu.roll(halo, 128 - 48, 1)
             if first:
-                share = 1.0 / (1.0 + d_ref[x, rows, :])
-                a_ref[x, held, :] = 2.0 * share
-                e_ref[x, held, :] = c_ref[x, rows, :] * share * (1.0 / 12.0)
-                share = 1.0 / (1.0 + pltpu.roll(halo, 128 - 16, 1))
-                for target, value in ((ha_ref, 2.0 * share), (he_ref, halo * share * (1.0 / 12.0))):
-                    spread = jnp.where(lane < 16, pltpu.roll(value, 32, 1), pltpu.roll(value, 48, 1))
-                    target[x, held, :] = jnp.where(lane < 32, spread, pltpu.roll(value, 64, 1))
+                for target, at in ((ha_ref, 96), (he_ref, 112)):
+                    spread = jnp.where(lane < 16, pltpu.roll(halo, 128 - at, 1), pltpu.roll(halo, 144 - at, 1))
+                    target[x, held, :] = jnp.where(lane < 32, spread, pltpu.roll(halo, 160 - at, 1))
         return carry
 
     lax.fori_loop(2, 22, prepare, 0)
 
-    def update(src, dst, hsrc, hdst, x, tile, with_halo):
+    def update(src, dst, x, tile):
         row = 8 + 8 * tile
         rows = pl.ds(row, 8)
-        halo = hsrc[x, rows, :]
-        a_each = a_ref[x, pl.ds(8 * tile, 8), :]
-        e_each = e_ref[x, pl.ds(8 * tile, 8), :]
+        held = pl.ds(8 * tile, 8)
+        halo = src[3, 2, rows, :]
+        a_each = a_ref[x, held, :]
+        e_each = e_ref[x, held, :]
         centres, fresh = [], []
+
+        def around(k, near, far):
+            near += (src[k, 1, rows, :] + src[k, 3, rows, :]) + (
+                src[k, 2, pl.ds(row - 1, 8), :] + src[k, 2, pl.ds(row + 1, 8), :]
+            )
+            far += (src[k, 0, rows, :] + src[k, 4, rows, :]) + (
+                src[k, 2, pl.ds(row - 2, 8), :] + src[k, 2, pl.ds(row + 2, 8), :]
+            )
+            return 16.0 * near - far
+
         for k in range(3):
-            v = src[k, x, rows, :]
+            v = src[k, 2, rows, :]
             beyond = pltpu.roll(halo, (128 - 16 * k - 8) % 128, 1)
             near = pltpu.roll(jnp.where(low1, beyond, v), 127, 1) + pltpu.roll(jnp.where(high1, beyond, v), 1, 1)
             far = pltpu.roll(jnp.where(low2, beyond, v), 126, 1) + pltpu.roll(jnp.where(high2, beyond, v), 2, 1)
-            near += (src[k, x - 1, rows, :] + src[k, x + 1, rows, :]) + (
-                src[k, x, pl.ds(row - 1, 8), :] + src[k, x, pl.ds(row + 1, 8), :]
-            )
-            far += (src[k, x - 2, rows, :] + src[k, x + 2, rows, :]) + (
-                src[k, x, pl.ds(row - 2, 8), :] + src[k, x, pl.ds(row + 2, 8), :]
-            )
-            laplace = 16.0 * near - far - 90.0 * v
+            laplace = around(k, near, far) - 90.0 * v
             old = dst[k, x, rows, :]
-            new = old + a_each * (v - old) + e_each * laplace
-            dst[k, x, rows, :] = new
+            fresh.append(old + a_each * (v - old) + e_each * laplace)
             centres.append(v)
-            fresh.append(new)
-        if with_halo:
-            edge = pack_faces(centres, lane)
-            near = pltpu.roll(jnp.where(up1, edge, halo), 127, 1) + pltpu.roll(jnp.where(down1, edge, halo), 1, 1)
-            far = pltpu.roll(jnp.where(up2, edge, halo), 126, 1) + pltpu.roll(jnp.where(down2, edge, halo), 2, 1)
-            near += (hsrc[x - 1, rows, :] + hsrc[x + 1, rows, :]) + (
-                hsrc[x, pl.ds(row - 1, 8), :] + hsrc[x, pl.ds(row + 1, 8), :]
-            )
-            far += (hsrc[x - 2, rows, :] + hsrc[x + 2, rows, :]) + (
-                hsrc[x, pl.ds(row - 2, 8), :] + hsrc[x, pl.ds(row + 2, 8), :]
-            )
-            laplace = 16.0 * near - far - 90.0 * halo
-            old = hdst[x, rows, :]
-            held = pl.ds(8 * tile, 8)
-            hdst[x, rows, :] = old + ha_ref[x, held, :] * (halo - old) + he_ref[x, held, :] * laplace
-        return fresh
-
-    def see(x, tile, fresh, step):
-        rows = pl.ds(8 * (tile - 1), 8)
-        seen = seen_out[x - 8, rows, :]
+        edge = pack_faces(centres, lane)
+        near = pltpu.roll(jnp.where(up1, edge, halo), 127, 1) + pltpu.roll(jnp.where(down1, edge, halo), 1, 1)
+        far = pltpu.roll(jnp.where(up2, edge, halo), 126, 1) + pltpu.roll(jnp.where(down2, edge, halo), 2, 1)
+        laplace = around(3, near, far) - 90.0 * halo
+        old = dst[3, x, rows, :]
+        fresh.append(old + ha_ref[x, held, :] * (halo - old) + he_ref[x, held, :] * laplace)
+        return fresh, edge
+
+    def one_step(step, carry):
+        dst = state_ref.at[(step + 1) % 2]
+
+        def plane(x, inside):
+            src = state_ref.at[step % 2, :, pl.ds(x - 2, 5)]
+            results = [update(src, dst, x, tile) for tile in range(4)]
+            for tile, (fresh, edge) in enumerate(results):
+                for k in range(4):
+                    dst[k, x, 8 + 8 * tile : 16 + 8 * tile, :] = fresh[k]
+                if tile in (1, 2):
+                    edge_ref[step, x, 8 * (tile - 1) : 8 * tile, :] = edge
+            return inside
+
+        lax.fori_loop(2 * step + 2, 22 - 2 * step, plane, 0)
+        return carry
+
+    lax.fori_loop(0, HALF, one_step, 0)
+
+    begin = 0 if first else HALF
+    block = pl.ds(16, 16)
+
+    def finish(x, carry):
         for k in range(3):
-            seen = jnp.where(lane == 3 * step + k, jnp.broadcast_to(fresh[k][:, 0:1], (8, 128)), seen)
-        seen_out[x - 8, rows, :] = seen
-
-    if first:
-        seen_out[...] = jnp.zeros((8, 16, 128), F32)
-    else:
-        seen_out[...] = seen_in[...]
-    begin = 0 if first else HALF
-    buffers = [(u_ref, hu_ref), (p_ref, hp_ref)]
-    for step in range(HALF - 1):
-        (src, hsrc), (dst, hdst) = buffers[step % 2], buffers[(step + 1) % 2]
-
-        def outer(x, carry, src=src, dst=dst, hsrc=hsrc, hdst=hdst):
-            for tile in range(4):
-                update(src, dst, hsrc, hdst, x, tile, True)
-            return carry
-
-        def own(x, carry, src=src, dst=dst, hsrc=hsrc, hdst=hdst, step=step):
-            for tile in range(4):
-                fresh = update(src, dst, hsrc, hdst, x, tile, True)
-                if tile in (1, 2):
-                    see(x, tile, fresh, begin + step)
-            return carry
-
-        lax.fori_loop(2 * step + 2, 8, outer, 0)
-        lax.fori_loop(8, 16, own, 0)
-        lax.fori_loop(16, 22 - 2 * step, outer, 0)
-
-    (src, hsrc), (dst, hdst) = buffers[1], buffers[0]
-
-    def last(x, carry):
-        for tile in (1, 2):
-            fresh = update(src, dst, hsrc, hdst, x, tile, False)
-            see(x, tile, fresh, begin + HALF - 1)
-            rows = pl.ds(8 * (tile - 1), 8)
-            for k in range(3):
-                u_out[k, x - 8, rows, :] = fresh[k]
+            u_out[k, x, :, :] = state_ref[0, k, 8 + x, block, :]
             if first:
-                before = [src[k, x, pl.ds(8 + 8 * tile, 8), :] for k in range(3)]
-                for k in range(3):
-                    p_out[k, x - 8, rows, :] = before[k]
-                face_out[x - 8, rows, :] = pack_faces(fresh + before, lane)
-        return carry
-
-    lax.fori_loop(8, 16, last, 0)
+                p_out[k, x, :, :] = state_ref[1, k, 8 + x, block, :]
+        for row in (0, 8):
+            rows = pl.ds(row, 8)
+            last = pack_faces([state_ref[0, k, 8 + x, pl.ds(16 + row, 8), :] for k in range(3)], lane)
+            if first:
+                after = pack_faces([state_ref[1, k, 8 + x, pl.ds(16 + row, 8), :] for k in range(3)], lane)
+                face_out[x, rows, :] = jnp.where(lane < 48, last, pltpu.roll(after, 48, 1))
+                seen = jnp.zeros((8, 128), F32)
+            else:
+                seen = seen_in[x, rows, :]
+            for step in range(HALF):
+                edge = last if step == HALF - 1 else edge_ref[step + 1, 8 + x, rows, :]
+                at = begin + step
+                seen = jnp.where((inner == 8 + at) & (lane < 48), pltpu.roll(edge, at, 1), seen)
+            seen_out[x, rows, :] = seen
+        return carry
+
+    lax.fori_loop(0, 8, finish, 0)
 
     if not first:
         motion = seen_out[...].reshape(128, 128).astype(jnp.bfloat16)
@@ -337,20 +345,28 @@
 ):
     own = (3, 8, 16, 128)
     plane = (8, 16, 128)
-    wide = [pltpu.VMEM((3, 24, 48, 128), F32)] * 2 + [pltpu.VMEM((24, 48, 128), F32)] * 2
-
-    (faces,) = call(pack_kernel, "faces", [plane], [displacement, previous, courant, damping])
-    received = exchange(displacement, previous, faces, (courant, damping))
+    wide = [pltpu.VMEM((2, 4, 24, 48, 128), F32), pltpu.VMEM((HALF, 24, 16, 128), F32)]
+
+    u, p, a, e, faces = call(
+        start_kernel,
+        "start",
+        [own, own, plane, plane, plane],
+        [displacement, previous, courant, damping],
+        specs=[pl.BlockSpec(memory_space=pltpu.HBM)] * 4,
+        scratch=[pltpu.VMEM(plane, F32)] * 2 + [pltpu.SemaphoreType.DMA((8,))],
+    )
+    received = exchange(u, p, faces, (a, e))
     u, p, faces, seen, *coefficients = call(
         functools.partial(steps_kernel, True),
         "steps_first",
         [own, own, plane, plane] + [(24, 32, 128)] * 4,
-        [displacement, previous, courant, damping, *received],
-        scratch=wide + [pltpu.VMEM((24, 48, 128), F32)] * 2,
+        [u, p, a, e, *received],
+        scratch=wide,
     )
     received = exchange(u, p, faces, ())
     owners, levels = lax.axis_size("gx"), lax.axis_size("gz")
-    filters = jnp.pad(modal_filter, ((0, 0), (0, 128 - 3 * STEPS)))
+    filters = jnp.swapaxes(modal_filter.reshape(CLASSES * MODES, STEPS, 3), 1, 2)
+    filters = jnp.pad(filters, ((0, 0), (0, 5), (16 - STEPS, 0))).reshape(CLASSES * MODES, 128)
     args = [u, p, *received, seen, *coefficients, send_cells.reshape(owners, 128), filters, mode_count]
     field, table = call(
         functools.partial(steps_kernel, False),

time: 180 us -> 181 us (level)
  transfers between devices with their start and end apart: 13 -> 13, of which waited for: 11 -> 11; matrix products, arithmetic and copies ran while one was open for 0% -> 1% of each run, Pallas kernels for 0% -> 0%
where the time goes in v2:
time: 181 us; the launch traced here: 180 us
  waiting for transfers between devices  87.6 us (48%)
  starting transfers between devices  43.7 us (24%)
  Pallas kernels  36.6 us (20%)
  local copies, waits for them, and re-layouts  11.2 us (6%)
    ppermute x6, waiting for transfers between devices, both_ways(): lax.ppermute(to_up, axis, forward)  49.3 us
    pallas_call x8, Pallas kernels, call(): pl.pallas_call(kernel, out_shape=out, in_specs=specs or [VM] * len(args),...  36.6 us
    ppermute x6, waiting for transfers between devices, both_ways(): lax.ppermute(to_down, axis, backward)  27.7 us
    ppermute x6, starting transfers between devices, both_ways(): lax.ppermute(to_up, axis, forward)  22.7 us
    ppermute x6, starting transfers between devices, both_ways(): lax.ppermute(to_down, axis, backward)  13.2 us
    all_to_all x1, waiting for transfers between devices, body(): lax.all_to_all(table, ('gx', 'gz'), split_axis=0, concat_axis=0, tiled=True)  10.6 us
    unnamed x43, local copies, waits for them, and re-layouts  9.69 us
    all_to_all x1, starting transfers between devices, body(): lax.all_to_all(table, ('gx', 'gz'), split_axis=0, concat_axis=0, tiled=True)  7.86 us
  transfers between devices with their start and end apart: 13, of which 11 were waited for; matrix products, arithmetic and copies ran while one was open for 1% of the time, Pallas kernels for 0%

profile of v2, /device:TPU:1, one launch (start us, length us, event | category | flops | bytes accessed | tf_op | source)
XLA Modules:
  0.0 179.9 jit_solution(6452492170183775266)
XLA Ops:
  0.6 0.9 copy-done.5
  1.6 0.9 copy-done.6
  4.2 1.4 start.1
  5.6 4.6 %collective-permute-start = (f32[8,16,128]{2,1,0:T(8,128)S(1)}, f32[8,16,128]{2,1,0:T(8,128)S(1)}, u32[]{:S(2)}, u32[]{:S(2)}) collective-permute-start(f32[8,16,128]{2,1,0:T(8,128)S(1)} %get-tuple-element.31), channel_id=1, source_target_pairs={{0,1},{1,2},{2,3},{4,5},{5,6},{6,7},{8,9},{9,10},{10,11},{12,13},{... | collective-permute-start | bytes 196616 | tf_op jit(solution)/shard_map/ppermute | solution.py:305
  10.2 5.5 %collective-permute-start.1 = (f32[8,16,128]{2,1,0:T(8,128)S(1)}, f32[8,16,128]{2,1,0:T(8,128)S(1)}, u32[]{:S(2)}, u32[]{:S(2)}) collective-permute-start(f32[8,16,128]{2,1,0:T(8,128)S(1)} %get-tuple-element.31), channel_id=1, source_target_pairs={{1,0},{2,1},{3,2},{5,4},{6,5},{7,6},{9,8},{10,9},{11,10},{13,12},{... | collective-permute-start | bytes 196616 | tf_op jit(solution)/shard_map/ppermute | solution.py:305
  15.7 0.9 collective-permute-done.1.refs_1_
  16.6 3.5 %collective-permute-start.2 = (f32[61,16,128]{2,1,0:T(8,128)S(1)}, f32[61,16,128]{2,1,0:T(8,128)S(1)}, u32[]{:S(2)}, u32[]{:S(2)}) collective-permute-start(f32[61,16,128]{2,1,0:T(8,128)S(1)} %get-tuple-element.33), channel_id=1, source_target_pairs={{0,32},{32,64},{64,96},{96,128},{128,160},{160,192},{192,224},{224... | collective-permute-start | bytes 1499144 | tf_op jit(solution)/shard_map/ppermute | solution.py:305
  20.1 1.3 collective-permute-start.3
  21.4 18.8 %collective-permute-done.2.refs_5_ = f32[61,16,128]{2,1,0:T(8,128)S(1)} collective-permute-done((f32[61,16,128]{2,1,0:T(8,128)S(1)}, f32[61,16,128]{2,1,0:T(8,128)S(1)}, u32[]{:S(2)}, u32[]{:S(2)}) %collective-permute-start.2) | collective-permute-done | bytes 499744 | tf_op jit(solution)/shard_map/ppermute | solution.py:305
  40.2 4.0 %collective-permute-done.3.refs_6_ = f32[61,16,128]{2,1,0:T(8,128)S(1)} collective-permute-done((f32[61,16,128]{2,1,0:T(8,128)S(1)}, f32[61,16,128]{2,1,0:T(8,128)S(1)}, u32[]{:S(2)}, u32[]{:S(2)}) %collective-permute-start.3) | collective-permute-done | bytes 499744 | tf_op jit(solution)/shard_map/ppermute | solution.py:305
  44.3 4.0 %collective-permute-start.4 = (f32[176,8,128]{2,1,0:T(8,128)S(1)}, f32[176,8,128]{2,1,0:T(8,128)S(1)}, u32[]{:S(2)}, u32[]{:S(2)}) collective-permute-start(f32[176,8,128]{2,1,0:T(8,128)S(1)} %get-tuple-element.35), channel_id=1, source_target_pairs={{0,4},{4,8},{8,12},{12,16},{16,20},{20,24},{24,28},{1,5},{5,9},{9,... | collective-permute-start | bytes 2162696 | tf_op jit(solution)/shard_map/ppermute | solution.py:305
  48.4 1.3 collective-permute-start.5
  49.7 13.8 %collective-permute-done.4.refs_7_ = f32[176,8,128]{2,1,0:T(8,128)S(1)} collective-permute-done((f32[176,8,128]{2,1,0:T(8,128)S(1)}, f32[176,8,128]{2,1,0:T(8,128)S(1)}, u32[]{:S(2)}, u32[]{:S(2)}) %collective-permute-start.4) | collective-permute-done | bytes 720928 | tf_op jit(solution)/shard_map/ppermute | solution.py:305
  63.4 4.8 %collective-permute-done.5.refs_8_ = f32[176,8,128]{2,1,0:T(8,128)S(1)} collective-permute-done((f32[176,8,128]{2,1,0:T(8,128)S(1)}, f32[176,8,128]{2,1,0:T(8,128)S(1)}, u32[]{:S(2)}, u32[]{:S(2)}) %collective-permute-start.5) | collective-permute-done | bytes 720928 | tf_op jit(solution)/shard_map/ppermute | solution.py:305
  68.2 16.0 %steps_first.1 = (f32[3,8,16,128]{3,2,1,0:T(8,128)S(1)}, f32[3,8,16,128]{3,2,1,0:T(8,128)S(1)}, f32[8,16,128]{2,1,0:T(8,128)S(1)}, f32[8,16,128]{2,1,0:T(8,128)S...) custom-call(f32[3,8,16,128]{3,2,1,0:T(8,128)S(1)} %get-tuple-element, ...), custom_call_target="tpu_custom_call" | custom-call | tf_op jit(solution)/shard_map/steps_first/pallas_call | solution.py:290
  84.2 1.9 %collective-permute-start.6 = (f32[8,16,128]{2,1,0:T(8,128)S(1)}, f32[8,16,128]{2,1,0:T(8,128)S(1)}, u32[]{:S(2)}, u32[]{:S(2)}) collective-permute-start(f32[8,16,128]{2,1,0:T(8,128)S(1)} %get-tuple-element.39), channel_id=1, source_target_pairs={{0,1},{1,2},{2,3},{4,5},{5,6},{6,7},{8,9},{9,10},{10,11},{12,13},{... | collective-permute-start | bytes 196616 | tf_op jit(solution)/shard_map/ppermute | solution.py:305
  86.1 2.5 %collective-permute-start.7 = (f32[8,16,128]{2,1,0:T(8,128)S(1)}, f32[8,16,128]{2,1,0:T(8,128)S(1)}, u32[]{:S(2)}, u32[]{:S(2)}) collective-permute-start(f32[8,16,128]{2,1,0:T(8,128)S(1)} %get-tuple-element.39), channel_id=1, source_target_pairs={{1,0},{2,1},{3,2},{5,4},{6,5},{7,6},{9,8},{10,9},{11,10},{13,12},{... | collective-permute-start | bytes 196616 | tf_op jit(solution)/shard_map/ppermute | solution.py:305
  88.6 3.1 %collective-permute-done.7.refs_1_ = f32[8,16,128]{2,1,0:T(8,128)S(1)} collective-permute-done((f32[8,16,128]{2,1,0:T(8,128)S(1)}, f32[8,16,128]{2,1,0:T(8,128)S(1)}, u32[]{:S(2)}, u32[]{:S(2)}) %collective-permute-start.7) | collective-permute-done | bytes 65568 | tf_op jit(solution)/shard_map/ppermute | solution.py:305
  91.7 4.7 %collective-permute-start.8 = (f32[49,16,128]{2,1,0:T(8,128)S(1)}, f32[49,16,128]{2,1,0:T(8,128)S(1)}, u32[]{:S(2)}, u32[]{:S(2)}) collective-permute-start(f32[49,16,128]{2,1,0:T(8,128)S(1)} %get-tuple-element.41), channel_id=1, source_target_pairs={{0,32},{32,64},{64,96},{96,128},{128,160},{160,192},{192,224},{224... | collective-permute-start | bytes 1204232 | tf_op jit(solution)/shard_map/ppermute | solution.py:305
  96.4 1.3 collective-permute-start.9
  97.7 6.5 %collective-permute-done.8.refs_3_ = f32[49,16,128]{2,1,0:T(8,128)S(1)} collective-permute-done((f32[49,16,128]{2,1,0:T(8,128)S(1)}, f32[49,16,128]{2,1,0:T(8,128)S(1)}, u32[]{:S(2)}, u32[]{:S(2)}) %collective-permute-start.8) | collective-permute-done | bytes 401440 | tf_op jit(solution)/shard_map/ppermute | solution.py:305
  104.2 9.2 %collective-permute-done.9.refs_4_ = f32[49,16,128]{2,1,0:T(8,128)S(1)} collective-permute-done((f32[49,16,128]{2,1,0:T(8,128)S(1)}, f32[49,16,128]{2,1,0:T(8,128)S(1)}, u32[]{:S(2)}, u32[]{:S(2)}) %collective-permute-start.9) | collective-permute-done | bytes 401440 | tf_op jit(solution)/shard_map/ppermute | solution.py:305
  113.4 1.1 y_message.3
  114.6 4.0 %collective-permute-start.10 = (f32[140,8,128]{2,1,0:T(8,128)}, f32[140,8,128]{2,1,0:T(8,128)S(1)}, u32[]{:S(2)}, u32[]{:S(2)}) collective-permute-start(f32[140,8,128]{2,1,0:T(8,128)} %get-tuple-element.43), channel_id=1, source_target_pairs={{0,4},{4,8},{8,12},{12,16},{16,20},{20,24},{24,28},{1,5},{5,9},{9,... | collective-permute-start | bytes 1720328 | tf_op jit(solution)/shard_map/ppermute | solution.py:305
  118.6 1.3 collective-permute-start.11
  121.4 10.2 %collective-permute-done.10.refs_5_ = f32[140,8,128]{2,1,0:T(8,128)S(1)} collective-permute-done((f32[140,8,128]{2,1,0:T(8,128)}, f32[140,8,128]{2,1,0:T(8,128)S(1)}, u32[]{:S(2)}, u32[]{:S(2)}) %collective-permute-start.10) | collective-permute-done | bytes 573472 | tf_op jit(solution)/shard_map/ppermute | solution.py:305
  131.6 5.9 %collective-permute-done.11.refs_6_ = f32[140,8,128]{2,1,0:T(8,128)S(1)} collective-permute-done((f32[140,8,128]{2,1,0:T(8,128)}, f32[140,8,128]{2,1,0:T(8,128)S(1)}, u32[]{:S(2)}, u32[]{:S(2)}) %collective-permute-start.11) | collective-permute-done | bytes 573472 | tf_op jit(solution)/shard_map/ppermute | solution.py:305
  138.1 1.0 copy-done.1
  140.8 16.9 %steps_second.1 = (f32[3,8,16,128]{3,2,1,0:T(8,128)}, f32[16,4,8,128]{3,2,1,0:T(8,128)S(1)}) custom-call(f32[3,8,16,128]{3,2,1,0:T(8,128)S(1)} %get-tuple-element.37.refs_2_.refs_0_, f32[3,8,16,128]{3,2,1,0:T(8,128)S(1)} %get-tuple-element.38.refs_3_.refs_1_, f32[8,16,128]{2,1,0:T(8,128)S(1)} %copy-done.3, ...), custom_call_target="tpu_custom_call" | custom-call | tf_op jit(solution)/shard_map/steps_second/pallas_call | solution.py:290
  158.4 7.9 %all-to-all-start = ((f32[64,8,128]{2,1,0:T(8,128)}), f32[64,8,128]{2,1,0:T(8,128)S(1)}, u32[]{:S(2)}, u32[]{:S(2)}) async-start(f32[64,8,128]{2,1,0:T(8,128)} %bitcast.16), calls=%async_computation | async-start | bytes 524288 | tf_op jit(solution)/shard_map/all_to_all | solution.py:380
  167.7 10.6 %all-to-all-done = f32[64,8,128]{2,1,0:T(8,128)S(1)} async-done(((f32[64,8,128]{2,1,0:T(8,128)}), f32[64,8,128]{2,1,0:T(8,128)S(1)}, u32[]{:S(2)}, u32[]{:S(2)}) %all-to-all-start) | async-done | bytes 262176 | tf_op jit(solution)/shard_map/all_to_all | solution.py:380
  179.0 0.9 fragility.1
  (52 shorter events, 8.6 us)
Async XLA Ops:
  0.6 0.9 copy-start.5
  1.6 0.9 copy-start.6
  2.5 0.8 copy-start.9
  3.3 0.8 copy-start.10
  5.6 10.1 %collective-permute-start = (f32[8,16,128]{2,1,0:T(8,128)S(1)}, f32[8,16,128]{2,1,0:T(8,128)S(1)}, u32[]{:S(2)}, u32[]{:S(2)}) collective-permute-start(f32[8,16,128]{2,1,0:T(8,128)S(1)} %get-tuple-element.31), channel_id=1, source_target_pairs={{0,1},{1,2},{2,3},{4,5},{5,6},{6,7},{8,9},{9,10},{10,11},{12,13},{... | collective-permute-start | bytes 196616 | tf_op jit(solution)/shard_map/ppermute | solution.py:305
  10.2 6.4 %collective-permute-start.1 = (f32[8,16,128]{2,1,0:T(8,128)S(1)}, f32[8,16,128]{2,1,0:T(8,128)S(1)}, u32[]{:S(2)}, u32[]{:S(2)}) collective-permute-start(f32[8,16,128]{2,1,0:T(8,128)S(1)} %get-tuple-element.31), channel_id=1, source_target_pairs={{1,0},{2,1},{3,2},{5,4},{6,5},{7,6},{9,8},{10,9},{11,10},{13,12},{... | collective-permute-start | bytes 196616 | tf_op jit(solution)/shard_map/ppermute | solution.py:305
  16.6 23.6 %collective-permute-start.2 = (f32[61,16,128]{2,1,0:T(8,128)S(1)}, f32[61,16,128]{2,1,0:T(8,128)S(1)}, u32[]{:S(2)}, u32[]{:S(2)}) collective-permute-start(f32[61,16,128]{2,1,0:T(8,128)S(1)} %get-tuple-element.33), channel_id=1, source_target_pairs={{0,32},{32,64},{64,96},{96,128},{128,160},{160,192},{192,224},{224... | collective-permute-start | bytes 1499144 | tf_op jit(solution)/shard_map/ppermute | solution.py:305
  20.1 24.1 %collective-permute-start.3 = (f32[61,16,128]{2,1,0:T(8,128)S(1)}, f32[61,16,128]{2,1,0:T(8,128)S(1)}, u32[]{:S(2)}, u32[]{:S(2)}) collective-permute-start(f32[61,16,128]{2,1,0:T(8,128)S(1)} %get-tuple-element.34), channel_id=1, source_target_pairs={{32,0},{64,32},{96,64},{128,96},{160,128},{192,160},{224,192},{256... | collective-permute-start | bytes 1499144 | tf_op jit(solution)/shard_map/ppermute | solution.py:305
  44.3 19.1 %collective-permute-start.4 = (f32[176,8,128]{2,1,0:T(8,128)S(1)}, f32[176,8,128]{2,1,0:T(8,128)S(1)}, u32[]{:S(2)}, u32[]{:S(2)}) collective-permute-start(f32[176,8,128]{2,1,0:T(8,128)S(1)} %get-tuple-element.35), channel_id=1, source_target_pairs={{0,4},{4,8},{8,12},{12,16},{16,20},{20,24},{24,28},{1,5},{5,9},{9,... | collective-permute-start | bytes 2162696 | tf_op jit(solution)/shard_map/ppermute | solution.py:305
  48.4 19.8 %collective-permute-start.5 = (f32[176,8,128]{2,1,0:T(8,128)S(1)}, f32[176,8,128]{2,1,0:T(8,128)S(1)}, u32[]{:S(2)}, u32[]{:S(2)}) collective-permute-start(f32[176,8,128]{2,1,0:T(8,128)S(1)} %get-tuple-element.36), channel_id=1, source_target_pairs={{4,0},{8,4},{12,8},{16,12},{20,16},{24,20},{28,24},{5,1},{9,5},{13... | collective-permute-start | bytes 2162696 | tf_op jit(solution)/shard_map/ppermute | solution.py:305
  84.2 7.6 %copy-start.7 = (f32[8,16,128]{2,1,0:T(8,128)}, f32[8,16,128]{2,1,0:T(8,128)S(1)}, u32[]{:S(2)}) copy-start(f32[8,16,128]{2,1,0:T(8,128)S(1)} %get-tuple-element.45.refs_7_) | copy-start | bytes 196612
  84.2 30.4 %copy-start = (f32[24,32,128]{2,1,0:T(8,128)}, f32[24,32,128]{2,1,0:T(8,128)S(1)}, u32[]{:S(2)}) copy-start(f32[24,32,128]{2,1,0:T(8,128)S(1)} %get-tuple-element.49.refs_11_) | copy-start | bytes 1179652
  84.2 4.4 %collective-permute-start.6 = (f32[8,16,128]{2,1,0:T(8,128)S(1)}, f32[8,16,128]{2,1,0:T(8,128)S(1)}, u32[]{:S(2)}, u32[]{:S(2)}) collective-permute-start(f32[8,16,128]{2,1,0:T(8,128)S(1)} %get-tuple-element.39), channel_id=1, source_target_pairs={{0,1},{1,2},{2,3},{4,5},{5,6},{6,7},{8,9},{9,10},{10,11},{12,13},{... | collective-permute-start | bytes 196616 | tf_op jit(solution)/shard_map/ppermute | solution.py:305
  86.1 5.6 %collective-permute-start.7 = (f32[8,16,128]{2,1,0:T(8,128)S(1)}, f32[8,16,128]{2,1,0:T(8,128)S(1)}, u32[]{:S(2)}, u32[]{:S(2)}) collective-permute-start(f32[8,16,128]{2,1,0:T(8,128)S(1)} %get-tuple-element.39), channel_id=1, source_target_pairs={{1,0},{2,1},{3,2},{5,4},{6,5},{7,6},{9,8},{10,9},{11,10},{13,12},{... | collective-permute-start | bytes 196616 | tf_op jit(solution)/shard_map/ppermute | solution.py:305
  91.7 22.8 %copy-start.2 = (f32[8,16,128]{2,1,0:T(8,128)}, f32[8,16,128]{2,1,0:T(8,128)S(1)}, u32[]{:S(2)}) copy-start(f32[8,16,128]{2,1,0:T(8,128)S(1)} %get-tuple-element.40.refs_2_) | copy-start | bytes 196612
  91.7 12.5 %collective-permute-start.8 = (f32[49,16,128]{2,1,0:T(8,128)S(1)}, f32[49,16,128]{2,1,0:T(8,128)S(1)}, u32[]{:S(2)}, u32[]{:S(2)}) collective-permute-start(f32[49,16,128]{2,1,0:T(8,128)S(1)} %get-tuple-element.41), channel_id=1, source_target_pairs={{0,32},{32,64},{64,96},{96,128},{128,160},{160,192},{192,224},{224... | collective-permute-start | bytes 1204232 | tf_op jit(solution)/shard_map/ppermute | solution.py:305
  96.4 17.0 %collective-permute-start.9 = (f32[49,16,128]{2,1,0:T(8,128)S(1)}, f32[49,16,128]{2,1,0:T(8,128)S(1)}, u32[]{:S(2)}, u32[]{:S(2)}) collective-permute-start(f32[49,16,128]{2,1,0:T(8,128)S(1)} %get-tuple-element.42), channel_id=1, source_target_pairs={{32,0},{64,32},{96,64},{128,96},{160,128},{192,160},{224,192},{256... | collective-permute-start | bytes 1204232 | tf_op jit(solution)/shard_map/ppermute | solution.py:305
  113.4 6.5 %copy-start.16 = (bf16[64,24]{0,1:T(8,128)(2,1)S(1)}, bf16[64,24]{0,1:T(8,128)(2,1)}, u32[]{:S(2)}) copy-start(bf16[64,24]{0,1:T(8,128)(2,1)} %param.22) | copy-start | bytes 9220
  114.6 17.0 %collective-permute-start.10 = (f32[140,8,128]{2,1,0:T(8,128)}, f32[140,8,128]{2,1,0:T(8,128)S(1)}, u32[]{:S(2)}, u32[]{:S(2)}) collective-permute-start(f32[140,8,128]{2,1,0:T(8,128)} %get-tuple-element.43), channel_id=1, source_target_pairs={{0,4},{4,8},{8,12},{12,16},{16,20},{20,24},{24,28},{1,5},{5,9},{9,... | collective-permute-start | bytes 1720328 | tf_op jit(solution)/shard_map/ppermute | solution.py:305
  118.6 18.9 %collective-permute-start.11 = (f32[140,8,128]{2,1,0:T(8,128)}, f32[140,8,128]{2,1,0:T(8,128)S(1)}, u32[]{:S(2)}, u32[]{:S(2)}) collective-permute-start(f32[140,8,128]{2,1,0:T(8,128)} %get-tuple-element.44), channel_id=1, source_target_pairs={{4,0},{8,4},{12,8},{16,12},{20,16},{24,20},{28,24},{5,1},{9,5},{13... | collective-permute-start | bytes 1720328 | tf_op jit(solution)/shard_map/ppermute | solution.py:305
  121.4 16.1 %copy-start.11 = (s32[16,1,128]{2,1,0:T(1,128)S(1)}, s32[16,1,128]{2,1,0:T(1,128)}, u32[]{:S(2)}) copy-start(s32[16,1,128]{2,1,0:T(1,128)} %param.17) | copy-start | bytes 24580
  137.5 0.7 copy-start.15
  138.1 1.0 copy-start.1
  139.1 0.8 copy-start.3
  139.9 0.8 copy-start.8
  157.7 0.7 copy-start.4
  158.4 7.9 %copy-start.17 = (f32[16,8]{0,1:T(8,128)S(1)}, f32[16,8]{0,1:T(8,128)}, u32[]{:S(2)}) copy-start(f32[16,8]{0,1:T(8,128)} %param.24) | copy-start | bytes 1540
  158.4 19.9 %all-to-all-start = ((f32[64,8,128]{2,1,0:T(8,128)}), f32[64,8,128]{2,1,0:T(8,128)S(1)}, u32[]{:S(2)}, u32[]{:S(2)}) async-start(f32[64,8,128]{2,1,0:T(8,128)} %bitcast.16), calls=%async_computation | async-start | bytes 524288 | tf_op jit(solution)/shard_map/all_to_all | solution.py:380
  166.3 0.7 copy-start.18
  178.3 0.7 copy-start.13
  178.3 0.7 copy-start.14
  178.3 0.7 copy-start.12
  (1 other events, 0.7 us)

commit v3 on v2

--- a/solution.py
+++ b/solution.py
@@ -16,7 +16,12 @@
 VMEM_LIMIT = 24 * 1024 * 1024
 
 XU, XP, XH = 8, 6, 7
-YU, YP, YH = 22, 18, 20
+YU, YP, YH = 24, 20, 20
+
+FULL = 32000.0
+BIAS = 200
+UNIT_A = 2.0 / FULL
+UNIT_E = 0.2 / 12.0 / FULL
 
 
 def lane_of():
@@ -55,85 +60,176 @@
     lax.fori_loop(0, 8, plane, 0)
 
 
+def exponent_of(peak):
+    peak = jnp.maximum(jnp.max(peak, axis=0, keepdims=True), 1e-30)
+    return jnp.broadcast_to(jnp.ceil(jnp.log2(peak)), (8, 128))
+
+
+def coded(values):
+    return jnp.round(values).astype(jnp.int32).astype(jnp.int16)
+
+
+def decoded(values):
+    return values.astype(jnp.int32).astype(F32)
+
+
+def twice(rows):
+    return jnp.concatenate([rows, rows], axis=0)
+
+
+def sent_exponents(message):
+    both = decoded(message[message.shape[0] - 1]) - BIAS
+    return both[0:8], both[8:16]
+
+
 def x_message_kernel(coefficients, *refs):
     if coefficients:
-        low_ref, high_ref, u_ref, p_ref, c_ref, d_ref, halo_ref, up_ref, down_ref = refs
+        low_ref, high_ref, u_ref, p_ref, a_ref, e_ref, halo_ref, up_ref, down_ref, power_ref = refs
     else:
-        low_ref, high_ref, u_ref, p_ref, halo_ref, up_ref, down_ref = refs
-    lane = lax.broadcasted_iota(jnp.int32, (8, 16, 128), 2)
-    halo = jnp.where(lane % 16 < 8, low_ref[...], high_ref[...])
-    halo_ref[...] = halo
-    at = 0
-    for k in range(3):
-        up_ref[at : at + 8] = u_ref[k]
-        down_ref[at : at + 8] = u_ref[k]
-        at += XU
-    parts = [p_ref.at[k] for k in range(3)] + ([c_ref, d_ref] if coefficients else [])
-    for part in parts:
-        up_ref[at : at + XP] = part[8 - XP : 8]
-        down_ref[at : at + XP] = part[0:XP]
-        at += XP
-    up_ref[at : at + XH] = halo[8 - XH : 8]
-    down_ref[at : at + XH] = halo[0:XH]
+        low_ref, high_ref, u_ref, p_ref, halo_ref, up_ref, down_ref, power_ref = refs
+    inner = lax.broadcasted_iota(jnp.int32, (16, 128), 1) % 16
+
+    def largest(x, carry):
+        field, face = carry
+        for k in range(3):
+            both = jnp.maximum(jnp.abs(u_ref[k, x]), jnp.abs(p_ref[k, x]))
+            field = jnp.maximum(field, jnp.maximum(both[0:8], both[8:16]))
+        halo = jnp.where(inner < 8, low_ref[x], high_ref[x])
+        halo_ref[x] = halo
+        halo = jnp.abs(halo)
+        return field, jnp.maximum(face, jnp.maximum(halo[0:8], halo[8:16]))
+
+    zero = jnp.zeros((8, 128), F32)
+    field, face = lax.fori_loop(0, 8, largest, (zero, zero))
+    powers = jnp.concatenate([exponent_of(field), exponent_of(face)], axis=0)
+    power_ref[...] = powers
+    up_ref[up_ref.shape[0] - 1] = coded(powers + BIAS)
+    down_ref[down_ref.shape[0] - 1] = coded(powers + BIAS)
+    scale = FULL * jnp.exp2(-powers)
+    field, face = twice(scale[0:8]), twice(scale[8:16])
+
+    def whole(x, carry):
+        for k in range(3):
+            code = coded(u_ref[k, x] * field)
+            up_ref[XU * k + x] = code
+            down_ref[XU * k + x] = code
+        return carry
+
+    def part(i, carry):
+        parts = [(p_ref.at[k], field) for k in range(3)]
+        if coefficients:
+            parts += [(a_ref, 1.0 / UNIT_A), (e_ref, 1.0 / UNIT_E)]
+        for at, (source, unit) in enumerate(parts):
+            up_ref[3 * XU + XP * at + i] = coded(source[8 - XP + i] * unit)
+            down_ref[3 * XU + XP * at + i] = coded(source[i] * unit)
+        return carry
+
+    at = 3 * XU + (5 if coefficients else 3) * XP
+
+    def side(i, carry):
+        up_ref[at + i] = coded(halo_ref[8 - XH + i] * face)
+        down_ref[at + i] = coded(halo_ref[i] * face)
+        return carry
+
+    lax.fori_loop(0, 8, whole, 0)
+    lax.fori_loop(0, XP, part, 0)
+    lax.fori_loop(0, XH, side, 0)
 
 
 def y_message_kernel(coefficients, *refs):
     if coefficients:
-        u_ref, p_ref, c_ref, d_ref, halo_ref, low_ref, high_ref, up_ref, down_ref = refs
+        u_ref, p_ref, a_ref, e_ref, halo_ref, power_ref, low_ref, high_ref, up_ref, down_ref = refs
     else:
-        u_ref, p_ref, halo_ref, low_ref, high_ref, up_ref, down_ref = refs
-    parts = [(u_ref.at[k], XU, YU) for k in range(3)] + [(p_ref.at[k], XP, YP) for k in range(3)]
+        u_ref, p_ref, halo_ref, power_ref, low_ref, high_ref, up_ref, down_ref = refs
+    powers = power_ref[...]
+    low_powers = jnp.concatenate(sent_exponents(low_ref), axis=0)
+    high_powers = jnp.concatenate(sent_exponents(high_ref), axis=0)
+    most = jnp.maximum(powers, jnp.maximum(low_powers, high_powers))
+    for out_ref in (up_ref, down_ref):
+        out_ref[out_ref.shape[0] - 1] = coded(most + BIAS)
+    own_scale = FULL * jnp.exp2(-most)
+    low_scale = jnp.exp2(low_powers - most)
+    high_scale = jnp.exp2(high_powers - most)
+    field = [twice(scale[0:8]) for scale in (own_scale, low_scale, high_scale)]
+    face = [twice(scale[8:16]) for scale in (own_scale, low_scale, high_scale)]
+
+    def put(at, pair):
+        up_ref[at] = coded(jnp.concatenate([pair[0][8:16], pair[1][8:16]], axis=0))
+        down_ref[at] = coded(jnp.concatenate([pair[0][0:8], pair[1][0:8]], axis=0))
+
+    def group(parts, x_planes, y_planes, x_at, y_at):
+        side = (y_planes - 8) // 4
+
+        def own(i, carry):
+            for at, (source, units) in enumerate(parts):
+                put(y_at + at * y_planes // 2 + side + i, [source[2 * i + j] * units[0] for j in (0, 1)])
+            return carry
+
+        def sides(i, carry):
+            for at, (_, units) in enumerate(parts):
+                start = x_at + at * x_planes
+                first = start + x_planes - 2 * side + 2 * i
+                put(y_at + at * y_planes // 2 + i, [decoded(low_ref[first + j]) * units[1] for j in (0, 1)])
+                first = start + 2 * i
+                pair = [decoded(high_ref[first + j]) * units[2] for j in (0, 1)]
+                put(y_at + at * y_planes // 2 + side + 4 + i, pair)
+            return carry
+
+        lax.fori_loop(0, 4, own, 0)
+        lax.fori_loop(0, side, sides, 0)
+        return x_at + len(parts) * x_planes, y_at + len(parts) * y_planes // 2
+
+    x_at, y_at = group([(u_ref.at[k], field) for k in range(3)], XU, YU, 0, 0)
+    parts = [(p_ref.at[k], field) for k in range(3)]
     if coefficients:
-        parts += [(c_ref, XP, YP), (d_ref, XP, YP)]
-    parts += [(halo_ref, XH, YH)]
-    x_at = y_at = 0
-    for own, x_planes, y_planes in parts:
-        side = (y_planes - 8) // 2
-        for out_ref, rows in ((up_ref, slice(8, 16)), (down_ref, slice(0, 8))):
-            out_ref[y_at : y_at + side] = low_ref[x_at + x_planes - side : x_at + x_planes, rows, :]
-            out_ref[y_at + side : y_at + side + 8] = own[:, rows, :]
-            out_ref[y_at + side + 8 : y_at + y_planes] = high_ref[x_at : x_at + side, rows, :]
-        x_at += x_planes
-        y_at += y_planes
+        parts += [(a_ref, (1.0 / UNIT_A, 1.0, 1.0)), (e_ref, (1.0 / UNIT_E, 1.0, 1.0))]
+    x_at, y_at = group(parts, XP, YP, x_at, y_at)
+    group([(halo_ref, face)], XH, YH, x_at, y_at)
 
 
 def fill(parts, x_low, x_high, y_low, y_high, x_at, x_planes, y_at, y_planes):
     count = len(parts)
+    side = (y_planes - 8) // 2
 
     def own(i, carry):
-        for (target, row), block in parts:
+        for target, row, block, _ in parts:
             target[8 + i, row + 8 : row + 24, :] = block[i]
         return carry
 
     def x_side(i, carry):
-        for at, ((target, row), _) in enumerate(parts):
-            target[8 - x_planes + i, row + 8 : row + 24, :] = x_low[x_at + at * x_planes + i]
-            target[16 + i, row + 8 : row + 24, :] = x_high[x_at + at * x_planes + i]
+        for at, (target, row, _, units) in enumerate(parts):
+            here = x_at + at * x_planes + i
+            target[8 - x_planes + i, row + 8 : row + 24, :] = decoded(x_low[here]) * units[0]
+            target[16 + i, row + 8 : row + 24, :] = decoded(x_high[here]) * units[1]
         return carry
 
     def y_side(i, carry):
-        side = (y_planes - 8) // 2
-        for at, ((target, row), _) in enumerate(parts):
-            target[8 - side + i, row : row + 8, :] = y_low[y_at + at * y_planes + i]
-            target[8 - side + i, row + 24 : row + 32, :] = y_high[y_at + at * y_planes + i]
+        for at, (target, row, _, units) in enumerate(parts):
+            here = y_at + at * y_planes // 2 + i
+            low = decoded(y_low[here]) * units[2]
+            high = decoded(y_high[here]) * units[3]
+            for j in (0, 1):
+                target[8 - side + 2 * i + j, row : row + 8, :] = low[8 * j : 8 * j + 8]
+                target[8 - side + 2 * i + j, row + 24 : row + 32, :] = high[8 * j : 8 * j + 8]
         return carry
 
     lax.fori_loop(0, 8, own, 0)
     lax.fori_loop(0, x_planes, x_side, 0)
-    lax.fori_loop(0, y_planes, y_side, 0)
-    return x_at + count * x_planes, y_at + count * y_planes
+    lax.fori_loop(0, y_planes // 2, y_side, 0)
+    return x_at + count * x_planes, y_at + count * y_planes // 2
 
 
 def steps_kernel(first, *refs):
     if first:
         (u_in, p_in, a_in, e_in, halo_in, x_low, x_high, y_low, y_high) = refs[:9]
-        (u_out, p_out, face_out, seen_out, a_ref, e_ref, ha_ref, he_ref) = refs[9:17]
-        state_ref, edge_ref = refs[17:]
+        (u_out, p_out, face_out, seen_out, rate_ref) = refs[9:14]
+        state_ref, edge_ref = refs[14:]
     else:
-        (u_in, p_in, halo_in, x_low, x_high, y_low, y_high, seen_in, a_ref, e_ref, ha_ref, he_ref) = refs[:12]
-        (cells_in, filter_in, count_in) = refs[12:15]
-        (u_out, table_out) = refs[15:17]
-        state_ref, edge_ref, seen_out = refs[17:]
+        (u_in, p_in, halo_in, x_low, x_high, y_low, y_high, seen_in, rate_ref) = refs[:9]
+        (cells_in, filter_in) = refs[9:11]
+        (u_out, table_out) = refs[11:13]
+        state_ref, edge_ref, seen_out = refs[13:]
+    a_ref, e_ref, ha_ref, he_ref = (rate_ref.at[at] for at in range(4))
     lane = lane_of()
     low1, low2 = lane == 0, lane < 2
     high1, high2 = lane == 127, lane >= 126
@@ -142,12 +238,15 @@
     down1, down2 = inner == 7, (inner == 7) | (inner == 6)
 
     sides = (x_low, x_high, y_low, y_high)
-    x_at, y_at = fill([((state_ref.at[0, k], 8), u_in.at[k]) for k in range(3)], *sides, 0, XU, 0, YU)
-    parts = [((state_ref.at[1, k], 8), p_in.at[k]) for k in range(3)]
+    powers = [sent_exponents(message) for message in sides]
+    field = [twice(jnp.exp2(power[0]) * (1.0 / FULL)) for power in powers]
+    face = [twice(jnp.exp2(power[1]) * (1.0 / FULL)) for power in powers]
+    x_at, y_at = fill([(state_ref.at[0, k], 8, u_in.at[k], field) for k in range(3)], *sides, 0, XU, 0, YU)
+    parts = [(state_ref.at[1, k], 8, p_in.at[k], field) for k in range(3)]
     if first:
-        parts += [((a_ref, 0), a_in), ((e_ref, 0), e_in)]
+        parts += [(a_ref, 0, a_in, (UNIT_A,) * 4), (e_ref, 0, e_in, (UNIT_E,) * 4)]
     x_at, y_at = fill(parts, *sides, x_at, XP, y_at, YP)
-    fill([((state_ref.at[0, 3], 8), halo_in)], *sides, x_at, XH, y_at, YH)
+    fill([(state_ref.at[0, 3], 8, halo_in, face)], *sides, x_at, XH, y_at, YH)
 
     def prepare(x, carry):
         for tile in range(4):
@@ -245,12 +344,10 @@
     if not first:
         motion = seen_out[...].reshape(128, 128).astype(jnp.bfloat16)
         modal = lax.dot_general(filter_in[...], motion, (((1,), (1,)), ((), ())), preferred_element_type=F32)
-        modes = lax.broadcasted_iota(jnp.int32, (MODES, 128), 0)
         energies = []
         for kind in range(CLASSES):
             part = modal[MODES * kind : MODES * (kind + 1), :]
-            part = jnp.where(modes < count_in[kind], part * part, 0.0)
-            energies.append(jnp.sum(part, axis=0, keepdims=True))
+            energies.append(jnp.sum(part * part, axis=0, keepdims=True))
         demand = 0.5 * jnp.log1p(jnp.concatenate(energies, axis=0))
         for owner in range(table_out.shape[0]):
             cells = jnp.broadcast_to(cells_in[owner : owner + 1, :], (CLASSES, 128))
@@ -282,11 +379,10 @@
 
 
 VM = pl.BlockSpec(memory_space=pltpu.VMEM)
-SM = pl.BlockSpec(memory_space=pltpu.SMEM)
 
 
 def call(kernel, name, shapes, args, specs=None, scratch=()):
-    out = [jax.ShapeDtypeStruct(s, F32) for s in shapes]
+    out = [s if isinstance(s, jax.ShapeDtypeStruct) else jax.ShapeDtypeStruct(s, F32) for s in shapes]
     return pl.pallas_call(
         kernel,
         out_shape=out,
@@ -309,20 +405,22 @@
     extra = list(coefficients)
     has = bool(extra)
     z_low, z_high = both_ways(faces, faces, "gz")
-    planes = 3 * XU + (3 + len(extra)) * XP + XH
-    halo, up, down = call(
+    planes = 3 * XU + (3 + len(extra)) * XP + XH + 1
+    message = jax.ShapeDtypeStruct((planes, 16, 128), jnp.int16)
+    halo, up, down, powers = call(
         functools.partial(x_message_kernel, has),
         "x_message",
-        [(8, 16, 128), (planes, 16, 128), (planes, 16, 128)],
+        [(8, 16, 128), message, message, (16, 128)],
         [z_low, z_high, u, p] + extra,
     )
     x_low, x_high = both_ways(up, down, "gx")
-    planes = 3 * YU + (3 + len(extra)) * YP + YH
+    planes = (3 * YU + (3 + len(extra)) * YP + YH) // 2 + 1
+    message = jax.ShapeDtypeStruct((planes, 16, 128), jnp.int16)
     up, down = call(
         functools.partial(y_message_kernel, has),
         "y_message",
-        [(planes, 8, 128), (planes, 8, 128)],
-        [u, p] + extra + [halo, x_low, x_high],
+        [message, message],
+        [u, p] + extra + [halo, powers, x_low, x_high],
     )
     y_low, y_high = both_ways(up, down, "gy")
     return halo, x_low, x_high, y_low, y_high
@@ -356,24 +454,25 @@
         scratch=[pltpu.VMEM(plane, F32)] * 2 + [pltpu.SemaphoreType.DMA((8,))],
     )
     received = exchange(u, p, faces, (a, e))
-    u, p, faces, seen, *coefficients = call(
+    u, p, faces, seen, rates = call(
         functools.partial(steps_kernel, True),
         "steps_first",
-        [own, own, plane, plane] + [(24, 32, 128)] * 4,
+        [own, own, plane, plane, (4, 24, 32, 128)],
         [u, p, a, e, *received],
         scratch=wide,
     )
     received = exchange(u, p, faces, ())
     owners, levels = lax.axis_size("gx"), lax.axis_size("gz")
-    filters = jnp.swapaxes(modal_filter.reshape(CLASSES * MODES, STEPS, 3), 1, 2)
+    used = jnp.arange(MODES)[None, :] < mode_count[:, None]
+    filters = jnp.where(used.reshape(CLASSES * MODES, 1), modal_filter, 0).astype(modal_filter.dtype)
+    filters = jnp.swapaxes(filters.reshape(CLASSES * MODES, STEPS, 3), 1, 2)
     filters = jnp.pad(filters, ((0, 0), (0, 5), (16 - STEPS, 0))).reshape(CLASSES * MODES, 128)
-    args = [u, p, *received, seen, *coefficients, send_cells.reshape(owners, 128), filters, mode_count]
+    args = [u, p, *received, seen, rates, send_cells.reshape(owners, 128), filters]
     field, table = call(
         functools.partial(steps_kernel, False),
         "steps_second",
         [own, (owners, levels, CLASSES, 128)],
         args,
-        specs=[VM] * (len(args) - 1) + [SM],
         scratch=wide + [pltpu.VMEM(plane, F32)],
     )
     table = table.reshape(owners * levels, CLASSES, 128)

time: 181 us -> 146 us (0.81)
  waiting for transfers between devices: 87.6 us -> 58.3 us
  local copies, waits for them, and re-layouts: 11.2 us -> 3.94 us
    ppermute x6, waiting for transfers between devices: 49.3 us -> 23 us  [both_ways(): lax.ppermute(to_up, axis, forward)]
    unnamed x43 -> x29, local copies, waits for them, and re-layouts: 9.69 us -> 3.72 us
    ppermute x6, waiting for transfers between devices: 27.7 us -> 23.5 us  [both_ways(): lax.ppermute(to_down, axis, backward)]
  transfers between devices with their start and end apart: 13 -> 13, of which waited for: 11 -> 11; matrix products, arithmetic and copies ran while one was open for 1% -> 0% of each run, Pallas kernels for 0% -> 0%
where the time goes in v3:
time: 146 us; the launch traced here: 145 us
  waiting for transfers between devices  58.3 us (40%)
  starting transfers between devices  45.2 us (31%)
  Pallas kernels  36.4 us (25%)
  local copies, waits for them, and re-layouts  3.94 us (3%)
    pallas_call x8, Pallas kernels, call(): pl.pallas_call(kernel, out_shape=out, in_specs=specs or [VM] * len(args),...  36.4 us
    ppermute x6, waiting for transfers between devices, both_ways(): lax.ppermute(to_down, axis, backward)  23.5 us
    ppermute x6, starting transfers between devices, both_ways(): lax.ppermute(to_up, axis, forward)  23.1 us
    ppermute x6, waiting for transfers between devices, both_ways(): lax.ppermute(to_up, axis, forward)  23 us
    ppermute x6, starting transfers between devices, both_ways(): lax.ppermute(to_down, axis, backward)  13.3 us
    all_to_all x1, waiting for transfers between devices, body(): lax.all_to_all(table, ('gx', 'gz'), split_axis=0, concat_axis=0, tiled=True)  11.8 us
    all_to_all x1, starting transfers between devices, body(): lax.all_to_all(table, ('gx', 'gz'), split_axis=0, concat_axis=0, tiled=True)  8.8 us
    unnamed x29, local copies, waits for them, and re-layouts  3.72 us
  transfers between devices with their start and end apart: 13, of which 11 were waited for; matrix products, arithmetic and copies ran while one was open for 0% of the time, Pallas kernels for 0%

profile of v3, /device:TPU:1, one launch (start us, length us, event | category | flops | bytes accessed | tf_op | source)
XLA Modules:
  0.0 144.9 jit_solution(17905896157939730298)
XLA Ops:
  0.6 0.9 copy-done
  1.6 0.9 copy-done.1
  2.5 0.8 copy-done.2
  4.2 1.4 start.1
  5.6 4.6 %collective-permute-start = (f32[8,16,128]{2,1,0:T(8,128)S(1)}, f32[8,16,128]{2,1,0:T(8,128)S(1)}, u32[]{:S(2)}, u32[]{:S(2)}) collective-permute-start(f32[8,16,128]{2,1,0:T(8,128)S(1)} %get-tuple-element.30), channel_id=1, source_target_pairs={{0,1},{1,2},{2,3},{4,5},{5,6},{6,7},{8,9},{9,10},{10,11},{12,13},{... | collective-permute-start | bytes 196616 | tf_op jit(solution)/shard_map/ppermute | solution.py:401
  10.2 5.5 %collective-permute-start.1 = (f32[8,16,128]{2,1,0:T(8,128)S(1)}, f32[8,16,128]{2,1,0:T(8,128)S(1)}, u32[]{:S(2)}, u32[]{:S(2)}) collective-permute-start(f32[8,16,128]{2,1,0:T(8,128)S(1)} %get-tuple-element.30), channel_id=1, source_target_pairs={{1,0},{2,1},{3,2},{5,4},{6,5},{7,6},{9,8},{10,9},{11,10},{13,12},{... | collective-permute-start | bytes 196616 | tf_op jit(solution)/shard_map/ppermute | solution.py:401
  15.7 0.9 collective-permute-done.1.refs_1_
  16.8 3.4 %collective-permute-start.2 = (s16[62,16,128]{2,1,0:T(8,128)(2,1)S(1)}, s16[62,16,128]{2,1,0:T(8,128)(2,1)S(1)}, u32[]{:S(2)}, u32[]{:S(2)}) collective-permute-start(s16[62,16,128]{2,1,0:T(8,128)(2,1)S(1)} %get-tuple-element.32), channel_id=1, source_target_pairs={{0,32},{32,64},{64,96},{96,128},{128,160},{160,192},{192,224},{224... | collective-permute-start | bytes 761864 | tf_op jit(solution)/shard_map/ppermute | solution.py:401
  20.3 1.3 collective-permute-start.3
  21.6 8.2 %collective-permute-done.2.refs_6_.refs_5_ = s16[62,16,128]{2,1,0:T(8,128)(2,1)S(1)} collective-permute-done((s16[62,16,128]{2,1,0:T(8,128)(2,1)S(1)}, s16[62,16,128]{2,1,0:T(8,128)(2,1)S(1)}, u32[]{:S(2)}, u32[]{:S(2)}) %collective-permute-start.2) | collective-permute-done | bytes 253984 | tf_op jit(solution)/shard_map/ppermute | solution.py:401
  29.8 3.9 %collective-permute-done.3.refs_7_.refs_6_ = s16[62,16,128]{2,1,0:T(8,128)(2,1)S(1)} collective-permute-done((s16[62,16,128]{2,1,0:T(8,128)(2,1)S(1)}, s16[62,16,128]{2,1,0:T(8,128)(2,1)S(1)}, u32[]{:S(2)}, u32[]{:S(2)}) %collective-permute-start.3) | collective-permute-done | bytes 253984 | tf_op jit(solution)/shard_map/ppermute | solution.py:401
  34.1 4.0 %collective-permute-start.4 = (s16[97,16,128]{2,1,0:T(8,128)(2,1)S(1)}, s16[97,16,128]{2,1,0:T(8,128)(2,1)S(1)}, u32[]{:S(2)}, u32[]{:S(2)}) collective-permute-start(s16[97,16,128]{2,1,0:T(8,128)(2,1)S(1)} %get-tuple-element.35), channel_id=1, source_target_pairs={{0,4},{4,8},{8,12},{12,16},{16,20},{20,24},{24,28},{1,5},{5,9},{9,... | collective-permute-start | bytes 1191944 | tf_op jit(solution)/shard_map/ppermute | solution.py:401
  38.1 1.4 collective-permute-start.5
  39.6 6.7 %collective-permute-done.4.refs_7_ = s16[97,16,128]{2,1,0:T(8,128)(2,1)S(1)} collective-permute-done((s16[97,16,128]{2,1,0:T(8,128)(2,1)S(1)}, s16[97,16,128]{2,1,0:T(8,128)(2,1)S(1)}, u32[]{:S(2)}, u32[]{:S(2)}) %collective-permute-start.4) | collective-permute-done | bytes 397344 | tf_op jit(solution)/shard_map/ppermute | solution.py:401
  46.3 4.9 %collective-permute-done.5.refs_8_ = s16[97,16,128]{2,1,0:T(8,128)(2,1)S(1)} collective-permute-done((s16[97,16,128]{2,1,0:T(8,128)(2,1)S(1)}, s16[97,16,128]{2,1,0:T(8,128)(2,1)S(1)}, u32[]{:S(2)}, u32[]{:S(2)}) %collective-permute-start.5) | collective-permute-done | bytes 397344 | tf_op jit(solution)/shard_map/ppermute | solution.py:401
  51.2 15.9 %steps_first.1 = (f32[3,8,16,128]{3,2,1,0:T(8,128)S(1)}, f32[3,8,16,128]{3,2,1,0:T(8,128)S(1)}, f32[8,16,128]{2,1,0:T(8,128)S(1)}, f32[8,16,128]{2,1,0:T(8,128)S(1)}, f32[4,24,32,128]{3,2,1,0:T(8,128)S(1)}) custom-call(f32[3,8,16,128]{3,2,1,0:T(8,128)S(1)} %get-tuple-element.26.refs_2_.refs_0_, f32[3,8,16,128]{3,2,1,0:T(8,128)S(1)} %get-tuple-element.27.refs_3_.refs_1_, ...), custom_call_target="tpu_custom_call" | custom-call | tf_op jit(solution)/shard_map/steps_first/pallas_call | solution.py:386
  67.0 1.9 %collective-permute-start.6 = (f32[8,16,128]{2,1,0:T(8,128)S(1)}, f32[8,16,128]{2,1,0:T(8,128)S(1)}, u32[]{:S(2)}, u32[]{:S(2)}) collective-permute-start(f32[8,16,128]{2,1,0:T(8,128)S(1)} %get-tuple-element.39), channel_id=1, source_target_pairs={{0,1},{1,2},{2,3},{4,5},{5,6},{6,7},{8,9},{9,10},{10,11},{12,13},{... | collective-permute-start | bytes 196616 | tf_op jit(solution)/shard_map/ppermute | solution.py:401
  69.0 2.5 %collective-permute-start.7 = (f32[8,16,128]{2,1,0:T(8,128)S(1)}, f32[8,16,128]{2,1,0:T(8,128)S(1)}, u32[]{:S(2)}, u32[]{:S(2)}) collective-permute-start(f32[8,16,128]{2,1,0:T(8,128)S(1)} %get-tuple-element.39), channel_id=1, source_target_pairs={{1,0},{2,1},{3,2},{5,4},{6,5},{7,6},{9,8},{10,9},{11,10},{13,12},{... | collective-permute-start | bytes 196616 | tf_op jit(solution)/shard_map/ppermute | solution.py:401
  71.5 3.1 %collective-permute-done.7.refs_1_ = f32[8,16,128]{2,1,0:T(8,128)S(1)} collective-permute-done((f32[8,16,128]{2,1,0:T(8,128)S(1)}, f32[8,16,128]{2,1,0:T(8,128)S(1)}, u32[]{:S(2)}, u32[]{:S(2)}) %collective-permute-start.7) | collective-permute-done | bytes 65568 | tf_op jit(solution)/shard_map/ppermute | solution.py:401
  74.8 5.2 %collective-permute-start.8 = (s16[50,16,128]{2,1,0:T(8,128)(2,1)S(1)}, s16[50,16,128]{2,1,0:T(8,128)(2,1)S(1)}, u32[]{:S(2)}, u32[]{:S(2)}) collective-permute-start(s16[50,16,128]{2,1,0:T(8,128)(2,1)S(1)} %get-tuple-element.41), channel_id=1, source_target_pairs={{0,32},{32,64},{64,96},{96,128},{128,160},{160,192},{192,224},{224... | collective-permute-start | bytes 614408 | tf_op jit(solution)/shard_map/ppermute | solution.py:401
  80.0 1.3 collective-permute-start.9
  81.3 2.2 %collective-permute-done.8.refs_4_.refs_3_ = s16[50,16,128]{2,1,0:T(8,128)(2,1)S(1)} collective-permute-done((s16[50,16,128]{2,1,0:T(8,128)(2,1)S(1)}, s16[50,16,128]{2,1,0:T(8,128)(2,1)S(1)}, u32[]{:S(2)}, u32[]{:S(2)}) %collective-permute-start.8) | collective-permute-done | bytes 204832 | tf_op jit(solution)/shard_map/ppermute | solution.py:401
  83.5 5.2 %collective-permute-done.9.refs_5_.refs_4_ = s16[50,16,128]{2,1,0:T(8,128)(2,1)S(1)} collective-permute-done((s16[50,16,128]{2,1,0:T(8,128)(2,1)S(1)}, s16[50,16,128]{2,1,0:T(8,128)(2,1)S(1)}, u32[]{:S(2)}, u32[]{:S(2)}) %collective-permute-start.9) | collective-permute-done | bytes 204832 | tf_op jit(solution)/shard_map/ppermute | solution.py:401
  88.7 1.0 y_message.3
  89.7 4.0 %collective-permute-start.10 = (s16[77,16,128]{2,1,0:T(8,128)(2,1)}, s16[77,16,128]{2,1,0:T(8,128)(2,1)S(1)}, u32[]{:S(2)}, u32[]{:S(2)}) collective-permute-start(s16[77,16,128]{2,1,0:T(8,128)(2,1)} %get-tuple-element.44), channel_id=1, source_target_pairs={{0,4},{4,8},{8,12},{12,16},{16,20},{20,24},{24,28},{1,5},{5,9},{9,... | collective-permute-start | bytes 946184 | tf_op jit(solution)/shard_map/ppermute | solution.py:401
  93.7 1.3 collective-permute-start.11
  95.3 5.9 %collective-permute-done.10.refs_5_ = s16[77,16,128]{2,1,0:T(8,128)(2,1)S(1)} collective-permute-done((s16[77,16,128]{2,1,0:T(8,128)(2,1)}, s16[77,16,128]{2,1,0:T(8,128)(2,1)S(1)}, u32[]{:S(2)}, u32[]{:S(2)}) %collective-permute-start.10) | collective-permute-done | bytes 315424 | tf_op jit(solution)/shard_map/ppermute | solution.py:401
  101.2 5.5 %collective-permute-done.11.refs_6_ = s16[77,16,128]{2,1,0:T(8,128)(2,1)S(1)} collective-permute-done((s16[77,16,128]{2,1,0:T(8,128)(2,1)S(1)}, s16[77,16,128]{2,1,0:T(8,128)(2,1)S(1)}, u32[]{:S(2)}, u32[]{:S(2)}) %collective-permute-start.11) | collective-permute-done | bytes 315424 | tf_op jit(solution)/shard_map/ppermute | solution.py:401
  106.8 16.4 %steps_second.1 = (f32[3,8,16,128]{3,2,1,0:T(8,128)}, f32[16,4,8,128]{3,2,1,0:T(8,128)}) custom-call(f32[3,8,16,128]{3,2,1,0:T(8,128)S(1)} %get-tuple-element.37.refs_2_.refs_0_, f32[3,8,16,128]{3,2,1,0:T(8,128)S(1)} %get-tuple-element.38.refs_3_.refs_1_, f32[8,16,128]{2,1,0:T(8,128)S(1)} %get-tuple-element.40.refs_2_, ...), custom_call_target="tpu_custom_call" | custom-call | tf_op jit(solution)/shard_map/steps_second/pallas_call | solution.py:386
  123.2 8.8 %all-to-all-start = ((f32[64,8,128]{2,1,0:T(8,128)}), f32[64,8,128]{2,1,0:T(8,128)S(1)}, u32[]{:S(2)}, u32[]{:S(2)}) async-start(f32[64,8,128]{2,1,0:T(8,128)} %bitcast.3), calls=%async_computation | async-start | bytes 524288 | tf_op jit(solution)/shard_map/all_to_all | solution.py:479
  132.2 11.8 %all-to-all-done = f32[64,8,128]{2,1,0:T(8,128)S(1)} async-done(((f32[64,8,128]{2,1,0:T(8,128)}), f32[64,8,128]{2,1,0:T(8,128)S(1)}, u32[]{:S(2)}, u32[]{:S(2)}) %all-to-all-start) | async-done | bytes 262176 | tf_op jit(solution)/shard_map/all_to_all | solution.py:479
  144.0 0.9 fragility.1
  (41 shorter events, 2.2 us)
Async XLA Ops:
  0.6 0.9 copy-start
  1.6 0.9 copy-start.1
  2.5 0.8 copy-start.2
  3.3 0.8 copy-start.3
  5.6 10.1 %collective-permute-start = (f32[8,16,128]{2,1,0:T(8,128)S(1)}, f32[8,16,128]{2,1,0:T(8,128)S(1)}, u32[]{:S(2)}, u32[]{:S(2)}) collective-permute-start(f32[8,16,128]{2,1,0:T(8,128)S(1)} %get-tuple-element.30), channel_id=1, source_target_pairs={{0,1},{1,2},{2,3},{4,5},{5,6},{6,7},{8,9},{9,10},{10,11},{12,13},{... | collective-permute-start | bytes 196616 | tf_op jit(solution)/shard_map/ppermute | solution.py:401
  10.2 6.4 %collective-permute-start.1 = (f32[8,16,128]{2,1,0:T(8,128)S(1)}, f32[8,16,128]{2,1,0:T(8,128)S(1)}, u32[]{:S(2)}, u32[]{:S(2)}) collective-permute-start(f32[8,16,128]{2,1,0:T(8,128)S(1)} %get-tuple-element.30), channel_id=1, source_target_pairs={{1,0},{2,1},{3,2},{5,4},{6,5},{7,6},{9,8},{10,9},{11,10},{13,12},{... | collective-permute-start | bytes 196616 | tf_op jit(solution)/shard_map/ppermute | solution.py:401
  16.8 13.0 %collective-permute-start.2 = (s16[62,16,128]{2,1,0:T(8,128)(2,1)S(1)}, s16[62,16,128]{2,1,0:T(8,128)(2,1)S(1)}, u32[]{:S(2)}, u32[]{:S(2)}) collective-permute-start(s16[62,16,128]{2,1,0:T(8,128)(2,1)S(1)} %get-tuple-element.32), channel_id=1, source_target_pairs={{0,32},{32,64},{64,96},{96,128},{128,160},{160,192},{192,224},{224... | collective-permute-start | bytes 761864 | tf_op jit(solution)/shard_map/ppermute | solution.py:401
  20.3 13.5 %collective-permute-start.3 = (s16[62,16,128]{2,1,0:T(8,128)(2,1)S(1)}, s16[62,16,128]{2,1,0:T(8,128)(2,1)S(1)}, u32[]{:S(2)}, u32[]{:S(2)}) collective-permute-start(s16[62,16,128]{2,1,0:T(8,128)(2,1)S(1)} %get-tuple-element.33), channel_id=1, source_target_pairs={{32,0},{64,32},{96,64},{128,96},{160,128},{192,160},{224,192},{256... | collective-permute-start | bytes 761864 | tf_op jit(solution)/shard_map/ppermute | solution.py:401
  34.1 12.2 %collective-permute-start.4 = (s16[97,16,128]{2,1,0:T(8,128)(2,1)S(1)}, s16[97,16,128]{2,1,0:T(8,128)(2,1)S(1)}, u32[]{:S(2)}, u32[]{:S(2)}) collective-permute-start(s16[97,16,128]{2,1,0:T(8,128)(2,1)S(1)} %get-tuple-element.35), channel_id=1, source_target_pairs={{0,4},{4,8},{8,12},{12,16},{16,20},{20,24},{24,28},{1,5},{5,9},{9,... | collective-permute-start | bytes 1191944 | tf_op jit(solution)/shard_map/ppermute | solution.py:401
  38.1 56.9 %copy-start.11 = (s32[8]{0:T(128)S(1)}, s32[8]{0:T(128)}, u32[]{:S(2)}) copy-start(s32[8]{0:T(128)} %param.21) | copy-start | bytes 100
  38.1 57.1 %copy-start.8 = (bf16[64,24]{0,1:T(8,128)(2,1)S(1)}, bf16[64,24]{0,1:T(8,128)(2,1)}, u32[]{:S(2)}) copy-start(bf16[64,24]{0,1:T(8,128)(2,1)} %param.22) | copy-start | bytes 9220
  38.1 68.6 %copy-start.4 = (s32[16,1,128]{2,1,0:T(1,128)S(1)}, s32[16,1,128]{2,1,0:T(1,128)}, u32[]{:S(2)}) copy-start(s32[16,1,128]{2,1,0:T(1,128)} %param.17) | copy-start | bytes 24580
  38.1 13.0 %collective-permute-start.5 = (s16[97,16,128]{2,1,0:T(8,128)(2,1)S(1)}, s16[97,16,128]{2,1,0:T(8,128)(2,1)S(1)}, u32[]{:S(2)}, u32[]{:S(2)}) collective-permute-start(s16[97,16,128]{2,1,0:T(8,128)(2,1)S(1)} %get-tuple-element.36), channel_id=1, source_target_pairs={{4,0},{8,4},{12,8},{16,12},{20,16},{24,20},{28,24},{5,1},{9,5},{13... | collective-permute-start | bytes 1191944 | tf_op jit(solution)/shard_map/ppermute | solution.py:401
  67.0 4.4 %collective-permute-start.6 = (f32[8,16,128]{2,1,0:T(8,128)S(1)}, f32[8,16,128]{2,1,0:T(8,128)S(1)}, u32[]{:S(2)}, u32[]{:S(2)}) collective-permute-start(f32[8,16,128]{2,1,0:T(8,128)S(1)} %get-tuple-element.39), channel_id=1, source_target_pairs={{0,1},{1,2},{2,3},{4,5},{5,6},{6,7},{8,9},{9,10},{10,11},{12,13},{... | collective-permute-start | bytes 196616 | tf_op jit(solution)/shard_map/ppermute | solution.py:401
  69.0 5.6 %collective-permute-start.7 = (f32[8,16,128]{2,1,0:T(8,128)S(1)}, f32[8,16,128]{2,1,0:T(8,128)S(1)}, u32[]{:S(2)}, u32[]{:S(2)}) collective-permute-start(f32[8,16,128]{2,1,0:T(8,128)S(1)} %get-tuple-element.39), channel_id=1, source_target_pairs={{1,0},{2,1},{3,2},{5,4},{6,5},{7,6},{9,8},{10,9},{11,10},{13,12},{... | collective-permute-start | bytes 196616 | tf_op jit(solution)/shard_map/ppermute | solution.py:401
  74.8 8.7 %collective-permute-start.8 = (s16[50,16,128]{2,1,0:T(8,128)(2,1)S(1)}, s16[50,16,128]{2,1,0:T(8,128)(2,1)S(1)}, u32[]{:S(2)}, u32[]{:S(2)}) collective-permute-start(s16[50,16,128]{2,1,0:T(8,128)(2,1)S(1)} %get-tuple-element.41), channel_id=1, source_target_pairs={{0,32},{32,64},{64,96},{96,128},{128,160},{160,192},{192,224},{224... | collective-permute-start | bytes 614408 | tf_op jit(solution)/shard_map/ppermute | solution.py:401
  80.0 8.7 %collective-permute-start.9 = (s16[50,16,128]{2,1,0:T(8,128)(2,1)S(1)}, s16[50,16,128]{2,1,0:T(8,128)(2,1)S(1)}, u32[]{:S(2)}, u32[]{:S(2)}) collective-permute-start(s16[50,16,128]{2,1,0:T(8,128)(2,1)S(1)} %get-tuple-element.42), channel_id=1, source_target_pairs={{32,0},{64,32},{96,64},{128,96},{160,128},{192,160},{224,192},{256... | collective-permute-start | bytes 614408 | tf_op jit(solution)/shard_map/ppermute | solution.py:401
  89.7 11.5 %collective-permute-start.10 = (s16[77,16,128]{2,1,0:T(8,128)(2,1)}, s16[77,16,128]{2,1,0:T(8,128)(2,1)S(1)}, u32[]{:S(2)}, u32[]{:S(2)}) collective-permute-start(s16[77,16,128]{2,1,0:T(8,128)(2,1)} %get-tuple-element.44), channel_id=1, source_target_pairs={{0,4},{4,8},{8,12},{12,16},{16,20},{20,24},{24,28},{1,5},{5,9},{9,... | collective-permute-start | bytes 946184 | tf_op jit(solution)/shard_map/ppermute | solution.py:401
  93.7 13.0 %collective-permute-start.11 = (s16[77,16,128]{2,1,0:T(8,128)(2,1)S(1)}, s16[77,16,128]{2,1,0:T(8,128)(2,1)S(1)}, u32[]{:S(2)}, u32[]{:S(2)}) collective-permute-start(s16[77,16,128]{2,1,0:T(8,128)(2,1)S(1)} %get-tuple-element.45), channel_id=1, source_target_pairs={{4,0},{8,4},{12,8},{16,12},{20,16},{24,20},{28,24},{5,1},{9,5},{13... | collective-permute-start | bytes 946184 | tf_op jit(solution)/shard_map/ppermute | solution.py:401
  106.7 25.2 %copy-start.9 = (f32[16,8]{0,1:T(8,128)S(1)}, f32[16,8]{0,1:T(8,128)}, u32[]{:S(2)}) copy-start(f32[16,8]{0,1:T(8,128)} %param.24) | copy-start | bytes 1540
  106.7 25.3 %copy-start.10 = (f32[16,8]{0,1:T(8,128)S(1)}, f32[16,8]{0,1:T(8,128)}, u32[]{:S(2)}) copy-start(f32[16,8]{0,1:T(8,128)} %param.25) | copy-start | bytes 1540
  106.7 25.4 %copy-start.12 = (f32[16]{0:T(128)S(1)}, f32[16]{0:T(128)}, u32[]{:S(2)}) copy-start(f32[16]{0:T(128)} %param.23) | copy-start | bytes 196
  106.8 37.2 %copy-start.5 = (s32[1024]{0:T(1024)S(1)}, s32[1024]{0:T(1024)}, u32[]{:S(2)}) copy-start(s32[1024]{0:T(1024)} %param.18) | copy-start | bytes 12292
  106.8 37.2 %copy-start.6 = (s32[1024]{0:T(1024)S(1)}, s32[1024]{0:T(1024)}, u32[]{:S(2)}) copy-start(s32[1024]{0:T(1024)} %param.19) | copy-start | bytes 12292
  106.8 37.2 %copy-start.7 = (s32[1024]{0:T(1024)S(1)}, s32[1024]{0:T(1024)}, u32[]{:S(2)}) copy-start(s32[1024]{0:T(1024)} %param.20) | copy-start | bytes 12292
  123.2 20.8 %all-to-all-start = ((f32[64,8,128]{2,1,0:T(8,128)}), f32[64,8,128]{2,1,0:T(8,128)S(1)}, u32[]{:S(2)}, u32[]{:S(2)}) async-start(f32[64,8,128]{2,1,0:T(8,128)} %bitcast.3), calls=%async_computation | async-start | bytes 524288 | tf_op jit(solution)/shard_map/all_to_all | solution.py:479

commit v4 on v3

--- a/solution.py
+++ b/solution.py
@@ -2,6 +2,7 @@
 
 import jax
 import jax.numpy as jnp
+import numpy as np
 from jax import lax
 from jax.experimental import pallas as pl
 from jax.experimental.pallas import tpu as pltpu
@@ -22,6 +23,23 @@
 BIAS = 200
 UNIT_A = 2.0 / FULL
 UNIT_E = 0.2 / 12.0 / FULL
+
+
+PLANES = 4
+
+
+def depth_weights():
+    lanes = np.arange(256)
+    result = np.zeros((3, 256, 256), np.float32)
+    for k in range(3):
+        at = lanes - 128 - 16 * k
+        depth = np.where(lanes < 128, lanes, np.where(at < 8, at - 8, at + 120))
+        used = (lanes < 128) | ((at >= 0) & (at < 16))
+        apart = np.abs(depth[:, None] - depth[None, :])
+        band = np.where(apart == 0, -90.0, np.where(apart == 1, 16.0, np.where(apart == 2, -1.0, 0.0)))
+        result[k] = np.where(used[:, None] & used[None, :], band, 0.0)
+        result[k, 0, 128 + 64 + 16 * k + 8] = 1.0
+    return result
 
 
 def lane_of():
@@ -213,29 +231,25 @@
                 target[8 - side + 2 * i + j, row + 24 : row + 32, :] = high[8 * j : 8 * j + 8]
         return carry
 
-    lax.fori_loop(0, 8, own, 0)
+    lax.fori_loop(0, 8, own, 0, unroll=2)
     lax.fori_loop(0, x_planes, x_side, 0)
-    lax.fori_loop(0, y_planes // 2, y_side, 0)
+    lax.fori_loop(0, y_planes // 2, y_side, 0, unroll=2)
     return x_at + count * x_planes, y_at + count * y_planes // 2
 
 
 def steps_kernel(first, *refs):
     if first:
-        (u_in, p_in, a_in, e_in, halo_in, x_low, x_high, y_low, y_high) = refs[:9]
-        (u_out, p_out, face_out, seen_out, rate_ref) = refs[9:14]
-        state_ref, edge_ref = refs[14:]
+        (u_in, p_in, a_in, e_in, halo_in, x_low, x_high, y_low, y_high, weight_in) = refs[:10]
+        (u_out, p_out, face_out, seen_out, rate_ref) = refs[10:15]
+        state_ref, edge_ref = refs[15:]
     else:
-        (u_in, p_in, halo_in, x_low, x_high, y_low, y_high, seen_in, rate_ref) = refs[:9]
-        (cells_in, filter_in) = refs[9:11]
-        (u_out, table_out) = refs[11:13]
-        state_ref, edge_ref, seen_out = refs[13:]
+        (u_in, p_in, halo_in, x_low, x_high, y_low, y_high, weight_in, seen_in, rate_ref) = refs[:10]
+        (cells_in, filter_in) = refs[10:12]
+        (u_out, table_out) = refs[12:14]
+        state_ref, edge_ref, seen_out = refs[14:]
     a_ref, e_ref, ha_ref, he_ref = (rate_ref.at[at] for at in range(4))
     lane = lane_of()
-    low1, low2 = lane == 0, lane < 2
-    high1, high2 = lane == 127, lane >= 126
     inner = lane % 16
-    up1, up2 = inner == 8, (inner == 8) | (inner == 9)
-    down1, down2 = inner == 7, (inner == 7) | (inner == 6)
 
     sides = (x_low, x_high, y_low, y_high)
     powers = [sent_exponents(message) for message in sides]
@@ -253,64 +267,61 @@
             rows = pl.ds(8 + 8 * tile, 8)
             held = pl.ds(8 * tile, 8)
             halo = state_ref[0, 3, x, rows, :]
-            state_ref[1, 3, x, rows, :] = pltpu.roll(halo, 128 - 48, 1)
+            state_ref[0, 3, x, rows, :] = jnp.where(lane < 48, halo, 0.0)
+            state_ref[1, 3, x, rows, :] = jnp.where(lane < 48, pltpu.roll(halo, 128 - 48, 1), 0.0)
             if first:
                 for target, at in ((ha_ref, 96), (he_ref, 112)):
                     spread = jnp.where(lane < 16, pltpu.roll(halo, 128 - at, 1), pltpu.roll(halo, 144 - at, 1))
-                    target[x, held, :] = jnp.where(lane < 32, spread, pltpu.roll(halo, 160 - at, 1))
-        return carry
-
-    lax.fori_loop(2, 22, prepare, 0)
-
-    def update(src, dst, x, tile):
-        row = 8 + 8 * tile
-        rows = pl.ds(row, 8)
-        held = pl.ds(8 * tile, 8)
-        halo = src[3, 2, rows, :]
-        a_each = a_ref[x, held, :]
-        e_each = e_ref[x, held, :]
-        centres, fresh = [], []
-
-        def around(k, near, far):
-            near += (src[k, 1, rows, :] + src[k, 3, rows, :]) + (
-                src[k, 2, pl.ds(row - 1, 8), :] + src[k, 2, pl.ds(row + 1, 8), :]
-            )
-            far += (src[k, 0, rows, :] + src[k, 4, rows, :]) + (
-                src[k, 2, pl.ds(row - 2, 8), :] + src[k, 2, pl.ds(row + 2, 8), :]
-            )
-            return 16.0 * near - far
-
+                    spread = jnp.where(lane < 32, spread, pltpu.roll(halo, 160 - at, 1))
+                    target[x, held, :] = jnp.where(lane < 48, spread, 0.0)
+        return carry
+
+    lax.fori_loop(2, 22, prepare, 0, unroll=4)
+
+    def split(v):
+        high = v.astype(jnp.bfloat16)
+        return high, (v - high.astype(F32)).astype(jnp.bfloat16)
+
+    def advance(src, dst, x):
+        rows = pl.ds(8, 32)
+        fields = [[src[k, 2 + j, rows, :] for j in range(PLANES)] for k in range(4)]
+        parts = [[split(v) for v in field] for field in fields]
+        depth = []
         for k in range(3):
-            v = src[k, 2, rows, :]
-            beyond = pltpu.roll(halo, (128 - 16 * k - 8) % 128, 1)
-            near = pltpu.roll(jnp.where(low1, beyond, v), 127, 1) + pltpu.roll(jnp.where(high1, beyond, v), 1, 1)
-            far = pltpu.roll(jnp.where(low2, beyond, v), 126, 1) + pltpu.roll(jnp.where(high2, beyond, v), 2, 1)
-            laplace = around(k, near, far) - 90.0 * v
-            old = dst[k, x, rows, :]
-            fresh.append(old + a_each * (v - old) + e_each * laplace)
-            centres.append(v)
-        edge = pack_faces(centres, lane)
-        near = pltpu.roll(jnp.where(up1, edge, halo), 127, 1) + pltpu.roll(jnp.where(down1, edge, halo), 1, 1)
-        far = pltpu.roll(jnp.where(up2, edge, halo), 126, 1) + pltpu.roll(jnp.where(down2, edge, halo), 2, 1)
-        laplace = around(3, near, far) - 90.0 * halo
-        old = dst[3, x, rows, :]
-        fresh.append(old + ha_ref[x, held, :] * (halo - old) + he_ref[x, held, :] * laplace)
-        return fresh, edge
+            pieces = [jnp.concatenate([parts[k][j][part], parts[3][j][part]], axis=1) for part in (0, 1) for j in range(PLANES)]
+            both = jnp.dot(jnp.concatenate(pieces, axis=0), weight_in[k], preferred_element_type=F32)
+            depth.append(both[0 : 32 * PLANES] + both[32 * PLANES :])
+        side = depth[0][:, 128:] + depth[1][:, 128:] + depth[2][:, 128:]
+        fresh = []
+        for j in range(PLANES):
+            for k in range(4):
+                v = fields[k][j]
+                near = (src[k, 1 + j, rows, :] + src[k, 3 + j, rows, :]) + (
+                    src[k, 2 + j, pl.ds(7, 32), :] + src[k, 2 + j, pl.ds(9, 32), :]
+                )
+                far = (src[k, j, rows, :] + src[k, 4 + j, rows, :]) + (
+                    src[k, 2 + j, pl.ds(6, 32), :] + src[k, 2 + j, pl.ds(10, 32), :]
+                )
+                along = side if k == 3 else depth[k][:, :128]
+                laplace = along[32 * j : 32 * j + 32] + (16.0 * near - far)
+                old = dst[k, x + j, rows, :]
+                a_each, e_each = (ha_ref, he_ref) if k == 3 else (a_ref, e_ref)
+                fresh.append((k, j, old + a_each[x + j] * (v - old) + e_each[x + j] * laplace))
+        return fresh, side
 
     def one_step(step, carry):
         dst = state_ref.at[(step + 1) % 2]
 
-        def plane(x, inside):
-            src = state_ref.at[step % 2, :, pl.ds(x - 2, 5)]
-            results = [update(src, dst, x, tile) for tile in range(4)]
-            for tile, (fresh, edge) in enumerate(results):
-                for k in range(4):
-                    dst[k, x, 8 + 8 * tile : 16 + 8 * tile, :] = fresh[k]
-                if tile in (1, 2):
-                    edge_ref[step, x, 8 * (tile - 1) : 8 * tile, :] = edge
+        def planes(at, inside):
+            x = 2 * step + 2 + PLANES * at
+            fresh, side = advance(state_ref.at[step % 2, :, pl.ds(x - 2, 4 + PLANES)], dst, x)
+            for k, j, value in fresh:
+                dst[k, x + j, 8:40, :] = value
+            for j in range(PLANES):
+                edge_ref[step, x + j, :, :] = side[32 * j + 8 : 32 * j + 24]
             return inside
 
-        lax.fori_loop(2 * step + 2, 22 - 2 * step, plane, 0)
+        lax.fori_loop(0, (20 - 4 * step) // PLANES, planes, 0)
         return carry
 
     lax.fori_loop(0, HALF, one_step, 0)
@@ -333,13 +344,13 @@
             else:
                 seen = seen_in[x, rows, :]
             for step in range(HALF):
-                edge = last if step == HALF - 1 else edge_ref[step + 1, 8 + x, rows, :]
+                edge = pltpu.roll(last, 64, 1) if step == HALF - 1 else edge_ref[step + 1, 8 + x, rows, :]
                 at = begin + step
-                seen = jnp.where((inner == 8 + at) & (lane < 48), pltpu.roll(edge, at, 1), seen)
+                seen = jnp.where((inner == 8 + at) & (lane >= 64) & (lane < 112), pltpu.roll(edge, at, 1), seen)
             seen_out[x, rows, :] = seen
         return carry
 
-    lax.fori_loop(0, 8, finish, 0)
+    lax.fori_loop(0, 8, finish, 0, unroll=4)
 
     if not first:
         motion = seen_out[...].reshape(128, 128).astype(jnp.bfloat16)
@@ -454,11 +465,12 @@
         scratch=[pltpu.VMEM(plane, F32)] * 2 + [pltpu.SemaphoreType.DMA((8,))],
     )
     received = exchange(u, p, faces, (a, e))
+    weights = jnp.asarray(depth_weights(), jnp.bfloat16)
     u, p, faces, seen, rates = call(
         functools.partial(steps_kernel, True),
         "steps_first",
         [own, own, plane, plane, (4, 24, 32, 128)],
-        [u, p, a, e, *received],
+        [u, p, a, e, *received, weights],
         scratch=wide,
     )
     received = exchange(u, p, faces, ())
@@ -466,8 +478,8 @@
     used = jnp.arange(MODES)[None, :] < mode_count[:, None]
     filters = jnp.where(used.reshape(CLASSES * MODES, 1), modal_filter, 0).astype(modal_filter.dtype)
     filters = jnp.swapaxes(filters.reshape(CLASSES * MODES, STEPS, 3), 1, 2)
-    filters = jnp.pad(filters, ((0, 0), (0, 5), (16 - STEPS, 0))).reshape(CLASSES * MODES, 128)
-    args = [u, p, *received, seen, rates, send_cells.reshape(owners, 128), filters]
+    filters = jnp.pad(filters, ((0, 0), (4, 1), (16 - STEPS, 0))).reshape(CLASSES * MODES, 128)
+    args = [u, p, *received, weights, seen, rates, send_cells.reshape(owners, 128), filters]
     field, table = call(
         functools.partial(steps_kernel, False),
         "steps_second",

time: 146 us -> 129 us (0.88)
  Pallas kernels: 36.4 us -> 17.9 us
  local copies, waits for them, and re-layouts: 3.94 us -> 5.52 us
    pallas_call x8, Pallas kernels: 36.4 us -> 17.9 us  [call(): pl.pallas_call(kernel, out_shape=out, in_specs=specs or [VM] * len(args),...]
    unnamed x29 -> x37, local copies, waits for them, and re-layouts: 3.72 us -> 5.31 us
where the time goes in v4:
time: 129 us; the launch traced here: 128 us
  waiting for transfers between devices  58.5 us (45%)
  starting transfers between devices  45.2 us (35%)
  Pallas kernels  17.9 us (14%)
  local copies, waits for them, and re-layouts  5.52 us (4%)
    ppermute x6, waiting for transfers between devices, both_ways(): lax.ppermute(to_down, axis, backward)  23.7 us
    ppermute x6, starting transfers between devices, both_ways(): lax.ppermute(to_up, axis, forward)  23.2 us
    ppermute x6, waiting for transfers between devices, both_ways(): lax.ppermute(to_up, axis, forward)  23 us
    pallas_call x8, Pallas kernels, call(): pl.pallas_call(kernel, out_shape=out, in_specs=specs or [VM] * len(args),...  17.9 us
    ppermute x6, starting transfers between devices, both_ways(): lax.ppermute(to_down, axis, backward)  13.3 us
    all_to_all x1, waiting for transfers between devices, body(): lax.all_to_all(table, ('gx', 'gz'), split_axis=0, concat_axis=0, tiled=True)  11.8 us
    all_to_all x1, starting transfers between devices, body(): lax.all_to_all(table, ('gx', 'gz'), split_axis=0, concat_axis=0, tiled=True)  8.8 us
    unnamed x37, local copies, waits for them, and re-layouts  5.31 us
  transfers between devices with their start and end apart: 13, of which 11 were waited for; matrix products, arithmetic and copies ran while one was open for 0% of the time, Pallas kernels for 0%

profile of v4, /device:TPU:1, one launch (start us, length us, event | category | flops | bytes accessed | tf_op | source)
XLA Modules:
  0.0 128.3 jit_solution(7885955428980772386)
XLA Ops:
  0.7 1.0 copy-done.2
  1.6 0.9 copy-done.3
  4.2 1.4 %start.1 = (f32[3,8,16,128]{3,2,1,0:T(8,128)S(1)}, f32[3,8,16,128]{3,2,1,0:T(8,128)S(1)}, f32[8,16,128]{2,1,0:T(8,128)S(1)}, f32[8,16,128]{2,1,0:T(8,128)S(1)}, f32[8,16,128]{2,1,0:T(8,128)S(1)}) custom-call(f32[3,8,16,128]{3,2,1,0:T(8,128)S(1)} %copy-done.2, f32[3,8,16,128]{3,2,1,0:T(8,128)S(1)} %copy-done.3, f32[8,16,128]{2,1,0:T(8,128)S(1)} %copy-done.6, ...), custom_call_target="tpu_custom_call" | custom-call | tf_op jit(solution)/shard_map/start/pallas_call | solution.py:397
  5.6 4.6 %collective-permute-start = (f32[8,16,128]{2,1,0:T(8,128)S(1)}, f32[8,16,128]{2,1,0:T(8,128)S(1)}, u32[]{:S(2)}, u32[]{:S(2)}) collective-permute-start(f32[8,16,128]{2,1,0:T(8,128)S(1)} %get-tuple-element.30), channel_id=1, source_target_pairs={{0,1},{1,2},{2,3},{4,5},{5,6},{6,7},{8,9},{9,10},{10,11},{12,13},{... | collective-permute-start | bytes 196616 | tf_op jit(solution)/shard_map/ppermute | solution.py:412
  10.2 5.5 %collective-permute-start.1 = (f32[8,16,128]{2,1,0:T(8,128)S(1)}, f32[8,16,128]{2,1,0:T(8,128)S(1)}, u32[]{:S(2)}, u32[]{:S(2)}) collective-permute-start(f32[8,16,128]{2,1,0:T(8,128)S(1)} %get-tuple-element.30), channel_id=1, source_target_pairs={{1,0},{2,1},{3,2},{5,4},{6,5},{7,6},{9,8},{10,9},{11,10},{13,12},{... | collective-permute-start | bytes 196616 | tf_op jit(solution)/shard_map/ppermute | solution.py:412
  15.7 0.9 collective-permute-done.1.refs_1_
  16.9 3.4 %collective-permute-start.2 = (s16[62,16,128]{2,1,0:T(8,128)(2,1)S(1)}, s16[62,16,128]{2,1,0:T(8,128)(2,1)S(1)}, u32[]{:S(2)}, u32[]{:S(2)}) collective-permute-start(s16[62,16,128]{2,1,0:T(8,128)(2,1)S(1)} %get-tuple-element.32), channel_id=1, source_target_pairs={{0,32},{32,64},{64,96},{96,128},{128,160},{160,192},{192,224},{224... | collective-permute-start | bytes 761864 | tf_op jit(solution)/shard_map/ppermute | solution.py:412
  20.3 1.3 %collective-permute-start.3 = (s16[62,16,128]{2,1,0:T(8,128)(2,1)S(1)}, s16[62,16,128]{2,1,0:T(8,128)(2,1)S(1)}, u32[]{:S(2)}, u32[]{:S(2)}) collective-permute-start(s16[62,16,128]{2,1,0:T(8,128)(2,1)S(1)} %get-tuple-element.33), channel_id=1, source_target_pairs={{32,0},{64,32},{96,64},{128,96},{160,128},{192,160},{224,192},{256... | collective-permute-start | bytes 761864 | tf_op jit(solution)/shard_map/ppermute | solution.py:412
  21.6 8.2 %collective-permute-done.2.refs_6_.refs_5_ = s16[62,16,128]{2,1,0:T(8,128)(2,1)S(1)} collective-permute-done((s16[62,16,128]{2,1,0:T(8,128)(2,1)S(1)}, s16[62,16,128]{2,1,0:T(8,128)(2,1)S(1)}, u32[]{:S(2)}, u32[]{:S(2)}) %collective-permute-start.2) | collective-permute-done | bytes 253984 | tf_op jit(solution)/shard_map/ppermute | solution.py:412
  29.9 3.9 %collective-permute-done.3.refs_7_.refs_6_ = s16[62,16,128]{2,1,0:T(8,128)(2,1)S(1)} collective-permute-done((s16[62,16,128]{2,1,0:T(8,128)(2,1)S(1)}, s16[62,16,128]{2,1,0:T(8,128)(2,1)S(1)}, u32[]{:S(2)}, u32[]{:S(2)}) %collective-permute-start.3) | collective-permute-done | bytes 253984 | tf_op jit(solution)/shard_map/ppermute | solution.py:412
  34.1 4.0 %collective-permute-start.4 = (s16[97,16,128]{2,1,0:T(8,128)(2,1)S(1)}, s16[97,16,128]{2,1,0:T(8,128)(2,1)S(1)}, u32[]{:S(2)}, u32[]{:S(2)}) collective-permute-start(s16[97,16,128]{2,1,0:T(8,128)(2,1)S(1)} %get-tuple-element.35), channel_id=1, source_target_pairs={{0,4},{4,8},{8,12},{12,16},{16,20},{20,24},{24,28},{1,5},{5,9},{9,... | collective-permute-start | bytes 1191944 | tf_op jit(solution)/shard_map/ppermute | solution.py:412
  38.2 1.4 %collective-permute-start.5 = (s16[97,16,128]{2,1,0:T(8,128)(2,1)S(1)}, s16[97,16,128]{2,1,0:T(8,128)(2,1)S(1)}, u32[]{:S(2)}, u32[]{:S(2)}) collective-permute-start(s16[97,16,128]{2,1,0:T(8,128)(2,1)S(1)} %get-tuple-element.36), channel_id=1, source_target_pairs={{4,0},{8,4},{12,8},{16,12},{20,16},{24,20},{28,24},{5,1},{9,5},{13... | collective-permute-start | bytes 1191944 | tf_op jit(solution)/shard_map/ppermute | solution.py:412
  39.6 6.7 %collective-permute-done.4.refs_7_ = s16[97,16,128]{2,1,0:T(8,128)(2,1)S(1)} collective-permute-done((s16[97,16,128]{2,1,0:T(8,128)(2,1)S(1)}, s16[97,16,128]{2,1,0:T(8,128)(2,1)S(1)}, u32[]{:S(2)}, u32[]{:S(2)}) %collective-permute-start.4) | collective-permute-done | bytes 397344 | tf_op jit(solution)/shard_map/ppermute | solution.py:412
  46.3 4.9 %collective-permute-done.5.refs_8_ = s16[97,16,128]{2,1,0:T(8,128)(2,1)S(1)} collective-permute-done((s16[97,16,128]{2,1,0:T(8,128)(2,1)S(1)}, s16[97,16,128]{2,1,0:T(8,128)(2,1)S(1)}, u32[]{:S(2)}, u32[]{:S(2)}) %collective-permute-start.5) | collective-permute-done | bytes 397344 | tf_op jit(solution)/shard_map/ppermute | solution.py:412
  51.2 6.6 %steps_first.1 = (f32[3,8,16,128]{3,2,1,0:T(8,128)S(1)}, f32[3,8,16,128]{3,2,1,0:T(8,128)S(1)}, f32[8,16,128]{2,1,0:T(8,128)S(1)}, f32[8,16,128]{2,1,0:T(8,128)S(1)}, f32[4,24,32,128]{3,2,1,0:T(8,128)S(1)}) custom-call(f32[3,8,16,128]{3,2,1,0:T(8,128)S(1)} %get-tuple-element.26.refs_2_.refs_0_, f32[3,8,16,128]{3,2,1,0:T(8,128)S(1)} %get-tuple-element.27.refs_3_.refs_1_, ...), custom_call_target="tpu_custom_call" | custom-call | tf_op jit(solution)/shard_map/steps_first/pallas_call | solution.py:397
  57.8 1.9 %collective-permute-start.6 = (f32[8,16,128]{2,1,0:T(8,128)S(1)}, f32[8,16,128]{2,1,0:T(8,128)S(1)}, u32[]{:S(2)}, u32[]{:S(2)}) collective-permute-start(f32[8,16,128]{2,1,0:T(8,128)S(1)} %get-tuple-element.39), channel_id=1, source_target_pairs={{0,1},{1,2},{2,3},{4,5},{5,6},{6,7},{8,9},{9,10},{10,11},{12,13},{... | collective-permute-start | bytes 196616 | tf_op jit(solution)/shard_map/ppermute | solution.py:412
  59.8 2.5 %collective-permute-start.7 = (f32[8,16,128]{2,1,0:T(8,128)S(1)}, f32[8,16,128]{2,1,0:T(8,128)S(1)}, u32[]{:S(2)}, u32[]{:S(2)}) collective-permute-start(f32[8,16,128]{2,1,0:T(8,128)S(1)} %get-tuple-element.39), channel_id=1, source_target_pairs={{1,0},{2,1},{3,2},{5,4},{6,5},{7,6},{9,8},{10,9},{11,10},{13,12},{... | collective-permute-start | bytes 196616 | tf_op jit(solution)/shard_map/ppermute | solution.py:412
  62.3 3.1 %collective-permute-done.7.refs_1_ = f32[8,16,128]{2,1,0:T(8,128)S(1)} collective-permute-done((f32[8,16,128]{2,1,0:T(8,128)S(1)}, f32[8,16,128]{2,1,0:T(8,128)S(1)}, u32[]{:S(2)}, u32[]{:S(2)}) %collective-permute-start.7) | collective-permute-done | bytes 65568 | tf_op jit(solution)/shard_map/ppermute | solution.py:412
  65.6 5.2 %collective-permute-start.8 = (s16[50,16,128]{2,1,0:T(8,128)(2,1)S(1)}, s16[50,16,128]{2,1,0:T(8,128)(2,1)S(1)}, u32[]{:S(2)}, u32[]{:S(2)}) collective-permute-start(s16[50,16,128]{2,1,0:T(8,128)(2,1)S(1)} %get-tuple-element.41), channel_id=1, source_target_pairs={{0,32},{32,64},{64,96},{96,128},{128,160},{160,192},{192,224},{224... | collective-permute-start | bytes 614408 | tf_op jit(solution)/shard_map/ppermute | solution.py:412
  70.8 1.3 %collective-permute-start.9 = (s16[50,16,128]{2,1,0:T(8,128)(2,1)S(1)}, s16[50,16,128]{2,1,0:T(8,128)(2,1)S(1)}, u32[]{:S(2)}, u32[]{:S(2)}) collective-permute-start(s16[50,16,128]{2,1,0:T(8,128)(2,1)S(1)} %get-tuple-element.42), channel_id=1, source_target_pairs={{32,0},{64,32},{96,64},{128,96},{160,128},{192,160},{224,192},{256... | collective-permute-start | bytes 614408 | tf_op jit(solution)/shard_map/ppermute | solution.py:412
  72.1 2.2 %collective-permute-done.8.refs_4_.refs_3_ = s16[50,16,128]{2,1,0:T(8,128)(2,1)S(1)} collective-permute-done((s16[50,16,128]{2,1,0:T(8,128)(2,1)S(1)}, s16[50,16,128]{2,1,0:T(8,128)(2,1)S(1)}, u32[]{:S(2)}, u32[]{:S(2)}) %collective-permute-start.8) | collective-permute-done | bytes 204832 | tf_op jit(solution)/shard_map/ppermute | solution.py:412
  74.3 5.2 %collective-permute-done.9.refs_5_.refs_4_ = s16[50,16,128]{2,1,0:T(8,128)(2,1)S(1)} collective-permute-done((s16[50,16,128]{2,1,0:T(8,128)(2,1)S(1)}, s16[50,16,128]{2,1,0:T(8,128)(2,1)S(1)}, u32[]{:S(2)}, u32[]{:S(2)}) %collective-permute-start.9) | collective-permute-done | bytes 204832 | tf_op jit(solution)/shard_map/ppermute | solution.py:412
  79.5 1.1 y_message.3
  80.6 4.0 %collective-permute-start.10 = (s16[77,16,128]{2,1,0:T(8,128)(2,1)}, s16[77,16,128]{2,1,0:T(8,128)(2,1)S(1)}, u32[]{:S(2)}, u32[]{:S(2)}) collective-permute-start(s16[77,16,128]{2,1,0:T(8,128)(2,1)} %get-tuple-element.44), channel_id=1, source_target_pairs={{0,4},{4,8},{8,12},{12,16},{16,20},{20,24},{24,28},{1,5},{5,9},{9,... | collective-permute-start | bytes 946184 | tf_op jit(solution)/shard_map/ppermute | solution.py:412
  84.7 1.3 %collective-permute-start.11 = (s16[77,16,128]{2,1,0:T(8,128)(2,1)}, s16[77,16,128]{2,1,0:T(8,128)(2,1)S(1)}, u32[]{:S(2)}, u32[]{:S(2)}) collective-permute-start(s16[77,16,128]{2,1,0:T(8,128)(2,1)} %get-tuple-element.45), channel_id=1, source_target_pairs={{4,0},{8,4},{12,8},{16,12},{20,16},{24,20},{28,24},{5,1},{9,5},{13... | collective-permute-start | bytes 946184 | tf_op jit(solution)/shard_map/ppermute | solution.py:412
  86.3 5.9 %collective-permute-done.10.refs_5_ = s16[77,16,128]{2,1,0:T(8,128)(2,1)S(1)} collective-permute-done((s16[77,16,128]{2,1,0:T(8,128)(2,1)}, s16[77,16,128]{2,1,0:T(8,128)(2,1)S(1)}, u32[]{:S(2)}, u32[]{:S(2)}) %collective-permute-start.10) | collective-permute-done | bytes 315424 | tf_op jit(solution)/shard_map/ppermute | solution.py:412
  92.2 5.7 %collective-permute-done.11.refs_6_ = s16[77,16,128]{2,1,0:T(8,128)(2,1)S(1)} collective-permute-done((s16[77,16,128]{2,1,0:T(8,128)(2,1)}, s16[77,16,128]{2,1,0:T(8,128)(2,1)S(1)}, u32[]{:S(2)}, u32[]{:S(2)}) %collective-permute-start.11) | collective-permute-done | bytes 315424 | tf_op jit(solution)/shard_map/ppermute | solution.py:412
  97.9 0.8 copy-done.5
  98.8 7.0 %steps_second.1 = (f32[3,8,16,128]{3,2,1,0:T(8,128)}, f32[16,4,8,128]{3,2,1,0:T(8,128)S(1)}) custom-call(f32[3,8,16,128]{3,2,1,0:T(8,128)S(1)} %get-tuple-element.37.refs_2_.refs_0_, f32[3,8,16,128]{3,2,1,0:T(8,128)S(1)} %get-tuple-element.38.refs_3_.refs_1_, f32[8,16,128]{2,1,0:T(8,128)S(1)} %get-tuple-element.40.refs_2_, ...), custom_call_target="tpu_custom_call" | custom-call | tf_op jit(solution)/shard_map/steps_second/pallas_call | solution.py:397
  106.5 8.8 %all-to-all-start = ((f32[64,8,128]{2,1,0:T(8,128)}), f32[64,8,128]{2,1,0:T(8,128)S(1)}, u32[]{:S(2)}, u32[]{:S(2)}) async-start(f32[64,8,128]{2,1,0:T(8,128)} %bitcast.16), calls=%async_computation | async-start | bytes 524288 | tf_op jit(solution)/shard_map/all_to_all | solution.py:491
  115.5 11.8 %all-to-all-done = f32[64,8,128]{2,1,0:T(8,128)S(1)} async-done(((f32[64,8,128]{2,1,0:T(8,128)}), f32[64,8,128]{2,1,0:T(8,128)S(1)}, u32[]{:S(2)}, u32[]{:S(2)}) %all-to-all-start) | async-done | bytes 262176 | tf_op jit(solution)/shard_map/all_to_all | solution.py:491
  127.3 0.9 fragility.1
  (49 shorter events, 3.7 us)
Async XLA Ops:
  0.6 50.6 %copy-start = (bf16[3,256,256]{2,1,0:T(8,128)(2,1)S(1)}, bf16[3,256,256]{2,1,0:T(8,128)(2,1)}, u32[]{:S(2)}) copy-start(bf16[3,256,256]{2,1,0:T(8,128)(2,1)} %constant.9.clone.refs_9_.refs_7_) | copy-start | bytes 1179652
  0.6 1.0 copy-start.2
  1.6 0.9 copy-start.3
  2.5 0.8 copy-start.6
  3.4 0.8 copy-start.7
  5.6 10.1 %collective-permute-start = (f32[8,16,128]{2,1,0:T(8,128)S(1)}, f32[8,16,128]{2,1,0:T(8,128)S(1)}, u32[]{:S(2)}, u32[]{:S(2)}) collective-permute-start(f32[8,16,128]{2,1,0:T(8,128)S(1)} %get-tuple-element.30), channel_id=1, source_target_pairs={{0,1},{1,2},{2,3},{4,5},{5,6},{6,7},{8,9},{9,10},{10,11},{12,13},{... | collective-permute-start | bytes 196616 | tf_op jit(solution)/shard_map/ppermute | solution.py:412
  10.2 6.4 %collective-permute-start.1 = (f32[8,16,128]{2,1,0:T(8,128)S(1)}, f32[8,16,128]{2,1,0:T(8,128)S(1)}, u32[]{:S(2)}, u32[]{:S(2)}) collective-permute-start(f32[8,16,128]{2,1,0:T(8,128)S(1)} %get-tuple-element.30), channel_id=1, source_target_pairs={{1,0},{2,1},{3,2},{5,4},{6,5},{7,6},{9,8},{10,9},{11,10},{13,12},{... | collective-permute-start | bytes 196616 | tf_op jit(solution)/shard_map/ppermute | solution.py:412
  16.9 13.0 %collective-permute-start.2 = (s16[62,16,128]{2,1,0:T(8,128)(2,1)S(1)}, s16[62,16,128]{2,1,0:T(8,128)(2,1)S(1)}, u32[]{:S(2)}, u32[]{:S(2)}) collective-permute-start(s16[62,16,128]{2,1,0:T(8,128)(2,1)S(1)} %get-tuple-element.32), channel_id=1, source_target_pairs={{0,32},{32,64},{64,96},{96,128},{128,160},{160,192},{192,224},{224... | collective-permute-start | bytes 761864 | tf_op jit(solution)/shard_map/ppermute | solution.py:412
  20.3 13.5 %collective-permute-start.3 = (s16[62,16,128]{2,1,0:T(8,128)(2,1)S(1)}, s16[62,16,128]{2,1,0:T(8,128)(2,1)S(1)}, u32[]{:S(2)}, u32[]{:S(2)}) collective-permute-start(s16[62,16,128]{2,1,0:T(8,128)(2,1)S(1)} %get-tuple-element.33), channel_id=1, source_target_pairs={{32,0},{64,32},{96,64},{128,96},{160,128},{192,160},{224,192},{256... | collective-permute-start | bytes 761864 | tf_op jit(solution)/shard_map/ppermute | solution.py:412
  34.1 12.2 %collective-permute-start.4 = (s16[97,16,128]{2,1,0:T(8,128)(2,1)S(1)}, s16[97,16,128]{2,1,0:T(8,128)(2,1)S(1)}, u32[]{:S(2)}, u32[]{:S(2)}) collective-permute-start(s16[97,16,128]{2,1,0:T(8,128)(2,1)S(1)} %get-tuple-element.35), channel_id=1, source_target_pairs={{0,4},{4,8},{8,12},{12,16},{16,20},{20,24},{24,28},{1,5},{5,9},{9,... | collective-permute-start | bytes 1191944 | tf_op jit(solution)/shard_map/ppermute | solution.py:412
  38.2 47.8 %copy-start.15 = (s32[8]{0:T(128)S(1)}, s32[8]{0:T(128)}, u32[]{:S(2)}) copy-start(s32[8]{0:T(128)} %param.22) | copy-start | bytes 100
  38.2 48.0 %copy-start.12 = (bf16[64,24]{0,1:T(8,128)(2,1)S(1)}, bf16[64,24]{0,1:T(8,128)(2,1)}, u32[]{:S(2)}) copy-start(bf16[64,24]{0,1:T(8,128)(2,1)} %param.23) | copy-start | bytes 9220
  38.2 59.7 %copy-start.8 = (s32[16,1,128]{2,1,0:T(1,128)S(1)}, s32[16,1,128]{2,1,0:T(1,128)}, u32[]{:S(2)}) copy-start(s32[16,1,128]{2,1,0:T(1,128)} %param.18) | copy-start | bytes 24580
  38.2 13.0 %collective-permute-start.5 = (s16[97,16,128]{2,1,0:T(8,128)(2,1)S(1)}, s16[97,16,128]{2,1,0:T(8,128)(2,1)S(1)}, u32[]{:S(2)}, u32[]{:S(2)}) collective-permute-start(s16[97,16,128]{2,1,0:T(8,128)(2,1)S(1)} %get-tuple-element.36), channel_id=1, source_target_pairs={{4,0},{8,4},{12,8},{16,12},{20,16},{24,20},{28,24},{5,1},{9,5},{13... | collective-permute-start | bytes 1191944 | tf_op jit(solution)/shard_map/ppermute | solution.py:412
  57.8 26.8 %copy-start.4 = (f32[8,16,128]{2,1,0:T(8,128)}, f32[8,16,128]{2,1,0:T(8,128)S(1)}, u32[]{:S(2)}) copy-start(f32[8,16,128]{2,1,0:T(8,128)S(1)} %get-tuple-element.46.refs_8_) | copy-start | bytes 196612
  57.8 4.4 %collective-permute-start.6 = (f32[8,16,128]{2,1,0:T(8,128)S(1)}, f32[8,16,128]{2,1,0:T(8,128)S(1)}, u32[]{:S(2)}, u32[]{:S(2)}) collective-permute-start(f32[8,16,128]{2,1,0:T(8,128)S(1)} %get-tuple-element.39), channel_id=1, source_target_pairs={{0,1},{1,2},{2,3},{4,5},{5,6},{6,7},{8,9},{9,10},{10,11},{12,13},{... | collective-permute-start | bytes 196616 | tf_op jit(solution)/shard_map/ppermute | solution.py:412
  59.8 5.6 %collective-permute-start.7 = (f32[8,16,128]{2,1,0:T(8,128)S(1)}, f32[8,16,128]{2,1,0:T(8,128)S(1)}, u32[]{:S(2)}, u32[]{:S(2)}) collective-permute-start(f32[8,16,128]{2,1,0:T(8,128)S(1)} %get-tuple-element.39), channel_id=1, source_target_pairs={{1,0},{2,1},{3,2},{5,4},{6,5},{7,6},{9,8},{10,9},{11,10},{13,12},{... | collective-permute-start | bytes 196616 | tf_op jit(solution)/shard_map/ppermute | solution.py:412
  65.6 8.7 %collective-permute-start.8 = (s16[50,16,128]{2,1,0:T(8,128)(2,1)S(1)}, s16[50,16,128]{2,1,0:T(8,128)(2,1)S(1)}, u32[]{:S(2)}, u32[]{:S(2)}) collective-permute-start(s16[50,16,128]{2,1,0:T(8,128)(2,1)S(1)} %get-tuple-element.41), channel_id=1, source_target_pairs={{0,32},{32,64},{64,96},{96,128},{128,160},{160,192},{192,224},{224... | collective-permute-start | bytes 614408 | tf_op jit(solution)/shard_map/ppermute | solution.py:412
  70.8 8.7 %collective-permute-start.9 = (s16[50,16,128]{2,1,0:T(8,128)(2,1)S(1)}, s16[50,16,128]{2,1,0:T(8,128)(2,1)S(1)}, u32[]{:S(2)}, u32[]{:S(2)}) collective-permute-start(s16[50,16,128]{2,1,0:T(8,128)(2,1)S(1)} %get-tuple-element.42), channel_id=1, source_target_pairs={{32,0},{64,32},{96,64},{128,96},{160,128},{192,160},{224,192},{256... | collective-permute-start | bytes 614408 | tf_op jit(solution)/shard_map/ppermute | solution.py:412
  80.6 11.5 %collective-permute-start.10 = (s16[77,16,128]{2,1,0:T(8,128)(2,1)}, s16[77,16,128]{2,1,0:T(8,128)(2,1)S(1)}, u32[]{:S(2)}, u32[]{:S(2)}) collective-permute-start(s16[77,16,128]{2,1,0:T(8,128)(2,1)} %get-tuple-element.44), channel_id=1, source_target_pairs={{0,4},{4,8},{8,12},{12,16},{16,20},{20,24},{24,28},{1,5},{5,9},{9,... | collective-permute-start | bytes 946184 | tf_op jit(solution)/shard_map/ppermute | solution.py:412
  84.7 13.2 %collective-permute-start.11 = (s16[77,16,128]{2,1,0:T(8,128)(2,1)}, s16[77,16,128]{2,1,0:T(8,128)(2,1)S(1)}, u32[]{:S(2)}, u32[]{:S(2)}) collective-permute-start(s16[77,16,128]{2,1,0:T(8,128)(2,1)} %get-tuple-element.45), channel_id=1, source_target_pairs={{4,0},{8,4},{12,8},{16,12},{20,16},{24,20},{28,24},{5,1},{9,5},{13... | collective-permute-start | bytes 946184 | tf_op jit(solution)/shard_map/ppermute | solution.py:412
  97.9 0.8 copy-start.5
  98.8 16.6 %copy-start.13 = (f32[16,8]{0,1:T(8,128)S(1)}, f32[16,8]{0,1:T(8,128)}, u32[]{:S(2)}) copy-start(f32[16,8]{0,1:T(8,128)} %param.25) | copy-start | bytes 1540
  98.8 16.6 %copy-start.14 = (f32[16,8]{0,1:T(8,128)S(1)}, f32[16,8]{0,1:T(8,128)}, u32[]{:S(2)}) copy-start(f32[16,8]{0,1:T(8,128)} %param.26) | copy-start | bytes 1540
  98.8 16.7 %copy-start.16 = (f32[16]{0:T(128)S(1)}, f32[16]{0:T(128)}, u32[]{:S(2)}) copy-start(f32[16]{0:T(128)} %param.24) | copy-start | bytes 196
  98.8 28.6 %copy-start.9 = (s32[1024]{0:T(1024)S(1)}, s32[1024]{0:T(1024)}, u32[]{:S(2)}) copy-start(s32[1024]{0:T(1024)} %param.19) | copy-start | bytes 12292
  98.8 28.6 %copy-start.10 = (s32[1024]{0:T(1024)S(1)}, s32[1024]{0:T(1024)}, u32[]{:S(2)}) copy-start(s32[1024]{0:T(1024)} %param.20) | copy-start | bytes 12292
  98.8 28.6 %copy-start.11 = (s32[1024]{0:T(1024)S(1)}, s32[1024]{0:T(1024)}, u32[]{:S(2)}) copy-start(s32[1024]{0:T(1024)} %param.21) | copy-start | bytes 12292
  105.8 0.7 copy-start.1
  106.5 20.8 %all-to-all-start = ((f32[64,8,128]{2,1,0:T(8,128)}), f32[64,8,128]{2,1,0:T(8,128)S(1)}, u32[]{:S(2)}, u32[]{:S(2)}) async-start(f32[64,8,128]{2,1,0:T(8,128)} %bitcast.16), calls=%async_computation | async-start | bytes 524288 | tf_op jit(solution)/shard_map/all_to_all | solution.py:491

commit v5 on v4

--- a/solution.py
+++ b/solution.py
@@ -13,6 +13,7 @@
 DEEP = 2 * HALF
 CLASSES = 8
 MODES = 8
+CITIES = 16
 F32 = jnp.float32
 VMEM_LIMIT = 24 * 1024 * 1024
 
@@ -102,9 +103,9 @@
 
 def x_message_kernel(coefficients, *refs):
     if coefficients:
-        low_ref, high_ref, u_ref, p_ref, a_ref, e_ref, halo_ref, up_ref, down_ref, power_ref = refs
+        z_low_ref, z_high_ref, u_ref, p_ref, a_ref, e_ref, halo_ref, up_ref, down_ref, power_ref = refs
     else:
-        low_ref, high_ref, u_ref, p_ref, halo_ref, up_ref, down_ref, power_ref = refs
+        z_low_ref, z_high_ref, u_ref, p_ref, halo_ref, up_ref, down_ref, power_ref = refs
     inner = lax.broadcasted_iota(jnp.int32, (16, 128), 1) % 16
 
     def largest(x, carry):
@@ -112,7 +113,7 @@
         for k in range(3):
             both = jnp.maximum(jnp.abs(u_ref[k, x]), jnp.abs(p_ref[k, x]))
             field = jnp.maximum(field, jnp.maximum(both[0:8], both[8:16]))
-        halo = jnp.where(inner < 8, low_ref[x], high_ref[x])
+        halo = jnp.where(inner < 8, z_low_ref[x], z_high_ref[x])
         halo_ref[x] = halo
         halo = jnp.abs(halo)
         return field, jnp.maximum(face, jnp.maximum(halo[0:8], halo[8:16]))
@@ -244,9 +245,9 @@
         state_ref, edge_ref = refs[15:]
     else:
         (u_in, p_in, halo_in, x_low, x_high, y_low, y_high, weight_in, seen_in, rate_ref) = refs[:10]
-        (cells_in, filter_in) = refs[10:12]
-        (u_out, table_out) = refs[12:14]
-        state_ref, edge_ref, seen_out = refs[14:]
+        (cells_in, filter_in, count_in) = refs[10:13]
+        (u_out, table_out) = refs[13:15]
+        state_ref, edge_ref, seen_out, filter_ref, count_ref = refs[15:]
     a_ref, e_ref, ha_ref, he_ref = (rate_ref.at[at] for at in range(4))
     lane = lane_of()
     inner = lane % 16
@@ -353,12 +354,24 @@
     lax.fori_loop(0, 8, finish, 0, unroll=4)
 
     if not first:
+        filter_ref[...] = filter_in[...].astype(F32)
+        blank = jnp.zeros((8, CLASSES * MODES), F32)
+        blocks = [blank] * 16
+        for k in range(3):
+            blocks[9 + 2 * k] = filter_ref[pl.ds(k, STEPS, stride=3), :]
+        filters = jnp.concatenate(blocks, axis=0).astype(jnp.bfloat16)
         motion = seen_out[...].reshape(128, 128).astype(jnp.bfloat16)
-        modal = lax.dot_general(filter_in[...], motion, (((1,), (1,)), ((), ())), preferred_element_type=F32)
+        modal = lax.dot_general(filters, motion, (((0,), (1,)), ((), ())), preferred_element_type=F32)
+        modes = lax.broadcasted_iota(jnp.int32, (MODES, 128), 0)
+        count_ref[...] = jnp.zeros((8, 128), jnp.int32)
+        count_ref[0:1, 0:CLASSES] = count_in[...]
+        counts = jnp.where(modes == lane, jnp.broadcast_to(count_ref[0:1, :], (8, 128)), 0)
+        counts = jnp.sum(counts, axis=1, keepdims=True)
         energies = []
         for kind in range(CLASSES):
             part = modal[MODES * kind : MODES * (kind + 1), :]
-            energies.append(jnp.sum(part * part, axis=0, keepdims=True))
+            part = jnp.where(modes < counts[kind : kind + 1, :], part * part, 0.0)
+            energies.append(jnp.sum(part, axis=0, keepdims=True))
         demand = 0.5 * jnp.log1p(jnp.concatenate(energies, axis=0))
         for owner in range(table_out.shape[0]):
             cells = jnp.broadcast_to(cells_in[owner : owner + 1, :], (CLASSES, 128))
@@ -367,7 +380,9 @@
                 table_out[owner, level] = chosen
 
 
-def fragility_kernel(table_ref, slot_ref, kind_ref, city_ref, amplify_ref, median_ref, spread_ref, out_ref):
+def fragility_kernel(
+    table_ref, slot_ref, kind_ref, city_ref, amplify_ref, median_ref, spread_ref, out_ref, gain_ref, tables_ref
+):
     sources = table_ref.shape[0]
     slot, kind, city = slot_ref[...], kind_ref[...], city_ref[...]
     column = slot % 128
@@ -375,17 +390,25 @@
     demand = jnp.zeros((8, 128), F32)
     for source in range(sources):
         for each in range(CLASSES):
-            row = jnp.broadcast_to(table_ref[source, each : each + 1, :], (8, 128))
+            row = jnp.broadcast_to(table_ref[source, 0, each : each + 1, :], (8, 128))
             found = jnp.take_along_axis(row, column, axis=1)
             demand = jnp.where(key == source * CLASSES + each, found, demand)
-    gain = jnp.log(jnp.broadcast_to(amplify_ref[...], (8, 128)))
+    gain_ref[...] = jnp.ones((8, 128), F32)
+    gain_ref[0:1, 0:CITIES] = amplify_ref[...]
+    gain = jnp.log(jnp.broadcast_to(gain_ref[0:1, :], (8, 128)))
     demand = demand + jnp.take_along_axis(gain, city, axis=1)
+    tables_ref[...] = jnp.ones((128, 128), F32)
+    batches = median_ref.shape[1]
+    tables_ref[0:CLASSES, 0:batches] = median_ref[...]
+    medians = tables_ref[...].T
+    tables_ref[0:CLASSES, 0:batches] = spread_ref[...]
+    spreads = tables_ref[...].T
     for group in range(8):
         level = jnp.broadcast_to(demand[group : group + 1, :], (8, 128))
         index = jnp.broadcast_to(kind[group : group + 1, :], (8, 128))
-        for half in (0, 8):
-            middle = jnp.take_along_axis(median_ref[half : half + 8, :], index, axis=1)
-            width = jnp.take_along_axis(spread_ref[half : half + 8, :], index, axis=1)
+        for half in range(0, batches, 8):
+            middle = jnp.take_along_axis(medians[half : half + 8, :], index, axis=1)
+            width = jnp.take_along_axis(spreads[half : half + 8, :], index, axis=1)
             out_ref[half : half + 8, 128 * group : 128 * group + 128] = jax.nn.sigmoid((level - middle) / width)
 
 
@@ -475,34 +498,31 @@
     )
     received = exchange(u, p, faces, ())
     owners, levels = lax.axis_size("gx"), lax.axis_size("gz")
-    used = jnp.arange(MODES)[None, :] < mode_count[:, None]
-    filters = jnp.where(used.reshape(CLASSES * MODES, 1), modal_filter, 0).astype(modal_filter.dtype)
-    filters = jnp.swapaxes(filters.reshape(CLASSES * MODES, STEPS, 3), 1, 2)
-    filters = jnp.pad(filters, ((0, 0), (4, 1), (16 - STEPS, 0))).reshape(CLASSES * MODES, 128)
-    args = [u, p, *received, weights, seen, rates, send_cells.reshape(owners, 128), filters]
+    args = [u, p, *received, weights, seen, rates, send_cells.reshape(owners, 128), modal_filter.T, mode_count.reshape(1, CLASSES)]
     field, table = call(
         functools.partial(steps_kernel, False),
         "steps_second",
         [own, (owners, levels, CLASSES, 128)],
         args,
-        scratch=wide + [pltpu.VMEM(plane, F32)],
+        scratch=wide
+        + [pltpu.VMEM(plane, F32), pltpu.VMEM((3 * STEPS, CLASSES * MODES), F32), pltpu.VMEM((8, 128), jnp.int32)],
     )
     table = table.reshape(owners * levels, CLASSES, 128)
     table = lax.all_to_all(table, ("gx", "gz"), split_axis=0, concat_axis=0, tiled=True)
-    table = table.reshape(owners, levels, CLASSES, 128)[:, 0]
     (probability,) = call(
         fragility_kernel,
         "fragility",
         [(16, 1024)],
         [
-            table,
+            table.reshape(owners, levels, CLASSES, 128),
             building_slot.reshape(8, 128),
             building_class.reshape(8, 128),
             city.reshape(8, 128),
-            jnp.pad(amplify, (0, 112), constant_values=1.0).reshape(1, 128),
-            jnp.pad(median, ((0, 0), (0, 120))),
-            jnp.pad(spread, ((0, 0), (0, 120)), constant_values=1.0),
+            amplify.reshape(1, CITIES),
+            median.T,
+            spread.T,
         ],
+        scratch=[pltpu.VMEM((8, 128), F32), pltpu.VMEM((128, 128), F32)],
     )
     return (field, probability)
 

time: 129 us -> 131 us (1.016)
  blocking collectives: 0 us -> 20.7 us
  starting transfers between devices: 45.2 us -> 35.5 us
  waiting for transfers between devices: 58.5 us -> 51.5 us
  local copies, waits for them, and re-layouts: 5.52 us -> 3.64 us
    all_to_all x0 -> x1, blocking collectives: none -> 20.7 us  [body(): lax.all_to_all(table, ('gx', 'gz'), split_axis=0, concat_axis=0, tiled=True)]
    all_to_all x1 -> x0, waiting for transfers between devices: 11.8 us -> none  [body(): lax.all_to_all(table, ('gx', 'gz'), split_axis=0, concat_axis=0, tiled=True)]
    all_to_all x1 -> x0, starting transfers between devices: 8.8 us -> none  [body(): lax.all_to_all(table, ('gx', 'gz'), split_axis=0, concat_axis=0, tiled=True)]
    ppermute x6, waiting for transfers between devices: 23 us -> 29.5 us  [both_ways(): lax.ppermute(to_up, axis, forward)]
    ppermute x6, starting transfers between devices: 23.2 us -> 18.3 us  [both_ways(): lax.ppermute(to_up, axis, forward)]
    ppermute x6, starting transfers between devices: 13.3 us -> 17.2 us  [both_ways(): lax.ppermute(to_down, axis, backward)]
    ppermute x6, waiting for transfers between devices: 23.7 us -> 22 us  [both_ways(): lax.ppermute(to_down, axis, backward)]
    unnamed x37 -> x28, local copies, waits for them, and re-layouts: 5.31 us -> 3.64 us
  transfers between devices with their start and end apart: 13 -> 12, of which waited for: 11 -> 10; matrix products, arithmetic and copies ran while one was open for 0% -> 0% of each run, Pallas kernels for 0% -> 0%
where the time goes in v5:
time: 131 us; the launch traced here: 130 us
  waiting for transfers between devices  51.5 us (39%)
  starting transfers between devices  35.5 us (27%)
  blocking collectives  20.7 us (16%)
  Pallas kernels  17.8 us (14%)
  local copies, waits for them, and re-layouts  3.64 us (3%)
    ppermute x6, waiting for transfers between devices, both_ways(): lax.ppermute(to_up, axis, forward)  29.5 us
    ppermute x6, waiting for transfers between devices, both_ways(): lax.ppermute(to_down, axis, backward)  22 us
    all_to_all x1, blocking collectives, body(): lax.all_to_all(table, ('gx', 'gz'), split_axis=0, concat_axis=0, tiled=True)  20.7 us
    ppermute x6, starting transfers between devices, both_ways(): lax.ppermute(to_up, axis, forward)  18.3 us
    pallas_call x8, Pallas kernels, call(): pl.pallas_call(kernel, out_shape=out, in_specs=specs or [VM] * len(args),...  17.8 us
    ppermute x6, starting transfers between devices, both_ways(): lax.ppermute(to_down, axis, backward)  17.2 us
    unnamed x28, local copies, waits for them, and re-layouts  3.64 us
  transfers between devices with their start and end apart: 12, of which 10 were waited for; matrix products, arithmetic and copies ran while one was open for 0% of the time, Pallas kernels for 0%

profile of v5, /device:TPU:1, one launch (start us, length us, event | category | flops | bytes accessed | tf_op | source)
XLA Modules:
  0.0 130.0 jit_solution(6152737249231909460)
XLA Ops:
  0.7 1.0 copy-done.1
  1.6 0.9 copy-done.2
  2.5 0.8 copy-done.3
  3.4 0.8 copy-done.4
  4.2 1.4 %start.1 = (f32[3,8,16,128]{3,2,1,0:T(8,128)S(1)}, f32[3,8,16,128]{3,2,1,0:T(8,128)S(1)}, f32[8,16,128]{2,1,0:T(8,128)S(1)}, f32[8,16,128]{2,1,0:T(8,128)S(1)}, f32[8,16,128]{2,1,0:T(8,128)S(1)}) custom-call(f32[3,8,16,128]{3,2,1,0:T(8,128)S(1)} %copy-done.1, f32[3,8,16,128]{3,2,1,0:T(8,128)S(1)} %copy-done.2, f32[8,16,128]{2,1,0:T(8,128)S(1)} %copy-done.3, ...), custom_call_target="tpu_custom_call" | custom-call | tf_op jit(solution)/shard_map/start/pallas_call | solution.py:420
  5.6 8.8 %collective-permute-start.1 = (f32[8,16,128]{2,1,0:T(8,128)S(1)}, f32[8,16,128]{2,1,0:T(8,128)S(1)}, u32[]{:S(2)}, u32[]{:S(2)}) collective-permute-start(f32[8,16,128]{2,1,0:T(8,128)S(1)} %get-tuple-element.30), channel_id=1, source_target_pairs={{1,0},{2,1},{3,2},{5,4},{6,5},{7,6},{9,8},{10,9},{11,10},{13,12},{... | collective-permute-start | bytes 196616 | tf_op jit(solution)/shard_map/ppermute | solution.py:435
  14.4 1.9 %collective-permute-start = (f32[8,16,128]{2,1,0:T(8,128)S(1)}, f32[8,16,128]{2,1,0:T(8,128)S(1)}, u32[]{:S(2)}, u32[]{:S(2)}) collective-permute-start(f32[8,16,128]{2,1,0:T(8,128)S(1)} %get-tuple-element.30), channel_id=1, source_target_pairs={{0,1},{1,2},{2,3},{4,5},{5,6},{6,7},{8,9},{9,10},{10,11},{12,13},{... | collective-permute-start | bytes 196616 | tf_op jit(solution)/shard_map/ppermute | solution.py:435
  16.4 1.3 collective-permute-done.refs_0_
  18.0 1.3 %collective-permute-start.2 = (s16[62,16,128]{2,1,0:T(8,128)(2,1)S(1)}, s16[62,16,128]{2,1,0:T(8,128)(2,1)S(1)}, u32[]{:S(2)}, u32[]{:S(2)}) collective-permute-start(s16[62,16,128]{2,1,0:T(8,128)(2,1)S(1)} %get-tuple-element.32), channel_id=1, source_target_pairs={{0,32},{32,64},{64,96},{96,128},{128,160},{160,192},{192,224},{224... | collective-permute-start | bytes 761864 | tf_op jit(solution)/shard_map/ppermute | solution.py:435
  19.3 1.3 collective-permute-start.3
  20.6 8.1 %collective-permute-done.2.refs_6_.refs_5_ = s16[62,16,128]{2,1,0:T(8,128)(2,1)S(1)} collective-permute-done((s16[62,16,128]{2,1,0:T(8,128)(2,1)S(1)}, s16[62,16,128]{2,1,0:T(8,128)(2,1)S(1)}, u32[]{:S(2)}, u32[]{:S(2)}) %collective-permute-start.2) | collective-permute-done | bytes 253984 | tf_op jit(solution)/shard_map/ppermute | solution.py:435
  28.7 5.9 %collective-permute-done.3.refs_7_.refs_6_ = s16[62,16,128]{2,1,0:T(8,128)(2,1)S(1)} collective-permute-done((s16[62,16,128]{2,1,0:T(8,128)(2,1)S(1)}, s16[62,16,128]{2,1,0:T(8,128)(2,1)S(1)}, u32[]{:S(2)}, u32[]{:S(2)}) %collective-permute-start.3) | collective-permute-done | bytes 253984 | tf_op jit(solution)/shard_map/ppermute | solution.py:435
  34.6 0.3 y_message.2
  35.0 4.0 %collective-permute-start.4 = (s16[97,16,128]{2,1,0:T(8,128)(2,1)S(1)}, s16[97,16,128]{2,1,0:T(8,128)(2,1)S(1)}, u32[]{:S(2)}, u32[]{:S(2)}) collective-permute-start(s16[97,16,128]{2,1,0:T(8,128)(2,1)S(1)} %get-tuple-element.35), channel_id=1, source_target_pairs={{0,4},{4,8},{8,12},{12,16},{16,20},{20,24},{24,28},{1,5},{5,9},{9,... | collective-permute-start | bytes 1191944 | tf_op jit(solution)/shard_map/ppermute | solution.py:435
  39.0 1.4 %collective-permute-start.5 = (s16[97,16,128]{2,1,0:T(8,128)(2,1)S(1)}, s16[97,16,128]{2,1,0:T(8,128)(2,1)S(1)}, u32[]{:S(2)}, u32[]{:S(2)}) collective-permute-start(s16[97,16,128]{2,1,0:T(8,128)(2,1)S(1)} %get-tuple-element.36), channel_id=1, source_target_pairs={{4,0},{8,4},{12,8},{16,12},{20,16},{24,20},{28,24},{5,1},{9,5},{13... | collective-permute-start | bytes 1191944 | tf_op jit(solution)/shard_map/ppermute | solution.py:435
  40.4 6.7 %collective-permute-done.4.refs_7_ = s16[97,16,128]{2,1,0:T(8,128)(2,1)S(1)} collective-permute-done((s16[97,16,128]{2,1,0:T(8,128)(2,1)S(1)}, s16[97,16,128]{2,1,0:T(8,128)(2,1)S(1)}, u32[]{:S(2)}, u32[]{:S(2)}) %collective-permute-start.4) | collective-permute-done | bytes 397344 | tf_op jit(solution)/shard_map/ppermute | solution.py:435
  47.1 4.9 %collective-permute-done.5.refs_8_ = s16[97,16,128]{2,1,0:T(8,128)(2,1)S(1)} collective-permute-done((s16[97,16,128]{2,1,0:T(8,128)(2,1)S(1)}, s16[97,16,128]{2,1,0:T(8,128)(2,1)S(1)}, u32[]{:S(2)}, u32[]{:S(2)}) %collective-permute-start.5) | collective-permute-done | bytes 397344 | tf_op jit(solution)/shard_map/ppermute | solution.py:435
  52.1 6.9 %steps_first.1 = (f32[3,8,16,128]{3,2,1,0:T(8,128)S(1)}, f32[3,8,16,128]{3,2,1,0:T(8,128)S(1)}, f32[8,16,128]{2,1,0:T(8,128)S(1)}, f32[8,16,128]{2,1,0:T(8,128)S(1)}, f32[4,24,32,128]{3,2,1,0:T(8,128)S(1)}) custom-call(f32[3,8,16,128]{3,2,1,0:T(8,128)S(1)} %get-tuple-element.26.refs_2_.refs_0_, f32[3,8,16,128]{3,2,1,0:T(8,128)S(1)} %get-tuple-element.27.refs_3_.refs_1_, ...), custom_call_target="tpu_custom_call" | custom-call | tf_op jit(solution)/shard_map/steps_first/pallas_call | solution.py:420
  59.0 3.1 %collective-permute-start.7 = (f32[8,16,128]{2,1,0:T(8,128)S(1)}, f32[8,16,128]{2,1,0:T(8,128)S(1)}, u32[]{:S(2)}, u32[]{:S(2)}) collective-permute-start(f32[8,16,128]{2,1,0:T(8,128)S(1)} %get-tuple-element.39), channel_id=1, source_target_pairs={{1,0},{2,1},{3,2},{5,4},{6,5},{7,6},{9,8},{10,9},{11,10},{13,12},{... | collective-permute-start | bytes 196616 | tf_op jit(solution)/shard_map/ppermute | solution.py:435
  62.1 2.4 %collective-permute-start.6 = (f32[8,16,128]{2,1,0:T(8,128)S(1)}, f32[8,16,128]{2,1,0:T(8,128)S(1)}, u32[]{:S(2)}, u32[]{:S(2)}) collective-permute-start(f32[8,16,128]{2,1,0:T(8,128)S(1)} %get-tuple-element.39), channel_id=1, source_target_pairs={{0,1},{1,2},{2,3},{4,5},{5,6},{6,7},{8,9},{9,10},{10,11},{12,13},{... | collective-permute-start | bytes 196616 | tf_op jit(solution)/shard_map/ppermute | solution.py:435
  64.6 1.3 collective-permute-done.6.refs_0_
  66.2 4.6 %collective-permute-start.8 = (s16[50,16,128]{2,1,0:T(8,128)(2,1)S(1)}, s16[50,16,128]{2,1,0:T(8,128)(2,1)S(1)}, u32[]{:S(2)}, u32[]{:S(2)}) collective-permute-start(s16[50,16,128]{2,1,0:T(8,128)(2,1)S(1)} %get-tuple-element.41), channel_id=1, source_target_pairs={{0,32},{32,64},{64,96},{96,128},{128,160},{160,192},{192,224},{224... | collective-permute-start | bytes 614408 | tf_op jit(solution)/shard_map/ppermute | solution.py:435
  70.7 1.3 collective-permute-start.9
  72.0 7.1 %collective-permute-done.8.refs_4_.refs_3_ = s16[50,16,128]{2,1,0:T(8,128)(2,1)S(1)} collective-permute-done((s16[50,16,128]{2,1,0:T(8,128)(2,1)S(1)}, s16[50,16,128]{2,1,0:T(8,128)(2,1)S(1)}, u32[]{:S(2)}, u32[]{:S(2)}) %collective-permute-start.8) | collective-permute-done | bytes 204832 | tf_op jit(solution)/shard_map/ppermute | solution.py:435
  79.1 5.1 %collective-permute-done.9.refs_5_.refs_4_ = s16[50,16,128]{2,1,0:T(8,128)(2,1)S(1)} collective-permute-done((s16[50,16,128]{2,1,0:T(8,128)(2,1)S(1)}, s16[50,16,128]{2,1,0:T(8,128)(2,1)S(1)}, u32[]{:S(2)}, u32[]{:S(2)}) %collective-permute-start.9) | collective-permute-done | bytes 204832 | tf_op jit(solution)/shard_map/ppermute | solution.py:435
  84.5 4.0 %collective-permute-start.10 = (s16[77,16,128]{2,1,0:T(8,128)(2,1)S(1)}, s16[77,16,128]{2,1,0:T(8,128)(2,1)S(1)}, u32[]{:S(2)}, u32[]{:S(2)}) collective-permute-start(s16[77,16,128]{2,1,0:T(8,128)(2,1)S(1)} %get-tuple-element.44), channel_id=1, source_target_pairs={{0,4},{4,8},{8,12},{12,16},{16,20},{20,24},{24,28},{1,5},{5,9},{9,... | collective-permute-start | bytes 946184 | tf_op jit(solution)/shard_map/ppermute | solution.py:435
  88.5 1.3 collective-permute-start.11
  89.8 5.1 %collective-permute-done.10.refs_5_ = s16[77,16,128]{2,1,0:T(8,128)(2,1)S(1)} collective-permute-done((s16[77,16,128]{2,1,0:T(8,128)(2,1)S(1)}, s16[77,16,128]{2,1,0:T(8,128)(2,1)S(1)}, u32[]{:S(2)}, u32[]{:S(2)}) %collective-permute-start.10) | collective-permute-done | bytes 315424 | tf_op jit(solution)/shard_map/ppermute | solution.py:435
  94.9 6.0 %collective-permute-done.11.refs_6_ = s16[77,16,128]{2,1,0:T(8,128)(2,1)S(1)} collective-permute-done((s16[77,16,128]{2,1,0:T(8,128)(2,1)S(1)}, s16[77,16,128]{2,1,0:T(8,128)(2,1)S(1)}, u32[]{:S(2)}, u32[]{:S(2)}) %collective-permute-start.11) | collective-permute-done | bytes 315424 | tf_op jit(solution)/shard_map/ppermute | solution.py:435
  101.0 7.4 %steps_second.1 = (f32[3,8,16,128]{3,2,1,0:T(8,128)}, f32[16,4,8,128]{3,2,1,0:T(8,128)S(1)}) custom-call(f32[3,8,16,128]{3,2,1,0:T(8,128)S(1)} %get-tuple-element.37.refs_2_.refs_0_, f32[3,8,16,128]{3,2,1,0:T(8,128)S(1)} %get-tuple-element.38.refs_3_.refs_1_, f32[8,16,128]{2,1,0:T(8,128)S(1)} %get-tuple-element.40.refs_2_, ...), custom_call_target="tpu_custom_call" | custom-call | tf_op jit(solution)/shard_map/steps_second/pallas_call | solution.py:420
  108.3 20.7 %all_to_all.5 = f32[64,8,128]{2,1,0:T(8,128)S(1)} all-to-all(f32[64,8,128]{2,1,0:T(8,128)S(1)} %bitcast.12), channel_id=1, replica_groups=mesh['gx'=16,'gy'=8,'gz'=4] {'gx','gz'}, dimensions={0} | all-to-all | bytes 524288 | tf_op jit(solution)/shard_map/all_to_all | solution.py:511
  129.1 1.0 fragility.1
  (29 shorter events, 0.9 us)
Async XLA Ops:
  0.6 51.4 %copy-start = (bf16[3,256,256]{2,1,0:T(8,128)(2,1)S(1)}, bf16[3,256,256]{2,1,0:T(8,128)(2,1)}, u32[]{:S(2)}) copy-start(bf16[3,256,256]{2,1,0:T(8,128)(2,1)} %constant.2.clone.refs_9_.refs_7_) | copy-start | bytes 1179652
  0.6 1.0 copy-start.1
  1.6 0.9 copy-start.2
  2.5 0.8 copy-start.3
  3.4 0.8 copy-start.4
  5.6 10.7 %collective-permute-start.1 = (f32[8,16,128]{2,1,0:T(8,128)S(1)}, f32[8,16,128]{2,1,0:T(8,128)S(1)}, u32[]{:S(2)}, u32[]{:S(2)}) collective-permute-start(f32[8,16,128]{2,1,0:T(8,128)S(1)} %get-tuple-element.30), channel_id=1, source_target_pairs={{1,0},{2,1},{3,2},{5,4},{6,5},{7,6},{9,8},{10,9},{11,10},{13,12},{... | collective-permute-start | bytes 196616 | tf_op jit(solution)/shard_map/ppermute | solution.py:435
  14.4 3.2 %collective-permute-start = (f32[8,16,128]{2,1,0:T(8,128)S(1)}, f32[8,16,128]{2,1,0:T(8,128)S(1)}, u32[]{:S(2)}, u32[]{:S(2)}) collective-permute-start(f32[8,16,128]{2,1,0:T(8,128)S(1)} %get-tuple-element.30), channel_id=1, source_target_pairs={{0,1},{1,2},{2,3},{4,5},{5,6},{6,7},{8,9},{9,10},{10,11},{12,13},{... | collective-permute-start | bytes 196616 | tf_op jit(solution)/shard_map/ppermute | solution.py:435
  18.0 10.8 %collective-permute-start.2 = (s16[62,16,128]{2,1,0:T(8,128)(2,1)S(1)}, s16[62,16,128]{2,1,0:T(8,128)(2,1)S(1)}, u32[]{:S(2)}, u32[]{:S(2)}) collective-permute-start(s16[62,16,128]{2,1,0:T(8,128)(2,1)S(1)} %get-tuple-element.32), channel_id=1, source_target_pairs={{0,32},{32,64},{64,96},{96,128},{128,160},{160,192},{192,224},{224... | collective-permute-start | bytes 761864 | tf_op jit(solution)/shard_map/ppermute | solution.py:435
  19.3 15.4 %collective-permute-start.3 = (s16[62,16,128]{2,1,0:T(8,128)(2,1)S(1)}, s16[62,16,128]{2,1,0:T(8,128)(2,1)S(1)}, u32[]{:S(2)}, u32[]{:S(2)}) collective-permute-start(s16[62,16,128]{2,1,0:T(8,128)(2,1)S(1)} %get-tuple-element.33), channel_id=1, source_target_pairs={{32,0},{64,32},{96,64},{128,96},{160,128},{192,160},{224,192},{256... | collective-permute-start | bytes 761864 | tf_op jit(solution)/shard_map/ppermute | solution.py:435
  35.0 12.2 %collective-permute-start.4 = (s16[97,16,128]{2,1,0:T(8,128)(2,1)S(1)}, s16[97,16,128]{2,1,0:T(8,128)(2,1)S(1)}, u32[]{:S(2)}, u32[]{:S(2)}) collective-permute-start(s16[97,16,128]{2,1,0:T(8,128)(2,1)S(1)} %get-tuple-element.35), channel_id=1, source_target_pairs={{0,4},{4,8},{8,12},{12,16},{16,20},{20,24},{24,28},{1,5},{5,9},{9,... | collective-permute-start | bytes 1191944 | tf_op jit(solution)/shard_map/ppermute | solution.py:435
  39.0 61.9 %copy-start.5 = (s32[16,1,128]{2,1,0:T(1,128)S(1)}, s32[16,1,128]{2,1,0:T(1,128)}, u32[]{:S(2)}) copy-start(s32[16,1,128]{2,1,0:T(1,128)} %param.18) | copy-start | bytes 24580
  39.0 61.9 %copy-start.6 = (bf16[64,24]{0,1:T(8,128)(2,1)S(1)}, bf16[64,24]{0,1:T(8,128)(2,1)}, u32[]{:S(2)}) copy-start(bf16[64,24]{0,1:T(8,128)(2,1)} %param.23) | copy-start | bytes 9220
  39.0 61.9 %copy-start.12 = (s32[8]{0:T(128)S(1)}, s32[8]{0:T(128)}, u32[]{:S(2)}) copy-start(s32[8]{0:T(128)} %param.22) | copy-start | bytes 100
  39.0 13.0 %collective-permute-start.5 = (s16[97,16,128]{2,1,0:T(8,128)(2,1)S(1)}, s16[97,16,128]{2,1,0:T(8,128)(2,1)S(1)}, u32[]{:S(2)}, u32[]{:S(2)}) collective-permute-start(s16[97,16,128]{2,1,0:T(8,128)(2,1)S(1)} %get-tuple-element.36), channel_id=1, source_target_pairs={{4,0},{8,4},{12,8},{16,12},{20,16},{24,20},{28,24},{5,1},{9,5},{13... | collective-permute-start | bytes 1191944 | tf_op jit(solution)/shard_map/ppermute | solution.py:435
  59.0 5.6 %collective-permute-start.7 = (f32[8,16,128]{2,1,0:T(8,128)S(1)}, f32[8,16,128]{2,1,0:T(8,128)S(1)}, u32[]{:S(2)}, u32[]{:S(2)}) collective-permute-start(f32[8,16,128]{2,1,0:T(8,128)S(1)} %get-tuple-element.39), channel_id=1, source_target_pairs={{1,0},{2,1},{3,2},{5,4},{6,5},{7,6},{9,8},{10,9},{11,10},{13,12},{... | collective-permute-start | bytes 196616 | tf_op jit(solution)/shard_map/ppermute | solution.py:435
  62.1 3.8 %collective-permute-start.6 = (f32[8,16,128]{2,1,0:T(8,128)S(1)}, f32[8,16,128]{2,1,0:T(8,128)S(1)}, u32[]{:S(2)}, u32[]{:S(2)}) collective-permute-start(f32[8,16,128]{2,1,0:T(8,128)S(1)} %get-tuple-element.39), channel_id=1, source_target_pairs={{0,1},{1,2},{2,3},{4,5},{5,6},{6,7},{8,9},{9,10},{10,11},{12,13},{... | collective-permute-start | bytes 196616 | tf_op jit(solution)/shard_map/ppermute | solution.py:435
  66.2 13.0 %collective-permute-start.8 = (s16[50,16,128]{2,1,0:T(8,128)(2,1)S(1)}, s16[50,16,128]{2,1,0:T(8,128)(2,1)S(1)}, u32[]{:S(2)}, u32[]{:S(2)}) collective-permute-start(s16[50,16,128]{2,1,0:T(8,128)(2,1)S(1)} %get-tuple-element.41), channel_id=1, source_target_pairs={{0,32},{32,64},{64,96},{96,128},{128,160},{160,192},{192,224},{224... | collective-permute-start | bytes 614408 | tf_op jit(solution)/shard_map/ppermute | solution.py:435
  70.7 13.5 %collective-permute-start.9 = (s16[50,16,128]{2,1,0:T(8,128)(2,1)S(1)}, s16[50,16,128]{2,1,0:T(8,128)(2,1)S(1)}, u32[]{:S(2)}, u32[]{:S(2)}) collective-permute-start(s16[50,16,128]{2,1,0:T(8,128)(2,1)S(1)} %get-tuple-element.42), channel_id=1, source_target_pairs={{32,0},{64,32},{96,64},{128,96},{160,128},{192,160},{224,192},{256... | collective-permute-start | bytes 614408 | tf_op jit(solution)/shard_map/ppermute | solution.py:435
  84.5 10.4 %collective-permute-start.10 = (s16[77,16,128]{2,1,0:T(8,128)(2,1)S(1)}, s16[77,16,128]{2,1,0:T(8,128)(2,1)S(1)}, u32[]{:S(2)}, u32[]{:S(2)}) collective-permute-start(s16[77,16,128]{2,1,0:T(8,128)(2,1)S(1)} %get-tuple-element.44), channel_id=1, source_target_pairs={{0,4},{4,8},{8,12},{12,16},{16,20},{20,24},{24,28},{1,5},{5,9},{9,... | collective-permute-start | bytes 946184 | tf_op jit(solution)/shard_map/ppermute | solution.py:435
  88.5 12.3 %collective-permute-start.11 = (s16[77,16,128]{2,1,0:T(8,128)(2,1)S(1)}, s16[77,16,128]{2,1,0:T(8,128)(2,1)S(1)}, u32[]{:S(2)}, u32[]{:S(2)}) collective-permute-start(s16[77,16,128]{2,1,0:T(8,128)(2,1)S(1)} %get-tuple-element.45), channel_id=1, source_target_pairs={{4,0},{8,4},{12,8},{16,12},{20,16},{24,20},{28,24},{5,1},{9,5},{13... | collective-permute-start | bytes 946184 | tf_op jit(solution)/shard_map/ppermute | solution.py:435
  100.9 28.1 %copy-start.7 = (s32[1024]{0:T(1024)S(1)}, s32[1024]{0:T(1024)}, u32[]{:S(2)}) copy-start(s32[1024]{0:T(1024)} %param.19) | copy-start | bytes 12292
  100.9 28.1 %copy-start.8 = (s32[1024]{0:T(1024)S(1)}, s32[1024]{0:T(1024)}, u32[]{:S(2)}) copy-start(s32[1024]{0:T(1024)} %param.20) | copy-start | bytes 12292
  100.9 28.1 %copy-start.9 = (s32[1024]{0:T(1024)S(1)}, s32[1024]{0:T(1024)}, u32[]{:S(2)}) copy-start(s32[1024]{0:T(1024)} %param.21) | copy-start | bytes 12292
  100.9 28.1 %copy-start.10 = (f32[16,8]{0,1:T(8,128)S(1)}, f32[16,8]{0,1:T(8,128)}, u32[]{:S(2)}) copy-start(f32[16,8]{0,1:T(8,128)} %param.25) | copy-start | bytes 1540
  100.9 28.1 %copy-start.11 = (f32[16,8]{0,1:T(8,128)S(1)}, f32[16,8]{0,1:T(8,128)}, u32[]{:S(2)}) copy-start(f32[16,8]{0,1:T(8,128)} %param.26) | copy-start | bytes 1540
  100.9 28.1 %copy-start.13 = (f32[16]{0:T(128)S(1)}, f32[16]{0:T(128)}, u32[]{:S(2)}) copy-start(f32[16]{0:T(128)} %param.24) | copy-start | bytes 196

commit v6 on v5

--- a/solution.py
+++ b/solution.py
@@ -41,6 +41,20 @@
         result[k] = np.where(used[:, None] & used[None, :], band, 0.0)
         result[k, 0, 128 + 64 + 16 * k + 8] = 1.0
     return result
+
+
+def slab_weights():
+    lanes = np.arange(128)
+    apart = np.abs(lanes[:, None] - lanes[None, :])
+    band = np.where(apart == 0, -90.0, np.where(apart == 1, 16.0, np.where(apart == 2, -1.0, 0.0)))
+    same = (lanes[:, None] // 16 == lanes[None, :] // 16) & (lanes[:, None] < 48)
+    band = np.where(same, band, 0.0)
+    return np.concatenate([band, band], axis=0)
+
+
+def split(v):
+    high = v.astype(jnp.bfloat16)
+    return high, (v - high.astype(F32)).astype(jnp.bfloat16)
 
 
 def lane_of():
@@ -241,13 +255,11 @@
 def steps_kernel(first, *refs):
     if first:
         (u_in, p_in, a_in, e_in, halo_in, x_low, x_high, y_low, y_high, weight_in) = refs[:10]
-        (u_out, p_out, face_out, seen_out, rate_ref) = refs[10:15]
-        state_ref, edge_ref = refs[15:]
+        (u_out, p_out, face_out, slab_out, seen_out, rate_ref) = refs[10:16]
+        state_ref, edge_ref = refs[16:]
     else:
-        (u_in, p_in, halo_in, x_low, x_high, y_low, y_high, weight_in, seen_in, rate_ref) = refs[:10]
-        (cells_in, filter_in, count_in) = refs[10:13]
-        (u_out, table_out) = refs[13:15]
-        state_ref, edge_ref, seen_out, filter_ref, count_ref = refs[15:]
+        (u_in, p_in, halo_in, x_low, x_high, y_low, y_high, weight_in, rate_ref) = refs[:9]
+        u_out, state_ref = refs[9:]
     a_ref, e_ref, ha_ref, he_ref = (rate_ref.at[at] for at in range(4))
     lane = lane_of()
     inner = lane % 16
@@ -278,10 +290,6 @@
         return carry
 
     lax.fori_loop(2, 22, prepare, 0, unroll=4)
-
-    def split(v):
-        high = v.astype(jnp.bfloat16)
-        return high, (v - high.astype(F32)).astype(jnp.bfloat16)
 
     def advance(src, dst, x):
         rows = pl.ds(8, 32)
@@ -318,8 +326,9 @@
             fresh, side = advance(state_ref.at[step % 2, :, pl.ds(x - 2, 4 + PLANES)], dst, x)
             for k, j, value in fresh:
                 dst[k, x + j, 8:40, :] = value
-            for j in range(PLANES):
-                edge_ref[step, x + j, :, :] = side[32 * j + 8 : 32 * j + 24]
+            if first:
+                for j in range(PLANES):
+                    edge_ref[step, x + j, :, :] = side[32 * j + 8 : 32 * j + 24]
             return inside
 
         lax.fori_loop(0, (20 - 4 * step) // PLANES, planes, 0)
@@ -327,7 +336,6 @@
 
     lax.fori_loop(0, HALF, one_step, 0)
 
-    begin = 0 if first else HALF
     block = pl.ds(16, 16)
 
     def finish(x, carry):
@@ -335,49 +343,135 @@
             u_out[k, x, :, :] = state_ref[0, k, 8 + x, block, :]
             if first:
                 p_out[k, x, :, :] = state_ref[1, k, 8 + x, block, :]
+        if first:
+            for row in (0, 8):
+                rows = pl.ds(row, 8)
+                values = [state_ref[slot, k, 8 + x, pl.ds(16 + row, 8), :] for slot in (0, 1) for k in range(3)]
+                last = pack_faces(values, lane)
+                face_out[x, rows, :] = last
+                slab = values[0]
+                for at in range(1, 6):
+                    slab = jnp.where(lane // 16 == at, pltpu.roll(values[at], 16 * at, 1), slab)
+                slab_out[x, rows, :] = slab
+                seen = jnp.zeros((8, 128), F32)
+                for step in range(HALF):
+                    if step < HALF - 1:
+                        sample = pltpu.roll(edge_ref[step + 1, 8 + x, rows, :], 56 + step, 1)
+                    else:
+                        sample = pltpu.roll(last, 120 + step, 1)
+                    seen = jnp.where((inner == step) & (lane < 48), sample, seen)
+                seen_out[x, rows, :] = seen
+        return carry
+
+    lax.fori_loop(0, 8, finish, 0, unroll=4)
+
+
+def slab_message_kernel(own_ref, low_ref, high_ref, up_ref, down_ref):
+    def plane(i, carry):
+        for at, source in ((0, low_ref), (8, own_ref), (16, high_ref)):
+            up_ref[at + i] = source[i, 8:16, :]
+            down_ref[at + i] = source[i, 0:8, :]
+        return carry
+
+    lax.fori_loop(0, 8, plane, 0, unroll=2)
+
+
+def surface_kernel(
+    own_in, x_low, x_high, y_low, y_high, weight_in, rate_in, seen_in, cells_in, filter_in, count_in,
+    table_out, state_ref, rate_ref, sample_ref, seen_ref, filter_ref, count_ref,
+):
+    lane = lane_of()
+    inner = lane % 16
+
+    def near_side(i, carry):
+        state_ref[0, i, 16:32, :] = x_low[i]
+        state_ref[0, 8 + i, 16:32, :] = own_in[i]
+        state_ref[0, 16 + i, 16:32, :] = x_high[i]
+        for part in range(3):
+            state_ref[0, 8 * part + i, 8:16, :] = y_low[8 * part + i]
+            state_ref[0, 8 * part + i, 32:40, :] = y_high[8 * part + i]
+        return carry
+
+    lax.fori_loop(0, 8, near_side, 0, unroll=2)
+
+    def prepare(x, carry):
+        for tile in range(4):
+            rows = pl.ds(8 + 8 * tile, 8)
+            held = pl.ds(8 * tile, 8)
+            value = state_ref[0, x, rows, :]
+            state_ref[0, x, rows, :] = jnp.where(lane < 48, value, 0.0)
+            state_ref[1, x, rows, :] = jnp.where(lane < 48, pltpu.roll(value, 128 - 48, 1), 0.0)
+            for at in (0, 1):
+                rate = rate_in[at, x, held, :]
+                spread = jnp.where(lane < 16, rate, jnp.where(lane < 32, pltpu.roll(rate, 16, 1), pltpu.roll(rate, 32, 1)))
+                rate_ref[at, x, held, :] = jnp.where(lane < 48, spread, 0.0)
+        return carry
+
+    lax.fori_loop(0, 24, prepare, 0, unroll=4)
+
+    def one_step(step, carry):
+        dst = state_ref.at[(step + 1) % 2]
+
+        def planes(at, inside):
+            x = 2 * step + 2 + PLANES * at
+            src = state_ref.at[step % 2, pl.ds(x - 2, 4 + PLANES)]
+            rows = pl.ds(8, 32)
+            fields = [src[2 + j, rows, :] for j in range(PLANES)]
+            halves = jnp.concatenate([jnp.concatenate(split(v), axis=1) for v in fields], axis=0)
+            depth = jnp.dot(halves, weight_in[...], preferred_element_type=F32)
+            fresh = []
+            for j, v in enumerate(fields):
+                near = (src[1 + j, rows, :] + src[3 + j, rows, :]) + (src[2 + j, pl.ds(7, 32), :] + src[2 + j, pl.ds(9, 32), :])
+                far = (src[j, rows, :] + src[4 + j, rows, :]) + (src[2 + j, pl.ds(6, 32), :] + src[2 + j, pl.ds(10, 32), :])
+                laplace = depth[32 * j : 32 * j + 32] + (16.0 * near - far)
+                old = dst[x + j, rows, :]
+                fresh.append(old + rate_ref[0, x + j] * (v - old) + rate_ref[1, x + j] * laplace)
+            for j, value in enumerate(fresh):
+                dst[x + j, 8:40, :] = value
+                sample_ref[step, x + j, :, :] = value[8:24]
+            return inside
+
+        lax.fori_loop(0, (20 - 4 * step) // PLANES, planes, 0)
+        return carry
+
+    lax.fori_loop(0, HALF, one_step, 0)
+
+    def finish(x, carry):
         for row in (0, 8):
             rows = pl.ds(row, 8)
-            last = pack_faces([state_ref[0, k, 8 + x, pl.ds(16 + row, 8), :] for k in range(3)], lane)
-            if first:
-                after = pack_faces([state_ref[1, k, 8 + x, pl.ds(16 + row, 8), :] for k in range(3)], lane)
-                face_out[x, rows, :] = jnp.where(lane < 48, last, pltpu.roll(after, 48, 1))
-                seen = jnp.zeros((8, 128), F32)
-            else:
-                seen = seen_in[x, rows, :]
+            seen = seen_in[x, rows, :]
             for step in range(HALF):
-                edge = pltpu.roll(last, 64, 1) if step == HALF - 1 else edge_ref[step + 1, 8 + x, rows, :]
-                at = begin + step
-                seen = jnp.where((inner == 8 + at) & (lane >= 64) & (lane < 112), pltpu.roll(edge, at, 1), seen)
-            seen_out[x, rows, :] = seen
+                at = HALF + step
+                sample = pltpu.roll(sample_ref[step, 8 + x, rows, :], at, 1)
+                seen = jnp.where((inner == at) & (lane < 48), sample, seen)
+            seen_ref[x, rows, :] = seen
         return carry
 
     lax.fori_loop(0, 8, finish, 0, unroll=4)
 
-    if not first:
-        filter_ref[...] = filter_in[...].astype(F32)
-        blank = jnp.zeros((8, CLASSES * MODES), F32)
-        blocks = [blank] * 16
-        for k in range(3):
-            blocks[9 + 2 * k] = filter_ref[pl.ds(k, STEPS, stride=3), :]
-        filters = jnp.concatenate(blocks, axis=0).astype(jnp.bfloat16)
-        motion = seen_out[...].reshape(128, 128).astype(jnp.bfloat16)
-        modal = lax.dot_general(filters, motion, (((0,), (1,)), ((), ())), preferred_element_type=F32)
-        modes = lax.broadcasted_iota(jnp.int32, (MODES, 128), 0)
-        count_ref[...] = jnp.zeros((8, 128), jnp.int32)
-        count_ref[0:1, 0:CLASSES] = count_in[...]
-        counts = jnp.where(modes == lane, jnp.broadcast_to(count_ref[0:1, :], (8, 128)), 0)
-        counts = jnp.sum(counts, axis=1, keepdims=True)
-        energies = []
-        for kind in range(CLASSES):
-            part = modal[MODES * kind : MODES * (kind + 1), :]
-            part = jnp.where(modes < counts[kind : kind + 1, :], part * part, 0.0)
-            energies.append(jnp.sum(part, axis=0, keepdims=True))
-        demand = 0.5 * jnp.log1p(jnp.concatenate(energies, axis=0))
-        for owner in range(table_out.shape[0]):
-            cells = jnp.broadcast_to(cells_in[owner : owner + 1, :], (CLASSES, 128))
-            chosen = jnp.take_along_axis(demand, cells, axis=1)
-            for level in range(table_out.shape[1]):
-                table_out[owner, level] = chosen
+    filter_ref[...] = filter_in[...].astype(F32)
+    blocks = [jnp.zeros((8, CLASSES * MODES), F32)] * 16
+    for k in range(3):
+        blocks[2 * k] = filter_ref[pl.ds(k, STEPS, stride=3), :]
+    filters = jnp.concatenate(blocks, axis=0).astype(jnp.bfloat16)
+    motion = seen_ref[...].reshape(128, 128).astype(jnp.bfloat16)
+    modal = lax.dot_general(filters, motion, (((0,), (1,)), ((), ())), preferred_element_type=F32)
+    modes = lax.broadcasted_iota(jnp.int32, (MODES, 128), 0)
+    count_ref[...] = jnp.zeros((8, 128), jnp.int32)
+    count_ref[0:1, 0:CLASSES] = count_in[...]
+    counts = jnp.where(modes == lane, jnp.broadcast_to(count_ref[0:1, :], (8, 128)), 0)
+    counts = jnp.sum(counts, axis=1, keepdims=True)
+    energies = []
+    for kind in range(CLASSES):
+        part = modal[MODES * kind : MODES * (kind + 1), :]
+        part = jnp.where(modes < counts[kind : kind + 1, :], part * part, 0.0)
+        energies.append(jnp.sum(part, axis=0, keepdims=True))
+    demand = 0.5 * jnp.log1p(jnp.concatenate(energies, axis=0))
+    for owner in range(table_out.shape[0]):
+        cells = jnp.broadcast_to(cells_in[owner : owner + 1, :], (CLASSES, 128))
+        chosen = jnp.take_along_axis(demand, cells, axis=1)
+        for level in range(table_out.shape[1]):
+            table_out[owner, level] = chosen
 
 
 def fragility_kernel(
@@ -477,7 +571,8 @@
 ):
     own = (3, 8, 16, 128)
     plane = (8, 16, 128)
-    wide = [pltpu.VMEM((2, 4, 24, 48, 128), F32), pltpu.VMEM((HALF, 24, 16, 128), F32)]
+    wide = pltpu.VMEM((2, 4, 24, 48, 128), F32)
+    samples = pltpu.VMEM((HALF, 24, 16, 128), F32)
 
     u, p, a, e, faces = call(
         start_kernel,
@@ -489,26 +584,38 @@
     )
     received = exchange(u, p, faces, (a, e))
     weights = jnp.asarray(depth_weights(), jnp.bfloat16)
-    u, p, faces, seen, rates = call(
+    u, p, faces, slab, seen, rates = call(
         functools.partial(steps_kernel, True),
         "steps_first",
-        [own, own, plane, plane, (4, 24, 32, 128)],
+        [own, own, plane, plane, plane, (4, 24, 32, 128)],
         [u, p, a, e, *received, weights],
-        scratch=wide,
-    )
-    received = exchange(u, p, faces, ())
+        scratch=[wide, samples],
+    )
+
+    x_low, x_high = both_ways(slab, slab, "gx")
+    y_low, y_high = both_ways(*call(slab_message_kernel, "slab_message", [(24, 8, 128)] * 2, [slab, x_low, x_high]), "gy")
     owners, levels = lax.axis_size("gx"), lax.axis_size("gz")
-    args = [u, p, *received, weights, seen, rates, send_cells.reshape(owners, 128), modal_filter.T, mode_count.reshape(1, CLASSES)]
-    field, table = call(
-        functools.partial(steps_kernel, False),
-        "steps_second",
-        [own, (owners, levels, CLASSES, 128)],
-        args,
-        scratch=wide
-        + [pltpu.VMEM(plane, F32), pltpu.VMEM((3 * STEPS, CLASSES * MODES), F32), pltpu.VMEM((8, 128), jnp.int32)],
+    (table,) = call(
+        surface_kernel,
+        "surface",
+        [(owners, levels, CLASSES, 128)],
+        [slab, x_low, x_high, y_low, y_high, jnp.asarray(slab_weights(), jnp.bfloat16), rates, seen]
+        + [send_cells.reshape(owners, 128), modal_filter.T, mode_count.reshape(1, CLASSES)],
+        scratch=[
+            pltpu.VMEM((2, 24, 48, 128), F32),
+            pltpu.VMEM((2, 24, 32, 128), F32),
+            samples,
+            pltpu.VMEM(plane, F32),
+            pltpu.VMEM((3 * STEPS, CLASSES * MODES), F32),
+            pltpu.VMEM((8, 128), jnp.int32),
+        ],
     )
     table = table.reshape(owners * levels, CLASSES, 128)
     table = lax.all_to_all(table, ("gx", "gz"), split_axis=0, concat_axis=0, tiled=True)
+    received = exchange(u, p, faces, ())
+    (field,) = call(
+        functools.partial(steps_kernel, False), "steps_second", [own], [u, p, *received, weights, rates], scratch=[wide]
+    )
     (probability,) = call(
         fragility_kernel,
         "fragility",

time: 131 us -> 132 us (level)
  starting transfers between devices: 35.5 us -> 65.8 us
  blocking collectives: 20.7 us -> 0 us
  waiting for transfers between devices: 51.5 us -> 40.1 us
  Pallas kernels: 17.8 us -> 20.9 us
    all_to_all x1 -> x0, blocking collectives: 20.7 us -> none  [body(): lax.all_to_all(table, ('gx', 'gz'), split_axis=0, concat_axis=0, tiled=True)]
    all_to_all x0 -> x1, starting transfers between devices: none -> 15 us  [body(): lax.all_to_all(table, ('gx', 'gz'), split_axis=0, concat_axis=0, tiled=True)]
    ppermute x6 -> x8, starting transfers between devices: 18.3 us -> 30.1 us  [both_ways(): lax.ppermute(to_up, axis, forward)]
    ppermute x6 -> x8, waiting for transfers between devices: 22 us -> 16.2 us  [both_ways(): lax.ppermute(to_down, axis, backward)]
    ppermute x6 -> x8, waiting for transfers between devices: 29.5 us -> 23.9 us  [both_ways(): lax.ppermute(to_up, axis, forward)]
    ppermute x6 -> x8, starting transfers between devices: 17.2 us -> 20.7 us  [both_ways(): lax.ppermute(to_down, axis, backward)]
    pallas_call x8 -> x10, Pallas kernels: 17.8 us -> 20.9 us  [call(): pl.pallas_call(kernel, out_shape=out, in_specs=specs or [VM] * len(args),...]
    unnamed x28 -> x30, local copies, waits for them, and re-layouts: 3.64 us -> 3.64 us
  transfers between devices with their start and end apart: 12 -> 17, of which waited for: 10 -> 9; matrix products, arithmetic and copies ran while one was open for 0% -> 0% of each run, Pallas kernels for 0% -> 9%
where the time goes in v6:
time: 132 us
  starting transfers between devices  65.8 us (50%)
  waiting for transfers between devices  40.1 us (30%)
  Pallas kernels  20.9 us (16%)
  local copies, waits for them, and re-layouts  3.64 us (3%)
    ppermute x8, starting transfers between devices, both_ways(): lax.ppermute(to_up, axis, forward)  30.1 us
    ppermute x8, waiting for transfers between devices, both_ways(): lax.ppermute(to_up, axis, forward)  23.9 us
    pallas_call x10, Pallas kernels, call(): pl.pallas_call(kernel, out_shape=out, in_specs=specs or [VM] * len(args),...  20.9 us
    ppermute x8, starting transfers between devices, both_ways(): lax.ppermute(to_down, axis, backward)  20.7 us
    ppermute x8, waiting for transfers between devices, both_ways(): lax.ppermute(to_down, axis, backward)  16.2 us
    all_to_all x1, starting transfers between devices, body(): lax.all_to_all(table, ('gx', 'gz'), split_axis=0, concat_axis=0, tiled=True)  15 us
    unnamed x30, local copies, waits for them, and re-layouts  3.64 us
  transfers between devices with their start and end apart: 17, of which 9 were waited for; matrix products, arithmetic and copies ran while one was open for 0% of the time, Pallas kernels for 9%

profile of v6, /device:TPU:1, one launch (start us, length us, event | category | flops | bytes accessed | tf_op | source)
XLA Modules:
  0.0 131.6 jit_solution(16908579808706822061)
XLA Ops:
  0.7 1.0 copy-done.1
  4.2 1.4 %start.1 = (f32[3,8,16,128]{3,2,1,0:T(8,128)S(1)}, f32[3,8,16,128]{3,2,1,0:T(8,128)S(1)}, f32[8,16,128]{2,1,0:T(8,128)S(1)}, f32[8,16,128]{2,1,0:T(8,128)S(1)}, f32[8,16,128]{2,1,0:T(8,128)S(1)}) custom-call(f32[3,8,16,128]{3,2,1,0:T(8,128)S(1)} %copy-done.1, f32[3,8,16,128]{3,2,1,0:T(8,128)S(1)} %copy-done.2, f32[8,16,128]{2,1,0:T(8,128)S(1)} %copy-done.4, ...), custom_call_target="tpu_custom_call" | custom-call | tf_op jit(solution)/shard_map/start/pallas_call | solution.py:514
  5.6 8.8 %collective-permute-start.1 = (f32[8,16,128]{2,1,0:T(8,128)S(1)}, f32[8,16,128]{2,1,0:T(8,128)S(1)}, u32[]{:S(2)}, u32[]{:S(2)}) collective-permute-start(f32[8,16,128]{2,1,0:T(8,128)S(1)} %get-tuple-element.31), channel_id=1, source_target_pairs={{1,0},{2,1},{3,2},{5,4},{6,5},{7,6},{9,8},{10,9},{11,10},{13,12},{... | collective-permute-start | bytes 196616 | tf_op jit(solution)/shard_map/ppermute | solution.py:529
  14.4 1.9 %collective-permute-start = (f32[8,16,128]{2,1,0:T(8,128)S(1)}, f32[8,16,128]{2,1,0:T(8,128)S(1)}, u32[]{:S(2)}, u32[]{:S(2)}) collective-permute-start(f32[8,16,128]{2,1,0:T(8,128)S(1)} %get-tuple-element.31), channel_id=1, source_target_pairs={{0,1},{1,2},{2,3},{4,5},{5,6},{6,7},{8,9},{9,10},{10,11},{12,13},{... | collective-permute-start | bytes 196616 | tf_op jit(solution)/shard_map/ppermute | solution.py:529
  16.4 1.3 collective-permute-done.refs_0_
  18.0 1.3 collective-permute-start.2
  19.3 1.3 collective-permute-start.3
  20.6 8.1 %collective-permute-done.2.refs_6_.refs_5_ = s16[62,16,128]{2,1,0:T(8,128)(2,1)S(1)} collective-permute-done((s16[62,16,128]{2,1,0:T(8,128)(2,1)S(1)}, s16[62,16,128]{2,1,0:T(8,128)(2,1)S(1)}, u32[]{:S(2)}, u32[]{:S(2)}) %collective-permute-start.2) | collective-permute-done | bytes 253984 | tf_op jit(solution)/shard_map/ppermute | solution.py:529
  28.7 5.9 %collective-permute-done.3.refs_7_.refs_6_ = s16[62,16,128]{2,1,0:T(8,128)(2,1)S(1)} collective-permute-done((s16[62,16,128]{2,1,0:T(8,128)(2,1)S(1)}, s16[62,16,128]{2,1,0:T(8,128)(2,1)S(1)}, u32[]{:S(2)}, u32[]{:S(2)}) %collective-permute-start.3) | collective-permute-done | bytes 253984 | tf_op jit(solution)/shard_map/ppermute | solution.py:529
  35.0 4.2 %collective-permute-start.4 = (s16[97,16,128]{2,1,0:T(8,128)(2,1)S(1)}, s16[97,16,128]{2,1,0:T(8,128)(2,1)S(1)}, u32[]{:S(2)}, u32[]{:S(2)}) collective-permute-start(s16[97,16,128]{2,1,0:T(8,128)(2,1)S(1)} %get-tuple-element.36), channel_id=1, source_target_pairs={{0,4},{4,8},{8,12},{12,16},{16,20},{20,24},{24,28},{1,5},{5,9},{9,... | collective-permute-start | bytes 1191944 | tf_op jit(solution)/shard_map/ppermute | solution.py:529
  39.2 1.3 collective-permute-start.5
  40.5 6.8 %collective-permute-done.4.refs_7_ = s16[97,16,128]{2,1,0:T(8,128)(2,1)S(1)} collective-permute-done((s16[97,16,128]{2,1,0:T(8,128)(2,1)S(1)}, s16[97,16,128]{2,1,0:T(8,128)(2,1)S(1)}, u32[]{:S(2)}, u32[]{:S(2)}) %collective-permute-start.4) | collective-permute-done | bytes 397344 | tf_op jit(solution)/shard_map/ppermute | solution.py:529
  47.3 4.8 %collective-permute-done.5.refs_8_ = s16[97,16,128]{2,1,0:T(8,128)(2,1)S(1)} collective-permute-done((s16[97,16,128]{2,1,0:T(8,128)(2,1)S(1)}, s16[97,16,128]{2,1,0:T(8,128)(2,1)S(1)}, u32[]{:S(2)}, u32[]{:S(2)}) %collective-permute-start.5) | collective-permute-done | bytes 397344 | tf_op jit(solution)/shard_map/ppermute | solution.py:529
  52.1 6.6 %steps_first.1 = (f32[3,8,16,128]{3,2,1,0:T(8,128)S(1)}, f32[3,8,16,128]{3,2,1,0:T(8,128)S(1)}, f32[8,16,128]{2,1,0:T(8,128)S(1)}, f32[8,16,128]{2,1,0:T(8,128)S...) custom-call(f32[3,8,16,128]{3,2,1,0:T(8,128)S(1)} %get-tuple-element.27.refs_2_.refs_0_, ...), custom_call_target="tpu_custom_call" | custom-call | tf_op jit(solution)/shard_map/steps_first/pallas_call | solution.py:514
  58.7 1.3 collective-permute-start.13
  60.0 5.2 %collective-permute-start.12 = (f32[8,16,128]{2,1,0:T(8,128)S(1)}, f32[8,16,128]{2,1,0:T(8,128)S(1)}, u32[]{:S(2)}, u32[]{:S(2)}) collective-permute-start(f32[8,16,128]{2,1,0:T(8,128)S(1)} %get-tuple-element.48.own_ref.own_in), channel_id=1, source_target_pairs={{0,32},{32,64},{64,96},{96,128},{128,160},{160,192},{192,224},{224... | collective-permute-start | bytes 196616 | tf_op jit(solution)/shard_map/ppermute | solution.py:529
  65.2 1.5 %collective-permute-done.12.low_ref.x_low = f32[8,16,128]{2,1,0:T(8,128)S(1)} collective-permute-done((f32[8,16,128]{2,1,0:T(8,128)S(1)}, f32[8,16,128]{2,1,0:T(8,128)S(1)}, u32[]{:S(2)}, u32[]{:S(2)}) %collective-permute-start.12) | collective-permute-done | bytes 65568 | tf_op jit(solution)/shard_map/ppermute | solution.py:529
  66.8 4.0 %collective-permute-start.14 = (f32[24,8,128]{2,1,0:T(8,128)S(1)}, f32[24,8,128]{2,1,0:T(8,128)S(1)}, u32[]{:S(2)}, u32[]{:S(2)}) collective-permute-start(f32[24,8,128]{2,1,0:T(8,128)S(1)} %get-tuple-element.49), channel_id=1, source_target_pairs={{0,4},{4,8},{8,12},{12,16},{16,20},{20,24},{24,28},{1,5},{5,9},{9,... | collective-permute-start | bytes 294920 | tf_op jit(solution)/shard_map/ppermute | solution.py:529
  70.8 1.3 collective-permute-start.15
  72.1 4.1 %collective-permute-start.7 = (f32[8,16,128]{2,1,0:T(8,128)S(1)}, f32[8,16,128]{2,1,0:T(8,128)S(1)}, u32[]{:S(2)}, u32[]{:S(2)}) collective-permute-start(f32[8,16,128]{2,1,0:T(8,128)S(1)} %get-tuple-element.40), channel_id=1, source_target_pairs={{1,0},{2,1},{3,2},{5,4},{6,5},{7,6},{9,8},{10,9},{11,10},{13,12},{... | collective-permute-start | bytes 196616 | tf_op jit(solution)/shard_map/ppermute | solution.py:529
  76.1 1.9 %collective-permute-start.6 = (f32[8,16,128]{2,1,0:T(8,128)S(1)}, f32[8,16,128]{2,1,0:T(8,128)S(1)}, u32[]{:S(2)}, u32[]{:S(2)}) collective-permute-start(f32[8,16,128]{2,1,0:T(8,128)S(1)} %get-tuple-element.40), channel_id=1, source_target_pairs={{0,1},{1,2},{2,3},{4,5},{5,6},{6,7},{8,9},{9,10},{10,11},{12,13},{... | collective-permute-start | bytes 196616 | tf_op jit(solution)/shard_map/ppermute | solution.py:529
  78.1 1.3 collective-permute-done.6.refs_0_
  79.6 5.8 %collective-permute-start.8 = (s16[50,16,128]{2,1,0:T(8,128)(2,1)S(1)}, s16[50,16,128]{2,1,0:T(8,128)(2,1)S(1)}, u32[]{:S(2)}, u32[]{:S(2)}) collective-permute-start(s16[50,16,128]{2,1,0:T(8,128)(2,1)S(1)} %get-tuple-element.42), channel_id=1, source_target_pairs={{0,32},{32,64},{64,96},{96,128},{128,160},{160,192},{192,224},{224... | collective-permute-start | bytes 614408 | tf_op jit(solution)/shard_map/ppermute | solution.py:529
  85.4 1.3 collective-permute-start.9
  86.8 4.4 %surface.1 = f32[16,4,8,128]{3,2,1,0:T(8,128)} custom-call(f32[8,16,128]{2,1,0:T(8,128)S(1)} %get-tuple-element.48.own_ref.own_in, f32[8,16,128]{2,1,0:T(8,128)S(1)} %collective-permute-done.12.low_ref.x_low, f32[8,16,128]{2,1,0:T(8,128)S(1)} %collective-permute-done.13.high_ref.x_high, f32[24,8,128]{2,1,0:T(8,128)S(1)} %collective-permute-done.14.y_low, ...), custom_call_target="tpu_custom_call" | custom-call | tf_op jit(solution)/shard_map/surface/pallas_call | solution.py:514
  91.2 15.0 %all-to-all-start = ((f32[64,8,128]{2,1,0:T(8,128)}), f32[64,8,128]{2,1,0:T(8,128)S(1)}, u32[]{:S(2)}, u32[]{:S(2)}) async-start(f32[64,8,128]{2,1,0:T(8,128)} %bitcast.3), calls=%async_computation | async-start | bytes 524288 | tf_op jit(solution)/shard_map/all_to_all | solution.py:614
  106.5 5.9 %collective-permute-start.10 = (s16[77,16,128]{2,1,0:T(8,128)(2,1)S(1)}, s16[77,16,128]{2,1,0:T(8,128)(2,1)S(1)}, u32[]{:S(2)}, u32[]{:S(2)}) collective-permute-start(s16[77,16,128]{2,1,0:T(8,128)(2,1)S(1)} %get-tuple-element.45), channel_id=1, source_target_pairs={{0,4},{4,8},{8,12},{12,16},{16,20},{20,24},{24,28},{1,5},{5,9},{9,... | collective-permute-start | bytes 946184 | tf_op jit(solution)/shard_map/ppermute | solution.py:529
  112.4 1.4 %collective-permute-start.11 = (s16[77,16,128]{2,1,0:T(8,128)(2,1)S(1)}, s16[77,16,128]{2,1,0:T(8,128)(2,1)S(1)}, u32[]{:S(2)}, u32[]{:S(2)}) collective-permute-start(s16[77,16,128]{2,1,0:T(8,128)(2,1)S(1)} %get-tuple-element.46), channel_id=1, source_target_pairs={{4,0},{8,4},{12,8},{16,12},{20,16},{24,20},{28,24},{5,1},{9,5},{13... | collective-permute-start | bytes 946184 | tf_op jit(solution)/shard_map/ppermute | solution.py:529
  113.8 4.8 %collective-permute-done.10.refs_5_ = s16[77,16,128]{2,1,0:T(8,128)(2,1)S(1)} collective-permute-done((s16[77,16,128]{2,1,0:T(8,128)(2,1)S(1)}, s16[77,16,128]{2,1,0:T(8,128)(2,1)S(1)}, u32[]{:S(2)}, u32[]{:S(2)}) %collective-permute-start.10) | collective-permute-done | bytes 315424 | tf_op jit(solution)/shard_map/ppermute | solution.py:529
  118.6 5.5 %collective-permute-done.11.refs_6_ = s16[77,16,128]{2,1,0:T(8,128)(2,1)S(1)} collective-permute-done((s16[77,16,128]{2,1,0:T(8,128)(2,1)S(1)}, s16[77,16,128]{2,1,0:T(8,128)(2,1)S(1)}, u32[]{:S(2)}, u32[]{:S(2)}) %collective-permute-start.11) | collective-permute-done | bytes 315424 | tf_op jit(solution)/shard_map/ppermute | solution.py:529
  124.2 6.4 %steps_second.1 = f32[3,8,16,128]{3,2,1,0:T(8,128)} custom-call(f32[3,8,16,128]{3,2,1,0:T(8,128)S(1)} %get-tuple-element.38.refs_2_.refs_0_, f32[3,8,16,128]{3,2,1,0:T(8,128)S(1)} %get-tuple-element.39.refs_3_.refs_1_, f32[8,16,128]{2,1,0:T(8,128)S(1)} %get-tuple-element.41.refs_2_, s16[50,16,128]{2,1,0:T(8,128)(2,1)S(1)} %collective-permute-done.8.refs_4_.refs_3_, ...), custom_call_target="tpu_custom_call" | custom-call | tf_op jit(solution)/shard_map/steps_second/pallas_call | solution.py:514
  130.6 1.0 fragility.1
  (42 shorter events, 3.9 us)
Async XLA Ops:
  0.6 51.4 %copy-start = (bf16[3,256,256]{2,1,0:T(8,128)(2,1)S(1)}, bf16[3,256,256]{2,1,0:T(8,128)(2,1)}, u32[]{:S(2)}) copy-start(bf16[3,256,256]{2,1,0:T(8,128)(2,1)} %constant.4.clone.refs_9_.refs_7_) | copy-start | bytes 1179652
  0.6 1.0 copy-start.1
  1.6 0.9 copy-start.2
  2.5 0.8 copy-start.4
  3.4 0.8 copy-start.5
  5.6 10.7 %collective-permute-start.1 = (f32[8,16,128]{2,1,0:T(8,128)S(1)}, f32[8,16,128]{2,1,0:T(8,128)S(1)}, u32[]{:S(2)}, u32[]{:S(2)}) collective-permute-start(f32[8,16,128]{2,1,0:T(8,128)S(1)} %get-tuple-element.31), channel_id=1, source_target_pairs={{1,0},{2,1},{3,2},{5,4},{6,5},{7,6},{9,8},{10,9},{11,10},{13,12},{... | collective-permute-start | bytes 196616 | tf_op jit(solution)/shard_map/ppermute | solution.py:529
  14.4 3.2 %collective-permute-start = (f32[8,16,128]{2,1,0:T(8,128)S(1)}, f32[8,16,128]{2,1,0:T(8,128)S(1)}, u32[]{:S(2)}, u32[]{:S(2)}) collective-permute-start(f32[8,16,128]{2,1,0:T(8,128)S(1)} %get-tuple-element.31), channel_id=1, source_target_pairs={{0,1},{1,2},{2,3},{4,5},{5,6},{6,7},{8,9},{9,10},{10,11},{12,13},{... | collective-permute-start | bytes 196616 | tf_op jit(solution)/shard_map/ppermute | solution.py:529
  18.0 10.8 %collective-permute-start.2 = (s16[62,16,128]{2,1,0:T(8,128)(2,1)S(1)}, s16[62,16,128]{2,1,0:T(8,128)(2,1)S(1)}, u32[]{:S(2)}, u32[]{:S(2)}) collective-permute-start(s16[62,16,128]{2,1,0:T(8,128)(2,1)S(1)} %get-tuple-element.33), channel_id=1, source_target_pairs={{0,32},{32,64},{64,96},{96,128},{128,160},{160,192},{192,224},{224... | collective-permute-start | bytes 761864 | tf_op jit(solution)/shard_map/ppermute | solution.py:529
  19.3 15.4 %collective-permute-start.3 = (s16[62,16,128]{2,1,0:T(8,128)(2,1)S(1)}, s16[62,16,128]{2,1,0:T(8,128)(2,1)S(1)}, u32[]{:S(2)}, u32[]{:S(2)}) collective-permute-start(s16[62,16,128]{2,1,0:T(8,128)(2,1)S(1)} %get-tuple-element.34), channel_id=1, source_target_pairs={{32,0},{64,32},{96,64},{128,96},{160,128},{192,160},{224,192},{256... | collective-permute-start | bytes 761864 | tf_op jit(solution)/shard_map/ppermute | solution.py:529
  35.0 51.8 %copy-start.3 = (bf16[256,128]{1,0:T(8,128)(2,1)S(1)}, bf16[256,128]{1,0:T(8,128)(2,1)}, u32[]{:S(2)}) copy-start(bf16[256,128]{1,0:T(8,128)(2,1)} %constant.5.clone.weight_in) | copy-start | bytes 196612
  35.0 51.8 %copy-start.6 = (s32[16,1,128]{2,1,0:T(1,128)S(1)}, s32[16,1,128]{2,1,0:T(1,128)}, u32[]{:S(2)}) copy-start(s32[16,1,128]{2,1,0:T(1,128)} %param.19) | copy-start | bytes 24580
  35.0 51.8 %copy-start.7 = (bf16[64,24]{0,1:T(8,128)(2,1)S(1)}, bf16[64,24]{0,1:T(8,128)(2,1)}, u32[]{:S(2)}) copy-start(bf16[64,24]{0,1:T(8,128)(2,1)} %param.24) | copy-start | bytes 9220
  35.0 51.8 %copy-start.13 = (s32[8]{0:T(128)S(1)}, s32[8]{0:T(128)}, u32[]{:S(2)}) copy-start(s32[8]{0:T(128)} %param.23) | copy-start | bytes 100
  35.0 12.3 %collective-permute-start.4 = (s16[97,16,128]{2,1,0:T(8,128)(2,1)S(1)}, s16[97,16,128]{2,1,0:T(8,128)(2,1)S(1)}, u32[]{:S(2)}, u32[]{:S(2)}) collective-permute-start(s16[97,16,128]{2,1,0:T(8,128)(2,1)S(1)} %get-tuple-element.36), channel_id=1, source_target_pairs={{0,4},{4,8},{8,12},{12,16},{16,20},{20,24},{24,28},{1,5},{5,9},{9,... | collective-permute-start | bytes 1191944 | tf_op jit(solution)/shard_map/ppermute | solution.py:529
  39.2 12.9 %collective-permute-start.5 = (s16[97,16,128]{2,1,0:T(8,128)(2,1)S(1)}, s16[97,16,128]{2,1,0:T(8,128)(2,1)S(1)}, u32[]{:S(2)}, u32[]{:S(2)}) collective-permute-start(s16[97,16,128]{2,1,0:T(8,128)(2,1)S(1)} %get-tuple-element.37), channel_id=1, source_target_pairs={{4,0},{8,4},{12,8},{16,12},{20,16},{24,20},{28,24},{5,1},{9,5},{13... | collective-permute-start | bytes 1191944 | tf_op jit(solution)/shard_map/ppermute | solution.py:529
  58.7 6.5 %collective-permute-start.13 = (f32[8,16,128]{2,1,0:T(8,128)S(1)}, f32[8,16,128]{2,1,0:T(8,128)S(1)}, u32[]{:S(2)}, u32[]{:S(2)}) collective-permute-start(f32[8,16,128]{2,1,0:T(8,128)S(1)} %get-tuple-element.48.own_ref.own_in), channel_id=1, source_target_pairs={{32,0},{64,32},{96,64},{128,96},{160,128},{192,160},{224,192},{256... | collective-permute-start | bytes 196616 | tf_op jit(solution)/shard_map/ppermute | solution.py:529
  60.0 6.8 %collective-permute-start.12 = (f32[8,16,128]{2,1,0:T(8,128)S(1)}, f32[8,16,128]{2,1,0:T(8,128)S(1)}, u32[]{:S(2)}, u32[]{:S(2)}) collective-permute-start(f32[8,16,128]{2,1,0:T(8,128)S(1)} %get-tuple-element.48.own_ref.own_in), channel_id=1, source_target_pairs={{0,32},{32,64},{64,96},{96,128},{128,160},{160,192},{192,224},{224... | collective-permute-start | bytes 196616 | tf_op jit(solution)/shard_map/ppermute | solution.py:529
  66.8 20.0 %collective-permute-start.14 = (f32[24,8,128]{2,1,0:T(8,128)S(1)}, f32[24,8,128]{2,1,0:T(8,128)S(1)}, u32[]{:S(2)}, u32[]{:S(2)}) collective-permute-start(f32[24,8,128]{2,1,0:T(8,128)S(1)} %get-tuple-element.49), channel_id=1, source_target_pairs={{0,4},{4,8},{8,12},{12,16},{16,20},{20,24},{24,28},{1,5},{5,9},{9,... | collective-permute-start | bytes 294920 | tf_op jit(solution)/shard_map/ppermute | solution.py:529
  70.8 16.0 %collective-permute-start.15 = (f32[24,8,128]{2,1,0:T(8,128)S(1)}, f32[24,8,128]{2,1,0:T(8,128)S(1)}, u32[]{:S(2)}, u32[]{:S(2)}) collective-permute-start(f32[24,8,128]{2,1,0:T(8,128)S(1)} %get-tuple-element.50), channel_id=1, source_target_pairs={{4,0},{8,4},{12,8},{16,12},{20,16},{24,20},{28,24},{5,1},{9,5},{13... | collective-permute-start | bytes 294920 | tf_op jit(solution)/shard_map/ppermute | solution.py:529
  72.1 6.0 %collective-permute-start.7 = (f32[8,16,128]{2,1,0:T(8,128)S(1)}, f32[8,16,128]{2,1,0:T(8,128)S(1)}, u32[]{:S(2)}, u32[]{:S(2)}) collective-permute-start(f32[8,16,128]{2,1,0:T(8,128)S(1)} %get-tuple-element.40), channel_id=1, source_target_pairs={{1,0},{2,1},{3,2},{5,4},{6,5},{7,6},{9,8},{10,9},{11,10},{13,12},{... | collective-permute-start | bytes 196616 | tf_op jit(solution)/shard_map/ppermute | solution.py:529
  76.1 3.2 %collective-permute-start.6 = (f32[8,16,128]{2,1,0:T(8,128)S(1)}, f32[8,16,128]{2,1,0:T(8,128)S(1)}, u32[]{:S(2)}, u32[]{:S(2)}) collective-permute-start(f32[8,16,128]{2,1,0:T(8,128)S(1)} %get-tuple-element.40), channel_id=1, source_target_pairs={{0,1},{1,2},{2,3},{4,5},{5,6},{6,7},{8,9},{9,10},{10,11},{12,13},{... | collective-permute-start | bytes 196616 | tf_op jit(solution)/shard_map/ppermute | solution.py:529
  79.6 26.5 %collective-permute-start.8 = (s16[50,16,128]{2,1,0:T(8,128)(2,1)S(1)}, s16[50,16,128]{2,1,0:T(8,128)(2,1)S(1)}, u32[]{:S(2)}, u32[]{:S(2)}) collective-permute-start(s16[50,16,128]{2,1,0:T(8,128)(2,1)S(1)} %get-tuple-element.42), channel_id=1, source_target_pairs={{0,32},{32,64},{64,96},{96,128},{128,160},{160,192},{192,224},{224... | collective-permute-start | bytes 614408 | tf_op jit(solution)/shard_map/ppermute | solution.py:529
  85.4 20.7 %collective-permute-start.9 = (s16[50,16,128]{2,1,0:T(8,128)(2,1)S(1)}, s16[50,16,128]{2,1,0:T(8,128)(2,1)S(1)}, u32[]{:S(2)}, u32[]{:S(2)}) collective-permute-start(s16[50,16,128]{2,1,0:T(8,128)(2,1)S(1)} %get-tuple-element.43), channel_id=1, source_target_pairs={{32,0},{64,32},{96,64},{128,96},{160,128},{192,160},{224,192},{256... | collective-permute-start | bytes 614408 | tf_op jit(solution)/shard_map/ppermute | solution.py:529
  91.2 39.4 %all-to-all-start = ((f32[64,8,128]{2,1,0:T(8,128)}), f32[64,8,128]{2,1,0:T(8,128)S(1)}, u32[]{:S(2)}, u32[]{:S(2)}) async-start(f32[64,8,128]{2,1,0:T(8,128)} %bitcast.3), calls=%async_computation | async-start | bytes 524288 | tf_op jit(solution)/shard_map/all_to_all | solution.py:614
  106.5 12.2 %collective-permute-start.10 = (s16[77,16,128]{2,1,0:T(8,128)(2,1)S(1)}, s16[77,16,128]{2,1,0:T(8,128)(2,1)S(1)}, u32[]{:S(2)}, u32[]{:S(2)}) collective-permute-start(s16[77,16,128]{2,1,0:T(8,128)(2,1)S(1)} %get-tuple-element.45), channel_id=1, source_target_pairs={{0,4},{4,8},{8,12},{12,16},{16,20},{20,24},{24,28},{1,5},{5,9},{9,... | collective-permute-start | bytes 946184 | tf_op jit(solution)/shard_map/ppermute | solution.py:529
  112.3 18.2 %copy-start.8 = (s32[1024]{0:T(1024)S(1)}, s32[1024]{0:T(1024)}, u32[]{:S(2)}) copy-start(s32[1024]{0:T(1024)} %param.20) | copy-start | bytes 12292
  112.3 18.2 %copy-start.9 = (s32[1024]{0:T(1024)S(1)}, s32[1024]{0:T(1024)}, u32[]{:S(2)}) copy-start(s32[1024]{0:T(1024)} %param.21) | copy-start | bytes 12292
  112.3 18.2 %copy-start.10 = (s32[1024]{0:T(1024)S(1)}, s32[1024]{0:T(1024)}, u32[]{:S(2)}) copy-start(s32[1024]{0:T(1024)} %param.22) | copy-start | bytes 12292
  112.4 18.2 %copy-start.11 = (f32[16,8]{0,1:T(8,128)S(1)}, f32[16,8]{0,1:T(8,128)}, u32[]{:S(2)}) copy-start(f32[16,8]{0,1:T(8,128)} %param.26) | copy-start | bytes 1540
  112.4 18.2 %copy-start.12 = (f32[16,8]{0,1:T(8,128)S(1)}, f32[16,8]{0,1:T(8,128)}, u32[]{:S(2)}) copy-start(f32[16,8]{0,1:T(8,128)} %param.27) | copy-start | bytes 1540
  112.4 18.2 %copy-start.14 = (f32[16]{0:T(128)S(1)}, f32[16]{0:T(128)}, u32[]{:S(2)}) copy-start(f32[16]{0:T(128)} %param.25) | copy-start | bytes 196
  112.4 11.8 %collective-permute-start.11 = (s16[77,16,128]{2,1,0:T(8,128)(2,1)S(1)}, s16[77,16,128]{2,1,0:T(8,128)(2,1)S(1)}, u32[]{:S(2)}, u32[]{:S(2)}) collective-permute-start(s16[77,16,128]{2,1,0:T(8,128)(2,1)S(1)} %get-tuple-element.46), channel_id=1, source_target_pairs={{4,0},{8,4},{12,8},{16,12},{20,16},{24,20},{28,24},{5,1},{9,5},{13... | collective-permute-start | bytes 946184 | tf_op jit(solution)/shard_map/ppermute | solution.py:529

commit v7 on v6

--- a/solution.py
+++ b/solution.py
@@ -366,7 +366,7 @@
     lax.fori_loop(0, 8, finish, 0, unroll=4)
 
 
-def slab_message_kernel(own_ref, low_ref, high_ref, up_ref, down_ref):
+def slab_message_kernel(own_ref, low_ref, high_ref, after_ref, up_ref, down_ref):
     def plane(i, carry):
         for at, source in ((0, low_ref), (8, own_ref), (16, high_ref)):
             up_ref[at + i] = source[i, 8:16, :]
@@ -377,7 +377,7 @@
 
 
 def surface_kernel(
-    own_in, x_low, x_high, y_low, y_high, weight_in, rate_in, seen_in, cells_in, filter_in, count_in,
+    own_in, x_low, x_high, y_low, y_high, weight_in, rate_in, seen_in, cells_in, filter_in, count_in, after_in,
     table_out, state_ref, rate_ref, sample_ref, seen_ref, filter_ref, count_ref,
 ):
     lane = lane_of()
@@ -509,6 +509,10 @@
 VM = pl.BlockSpec(memory_space=pltpu.VMEM)
 
 
+TIMES = {"start": 1.4, "steps_first": 6.7, "steps_second": 6.5, "surface": 4.5, "fragility": 1.0}
+FLOPS_A_US = 1.15e9
+
+
 def call(kernel, name, shapes, args, specs=None, scratch=()):
     out = [s if isinstance(s, jax.ShapeDtypeStruct) else jax.ShapeDtypeStruct(s, F32) for s in shapes]
     return pl.pallas_call(
@@ -518,6 +522,7 @@
         out_specs=[VM] * len(out),
         scratch_shapes=list(scratch),
         compiler_params=pltpu.CompilerParams(vmem_limit_bytes=VMEM_LIMIT),
+        cost_estimate=pl.CostEstimate(flops=int(TIMES.get(name, 0.3) * FLOPS_A_US), bytes_accessed=0, transcendentals=0),
         name=name,
     )(*args)
 
@@ -529,29 +534,30 @@
     return lax.ppermute(to_up, axis, forward), lax.ppermute(to_down, axis, backward)
 
 
-def exchange(u, p, faces, coefficients):
+def exchange_x(u, p, faces, coefficients):
     extra = list(coefficients)
-    has = bool(extra)
     z_low, z_high = both_ways(faces, faces, "gz")
     planes = 3 * XU + (3 + len(extra)) * XP + XH + 1
     message = jax.ShapeDtypeStruct((planes, 16, 128), jnp.int16)
     halo, up, down, powers = call(
-        functools.partial(x_message_kernel, has),
+        functools.partial(x_message_kernel, bool(extra)),
         "x_message",
         [(8, 16, 128), message, message, (16, 128)],
         [z_low, z_high, u, p] + extra,
     )
-    x_low, x_high = both_ways(up, down, "gx")
+    return halo, powers, *both_ways(up, down, "gx")
+
+
+def y_messages(u, p, coefficients, halo, powers, x_low, x_high):
+    extra = list(coefficients)
     planes = (3 * YU + (3 + len(extra)) * YP + YH) // 2 + 1
     message = jax.ShapeDtypeStruct((planes, 16, 128), jnp.int16)
-    up, down = call(
-        functools.partial(y_message_kernel, has),
+    return call(
+        functools.partial(y_message_kernel, bool(extra)),
         "y_message",
         [message, message],
         [u, p] + extra + [halo, powers, x_low, x_high],
     )
-    y_low, y_high = both_ways(up, down, "gy")
-    return halo, x_low, x_high, y_low, y_high
 
 
 def body(
@@ -582,7 +588,9 @@
         specs=[pl.BlockSpec(memory_space=pltpu.HBM)] * 4,
         scratch=[pltpu.VMEM(plane, F32)] * 2 + [pltpu.SemaphoreType.DMA((8,))],
     )
-    received = exchange(u, p, faces, (a, e))
+    halo, powers, x_low, x_high = exchange_x(u, p, faces, (a, e))
+    messages = y_messages(u, p, (a, e), halo, powers, x_low, x_high)
+    received = (halo, x_low, x_high, *both_ways(*messages, "gy"))
     weights = jnp.asarray(depth_weights(), jnp.bfloat16)
     u, p, faces, slab, seen, rates = call(
         functools.partial(steps_kernel, True),
@@ -592,15 +600,20 @@
         scratch=[wide, samples],
     )
 
-    x_low, x_high = both_ways(slab, slab, "gx")
-    y_low, y_high = both_ways(*call(slab_message_kernel, "slab_message", [(24, 8, 128)] * 2, [slab, x_low, x_high]), "gy")
+    near_low, near_high = both_ways(slab, slab, "gx")
+    halo, powers, x_low, x_high = exchange_x(u, p, faces, ())
+    slab_messages = call(slab_message_kernel, "slab_message", [(24, 8, 128)] * 2, [slab, near_low, near_high, powers])
+    side_low, side_high = both_ways(*slab_messages, "gy")
+    messages = y_messages(u, p, (), halo, powers, x_low, x_high)
+    received = (halo, x_low, x_high, *both_ways(*messages, "gy"))
     owners, levels = lax.axis_size("gx"), lax.axis_size("gz")
     (table,) = call(
         surface_kernel,
         "surface",
         [(owners, levels, CLASSES, 128)],
-        [slab, x_low, x_high, y_low, y_high, jnp.asarray(slab_weights(), jnp.bfloat16), rates, seen]
-        + [send_cells.reshape(owners, 128), modal_filter.T, mode_count.reshape(1, CLASSES)],
+        [slab, near_low, near_high, side_low, side_high, jnp.asarray(slab_weights(), jnp.bfloat16), rates, seen]
+        + [send_cells.reshape(owners, 128), modal_filter.T, mode_count.reshape(1, CLASSES), messages[0]],
+        specs=[VM] * 11 + [pl.BlockSpec(memory_space=pl.ANY)],
         scratch=[
             pltpu.VMEM((2, 24, 48, 128), F32),
             pltpu.VMEM((2, 24, 32, 128), F32),
@@ -612,7 +625,6 @@
     )
     table = table.reshape(owners * levels, CLASSES, 128)
     table = lax.all_to_all(table, ("gx", "gz"), split_axis=0, concat_axis=0, tiled=True)
-    received = exchange(u, p, faces, ())
     (field,) = call(
         functools.partial(steps_kernel, False), "steps_second", [own], [u, p, *received, weights, rates], scratch=[wide]
     )

time: 132 us -> 128 us (0.970)
  starting transfers between devices: 65.8 us -> 58.9 us
  local copies, waits for them, and re-layouts: 3.64 us -> 5 us
    ppermute x8, waiting for transfers between devices: 23.9 us -> 17.6 us  [both_ways(): lax.ppermute(to_up, axis, forward)]
    all_to_all x1, starting transfers between devices: 15 us -> 8.74 us  [body(): lax.all_to_all(table, ('gx', 'gz'), split_axis=0, concat_axis=0, tiled=True)]
    all_to_all x1, waiting for transfers between devices: 0.01 us -> 4.13 us  [body(): lax.all_to_all(table, ('gx', 'gz'), split_axis=0, concat_axis=0, tiled=True)]
    ppermute x8, waiting for transfers between devices: 16.2 us -> 18.9 us  [both_ways(): lax.ppermute(to_down, axis, backward)]
    unnamed x30 -> x34, local copies, waits for them, and re-layouts: 3.64 us -> 5 us
  transfers between devices with their start and end apart: 17 -> 17, of which waited for: 9 -> 8; matrix products, arithmetic and copies ran while one was open for 0% -> 0% of each run, Pallas kernels for 9% -> 9%
where the time goes in v7:
time: 128 us; the launch traced here: 127 us
  starting transfers between devices  58.9 us (46%)
  waiting for transfers between devices  40.6 us (32%)
  Pallas kernels  21.2 us (17%)
  local copies, waits for them, and re-layouts  5 us (4%)
    ppermute x8, starting transfers between devices, both_ways(): lax.ppermute(to_up, axis, forward)  30.4 us
    pallas_call x10, Pallas kernels, call(): pl.pallas_call(kernel, out_shape=out, in_specs=specs or [VM] * len(args),...  21.2 us
    ppermute x8, starting transfers between devices, both_ways(): lax.ppermute(to_down, axis, backward)  19.8 us
    ppermute x8, waiting for transfers between devices, both_ways(): lax.ppermute(to_down, axis, backward)  18.9 us
    ppermute x8, waiting for transfers between devices, both_ways(): lax.ppermute(to_up, axis, forward)  17.6 us
    all_to_all x1, starting transfers between devices, body(): lax.all_to_all(table, ('gx', 'gz'), split_axis=0, concat_axis=0, tiled=True)  8.74 us
    unnamed x34, local copies, waits for them, and re-layouts  5 us
    all_to_all x1, waiting for transfers between devices, body(): lax.all_to_all(table, ('gx', 'gz'), split_axis=0, concat_axis=0, tiled=True)  4.13 us
  transfers between devices with their start and end apart: 17, of which 8 were waited for; matrix products, arithmetic and copies ran while one was open for 0% of the time, Pallas kernels for 9%

profile of v7, /device:TPU:1, one launch (start us, length us, event | category | flops | bytes accessed | tf_op | source)
XLA Modules:
  0.0 126.8 jit_solution(396253404824788848)
XLA Ops:
  1.6 0.9 copy-done.1
  4.2 1.4 %start.1 = (f32[3,8,16,128]{3,2,1,0:T(8,128)S(1)}, f32[3,8,16,128]{3,2,1,0:T(8,128)S(1)}, f32[8,16,128]{2,1,0:T(8,128)S(1)}, f32[8,16,128]{2,1,0:T(8,128)S(1)}, f32[8,16,128]{2,1,0:T(8,128)S(1)}) custom-call(f32[3,8,16,128]{3,2,1,0:T(8,128)S(1)} %copy-done, f32[3,8,16,128]{3,2,1,0:T(8,128)S(1)} %copy-done.1, f32[8,16,128]{2,1,0:T(8,128)S(1)} %copy-done.2, ...), custom_call_target="tpu_custom_call" | custom-call | flops 1610000000 | tf_op jit(solution)/shard_map/start/pallas_call | solution.py:518
  5.6 8.9 %collective-permute-start.1 = (f32[8,16,128]{2,1,0:T(8,128)S(1)}, f32[8,16,128]{2,1,0:T(8,128)S(1)}, u32[]{:S(2)}, u32[]{:S(2)}) collective-permute-start(f32[8,16,128]{2,1,0:T(8,128)S(1)} %get-tuple-element.31), channel_id=1, source_target_pairs={{1,0},{2,1},{3,2},{5,4},{6,5},{7,6},{9,8},{10,9},{11,10},{13,12},{... | collective-permute-start | bytes 196616 | tf_op jit(solution)/shard_map/ppermute | solution.py:534
  14.5 1.9 %collective-permute-start = (f32[8,16,128]{2,1,0:T(8,128)S(1)}, f32[8,16,128]{2,1,0:T(8,128)S(1)}, u32[]{:S(2)}, u32[]{:S(2)}) collective-permute-start(f32[8,16,128]{2,1,0:T(8,128)S(1)} %get-tuple-element.31), channel_id=1, source_target_pairs={{0,1},{1,2},{2,3},{4,5},{5,6},{6,7},{8,9},{9,10},{10,11},{12,13},{... | collective-permute-start | bytes 196616 | tf_op jit(solution)/shard_map/ppermute | solution.py:534
  16.5 1.3 %collective-permute-done.refs_0_ = f32[8,16,128]{2,1,0:T(8,128)S(1)} collective-permute-done((f32[8,16,128]{2,1,0:T(8,128)S(1)}, f32[8,16,128]{2,1,0:T(8,128)S(1)}, u32[]{:S(2)}, u32[]{:S(2)}) %collective-permute-start) | collective-permute-done | bytes 65568 | tf_op jit(solution)/shard_map/ppermute | solution.py:534
  18.0 1.3 %collective-permute-start.2 = (s16[62,16,128]{2,1,0:T(8,128)(2,1)S(1)}, s16[62,16,128]{2,1,0:T(8,128)(2,1)S(1)}, u32[]{:S(2)}, u32[]{:S(2)}) collective-permute-start(s16[62,16,128]{2,1,0:T(8,128)(2,1)S(1)} %get-tuple-element.33), channel_id=1, source_target_pairs={{0,32},{32,64},{64,96},{96,128},{128,160},{160,192},{192,224},{224... | collective-permute-start | bytes 761864 | tf_op jit(solution)/shard_map/ppermute | solution.py:534
  19.3 1.3 %collective-permute-start.3 = (s16[62,16,128]{2,1,0:T(8,128)(2,1)S(1)}, s16[62,16,128]{2,1,0:T(8,128)(2,1)S(1)}, u32[]{:S(2)}, u32[]{:S(2)}) collective-permute-start(s16[62,16,128]{2,1,0:T(8,128)(2,1)S(1)} %get-tuple-element.34), channel_id=1, source_target_pairs={{32,0},{64,32},{96,64},{128,96},{160,128},{192,160},{224,192},{256... | collective-permute-start | bytes 761864 | tf_op jit(solution)/shard_map/ppermute | solution.py:534
  20.6 8.1 %collective-permute-done.2.refs_6_.refs_5_ = s16[62,16,128]{2,1,0:T(8,128)(2,1)S(1)} collective-permute-done((s16[62,16,128]{2,1,0:T(8,128)(2,1)S(1)}, s16[62,16,128]{2,1,0:T(8,128)(2,1)S(1)}, u32[]{:S(2)}, u32[]{:S(2)}) %collective-permute-start.2) | collective-permute-done | bytes 253984 | tf_op jit(solution)/shard_map/ppermute | solution.py:534
  28.8 5.9 %collective-permute-done.3.refs_7_.refs_6_ = s16[62,16,128]{2,1,0:T(8,128)(2,1)S(1)} collective-permute-done((s16[62,16,128]{2,1,0:T(8,128)(2,1)S(1)}, s16[62,16,128]{2,1,0:T(8,128)(2,1)S(1)}, u32[]{:S(2)}, u32[]{:S(2)}) %collective-permute-start.3) | collective-permute-done | bytes 253984 | tf_op jit(solution)/shard_map/ppermute | solution.py:534
  35.0 4.0 %collective-permute-start.4 = (s16[97,16,128]{2,1,0:T(8,128)(2,1)S(1)}, s16[97,16,128]{2,1,0:T(8,128)(2,1)S(1)}, u32[]{:S(2)}, u32[]{:S(2)}) collective-permute-start(s16[97,16,128]{2,1,0:T(8,128)(2,1)S(1)} %get-tuple-element.36), channel_id=1, source_target_pairs={{0,4},{4,8},{8,12},{12,16},{16,20},{20,24},{24,28},{1,5},{5,9},{9,... | collective-permute-start | bytes 1191944 | tf_op jit(solution)/shard_map/ppermute | solution.py:534
  39.1 1.3 %collective-permute-start.5 = (s16[97,16,128]{2,1,0:T(8,128)(2,1)S(1)}, s16[97,16,128]{2,1,0:T(8,128)(2,1)S(1)}, u32[]{:S(2)}, u32[]{:S(2)}) collective-permute-start(s16[97,16,128]{2,1,0:T(8,128)(2,1)S(1)} %get-tuple-element.37), channel_id=1, source_target_pairs={{4,0},{8,4},{12,8},{16,12},{20,16},{24,20},{28,24},{5,1},{9,5},{13... | collective-permute-start | bytes 1191944 | tf_op jit(solution)/shard_map/ppermute | solution.py:534
  40.4 6.8 %collective-permute-done.4.refs_7_ = s16[97,16,128]{2,1,0:T(8,128)(2,1)S(1)} collective-permute-done((s16[97,16,128]{2,1,0:T(8,128)(2,1)S(1)}, s16[97,16,128]{2,1,0:T(8,128)(2,1)S(1)}, u32[]{:S(2)}, u32[]{:S(2)}) %collective-permute-start.4) | collective-permute-done | bytes 397344 | tf_op jit(solution)/shard_map/ppermute | solution.py:534
  47.2 4.8 %collective-permute-done.5.refs_8_ = s16[97,16,128]{2,1,0:T(8,128)(2,1)S(1)} collective-permute-done((s16[97,16,128]{2,1,0:T(8,128)(2,1)S(1)}, s16[97,16,128]{2,1,0:T(8,128)(2,1)S(1)}, u32[]{:S(2)}, u32[]{:S(2)}) %collective-permute-start.5) | collective-permute-done | bytes 397344 | tf_op jit(solution)/shard_map/ppermute | solution.py:534
  52.0 7.0 %steps_first.1 = (f32[3,8,16,128]{3,2,1,0:T(8,128)S(1)}, f32[3,8,16,128]{3,2,1,0:T(8,128)S(1)}, f32[8,16,128]{2,1,0:T(8,128)S(1)}, f32[8,16,128]{2,1,0:T(8,128)S...) custom-call(f32[3,8,16,128]{3,2,1,0:T(8,128)S(1)} %get-tuple-element.27.refs_2_.refs_0_, ...), custom_call_target="tpu_custom_call" | custom-call | flops 7704999936 | tf_op jit(solution)/shard_map/steps_first/pallas_call | solution.py:518
  58.9 3.1 %collective-permute-start.7 = (f32[8,16,128]{2,1,0:T(8,128)S(1)}, f32[8,16,128]{2,1,0:T(8,128)S(1)}, u32[]{:S(2)}, u32[]{:S(2)}) collective-permute-start(f32[8,16,128]{2,1,0:T(8,128)S(1)} %get-tuple-element.40), channel_id=1, source_target_pairs={{1,0},{2,1},{3,2},{5,4},{6,5},{7,6},{9,8},{10,9},{11,10},{13,12},{... | collective-permute-start | bytes 196616 | tf_op jit(solution)/shard_map/ppermute | solution.py:534
  62.1 2.4 %collective-permute-start.6 = (f32[8,16,128]{2,1,0:T(8,128)S(1)}, f32[8,16,128]{2,1,0:T(8,128)S(1)}, u32[]{:S(2)}, u32[]{:S(2)}) collective-permute-start(f32[8,16,128]{2,1,0:T(8,128)S(1)} %get-tuple-element.40), channel_id=1, source_target_pairs={{0,1},{1,2},{2,3},{4,5},{5,6},{6,7},{8,9},{9,10},{10,11},{12,13},{... | collective-permute-start | bytes 196616 | tf_op jit(solution)/shard_map/ppermute | solution.py:534
  64.5 1.3 %collective-permute-done.6.refs_0_ = f32[8,16,128]{2,1,0:T(8,128)S(1)} collective-permute-done((f32[8,16,128]{2,1,0:T(8,128)S(1)}, f32[8,16,128]{2,1,0:T(8,128)S(1)}, u32[]{:S(2)}, u32[]{:S(2)}) %collective-permute-start.6) | collective-permute-done | bytes 65568 | tf_op jit(solution)/shard_map/ppermute | solution.py:534
  66.1 4.7 %collective-permute-start.8 = (s16[50,16,128]{2,1,0:T(8,128)(2,1)S(1)}, s16[50,16,128]{2,1,0:T(8,128)(2,1)S(1)}, u32[]{:S(2)}, u32[]{:S(2)}) collective-permute-start(s16[50,16,128]{2,1,0:T(8,128)(2,1)S(1)} %get-tuple-element.42), channel_id=1, source_target_pairs={{0,32},{32,64},{64,96},{96,128},{128,160},{160,192},{192,224},{224... | collective-permute-start | bytes 614408 | tf_op jit(solution)/shard_map/ppermute | solution.py:534
  70.9 1.3 %collective-permute-start.9 = (s16[50,16,128]{2,1,0:T(8,128)(2,1)S(1)}, s16[50,16,128]{2,1,0:T(8,128)(2,1)S(1)}, u32[]{:S(2)}, u32[]{:S(2)}) collective-permute-start(s16[50,16,128]{2,1,0:T(8,128)(2,1)S(1)} %get-tuple-element.43), channel_id=1, source_target_pairs={{32,0},{64,32},{96,64},{128,96},{160,128},{192,160},{224,192},{256... | collective-permute-start | bytes 614408 | tf_op jit(solution)/shard_map/ppermute | solution.py:534
  72.2 1.3 %collective-permute-start.13 = (f32[8,16,128]{2,1,0:T(8,128)S(1)}, f32[8,16,128]{2,1,0:T(8,128)S(1)}, u32[]{:S(2)}, u32[]{:S(2)}) collective-permute-start(f32[8,16,128]{2,1,0:T(8,128)S(1)} %get-tuple-element.48.own_ref.own_in), channel_id=1, source_target_pairs={{32,0},{64,32},{96,64},{128,96},{160,128},{192,160},{224,192},{256... | collective-permute-start | bytes 196616 | tf_op jit(solution)/shard_map/ppermute | solution.py:534
  73.5 5.5 %collective-permute-start.12 = (f32[8,16,128]{2,1,0:T(8,128)S(1)}, f32[8,16,128]{2,1,0:T(8,128)S(1)}, u32[]{:S(2)}, u32[]{:S(2)}) collective-permute-start(f32[8,16,128]{2,1,0:T(8,128)S(1)} %get-tuple-element.48.own_ref.own_in), channel_id=1, source_target_pairs={{0,32},{32,64},{64,96},{96,128},{128,160},{160,192},{192,224},{224... | collective-permute-start | bytes 196616 | tf_op jit(solution)/shard_map/ppermute | solution.py:534
  79.0 8.2 %collective-permute-done.13.high_ref.x_high = f32[8,16,128]{2,1,0:T(8,128)S(1)} collective-permute-done((f32[8,16,128]{2,1,0:T(8,128)S(1)}, f32[8,16,128]{2,1,0:T(8,128)S(1)}, u32[]{:S(2)}, u32[]{:S(2)}) %collective-permute-start.13) | collective-permute-done | bytes 65568 | tf_op jit(solution)/shard_map/ppermute | solution.py:534
  87.2 4.0 %collective-permute-start.14 = (f32[24,8,128]{2,1,0:T(8,128)S(1)}, f32[24,8,128]{2,1,0:T(8,128)S(1)}, u32[]{:S(2)}, u32[]{:S(2)}) collective-permute-start(f32[24,8,128]{2,1,0:T(8,128)S(1)} %get-tuple-element.49), channel_id=1, source_target_pairs={{0,4},{4,8},{8,12},{12,16},{16,20},{20,24},{24,28},{1,5},{5,9},{9,... | collective-permute-start | bytes 294920 | tf_op jit(solution)/shard_map/ppermute | solution.py:534
  91.2 1.3 %collective-permute-start.15 = (f32[24,8,128]{2,1,0:T(8,128)S(1)}, f32[24,8,128]{2,1,0:T(8,128)S(1)}, u32[]{:S(2)}, u32[]{:S(2)}) collective-permute-start(f32[24,8,128]{2,1,0:T(8,128)S(1)} %get-tuple-element.50), channel_id=1, source_target_pairs={{4,0},{8,4},{12,8},{16,12},{20,16},{24,20},{28,24},{5,1},{9,5},{13... | collective-permute-start | bytes 294920 | tf_op jit(solution)/shard_map/ppermute | solution.py:534
  92.8 1.3 %collective-permute-start.11 = (s16[77,16,128]{2,1,0:T(8,128)(2,1)S(1)}, s16[77,16,128]{2,1,0:T(8,128)(2,1)S(1)}, u32[]{:S(2)}, u32[]{:S(2)}) collective-permute-start(s16[77,16,128]{2,1,0:T(8,128)(2,1)S(1)} %get-tuple-element.46), channel_id=1, source_target_pairs={{4,0},{8,4},{12,8},{16,12},{20,16},{24,20},{28,24},{5,1},{9,5},{13... | collective-permute-start | bytes 946184 | tf_op jit(solution)/shard_map/ppermute | solution.py:534
  94.1 6.5 %collective-permute-start.10 = (s16[77,16,128]{2,1,0:T(8,128)(2,1)S(1)}, s16[77,16,128]{2,1,0:T(8,128)(2,1)S(1)}, u32[]{:S(2)}, u32[]{:S(2)}) collective-permute-start(s16[77,16,128]{2,1,0:T(8,128)(2,1)S(1)} %get-tuple-element.45.after_in), channel_id=1, source_target_pairs={{0,4},{4,8},{8,12},{12,16},{16,20},{20,24},{24,28},{1,5},{5,9},{9,... | collective-permute-start | bytes 946184 | tf_op jit(solution)/shard_map/ppermute | solution.py:534
  100.7 4.4 %surface.1 = f32[16,4,8,128]{3,2,1,0:T(8,128)} custom-call(f32[8,16,128]{2,1,0:T(8,128)S(1)} %get-tuple-element.48.own_ref.own_in, f32[8,16,128]{2,1,0:T(8,128)S(1)} %collective-permute-done.12.low_ref.x_low, f32[8,16,128]{2,1,0:T(8,128)S(1)} %collective-permute-done.13.high_ref.x_high, f32[24,8,128]{2,1,0:T(8,128)S(1)} %collective-permute-done.14.y_low, ...), custom_call_target="tpu_custom_call" | custom-call | flops 5175000064 | tf_op jit(solution)/shard_map/surface/pallas_call | solution.py:518
  105.1 8.7 %all-to-all-start = ((f32[64,8,128]{2,1,0:T(8,128)}), f32[64,8,128]{2,1,0:T(8,128)S(1)}, u32[]{:S(2)}, u32[]{:S(2)}) async-start(f32[64,8,128]{2,1,0:T(8,128)} %bitcast.3), calls=%async_computation | async-start | bytes 524288 | tf_op jit(solution)/shard_map/all_to_all | solution.py:627
  113.9 1.4 %copy-done.16 = f32[4,24,32,128]{3,2,1,0:T(8,128)S(1)} copy-done((f32[4,24,32,128]{3,2,1,0:T(8,128)S(1)}, f32[4,24,32,128]{3,2,1,0:T(8,128)}, u32[]{:S(2)}) %copy-start.16) | copy-done | bytes 1572888
  115.3 6.4 %steps_second.1 = f32[3,8,16,128]{3,2,1,0:T(8,128)} custom-call(f32[3,8,16,128]{3,2,1,0:T(8,128)S(1)} %get-tuple-element.38.refs_2_.refs_0_, f32[3,8,16,128]{3,2,1,0:T(8,128)S(1)} %get-tuple-element.39.refs_3_.refs_1_, f32[8,16,128]{2,1,0:T(8,128)S(1)} %get-tuple-element.41.refs_2_, s16[50,16,128]{2,1,0:T(8,128)(2,1)S(1)} %collective-permute-done.8.refs_4_.refs_3_, ...), custom_call_target="tpu_custom_call" | custom-call | flops 7474999808 | tf_op jit(solution)/shard_map/steps_second/pallas_call | solution.py:518
  121.7 4.1 %all-to-all-done = f32[64,8,128]{2,1,0:T(8,128)S(1)} async-done(((f32[64,8,128]{2,1,0:T(8,128)}), f32[64,8,128]{2,1,0:T(8,128)S(1)}, u32[]{:S(2)}, u32[]{:S(2)}) %all-to-all-start) | async-done | bytes 262176 | tf_op jit(solution)/shard_map/all_to_all | solution.py:627
  125.9 1.0 fragility.1
  (46 shorter events, 3.9 us)
Async XLA Ops:
  0.6 0.9 copy-start
  1.6 0.9 copy-start.1
  5.6 46.4 %copy-start.13 = (bf16[3,256,256]{2,1,0:T(8,128)(2,1)S(1)}, bf16[3,256,256]{2,1,0:T(8,128)(2,1)}, u32[]{:S(2)}) copy-start(bf16[3,256,256]{2,1,0:T(8,128)(2,1)} %constant.4.clone.refs_9_.refs_7_) | copy-start | bytes 1179652
  5.6 10.9 %collective-permute-start.1 = (f32[8,16,128]{2,1,0:T(8,128)S(1)}, f32[8,16,128]{2,1,0:T(8,128)S(1)}, u32[]{:S(2)}, u32[]{:S(2)}) collective-permute-start(f32[8,16,128]{2,1,0:T(8,128)S(1)} %get-tuple-element.31), channel_id=1, source_target_pairs={{1,0},{2,1},{3,2},{5,4},{6,5},{7,6},{9,8},{10,9},{11,10},{13,12},{... | collective-permute-start | bytes 196616 | tf_op jit(solution)/shard_map/ppermute | solution.py:534
  14.5 3.2 %collective-permute-start = (f32[8,16,128]{2,1,0:T(8,128)S(1)}, f32[8,16,128]{2,1,0:T(8,128)S(1)}, u32[]{:S(2)}, u32[]{:S(2)}) collective-permute-start(f32[8,16,128]{2,1,0:T(8,128)S(1)} %get-tuple-element.31), channel_id=1, source_target_pairs={{0,1},{1,2},{2,3},{4,5},{5,6},{6,7},{8,9},{9,10},{10,11},{12,13},{... | collective-permute-start | bytes 196616 | tf_op jit(solution)/shard_map/ppermute | solution.py:534
  18.0 10.8 %collective-permute-start.2 = (s16[62,16,128]{2,1,0:T(8,128)(2,1)S(1)}, s16[62,16,128]{2,1,0:T(8,128)(2,1)S(1)}, u32[]{:S(2)}, u32[]{:S(2)}) collective-permute-start(s16[62,16,128]{2,1,0:T(8,128)(2,1)S(1)} %get-tuple-element.33), channel_id=1, source_target_pairs={{0,32},{32,64},{64,96},{96,128},{128,160},{160,192},{192,224},{224... | collective-permute-start | bytes 761864 | tf_op jit(solution)/shard_map/ppermute | solution.py:534
  19.3 15.4 %collective-permute-start.3 = (s16[62,16,128]{2,1,0:T(8,128)(2,1)S(1)}, s16[62,16,128]{2,1,0:T(8,128)(2,1)S(1)}, u32[]{:S(2)}, u32[]{:S(2)}) collective-permute-start(s16[62,16,128]{2,1,0:T(8,128)(2,1)S(1)} %get-tuple-element.34), channel_id=1, source_target_pairs={{32,0},{64,32},{96,64},{128,96},{160,128},{192,160},{224,192},{256... | collective-permute-start | bytes 761864 | tf_op jit(solution)/shard_map/ppermute | solution.py:534
  35.0 12.2 %collective-permute-start.4 = (s16[97,16,128]{2,1,0:T(8,128)(2,1)S(1)}, s16[97,16,128]{2,1,0:T(8,128)(2,1)S(1)}, u32[]{:S(2)}, u32[]{:S(2)}) collective-permute-start(s16[97,16,128]{2,1,0:T(8,128)(2,1)S(1)} %get-tuple-element.36), channel_id=1, source_target_pairs={{0,4},{4,8},{8,12},{12,16},{16,20},{20,24},{24,28},{1,5},{5,9},{9,... | collective-permute-start | bytes 1191944 | tf_op jit(solution)/shard_map/ppermute | solution.py:534
  39.1 12.9 %collective-permute-start.5 = (s16[97,16,128]{2,1,0:T(8,128)(2,1)S(1)}, s16[97,16,128]{2,1,0:T(8,128)(2,1)S(1)}, u32[]{:S(2)}, u32[]{:S(2)}) collective-permute-start(s16[97,16,128]{2,1,0:T(8,128)(2,1)S(1)} %get-tuple-element.37), channel_id=1, source_target_pairs={{4,0},{8,4},{12,8},{16,12},{20,16},{24,20},{28,24},{5,1},{9,5},{13... | collective-permute-start | bytes 1191944 | tf_op jit(solution)/shard_map/ppermute | solution.py:534
  58.9 41.7 %copy-start.15 = (f32[4,24,32,128]{3,2,1,0:T(8,128)}, f32[4,24,32,128]{3,2,1,0:T(8,128)S(1)}, u32[]{:S(2)}) copy-start(f32[4,24,32,128]{3,2,1,0:T(8,128)S(1)} %get-tuple-element.47.refs_8_.rate_in) | copy-start | bytes 4718596
  58.9 5.6 %collective-permute-start.7 = (f32[8,16,128]{2,1,0:T(8,128)S(1)}, f32[8,16,128]{2,1,0:T(8,128)S(1)}, u32[]{:S(2)}, u32[]{:S(2)}) collective-permute-start(f32[8,16,128]{2,1,0:T(8,128)S(1)} %get-tuple-element.40), channel_id=1, source_target_pairs={{1,0},{2,1},{3,2},{5,4},{6,5},{7,6},{9,8},{10,9},{11,10},{13,12},{... | collective-permute-start | bytes 196616 | tf_op jit(solution)/shard_map/ppermute | solution.py:534
  62.1 3.7 %collective-permute-start.6 = (f32[8,16,128]{2,1,0:T(8,128)S(1)}, f32[8,16,128]{2,1,0:T(8,128)S(1)}, u32[]{:S(2)}, u32[]{:S(2)}) collective-permute-start(f32[8,16,128]{2,1,0:T(8,128)S(1)} %get-tuple-element.40), channel_id=1, source_target_pairs={{0,1},{1,2},{2,3},{4,5},{5,6},{6,7},{8,9},{9,10},{10,11},{12,13},{... | collective-permute-start | bytes 196616 | tf_op jit(solution)/shard_map/ppermute | solution.py:534
  66.1 34.6 %copy-start.4 = (s32[16,1,128]{2,1,0:T(1,128)S(1)}, s32[16,1,128]{2,1,0:T(1,128)}, u32[]{:S(2)}) copy-start(s32[16,1,128]{2,1,0:T(1,128)} %param.19) | copy-start | bytes 24580
  66.1 34.6 %copy-start.5 = (bf16[64,24]{0,1:T(8,128)(2,1)S(1)}, bf16[64,24]{0,1:T(8,128)(2,1)}, u32[]{:S(2)}) copy-start(bf16[64,24]{0,1:T(8,128)(2,1)} %param.24) | copy-start | bytes 9220
  66.1 34.6 %copy-start.11 = (s32[8]{0:T(128)S(1)}, s32[8]{0:T(128)}, u32[]{:S(2)}) copy-start(s32[8]{0:T(128)} %param.23) | copy-start | bytes 100
  66.1 34.6 %copy-start.14 = (bf16[256,128]{1,0:T(8,128)(2,1)S(1)}, bf16[256,128]{1,0:T(8,128)(2,1)}, u32[]{:S(2)}) copy-start(bf16[256,128]{1,0:T(8,128)(2,1)} %constant.5.clone.weight_in) | copy-start | bytes 196612
  66.1 26.4 %collective-permute-start.8 = (s16[50,16,128]{2,1,0:T(8,128)(2,1)S(1)}, s16[50,16,128]{2,1,0:T(8,128)(2,1)S(1)}, u32[]{:S(2)}, u32[]{:S(2)}) collective-permute-start(s16[50,16,128]{2,1,0:T(8,128)(2,1)S(1)} %get-tuple-element.42), channel_id=1, source_target_pairs={{0,32},{32,64},{64,96},{96,128},{128,160},{160,192},{192,224},{224... | collective-permute-start | bytes 614408 | tf_op jit(solution)/shard_map/ppermute | solution.py:534
  70.9 21.7 %collective-permute-start.9 = (s16[50,16,128]{2,1,0:T(8,128)(2,1)S(1)}, s16[50,16,128]{2,1,0:T(8,128)(2,1)S(1)}, u32[]{:S(2)}, u32[]{:S(2)}) collective-permute-start(s16[50,16,128]{2,1,0:T(8,128)(2,1)S(1)} %get-tuple-element.43), channel_id=1, source_target_pairs={{32,0},{64,32},{96,64},{128,96},{160,128},{192,160},{224,192},{256... | collective-permute-start | bytes 614408 | tf_op jit(solution)/shard_map/ppermute | solution.py:534
  72.2 15.0 %collective-permute-start.13 = (f32[8,16,128]{2,1,0:T(8,128)S(1)}, f32[8,16,128]{2,1,0:T(8,128)S(1)}, u32[]{:S(2)}, u32[]{:S(2)}) collective-permute-start(f32[8,16,128]{2,1,0:T(8,128)S(1)} %get-tuple-element.48.own_ref.own_in), channel_id=1, source_target_pairs={{32,0},{64,32},{96,64},{128,96},{160,128},{192,160},{224,192},{256... | collective-permute-start | bytes 196616 | tf_op jit(solution)/shard_map/ppermute | solution.py:534
  73.5 13.7 %collective-permute-start.12 = (f32[8,16,128]{2,1,0:T(8,128)S(1)}, f32[8,16,128]{2,1,0:T(8,128)S(1)}, u32[]{:S(2)}, u32[]{:S(2)}) collective-permute-start(f32[8,16,128]{2,1,0:T(8,128)S(1)} %get-tuple-element.48.own_ref.own_in), channel_id=1, source_target_pairs={{0,32},{32,64},{64,96},{96,128},{128,160},{160,192},{192,224},{224... | collective-permute-start | bytes 196616 | tf_op jit(solution)/shard_map/ppermute | solution.py:534
  87.2 13.4 %collective-permute-start.14 = (f32[24,8,128]{2,1,0:T(8,128)S(1)}, f32[24,8,128]{2,1,0:T(8,128)S(1)}, u32[]{:S(2)}, u32[]{:S(2)}) collective-permute-start(f32[24,8,128]{2,1,0:T(8,128)S(1)} %get-tuple-element.49), channel_id=1, source_target_pairs={{0,4},{4,8},{8,12},{12,16},{16,20},{20,24},{24,28},{1,5},{5,9},{9,... | collective-permute-start | bytes 294920 | tf_op jit(solution)/shard_map/ppermute | solution.py:534
  91.2 9.4 %collective-permute-start.15 = (f32[24,8,128]{2,1,0:T(8,128)S(1)}, f32[24,8,128]{2,1,0:T(8,128)S(1)}, u32[]{:S(2)}, u32[]{:S(2)}) collective-permute-start(f32[24,8,128]{2,1,0:T(8,128)S(1)} %get-tuple-element.50), channel_id=1, source_target_pairs={{4,0},{8,4},{12,8},{16,12},{20,16},{24,20},{28,24},{5,1},{9,5},{13... | collective-permute-start | bytes 294920 | tf_op jit(solution)/shard_map/ppermute | solution.py:534
  92.8 21.1 %collective-permute-start.11 = (s16[77,16,128]{2,1,0:T(8,128)(2,1)S(1)}, s16[77,16,128]{2,1,0:T(8,128)(2,1)S(1)}, u32[]{:S(2)}, u32[]{:S(2)}) collective-permute-start(s16[77,16,128]{2,1,0:T(8,128)(2,1)S(1)} %get-tuple-element.46), channel_id=1, source_target_pairs={{4,0},{8,4},{12,8},{16,12},{20,16},{24,20},{28,24},{5,1},{9,5},{13... | collective-permute-start | bytes 946184 | tf_op jit(solution)/shard_map/ppermute | solution.py:534
  94.1 19.8 %collective-permute-start.10 = (s16[77,16,128]{2,1,0:T(8,128)(2,1)S(1)}, s16[77,16,128]{2,1,0:T(8,128)(2,1)S(1)}, u32[]{:S(2)}, u32[]{:S(2)}) collective-permute-start(s16[77,16,128]{2,1,0:T(8,128)(2,1)S(1)} %get-tuple-element.45.after_in), channel_id=1, source_target_pairs={{0,4},{4,8},{8,12},{12,16},{16,20},{20,24},{24,28},{1,5},{5,9},{9,... | collective-permute-start | bytes 946184 | tf_op jit(solution)/shard_map/ppermute | solution.py:534
  105.1 20.7 %all-to-all-start = ((f32[64,8,128]{2,1,0:T(8,128)}), f32[64,8,128]{2,1,0:T(8,128)S(1)}, u32[]{:S(2)}, u32[]{:S(2)}) async-start(f32[64,8,128]{2,1,0:T(8,128)} %bitcast.3), calls=%async_computation | async-start | bytes 524288 | tf_op jit(solution)/shard_map/all_to_all | solution.py:627
  113.8 12.0 %copy-start.6 = (s32[1024]{0:T(1024)S(1)}, s32[1024]{0:T(1024)}, u32[]{:S(2)}) copy-start(s32[1024]{0:T(1024)} %param.20) | copy-start | bytes 12292
  113.8 12.0 %copy-start.7 = (s32[1024]{0:T(1024)S(1)}, s32[1024]{0:T(1024)}, u32[]{:S(2)}) copy-start(s32[1024]{0:T(1024)} %param.21) | copy-start | bytes 12292
  113.9 12.0 %copy-start.8 = (s32[1024]{0:T(1024)S(1)}, s32[1024]{0:T(1024)}, u32[]{:S(2)}) copy-start(s32[1024]{0:T(1024)} %param.22) | copy-start | bytes 12292
  113.9 12.0 %copy-start.9 = (f32[16,8]{0,1:T(8,128)S(1)}, f32[16,8]{0,1:T(8,128)}, u32[]{:S(2)}) copy-start(f32[16,8]{0,1:T(8,128)} %param.26) | copy-start | bytes 1540
  113.9 12.0 %copy-start.10 = (f32[16,8]{0,1:T(8,128)S(1)}, f32[16,8]{0,1:T(8,128)}, u32[]{:S(2)}) copy-start(f32[16,8]{0,1:T(8,128)} %param.27) | copy-start | bytes 1540
  113.9 12.0 %copy-start.12 = (f32[16]{0:T(128)S(1)}, f32[16]{0:T(128)}, u32[]{:S(2)}) copy-start(f32[16]{0:T(128)} %param.25) | copy-start | bytes 196
  113.9 1.4 %copy-start.16 = (f32[4,24,32,128]{3,2,1,0:T(8,128)S(1)}, f32[4,24,32,128]{3,2,1,0:T(8,128)}, u32[]{:S(2)}) copy-start(f32[4,24,32,128]{3,2,1,0:T(8,128)} %copy-done.15) | copy-start | bytes 4718596
  (2 other events, 1.7 us)

commit v8 on v7

--- a/solution.py
+++ b/solution.py
@@ -510,7 +510,7 @@
 
 
 TIMES = {"start": 1.4, "steps_first": 6.7, "steps_second": 6.5, "surface": 4.5, "fragility": 1.0}
-FLOPS_A_US = 1.15e9
+FLOPS_A_US = 1.15e10
 
 
 def call(kernel, name, shapes, args, specs=None, scratch=()):

time: 128 us -> 124 us (0.969); the launches traced: 127 us -> 121 us
  waiting for transfers between devices: 40.6 us -> 34.6 us
    ppermute x8, waiting for transfers between devices: 18.9 us -> 14.2 us  [both_ways(): lax.ppermute(to_down, axis, backward)]
    all_to_all x1, starting transfers between devices: 8.74 us -> 10.9 us  [body(): lax.all_to_all(table, ('gx', 'gz'), split_axis=0, concat_axis=0, tiled=True)]
    ppermute x8, starting transfers between devices: 30.4 us -> 29 us  [both_ways(): lax.ppermute(to_up, axis, forward)]
    ppermute x8, waiting for transfers between devices: 17.6 us -> 16.3 us  [both_ways(): lax.ppermute(to_up, axis, forward)]
  transfers between devices with their start and end apart: 17 -> 17, of which waited for: 8 -> 7; matrix products, arithmetic and copies ran while one was open for 0% -> 0% of each run, Pallas kernels for 9% -> 9%
where the time goes in v8:
time: 124 us; the launch traced here: 121 us
  starting transfers between devices  59.5 us (48%)
  waiting for transfers between devices  34.6 us (28%)
  Pallas kernels  21.3 us (17%)
  local copies, waits for them, and re-layouts  4.99 us (4%)
    ppermute x8, starting transfers between devices, both_ways(): lax.ppermute(to_up, axis, forward)  29 us
    pallas_call x10, Pallas kernels, call(): pl.pallas_call(kernel, out_shape=out, in_specs=specs or [VM] * len(args),...  21.3 us
    ppermute x8, starting transfers between devices, both_ways(): lax.ppermute(to_down, axis, backward)  19.7 us
    ppermute x8, waiting for transfers between devices, both_ways(): lax.ppermute(to_up, axis, forward)  16.3 us
    ppermute x8, waiting for transfers between devices, both_ways(): lax.ppermute(to_down, axis, backward)  14.2 us
    all_to_all x1, starting transfers between devices, body(): lax.all_to_all(table, ('gx', 'gz'), split_axis=0, concat_axis=0, tiled=True)  10.9 us
    unnamed x34, local copies, waits for them, and re-layouts  4.99 us
    all_to_all x1, waiting for transfers between devices, body(): lax.all_to_all(table, ('gx', 'gz'), split_axis=0, concat_axis=0, tiled=True)  4.12 us
  transfers between devices with their start and end apart: 17, of which 7 were waited for; matrix products, arithmetic and copies ran while one was open for 0% of the time, Pallas kernels for 9%

profile of v8, /device:TPU:1, one launch (start us, length us, event | category | flops | bytes accessed | tf_op | source)
XLA Modules:
  0.0 121.4 jit_solution(2435637024146763505)
XLA Ops:
  0.6 0.9 copy-done
  1.6 0.9 copy-done.1
  4.2 1.4 %start.1 = (f32[3,8,16,128]{3,2,1,0:T(8,128)S(1)}, f32[3,8,16,128]{3,2,1,0:T(8,128)S(1)}, f32[8,16,128]{2,1,0:T(8,128)S(1)}, f32[8,16,128]{2,1,0:T(8,128)S(1)}, f32[8,16,128]{2,1,0:T(8,128)S(1)}) custom-call(f32[3,8,16,128]{3,2,1,0:T(8,128)S(1)} %copy-done, f32[3,8,16,128]{3,2,1,0:T(8,128)S(1)} %copy-done.1, f32[8,16,128]{2,1,0:T(8,128)S(1)} %copy-done.2, ...), custom_call_target="tpu_custom_call" | custom-call | flops 16099999744 | tf_op jit(solution)/shard_map/start/pallas_call | solution.py:518
  5.6 8.8 %collective-permute-start.1 = (f32[8,16,128]{2,1,0:T(8,128)S(1)}, f32[8,16,128]{2,1,0:T(8,128)S(1)}, u32[]{:S(2)}, u32[]{:S(2)}) collective-permute-start(f32[8,16,128]{2,1,0:T(8,128)S(1)} %get-tuple-element.31), channel_id=1, source_target_pairs={{1,0},{2,1},{3,2},{5,4},{6,5},{7,6},{9,8},{10,9},{11,10},{13,12},{... | collective-permute-start | bytes 196616 | tf_op jit(solution)/shard_map/ppermute | solution.py:534
  14.4 1.9 %collective-permute-start = (f32[8,16,128]{2,1,0:T(8,128)S(1)}, f32[8,16,128]{2,1,0:T(8,128)S(1)}, u32[]{:S(2)}, u32[]{:S(2)}) collective-permute-start(f32[8,16,128]{2,1,0:T(8,128)S(1)} %get-tuple-element.31), channel_id=1, source_target_pairs={{0,1},{1,2},{2,3},{4,5},{5,6},{6,7},{8,9},{9,10},{10,11},{12,13},{... | collective-permute-start | bytes 196616 | tf_op jit(solution)/shard_map/ppermute | solution.py:534
  16.3 1.3 %collective-permute-done.refs_0_ = f32[8,16,128]{2,1,0:T(8,128)S(1)} collective-permute-done((f32[8,16,128]{2,1,0:T(8,128)S(1)}, f32[8,16,128]{2,1,0:T(8,128)S(1)}, u32[]{:S(2)}, u32[]{:S(2)}) %collective-permute-start) | collective-permute-done | bytes 65568 | tf_op jit(solution)/shard_map/ppermute | solution.py:534
  17.9 1.3 %collective-permute-start.2 = (s16[62,16,128]{2,1,0:T(8,128)(2,1)S(1)}, s16[62,16,128]{2,1,0:T(8,128)(2,1)S(1)}, u32[]{:S(2)}, u32[]{:S(2)}) collective-permute-start(s16[62,16,128]{2,1,0:T(8,128)(2,1)S(1)} %get-tuple-element.33), channel_id=1, source_target_pairs={{0,32},{32,64},{64,96},{96,128},{128,160},{160,192},{192,224},{224... | collective-permute-start | bytes 761864 | tf_op jit(solution)/shard_map/ppermute | solution.py:534
  19.2 1.3 %collective-permute-start.3 = (s16[62,16,128]{2,1,0:T(8,128)(2,1)S(1)}, s16[62,16,128]{2,1,0:T(8,128)(2,1)S(1)}, u32[]{:S(2)}, u32[]{:S(2)}) collective-permute-start(s16[62,16,128]{2,1,0:T(8,128)(2,1)S(1)} %get-tuple-element.34), channel_id=1, source_target_pairs={{32,0},{64,32},{96,64},{128,96},{160,128},{192,160},{224,192},{256... | collective-permute-start | bytes 761864 | tf_op jit(solution)/shard_map/ppermute | solution.py:534
  20.5 8.1 %collective-permute-done.2.refs_6_.refs_5_ = s16[62,16,128]{2,1,0:T(8,128)(2,1)S(1)} collective-permute-done((s16[62,16,128]{2,1,0:T(8,128)(2,1)S(1)}, s16[62,16,128]{2,1,0:T(8,128)(2,1)S(1)}, u32[]{:S(2)}, u32[]{:S(2)}) %collective-permute-start.2) | collective-permute-done | bytes 253984 | tf_op jit(solution)/shard_map/ppermute | solution.py:534
  28.6 5.9 %collective-permute-done.3.refs_7_.refs_6_ = s16[62,16,128]{2,1,0:T(8,128)(2,1)S(1)} collective-permute-done((s16[62,16,128]{2,1,0:T(8,128)(2,1)S(1)}, s16[62,16,128]{2,1,0:T(8,128)(2,1)S(1)}, u32[]{:S(2)}, u32[]{:S(2)}) %collective-permute-start.3) | collective-permute-done | bytes 253984 | tf_op jit(solution)/shard_map/ppermute | solution.py:534
  34.9 4.0 %collective-permute-start.4 = (s16[97,16,128]{2,1,0:T(8,128)(2,1)S(1)}, s16[97,16,128]{2,1,0:T(8,128)(2,1)S(1)}, u32[]{:S(2)}, u32[]{:S(2)}) collective-permute-start(s16[97,16,128]{2,1,0:T(8,128)(2,1)S(1)} %get-tuple-element.36), channel_id=1, source_target_pairs={{0,4},{4,8},{8,12},{12,16},{16,20},{20,24},{24,28},{1,5},{5,9},{9,... | collective-permute-start | bytes 1191944 | tf_op jit(solution)/shard_map/ppermute | solution.py:534
  38.9 1.3 %collective-permute-start.5 = (s16[97,16,128]{2,1,0:T(8,128)(2,1)S(1)}, s16[97,16,128]{2,1,0:T(8,128)(2,1)S(1)}, u32[]{:S(2)}, u32[]{:S(2)}) collective-permute-start(s16[97,16,128]{2,1,0:T(8,128)(2,1)S(1)} %get-tuple-element.37), channel_id=1, source_target_pairs={{4,0},{8,4},{12,8},{16,12},{20,16},{24,20},{28,24},{5,1},{9,5},{13... | collective-permute-start | bytes 1191944 | tf_op jit(solution)/shard_map/ppermute | solution.py:534
  40.2 6.8 %collective-permute-done.4.refs_7_ = s16[97,16,128]{2,1,0:T(8,128)(2,1)S(1)} collective-permute-done((s16[97,16,128]{2,1,0:T(8,128)(2,1)S(1)}, s16[97,16,128]{2,1,0:T(8,128)(2,1)S(1)}, u32[]{:S(2)}, u32[]{:S(2)}) %collective-permute-start.4) | collective-permute-done | bytes 397344 | tf_op jit(solution)/shard_map/ppermute | solution.py:534
  47.1 4.8 %collective-permute-done.5.refs_8_ = s16[97,16,128]{2,1,0:T(8,128)(2,1)S(1)} collective-permute-done((s16[97,16,128]{2,1,0:T(8,128)(2,1)S(1)}, s16[97,16,128]{2,1,0:T(8,128)(2,1)S(1)}, u32[]{:S(2)}, u32[]{:S(2)}) %collective-permute-start.5) | collective-permute-done | bytes 397344 | tf_op jit(solution)/shard_map/ppermute | solution.py:534
  51.8 7.0 %steps_first.1 = (f32[3,8,16,128]{3,2,1,0:T(8,128)S(1)}, f32[3,8,16,128]{3,2,1,0:T(8,128)S(1)}, f32[8,16,128]{2,1,0:T(8,128)S(1)}, f32[8,16,128]{2,1,0:T(8,128)S...) custom-call(f32[3,8,16,128]{3,2,1,0:T(8,128)S(1)} %get-tuple-element.27.refs_2_.refs_0_, ...), custom_call_target="tpu_custom_call" | custom-call | flops 77050003456 | tf_op jit(solution)/shard_map/steps_first/pallas_call | solution.py:518
  58.8 3.1 %collective-permute-start.7 = (f32[8,16,128]{2,1,0:T(8,128)S(1)}, f32[8,16,128]{2,1,0:T(8,128)S(1)}, u32[]{:S(2)}, u32[]{:S(2)}) collective-permute-start(f32[8,16,128]{2,1,0:T(8,128)S(1)} %get-tuple-element.40), channel_id=1, source_target_pairs={{1,0},{2,1},{3,2},{5,4},{6,5},{7,6},{9,8},{10,9},{11,10},{13,12},{... | collective-permute-start | bytes 196616 | tf_op jit(solution)/shard_map/ppermute | solution.py:534
  61.9 2.4 %collective-permute-start.6 = (f32[8,16,128]{2,1,0:T(8,128)S(1)}, f32[8,16,128]{2,1,0:T(8,128)S(1)}, u32[]{:S(2)}, u32[]{:S(2)}) collective-permute-start(f32[8,16,128]{2,1,0:T(8,128)S(1)} %get-tuple-element.40), channel_id=1, source_target_pairs={{0,1},{1,2},{2,3},{4,5},{5,6},{6,7},{8,9},{9,10},{10,11},{12,13},{... | collective-permute-start | bytes 196616 | tf_op jit(solution)/shard_map/ppermute | solution.py:534
  64.4 1.3 %collective-permute-start.13 = (f32[8,16,128]{2,1,0:T(8,128)S(1)}, f32[8,16,128]{2,1,0:T(8,128)S(1)}, u32[]{:S(2)}, u32[]{:S(2)}) collective-permute-start(f32[8,16,128]{2,1,0:T(8,128)S(1)} %get-tuple-element.48.own_ref.own_in), channel_id=1, source_target_pairs={{32,0},{64,32},{96,64},{128,96},{160,128},{192,160},{224,192},{256... | collective-permute-start | bytes 196616 | tf_op jit(solution)/shard_map/ppermute | solution.py:534
  65.7 5.2 %collective-permute-start.12 = (f32[8,16,128]{2,1,0:T(8,128)S(1)}, f32[8,16,128]{2,1,0:T(8,128)S(1)}, u32[]{:S(2)}, u32[]{:S(2)}) collective-permute-start(f32[8,16,128]{2,1,0:T(8,128)S(1)} %get-tuple-element.48.own_ref.own_in), channel_id=1, source_target_pairs={{0,32},{32,64},{64,96},{96,128},{128,160},{160,192},{192,224},{224... | collective-permute-start | bytes 196616 | tf_op jit(solution)/shard_map/ppermute | solution.py:534
  71.2 5.5 %collective-permute-start.8 = (s16[50,16,128]{2,1,0:T(8,128)(2,1)S(1)}, s16[50,16,128]{2,1,0:T(8,128)(2,1)S(1)}, u32[]{:S(2)}, u32[]{:S(2)}) collective-permute-start(s16[50,16,128]{2,1,0:T(8,128)(2,1)S(1)} %get-tuple-element.42), channel_id=1, source_target_pairs={{0,32},{32,64},{64,96},{96,128},{128,160},{160,192},{192,224},{224... | collective-permute-start | bytes 614408 | tf_op jit(solution)/shard_map/ppermute | solution.py:534
  76.7 1.3 %collective-permute-start.9 = (s16[50,16,128]{2,1,0:T(8,128)(2,1)S(1)}, s16[50,16,128]{2,1,0:T(8,128)(2,1)S(1)}, u32[]{:S(2)}, u32[]{:S(2)}) collective-permute-start(s16[50,16,128]{2,1,0:T(8,128)(2,1)S(1)} %get-tuple-element.43), channel_id=1, source_target_pairs={{32,0},{64,32},{96,64},{128,96},{160,128},{192,160},{224,192},{256... | collective-permute-start | bytes 614408 | tf_op jit(solution)/shard_map/ppermute | solution.py:534
  78.0 4.0 %collective-permute-start.14 = (f32[24,8,128]{2,1,0:T(8,128)S(1)}, f32[24,8,128]{2,1,0:T(8,128)S(1)}, u32[]{:S(2)}, u32[]{:S(2)}) collective-permute-start(f32[24,8,128]{2,1,0:T(8,128)S(1)} %get-tuple-element.49), channel_id=1, source_target_pairs={{0,4},{4,8},{8,12},{12,16},{16,20},{20,24},{24,28},{1,5},{5,9},{9,... | collective-permute-start | bytes 294920 | tf_op jit(solution)/shard_map/ppermute | solution.py:534
  82.0 1.3 %collective-permute-start.15 = (f32[24,8,128]{2,1,0:T(8,128)S(1)}, f32[24,8,128]{2,1,0:T(8,128)S(1)}, u32[]{:S(2)}, u32[]{:S(2)}) collective-permute-start(f32[24,8,128]{2,1,0:T(8,128)S(1)} %get-tuple-element.50), channel_id=1, source_target_pairs={{4,0},{8,4},{12,8},{16,12},{20,16},{24,20},{28,24},{5,1},{9,5},{13... | collective-permute-start | bytes 294920 | tf_op jit(solution)/shard_map/ppermute | solution.py:534
  83.3 3.5 %collective-permute-done.9.refs_5_.refs_4_ = s16[50,16,128]{2,1,0:T(8,128)(2,1)S(1)} collective-permute-done((s16[50,16,128]{2,1,0:T(8,128)(2,1)S(1)}, s16[50,16,128]{2,1,0:T(8,128)(2,1)S(1)}, u32[]{:S(2)}, u32[]{:S(2)}) %collective-permute-start.9) | collective-permute-done | bytes 204832 | tf_op jit(solution)/shard_map/ppermute | solution.py:534
  87.2 1.3 %collective-permute-start.11 = (s16[77,16,128]{2,1,0:T(8,128)(2,1)S(1)}, s16[77,16,128]{2,1,0:T(8,128)(2,1)S(1)}, u32[]{:S(2)}, u32[]{:S(2)}) collective-permute-start(s16[77,16,128]{2,1,0:T(8,128)(2,1)S(1)} %get-tuple-element.46), channel_id=1, source_target_pairs={{4,0},{8,4},{12,8},{16,12},{20,16},{24,20},{28,24},{5,1},{9,5},{13... | collective-permute-start | bytes 946184 | tf_op jit(solution)/shard_map/ppermute | solution.py:534
  88.5 4.6 %collective-permute-start.10 = (s16[77,16,128]{2,1,0:T(8,128)(2,1)S(1)}, s16[77,16,128]{2,1,0:T(8,128)(2,1)S(1)}, u32[]{:S(2)}, u32[]{:S(2)}) collective-permute-start(s16[77,16,128]{2,1,0:T(8,128)(2,1)S(1)} %get-tuple-element.45.after_in), channel_id=1, source_target_pairs={{0,4},{4,8},{8,12},{12,16},{16,20},{20,24},{24,28},{1,5},{5,9},{9,... | collective-permute-start | bytes 946184 | tf_op jit(solution)/shard_map/ppermute | solution.py:534
  93.2 4.4 %surface.1 = f32[16,4,8,128]{3,2,1,0:T(8,128)} custom-call(f32[8,16,128]{2,1,0:T(8,128)S(1)} %get-tuple-element.48.own_ref.own_in, f32[8,16,128]{2,1,0:T(8,128)S(1)} %collective-permute-done.12.low_ref.x_low, f32[8,16,128]{2,1,0:T(8,128)S(1)} %collective-permute-done.13.high_ref.x_high, f32[24,8,128]{2,1,0:T(8,128)S(1)} %collective-permute-done.14.y_low, ...), custom_call_target="tpu_custom_call" | custom-call | flops 51749998592 | tf_op jit(solution)/shard_map/surface/pallas_call | solution.py:518
  97.6 10.9 %all-to-all-start = ((f32[64,8,128]{2,1,0:T(8,128)}), f32[64,8,128]{2,1,0:T(8,128)S(1)}, u32[]{:S(2)}, u32[]{:S(2)}) async-start(f32[64,8,128]{2,1,0:T(8,128)} %bitcast.3), calls=%async_computation | async-start | bytes 524288 | tf_op jit(solution)/shard_map/all_to_all | solution.py:627
  108.5 1.4 %copy-done.16 = f32[4,24,32,128]{3,2,1,0:T(8,128)S(1)} copy-done((f32[4,24,32,128]{3,2,1,0:T(8,128)S(1)}, f32[4,24,32,128]{3,2,1,0:T(8,128)}, u32[]{:S(2)}) %copy-start.16) | copy-done | bytes 1572888
  109.9 6.4 %steps_second.1 = f32[3,8,16,128]{3,2,1,0:T(8,128)} custom-call(f32[3,8,16,128]{3,2,1,0:T(8,128)S(1)} %get-tuple-element.38.refs_2_.refs_0_, f32[3,8,16,128]{3,2,1,0:T(8,128)S(1)} %get-tuple-element.39.refs_3_.refs_1_, f32[8,16,128]{2,1,0:T(8,128)S(1)} %get-tuple-element.41.refs_2_, s16[50,16,128]{2,1,0:T(8,128)(2,1)S(1)} %collective-permute-done.8.refs_4_.refs_3_, ...), custom_call_target="tpu_custom_call" | custom-call | flops 74750001152 | tf_op jit(solution)/shard_map/steps_second/pallas_call | solution.py:518
  116.3 4.1 %all-to-all-done = f32[64,8,128]{2,1,0:T(8,128)S(1)} async-done(((f32[64,8,128]{2,1,0:T(8,128)}), f32[64,8,128]{2,1,0:T(8,128)S(1)}, u32[]{:S(2)}, u32[]{:S(2)}) %all-to-all-start) | async-done | bytes 262176 | tf_op jit(solution)/shard_map/all_to_all | solution.py:627
  120.5 1.0 fragility.1
  (46 shorter events, 2.9 us)
Async XLA Ops:
  0.6 0.9 copy-start
  1.6 0.9 copy-start.1
  5.6 10.7 %collective-permute-start.1 = (f32[8,16,128]{2,1,0:T(8,128)S(1)}, f32[8,16,128]{2,1,0:T(8,128)S(1)}, u32[]{:S(2)}, u32[]{:S(2)}) collective-permute-start(f32[8,16,128]{2,1,0:T(8,128)S(1)} %get-tuple-element.31), channel_id=1, source_target_pairs={{1,0},{2,1},{3,2},{5,4},{6,5},{7,6},{9,8},{10,9},{11,10},{13,12},{... | collective-permute-start | bytes 196616 | tf_op jit(solution)/shard_map/ppermute | solution.py:534
  14.4 3.2 %collective-permute-start = (f32[8,16,128]{2,1,0:T(8,128)S(1)}, f32[8,16,128]{2,1,0:T(8,128)S(1)}, u32[]{:S(2)}, u32[]{:S(2)}) collective-permute-start(f32[8,16,128]{2,1,0:T(8,128)S(1)} %get-tuple-element.31), channel_id=1, source_target_pairs={{0,1},{1,2},{2,3},{4,5},{5,6},{6,7},{8,9},{9,10},{10,11},{12,13},{... | collective-permute-start | bytes 196616 | tf_op jit(solution)/shard_map/ppermute | solution.py:534
  17.9 10.8 %collective-permute-start.2 = (s16[62,16,128]{2,1,0:T(8,128)(2,1)S(1)}, s16[62,16,128]{2,1,0:T(8,128)(2,1)S(1)}, u32[]{:S(2)}, u32[]{:S(2)}) collective-permute-start(s16[62,16,128]{2,1,0:T(8,128)(2,1)S(1)} %get-tuple-element.33), channel_id=1, source_target_pairs={{0,32},{32,64},{64,96},{96,128},{128,160},{160,192},{192,224},{224... | collective-permute-start | bytes 761864 | tf_op jit(solution)/shard_map/ppermute | solution.py:534
  19.2 15.4 %collective-permute-start.3 = (s16[62,16,128]{2,1,0:T(8,128)(2,1)S(1)}, s16[62,16,128]{2,1,0:T(8,128)(2,1)S(1)}, u32[]{:S(2)}, u32[]{:S(2)}) collective-permute-start(s16[62,16,128]{2,1,0:T(8,128)(2,1)S(1)} %get-tuple-element.34), channel_id=1, source_target_pairs={{32,0},{64,32},{96,64},{128,96},{160,128},{192,160},{224,192},{256... | collective-permute-start | bytes 761864 | tf_op jit(solution)/shard_map/ppermute | solution.py:534
  34.6 17.3 %copy-start.13 = (bf16[3,256,256]{2,1,0:T(8,128)(2,1)S(1)}, bf16[3,256,256]{2,1,0:T(8,128)(2,1)}, u32[]{:S(2)}) copy-start(bf16[3,256,256]{2,1,0:T(8,128)(2,1)} %constant.4.clone.refs_9_.refs_7_) | copy-start | bytes 1179652
  34.9 12.2 %collective-permute-start.4 = (s16[97,16,128]{2,1,0:T(8,128)(2,1)S(1)}, s16[97,16,128]{2,1,0:T(8,128)(2,1)S(1)}, u32[]{:S(2)}, u32[]{:S(2)}) collective-permute-start(s16[97,16,128]{2,1,0:T(8,128)(2,1)S(1)} %get-tuple-element.36), channel_id=1, source_target_pairs={{0,4},{4,8},{8,12},{12,16},{16,20},{20,24},{24,28},{1,5},{5,9},{9,... | collective-permute-start | bytes 1191944 | tf_op jit(solution)/shard_map/ppermute | solution.py:534
  38.9 12.9 %collective-permute-start.5 = (s16[97,16,128]{2,1,0:T(8,128)(2,1)S(1)}, s16[97,16,128]{2,1,0:T(8,128)(2,1)S(1)}, u32[]{:S(2)}, u32[]{:S(2)}) collective-permute-start(s16[97,16,128]{2,1,0:T(8,128)(2,1)S(1)} %get-tuple-element.37), channel_id=1, source_target_pairs={{4,0},{8,4},{12,8},{16,12},{20,16},{24,20},{28,24},{5,1},{9,5},{13... | collective-permute-start | bytes 1191944 | tf_op jit(solution)/shard_map/ppermute | solution.py:534
  58.8 34.4 %copy-start.15 = (f32[4,24,32,128]{3,2,1,0:T(8,128)}, f32[4,24,32,128]{3,2,1,0:T(8,128)S(1)}, u32[]{:S(2)}) copy-start(f32[4,24,32,128]{3,2,1,0:T(8,128)S(1)} %get-tuple-element.47.refs_8_.rate_in) | copy-start | bytes 4718596
  58.8 12.1 %collective-permute-start.7 = (f32[8,16,128]{2,1,0:T(8,128)S(1)}, f32[8,16,128]{2,1,0:T(8,128)S(1)}, u32[]{:S(2)}, u32[]{:S(2)}) collective-permute-start(f32[8,16,128]{2,1,0:T(8,128)S(1)} %get-tuple-element.40), channel_id=1, source_target_pairs={{1,0},{2,1},{3,2},{5,4},{6,5},{7,6},{9,8},{10,9},{11,10},{13,12},{... | collective-permute-start | bytes 196616 | tf_op jit(solution)/shard_map/ppermute | solution.py:534
  61.9 9.0 %collective-permute-start.6 = (f32[8,16,128]{2,1,0:T(8,128)S(1)}, f32[8,16,128]{2,1,0:T(8,128)S(1)}, u32[]{:S(2)}, u32[]{:S(2)}) collective-permute-start(f32[8,16,128]{2,1,0:T(8,128)S(1)} %get-tuple-element.40), channel_id=1, source_target_pairs={{0,1},{1,2},{2,3},{4,5},{5,6},{6,7},{8,9},{9,10},{10,11},{12,13},{... | collective-permute-start | bytes 196616 | tf_op jit(solution)/shard_map/ppermute | solution.py:534
  64.4 13.6 %collective-permute-start.13 = (f32[8,16,128]{2,1,0:T(8,128)S(1)}, f32[8,16,128]{2,1,0:T(8,128)S(1)}, u32[]{:S(2)}, u32[]{:S(2)}) collective-permute-start(f32[8,16,128]{2,1,0:T(8,128)S(1)} %get-tuple-element.48.own_ref.own_in), channel_id=1, source_target_pairs={{32,0},{64,32},{96,64},{128,96},{160,128},{192,160},{224,192},{256... | collective-permute-start | bytes 196616 | tf_op jit(solution)/shard_map/ppermute | solution.py:534
  65.7 12.3 %collective-permute-start.12 = (f32[8,16,128]{2,1,0:T(8,128)S(1)}, f32[8,16,128]{2,1,0:T(8,128)S(1)}, u32[]{:S(2)}, u32[]{:S(2)}) collective-permute-start(f32[8,16,128]{2,1,0:T(8,128)S(1)} %get-tuple-element.48.own_ref.own_in), channel_id=1, source_target_pairs={{0,32},{32,64},{64,96},{96,128},{128,160},{160,192},{192,224},{224... | collective-permute-start | bytes 196616 | tf_op jit(solution)/shard_map/ppermute | solution.py:534
  71.2 12.2 %collective-permute-start.8 = (s16[50,16,128]{2,1,0:T(8,128)(2,1)S(1)}, s16[50,16,128]{2,1,0:T(8,128)(2,1)S(1)}, u32[]{:S(2)}, u32[]{:S(2)}) collective-permute-start(s16[50,16,128]{2,1,0:T(8,128)(2,1)S(1)} %get-tuple-element.42), channel_id=1, source_target_pairs={{0,32},{32,64},{64,96},{96,128},{128,160},{160,192},{192,224},{224... | collective-permute-start | bytes 614408 | tf_op jit(solution)/shard_map/ppermute | solution.py:534
  76.7 10.2 %collective-permute-start.9 = (s16[50,16,128]{2,1,0:T(8,128)(2,1)S(1)}, s16[50,16,128]{2,1,0:T(8,128)(2,1)S(1)}, u32[]{:S(2)}, u32[]{:S(2)}) collective-permute-start(s16[50,16,128]{2,1,0:T(8,128)(2,1)S(1)} %get-tuple-element.43), channel_id=1, source_target_pairs={{32,0},{64,32},{96,64},{128,96},{160,128},{192,160},{224,192},{256... | collective-permute-start | bytes 614408 | tf_op jit(solution)/shard_map/ppermute | solution.py:534
  78.0 15.1 %collective-permute-start.14 = (f32[24,8,128]{2,1,0:T(8,128)S(1)}, f32[24,8,128]{2,1,0:T(8,128)S(1)}, u32[]{:S(2)}, u32[]{:S(2)}) collective-permute-start(f32[24,8,128]{2,1,0:T(8,128)S(1)} %get-tuple-element.49), channel_id=1, source_target_pairs={{0,4},{4,8},{8,12},{12,16},{16,20},{20,24},{24,28},{1,5},{5,9},{9,... | collective-permute-start | bytes 294920 | tf_op jit(solution)/shard_map/ppermute | solution.py:534
  82.0 11.1 %collective-permute-start.15 = (f32[24,8,128]{2,1,0:T(8,128)S(1)}, f32[24,8,128]{2,1,0:T(8,128)S(1)}, u32[]{:S(2)}, u32[]{:S(2)}) collective-permute-start(f32[24,8,128]{2,1,0:T(8,128)S(1)} %get-tuple-element.50), channel_id=1, source_target_pairs={{4,0},{8,4},{12,8},{16,12},{20,16},{24,20},{28,24},{5,1},{9,5},{13... | collective-permute-start | bytes 294920 | tf_op jit(solution)/shard_map/ppermute | solution.py:534
  86.9 6.3 %copy-start.4 = (s32[16,1,128]{2,1,0:T(1,128)S(1)}, s32[16,1,128]{2,1,0:T(1,128)}, u32[]{:S(2)}) copy-start(s32[16,1,128]{2,1,0:T(1,128)} %param.19) | copy-start | bytes 24580
  86.9 6.3 %copy-start.5 = (bf16[64,24]{0,1:T(8,128)(2,1)S(1)}, bf16[64,24]{0,1:T(8,128)(2,1)}, u32[]{:S(2)}) copy-start(bf16[64,24]{0,1:T(8,128)(2,1)} %param.24) | copy-start | bytes 9220
  86.9 6.3 %copy-start.11 = (s32[8]{0:T(128)S(1)}, s32[8]{0:T(128)}, u32[]{:S(2)}) copy-start(s32[8]{0:T(128)} %param.23) | copy-start | bytes 100
  86.9 6.3 %copy-start.14 = (bf16[256,128]{1,0:T(8,128)(2,1)S(1)}, bf16[256,128]{1,0:T(8,128)(2,1)}, u32[]{:S(2)}) copy-start(bf16[256,128]{1,0:T(8,128)(2,1)} %constant.5.clone.weight_in) | copy-start | bytes 196612
  87.2 21.4 %collective-permute-start.11 = (s16[77,16,128]{2,1,0:T(8,128)(2,1)S(1)}, s16[77,16,128]{2,1,0:T(8,128)(2,1)S(1)}, u32[]{:S(2)}, u32[]{:S(2)}) collective-permute-start(s16[77,16,128]{2,1,0:T(8,128)(2,1)S(1)} %get-tuple-element.46), channel_id=1, source_target_pairs={{4,0},{8,4},{12,8},{16,12},{20,16},{24,20},{28,24},{5,1},{9,5},{13... | collective-permute-start | bytes 946184 | tf_op jit(solution)/shard_map/ppermute | solution.py:534
  88.5 20.1 %collective-permute-start.10 = (s16[77,16,128]{2,1,0:T(8,128)(2,1)S(1)}, s16[77,16,128]{2,1,0:T(8,128)(2,1)S(1)}, u32[]{:S(2)}, u32[]{:S(2)}) collective-permute-start(s16[77,16,128]{2,1,0:T(8,128)(2,1)S(1)} %get-tuple-element.45.after_in), channel_id=1, source_target_pairs={{0,4},{4,8},{8,12},{12,16},{16,20},{20,24},{24,28},{1,5},{5,9},{9,... | collective-permute-start | bytes 946184 | tf_op jit(solution)/shard_map/ppermute | solution.py:534
  97.6 22.9 %all-to-all-start = ((f32[64,8,128]{2,1,0:T(8,128)}), f32[64,8,128]{2,1,0:T(8,128)S(1)}, u32[]{:S(2)}, u32[]{:S(2)}) async-start(f32[64,8,128]{2,1,0:T(8,128)} %bitcast.3), calls=%async_computation | async-start | bytes 524288 | tf_op jit(solution)/shard_map/all_to_all | solution.py:627
  108.4 12.0 %copy-start.6 = (s32[1024]{0:T(1024)S(1)}, s32[1024]{0:T(1024)}, u32[]{:S(2)}) copy-start(s32[1024]{0:T(1024)} %param.20) | copy-start | bytes 12292
  108.5 12.0 %copy-start.7 = (s32[1024]{0:T(1024)S(1)}, s32[1024]{0:T(1024)}, u32[]{:S(2)}) copy-start(s32[1024]{0:T(1024)} %param.21) | copy-start | bytes 12292
  108.5 12.0 %copy-start.8 = (s32[1024]{0:T(1024)S(1)}, s32[1024]{0:T(1024)}, u32[]{:S(2)}) copy-start(s32[1024]{0:T(1024)} %param.22) | copy-start | bytes 12292
  108.5 12.0 %copy-start.9 = (f32[16,8]{0,1:T(8,128)S(1)}, f32[16,8]{0,1:T(8,128)}, u32[]{:S(2)}) copy-start(f32[16,8]{0,1:T(8,128)} %param.26) | copy-start | bytes 1540
  108.5 12.0 %copy-start.10 = (f32[16,8]{0,1:T(8,128)S(1)}, f32[16,8]{0,1:T(8,128)}, u32[]{:S(2)}) copy-start(f32[16,8]{0,1:T(8,128)} %param.27) | copy-start | bytes 1540
  108.5 12.0 %copy-start.12 = (f32[16]{0:T(128)S(1)}, f32[16]{0:T(128)}, u32[]{:S(2)}) copy-start(f32[16]{0:T(128)} %param.25) | copy-start | bytes 196
  108.5 1.4 %copy-start.16 = (f32[4,24,32,128]{3,2,1,0:T(8,128)S(1)}, f32[4,24,32,128]{3,2,1,0:T(8,128)}, u32[]{:S(2)}) copy-start(f32[4,24,32,128]{3,2,1,0:T(8,128)} %copy-done.15) | copy-start | bytes 4718596
  (2 other events, 1.7 us)

commit v9 on v8

--- a/solution.py
+++ b/solution.py
@@ -16,6 +16,7 @@
 CITIES = 16
 F32 = jnp.float32
 VMEM_LIMIT = 24 * 1024 * 1024
+START_LIMIT = int(53.8 * 1024 * 1024)
 
 XU, XP, XH = 8, 6, 7
 YU, YP, YH = 24, 20, 20
@@ -68,7 +69,7 @@
     return packed
 
 
-def start_kernel(u_in, p_in, c_in, d_in, u_ref, p_ref, a_ref, e_ref, face_ref, c_ref, d_ref, sems):
+def start_kernel(u_in, p_in, c_in, d_in, a_ref, e_ref, face_ref, u_ref, p_ref, c_ref, d_ref, sems):
     copies = [pltpu.make_async_copy(c_in, c_ref, sems.at[0]), pltpu.make_async_copy(d_in, d_ref, sems.at[1])]
     for k in range(3):
         copies.append(pltpu.make_async_copy(u_in.at[k], u_ref.at[k], sems.at[2 + k]))
@@ -255,11 +256,11 @@
 def steps_kernel(first, *refs):
     if first:
         (u_in, p_in, a_in, e_in, halo_in, x_low, x_high, y_low, y_high, weight_in) = refs[:10]
-        (u_out, p_out, face_out, slab_out, seen_out, rate_ref) = refs[10:16]
-        state_ref, edge_ref = refs[16:]
+        (u_out, p_out, face_out, slab_out, seen_out, code_ref) = refs[10:16]
+        state_ref, rate_ref, edge_ref = refs[16:]
     else:
-        (u_in, p_in, halo_in, x_low, x_high, y_low, y_high, weight_in, rate_ref) = refs[:9]
-        u_out, state_ref = refs[9:]
+        (u_in, p_in, halo_in, x_low, x_high, y_low, y_high, weight_in, code_ref) = refs[:9]
+        u_out, state_ref, rate_ref = refs[9:]
     a_ref, e_ref, ha_ref, he_ref = (rate_ref.at[at] for at in range(4))
     lane = lane_of()
     inner = lane % 16
@@ -275,18 +276,31 @@
     x_at, y_at = fill(parts, *sides, x_at, XP, y_at, YP)
     fill([(state_ref.at[0, 3], 8, halo_in, face)], *sides, x_at, XH, y_at, YH)
 
+    unit = jnp.where(lane < 112, UNIT_A, UNIT_E)
+
     def prepare(x, carry):
-        for tile in range(4):
-            rows = pl.ds(8 + 8 * tile, 8)
-            held = pl.ds(8 * tile, 8)
-            halo = state_ref[0, 3, x, rows, :]
-            state_ref[0, 3, x, rows, :] = jnp.where(lane < 48, halo, 0.0)
-            state_ref[1, 3, x, rows, :] = jnp.where(lane < 48, pltpu.roll(halo, 128 - 48, 1), 0.0)
+        for half in (0, 16):
+            held = pl.ds(half, 16)
             if first:
+                code_ref[0, x - 2, held, :] = coded(a_ref[x, held, :] * (1.0 / UNIT_A))
+                code_ref[1, x - 2, held, :] = coded(e_ref[x, held, :] * (1.0 / UNIT_E))
+                sides = state_ref[0, 3, x, pl.ds(8 + half, 16), :]
+                scale = twice(jnp.where(lane < 96, 0.0, 1.0 / unit))
+                code_ref[2, x - 2, held, :] = coded(jnp.where(scale > 0.0, sides * scale, 0.0))
+            else:
+                a_ref[x, held, :] = decoded(code_ref[0, x - 2, held, :]) * UNIT_A
+                e_ref[x, held, :] = decoded(code_ref[1, x - 2, held, :]) * UNIT_E
+                sides = decoded(code_ref[2, x - 2, held, :]) * twice(unit)
+            for tile in (0, 8):
+                rows = pl.ds(8 + half + tile, 8)
+                halo = state_ref[0, 3, x, rows, :]
+                state_ref[0, 3, x, rows, :] = jnp.where(lane < 48, halo, 0.0)
+                state_ref[1, 3, x, rows, :] = jnp.where(lane < 48, pltpu.roll(halo, 128 - 48, 1), 0.0)
+                side = sides[tile : tile + 8]
                 for target, at in ((ha_ref, 96), (he_ref, 112)):
-                    spread = jnp.where(lane < 16, pltpu.roll(halo, 128 - at, 1), pltpu.roll(halo, 144 - at, 1))
-                    spread = jnp.where(lane < 32, spread, pltpu.roll(halo, 160 - at, 1))
-                    target[x, held, :] = jnp.where(lane < 48, spread, 0.0)
+                    spread = jnp.where(lane < 16, pltpu.roll(side, 128 - at, 1), pltpu.roll(side, 144 - at, 1))
+                    spread = jnp.where(lane < 32, spread, pltpu.roll(side, 160 - at, 1))
+                    target[x, pl.ds(half + tile, 8), :] = jnp.where(lane < 48, spread, 0.0)
         return carry
 
     lax.fori_loop(2, 22, prepare, 0, unroll=4)
@@ -377,8 +391,8 @@
 
 
 def surface_kernel(
-    own_in, x_low, x_high, y_low, y_high, weight_in, rate_in, seen_in, cells_in, filter_in, count_in, after_in,
-    table_out, state_ref, rate_ref, sample_ref, seen_ref, filter_ref, count_ref,
+    own_in, x_low, x_high, y_low, y_high, weight_in, code_in, seen_in, filter_in, count_in,
+    demand_out, state_ref, rate_ref, sample_ref, seen_ref, filter_ref, count_ref,
 ):
     lane = lane_of()
     inner = lane % 16
@@ -397,17 +411,24 @@
     def prepare(x, carry):
         for tile in range(4):
             rows = pl.ds(8 + 8 * tile, 8)
-            held = pl.ds(8 * tile, 8)
             value = state_ref[0, x, rows, :]
             state_ref[0, x, rows, :] = jnp.where(lane < 48, value, 0.0)
             state_ref[1, x, rows, :] = jnp.where(lane < 48, pltpu.roll(value, 128 - 48, 1), 0.0)
-            for at in (0, 1):
-                rate = rate_in[at, x, held, :]
-                spread = jnp.where(lane < 16, rate, jnp.where(lane < 32, pltpu.roll(rate, 16, 1), pltpu.roll(rate, 32, 1)))
-                rate_ref[at, x, held, :] = jnp.where(lane < 48, spread, 0.0)
+        return carry
+
+    def rates(x, carry):
+        for at, unit in ((0, UNIT_A), (1, UNIT_E)):
+            for half in (0, 16):
+                both = decoded(code_in[at, x - 2, half : half + 16, :]) * unit
+                for tile in (0, 8):
+                    rate = both[tile : tile + 8]
+                    spread = jnp.where(lane < 32, pltpu.roll(rate, 16, 1), pltpu.roll(rate, 32, 1))
+                    spread = jnp.where(lane < 16, rate, spread)
+                    rate_ref[at, x, pl.ds(half + tile, 8), :] = jnp.where(lane < 48, spread, 0.0)
         return carry
 
     lax.fori_loop(0, 24, prepare, 0, unroll=4)
+    lax.fori_loop(2, 22, rates, 0, unroll=4)
 
     def one_step(step, carry):
         dst = state_ref.at[(step + 1) % 2]
@@ -466,9 +487,13 @@
         part = modal[MODES * kind : MODES * (kind + 1), :]
         part = jnp.where(modes < counts[kind : kind + 1, :], part * part, 0.0)
         energies.append(jnp.sum(part, axis=0, keepdims=True))
-    demand = 0.5 * jnp.log1p(jnp.concatenate(energies, axis=0))
+    demand_out[...] = 0.5 * jnp.log1p(jnp.concatenate(energies, axis=0))
+
+
+def table_kernel(demand_ref, cells_ref, after_ref, table_out):
+    demand = demand_ref[...]
     for owner in range(table_out.shape[0]):
-        cells = jnp.broadcast_to(cells_in[owner : owner + 1, :], (CLASSES, 128))
+        cells = jnp.broadcast_to(cells_ref[owner : owner + 1, :], (CLASSES, 128))
         chosen = jnp.take_along_axis(demand, cells, axis=1)
         for level in range(table_out.shape[1]):
             table_out[owner, level] = chosen
@@ -509,11 +534,11 @@
 VM = pl.BlockSpec(memory_space=pltpu.VMEM)
 
 
-TIMES = {"start": 1.4, "steps_first": 6.7, "steps_second": 6.5, "surface": 4.5, "fragility": 1.0}
-FLOPS_A_US = 1.15e10
-
-
-def call(kernel, name, shapes, args, specs=None, scratch=()):
+WEIGHTS = {"start": 1.4, "steps_first": 6.7, "steps_second": 6.5, "slab_message": 4.0, "surface": 0.02, "table": 4.0, "fragility": 1.0}
+UNIT_FLOPS = 1.15e10
+
+
+def call(kernel, name, shapes, args, specs=None, scratch=(), limit=VMEM_LIMIT):
     out = [s if isinstance(s, jax.ShapeDtypeStruct) else jax.ShapeDtypeStruct(s, F32) for s in shapes]
     return pl.pallas_call(
         kernel,
@@ -521,8 +546,8 @@
         in_specs=specs or [VM] * len(args),
         out_specs=[VM] * len(out),
         scratch_shapes=list(scratch),
-        compiler_params=pltpu.CompilerParams(vmem_limit_bytes=VMEM_LIMIT),
-        cost_estimate=pl.CostEstimate(flops=int(TIMES.get(name, 0.3) * FLOPS_A_US), bytes_accessed=0, transcendentals=0),
+        compiler_params=pltpu.CompilerParams(vmem_limit_bytes=limit),
+        cost_estimate=pl.CostEstimate(flops=int(WEIGHTS.get(name, 0.3) * UNIT_FLOPS), bytes_accessed=0, transcendentals=0),
         name=name,
     )(*args)
 
@@ -578,42 +603,41 @@
     own = (3, 8, 16, 128)
     plane = (8, 16, 128)
     wide = pltpu.VMEM((2, 4, 24, 48, 128), F32)
+    rates = pltpu.VMEM((4, 24, 32, 128), F32)
     samples = pltpu.VMEM((HALF, 24, 16, 128), F32)
 
-    u, p, a, e, faces = call(
+    u, p = displacement, previous
+    a, e, faces = call(
         start_kernel,
         "start",
-        [own, own, plane, plane, plane],
-        [displacement, previous, courant, damping],
+        [plane, plane, plane],
+        [u, p, courant, damping],
         specs=[pl.BlockSpec(memory_space=pltpu.HBM)] * 4,
-        scratch=[pltpu.VMEM(plane, F32)] * 2 + [pltpu.SemaphoreType.DMA((8,))],
+        scratch=[pltpu.VMEM(own, F32)] * 2 + [pltpu.VMEM(plane, F32)] * 2 + [pltpu.SemaphoreType.DMA((8,))],
+        limit=START_LIMIT,
     )
     halo, powers, x_low, x_high = exchange_x(u, p, faces, (a, e))
     messages = y_messages(u, p, (a, e), halo, powers, x_low, x_high)
     received = (halo, x_low, x_high, *both_ways(*messages, "gy"))
     weights = jnp.asarray(depth_weights(), jnp.bfloat16)
-    u, p, faces, slab, seen, rates = call(
+    u, p, faces, slab, seen, codes = call(
         functools.partial(steps_kernel, True),
         "steps_first",
-        [own, own, plane, plane, plane, (4, 24, 32, 128)],
+        [own, own, plane, plane, plane, jax.ShapeDtypeStruct((3, 20, 32, 128), jnp.int16)],
         [u, p, a, e, *received, weights],
-        scratch=[wide, samples],
+        scratch=[wide, rates, samples],
     )
 
     near_low, near_high = both_ways(slab, slab, "gx")
     halo, powers, x_low, x_high = exchange_x(u, p, faces, ())
     slab_messages = call(slab_message_kernel, "slab_message", [(24, 8, 128)] * 2, [slab, near_low, near_high, powers])
     side_low, side_high = both_ways(*slab_messages, "gy")
-    messages = y_messages(u, p, (), halo, powers, x_low, x_high)
-    received = (halo, x_low, x_high, *both_ways(*messages, "gy"))
-    owners, levels = lax.axis_size("gx"), lax.axis_size("gz")
-    (table,) = call(
+    (demand,) = call(
         surface_kernel,
         "surface",
-        [(owners, levels, CLASSES, 128)],
-        [slab, near_low, near_high, side_low, side_high, jnp.asarray(slab_weights(), jnp.bfloat16), rates, seen]
-        + [send_cells.reshape(owners, 128), modal_filter.T, mode_count.reshape(1, CLASSES), messages[0]],
-        specs=[VM] * 11 + [pl.BlockSpec(memory_space=pl.ANY)],
+        [(CLASSES, 128)],
+        [slab, near_low, near_high, side_low, side_high, jnp.asarray(slab_weights(), jnp.bfloat16), codes, seen]
+        + [modal_filter.T, mode_count.reshape(1, CLASSES)],
         scratch=[
             pltpu.VMEM((2, 24, 48, 128), F32),
             pltpu.VMEM((2, 24, 32, 128), F32),
@@ -623,10 +647,20 @@
             pltpu.VMEM((8, 128), jnp.int32),
         ],
     )
+    messages = y_messages(u, p, (), halo, powers, x_low, x_high)
+    received = (halo, x_low, x_high, *both_ways(*messages, "gy"))
+    owners, levels = lax.axis_size("gx"), lax.axis_size("gz")
+    (table,) = call(
+        table_kernel,
+        "table",
+        [(owners, levels, CLASSES, 128)],
+        [demand, send_cells.reshape(owners, 128), messages[0]],
+        specs=[VM, VM, pl.BlockSpec(memory_space=pl.ANY)],
+    )
     table = table.reshape(owners * levels, CLASSES, 128)
     table = lax.all_to_all(table, ("gx", "gz"), split_axis=0, concat_axis=0, tiled=True)
     (field,) = call(
-        functools.partial(steps_kernel, False), "steps_second", [own], [u, p, *received, weights, rates], scratch=[wide]
+        functools.partial(steps_kernel, False), "steps_second", [own], [u, p, *received, weights, codes], scratch=[wide, rates]
     )
     (probability,) = call(
         fragility_kernel,

time: 124 us -> 125 us (level); the launches traced: 121 us -> 124 us
  waiting for transfers between devices: 34.6 us -> 38.3 us
  local copies, waits for them, and re-layouts: 4.99 us -> 1.38 us
  Pallas kernels: 21.3 us -> 22.7 us
    unnamed x34 -> x26, local copies, waits for them, and re-layouts: 4.99 us -> 1.38 us
    ppermute x8, waiting for transfers between devices: 16.3 us -> 18 us  [both_ways(): lax.ppermute(to_up, axis, forward)]
    pallas_call x10 -> x11, Pallas kernels: 21.3 us -> 22.7 us  [call(): pl.pallas_call(kernel, out_shape=out, in_specs=specs or [VM] * len(args),...]
  transfers between devices with their start and end apart: 17 -> 17, of which waited for: 7 -> 8; matrix products, arithmetic and copies ran while one was open for 0% -> 0% of each run, Pallas kernels for 9% -> 9%
where the time goes in v9:
time: 125 us; the launch traced here: 124 us
  starting transfers between devices  60.7 us (49%)
  waiting for transfers between devices  38.3 us (31%)
  Pallas kernels  22.7 us (18%)
  local copies, waits for them, and re-layouts  1.38 us (1%)
    ppermute x8, starting transfers between devices, both_ways(): lax.ppermute(to_up, axis, forward)  29.3 us
    pallas_call x11, Pallas kernels, call(): pl.pallas_call(kernel, out_shape=out, in_specs=specs or [VM] * len(args),...  22.7 us
    ppermute x8, starting transfers between devices, both_ways(): lax.ppermute(to_down, axis, backward)  19.7 us
    ppermute x8, waiting for transfers between devices, both_ways(): lax.ppermute(to_up, axis, forward)  18 us
    ppermute x8, waiting for transfers between devices, both_ways(): lax.ppermute(to_down, axis, backward)  15.1 us
    all_to_all x1, starting transfers between devices, body(): lax.all_to_all(table, ('gx', 'gz'), split_axis=0, concat_axis=0, tiled=True)  11.8 us
    all_to_all x1, waiting for transfers between devices, body(): lax.all_to_all(table, ('gx', 'gz'), split_axis=0, concat_axis=0, tiled=True)  5.16 us
  transfers between devices with their start and end apart: 17, of which 8 were waited for; matrix products, arithmetic and copies ran while one was open for 0% of the time, Pallas kernels for 9%

profile of v9, /device:TPU:1, one launch (start us, length us, event | category | flops | bytes accessed | tf_op | source)
XLA Modules:
  0.0 124.0 jit_solution(1495750289924318304)
XLA Ops:
  0.7 2.5 %start.1 = (f32[8,16,128]{2,1,0:T(8,128)S(1)}, f32[8,16,128]{2,1,0:T(8,128)S(1)}, f32[8,16,128]{2,1,0:T(8,128)}) custom-call(f32[3,8,16,128]{3,2,1,0:T(8,128)} %refs_0_.3, f32[3,8,16,128]{3,2,1,0:T(8,128)} %refs_1_.3, f32[8,16,128]{2,1,0:T(8,128)} %c_in.1, f32[8,16,128]{2,1,0:T(8,128)} %d_in.1), custom_call_target="tpu_custom_call" | custom-call | flops 16099999744 | tf_op jit(solution)/shard_map/start/pallas_call | solution.py:543
  3.1 8.8 %collective-permute-start.1 = (f32[8,16,128]{2,1,0:T(8,128)}, f32[8,16,128]{2,1,0:T(8,128)S(1)}, u32[]{:S(2)}, u32[]{:S(2)}) collective-permute-start(f32[8,16,128]{2,1,0:T(8,128)} %get-tuple-element.27), channel_id=1, source_target_pairs={{1,0},{2,1},{3,2},{5,4},{6,5},{7,6},{9,8},{10,9},{11,10},{13,12},{... | collective-permute-start | bytes 196616 | tf_op jit(solution)/shard_map/ppermute | solution.py:559
  11.9 1.9 %collective-permute-start = (f32[8,16,128]{2,1,0:T(8,128)}, f32[8,16,128]{2,1,0:T(8,128)S(1)}, u32[]{:S(2)}, u32[]{:S(2)}) collective-permute-start(f32[8,16,128]{2,1,0:T(8,128)} %get-tuple-element.27), channel_id=1, source_target_pairs={{0,1},{1,2},{2,3},{4,5},{5,6},{6,7},{8,9},{9,10},{10,11},{12,13},{... | collective-permute-start | bytes 196616 | tf_op jit(solution)/shard_map/ppermute | solution.py:559
  13.9 1.6 %collective-permute-done.refs_0_ = f32[8,16,128]{2,1,0:T(8,128)S(1)} collective-permute-done((f32[8,16,128]{2,1,0:T(8,128)}, f32[8,16,128]{2,1,0:T(8,128)S(1)}, u32[]{:S(2)}, u32[]{:S(2)}) %collective-permute-start) | collective-permute-done | bytes 65568 | tf_op jit(solution)/shard_map/ppermute | solution.py:559
  15.8 1.3 %collective-permute-start.2 = (s16[62,16,128]{2,1,0:T(8,128)(2,1)S(1)}, s16[62,16,128]{2,1,0:T(8,128)(2,1)S(1)}, u32[]{:S(2)}, u32[]{:S(2)}) collective-permute-start(s16[62,16,128]{2,1,0:T(8,128)(2,1)S(1)} %get-tuple-element.29), channel_id=1, source_target_pairs={{0,32},{32,64},{64,96},{96,128},{128,160},{160,192},{192,224},{224... | collective-permute-start | bytes 761864 | tf_op jit(solution)/shard_map/ppermute | solution.py:559
  17.1 1.3 %collective-permute-start.3 = (s16[62,16,128]{2,1,0:T(8,128)(2,1)S(1)}, s16[62,16,128]{2,1,0:T(8,128)(2,1)S(1)}, u32[]{:S(2)}, u32[]{:S(2)}) collective-permute-start(s16[62,16,128]{2,1,0:T(8,128)(2,1)S(1)} %get-tuple-element.30), channel_id=1, source_target_pairs={{32,0},{64,32},{96,64},{128,96},{160,128},{192,160},{224,192},{256... | collective-permute-start | bytes 761864 | tf_op jit(solution)/shard_map/ppermute | solution.py:559
  18.4 9.3 %collective-permute-done.2.refs_6_.refs_5_ = s16[62,16,128]{2,1,0:T(8,128)(2,1)S(1)} collective-permute-done((s16[62,16,128]{2,1,0:T(8,128)(2,1)S(1)}, s16[62,16,128]{2,1,0:T(8,128)(2,1)S(1)}, u32[]{:S(2)}, u32[]{:S(2)}) %collective-permute-start.2) | collective-permute-done | bytes 253984 | tf_op jit(solution)/shard_map/ppermute | solution.py:559
  27.7 4.7 %collective-permute-done.3.refs_7_.refs_6_ = s16[62,16,128]{2,1,0:T(8,128)(2,1)S(1)} collective-permute-done((s16[62,16,128]{2,1,0:T(8,128)(2,1)S(1)}, s16[62,16,128]{2,1,0:T(8,128)(2,1)S(1)}, u32[]{:S(2)}, u32[]{:S(2)}) %collective-permute-start.3) | collective-permute-done | bytes 253984 | tf_op jit(solution)/shard_map/ppermute | solution.py:559
  32.7 4.0 %collective-permute-start.4 = (s16[97,16,128]{2,1,0:T(8,128)(2,1)S(1)}, s16[97,16,128]{2,1,0:T(8,128)(2,1)S(1)}, u32[]{:S(2)}, u32[]{:S(2)}) collective-permute-start(s16[97,16,128]{2,1,0:T(8,128)(2,1)S(1)} %get-tuple-element.32), channel_id=1, source_target_pairs={{0,4},{4,8},{8,12},{12,16},{16,20},{20,24},{24,28},{1,5},{5,9},{9,... | collective-permute-start | bytes 1191944 | tf_op jit(solution)/shard_map/ppermute | solution.py:559
  36.7 1.3 %collective-permute-start.5 = (s16[97,16,128]{2,1,0:T(8,128)(2,1)S(1)}, s16[97,16,128]{2,1,0:T(8,128)(2,1)S(1)}, u32[]{:S(2)}, u32[]{:S(2)}) collective-permute-start(s16[97,16,128]{2,1,0:T(8,128)(2,1)S(1)} %get-tuple-element.33), channel_id=1, source_target_pairs={{4,0},{8,4},{12,8},{16,12},{20,16},{24,20},{28,24},{5,1},{9,5},{13... | collective-permute-start | bytes 1191944 | tf_op jit(solution)/shard_map/ppermute | solution.py:559
  38.0 6.8 %collective-permute-done.4.refs_7_ = s16[97,16,128]{2,1,0:T(8,128)(2,1)S(1)} collective-permute-done((s16[97,16,128]{2,1,0:T(8,128)(2,1)S(1)}, s16[97,16,128]{2,1,0:T(8,128)(2,1)S(1)}, u32[]{:S(2)}, u32[]{:S(2)}) %collective-permute-start.4) | collective-permute-done | bytes 397344 | tf_op jit(solution)/shard_map/ppermute | solution.py:559
  44.8 4.8 %collective-permute-done.5.refs_8_ = s16[97,16,128]{2,1,0:T(8,128)(2,1)S(1)} collective-permute-done((s16[97,16,128]{2,1,0:T(8,128)(2,1)S(1)}, s16[97,16,128]{2,1,0:T(8,128)(2,1)S(1)}, u32[]{:S(2)}, u32[]{:S(2)}) %collective-permute-start.5) | collective-permute-done | bytes 397344 | tf_op jit(solution)/shard_map/ppermute | solution.py:559
  49.6 6.7 %steps_first.1 = (f32[3,8,16,128]{3,2,1,0:T(8,128)S(1)}, f32[3,8,16,128]{3,2,1,0:T(8,128)S(1)}, f32[8,16,128]{2,1,0:T(8,128)S(1)}, f32[8,16,128]{2,1,0:T(8,128)S...) custom-call(f32[3,8,16,128]{3,2,1,0:T(8,128)S(1)} %copy-done.3, f32[3,8,16,128]{3,2,1,0:T(8,128)S(1)} %copy-done.4, ...), custom_call_target="tpu_custom_call" | custom-call | flops 77050003456 | tf_op jit(solution)/shard_map/steps_first/pallas_call | solution.py:543
  56.3 3.1 %collective-permute-start.7 = (f32[8,16,128]{2,1,0:T(8,128)S(1)}, f32[8,16,128]{2,1,0:T(8,128)S(1)}, u32[]{:S(2)}, u32[]{:S(2)}) collective-permute-start(f32[8,16,128]{2,1,0:T(8,128)S(1)} %get-tuple-element.36), channel_id=1, source_target_pairs={{1,0},{2,1},{3,2},{5,4},{6,5},{7,6},{9,8},{10,9},{11,10},{13,12},{... | collective-permute-start | bytes 196616 | tf_op jit(solution)/shard_map/ppermute | solution.py:559
  59.4 2.4 %collective-permute-start.6 = (f32[8,16,128]{2,1,0:T(8,128)S(1)}, f32[8,16,128]{2,1,0:T(8,128)S(1)}, u32[]{:S(2)}, u32[]{:S(2)}) collective-permute-start(f32[8,16,128]{2,1,0:T(8,128)S(1)} %get-tuple-element.36), channel_id=1, source_target_pairs={{0,1},{1,2},{2,3},{4,5},{5,6},{6,7},{8,9},{9,10},{10,11},{12,13},{... | collective-permute-start | bytes 196616 | tf_op jit(solution)/shard_map/ppermute | solution.py:559
  61.9 1.3 %collective-permute-start.13 = (f32[8,16,128]{2,1,0:T(8,128)S(1)}, f32[8,16,128]{2,1,0:T(8,128)S(1)}, u32[]{:S(2)}, u32[]{:S(2)}) collective-permute-start(f32[8,16,128]{2,1,0:T(8,128)S(1)} %get-tuple-element.44.own_ref.own_in), channel_id=1, source_target_pairs={{32,0},{64,32},{96,64},{128,96},{160,128},{192,160},{224,192},{256... | collective-permute-start | bytes 196616 | tf_op jit(solution)/shard_map/ppermute | solution.py:559
  63.2 5.2 %collective-permute-start.12 = (f32[8,16,128]{2,1,0:T(8,128)S(1)}, f32[8,16,128]{2,1,0:T(8,128)S(1)}, u32[]{:S(2)}, u32[]{:S(2)}) collective-permute-start(f32[8,16,128]{2,1,0:T(8,128)S(1)} %get-tuple-element.44.own_ref.own_in), channel_id=1, source_target_pairs={{0,32},{32,64},{64,96},{96,128},{128,160},{160,192},{192,224},{224... | collective-permute-start | bytes 196616 | tf_op jit(solution)/shard_map/ppermute | solution.py:559
  68.7 5.5 %collective-permute-start.8 = (s16[50,16,128]{2,1,0:T(8,128)(2,1)S(1)}, s16[50,16,128]{2,1,0:T(8,128)(2,1)S(1)}, u32[]{:S(2)}, u32[]{:S(2)}) collective-permute-start(s16[50,16,128]{2,1,0:T(8,128)(2,1)S(1)} %get-tuple-element.38), channel_id=1, source_target_pairs={{0,32},{32,64},{64,96},{96,128},{128,160},{160,192},{192,224},{224... | collective-permute-start | bytes 614408 | tf_op jit(solution)/shard_map/ppermute | solution.py:559
  74.2 1.3 %collective-permute-start.9 = (s16[50,16,128]{2,1,0:T(8,128)(2,1)S(1)}, s16[50,16,128]{2,1,0:T(8,128)(2,1)S(1)}, u32[]{:S(2)}, u32[]{:S(2)}) collective-permute-start(s16[50,16,128]{2,1,0:T(8,128)(2,1)S(1)} %get-tuple-element.39), channel_id=1, source_target_pairs={{32,0},{64,32},{96,64},{128,96},{160,128},{192,160},{224,192},{256... | collective-permute-start | bytes 614408 | tf_op jit(solution)/shard_map/ppermute | solution.py:559
  75.6 4.0 %collective-permute-start.14 = (f32[24,8,128]{2,1,0:T(8,128)S(1)}, f32[24,8,128]{2,1,0:T(8,128)S(1)}, u32[]{:S(2)}, u32[]{:S(2)}) collective-permute-start(f32[24,8,128]{2,1,0:T(8,128)S(1)} %get-tuple-element.45), channel_id=1, source_target_pairs={{0,4},{4,8},{8,12},{12,16},{16,20},{20,24},{24,28},{1,5},{5,9},{9,... | collective-permute-start | bytes 294920 | tf_op jit(solution)/shard_map/ppermute | solution.py:559
  79.6 1.3 %collective-permute-start.15 = (f32[24,8,128]{2,1,0:T(8,128)S(1)}, f32[24,8,128]{2,1,0:T(8,128)S(1)}, u32[]{:S(2)}, u32[]{:S(2)}) collective-permute-start(f32[24,8,128]{2,1,0:T(8,128)S(1)} %get-tuple-element.46), channel_id=1, source_target_pairs={{4,0},{8,4},{12,8},{16,12},{20,16},{24,20},{28,24},{5,1},{9,5},{13... | collective-permute-start | bytes 294920 | tf_op jit(solution)/shard_map/ppermute | solution.py:559
  81.2 5.6 %collective-permute-done.15.y_high = f32[24,8,128]{2,1,0:T(8,128)S(1)} collective-permute-done((f32[24,8,128]{2,1,0:T(8,128)S(1)}, f32[24,8,128]{2,1,0:T(8,128)S(1)}, u32[]{:S(2)}, u32[]{:S(2)}) %collective-permute-start.15) | collective-permute-done | bytes 98336 | tf_op jit(solution)/shard_map/ppermute | solution.py:559
  86.8 0.6 copy-done.2
  87.4 3.8 %surface.1.demand_ref = f32[8,128]{1,0:T(8,128)S(1)} custom-call(f32[8,16,128]{2,1,0:T(8,128)S(1)} %get-tuple-element.44.own_ref.own_in, f32[8,16,128]{2,1,0:T(8,128)S(1)} %collective-permute-done.12.low_ref.x_low, f32[8,16,128]{2,1,0:T(8,128)S(1)} %collective-permute-done.13.high_ref.x_high, f32[24,8,128]{2,1,0:T(8,128)S(1)} %collective-permute-done.14.y_low, ...), custom_call_target="tpu_custom_call" | custom-call | flops 230000000 | tf_op jit(solution)/shard_map/surface/pallas_call | solution.py:543
  91.5 1.3 %collective-permute-start.11 = (s16[77,16,128]{2,1,0:T(8,128)(2,1)S(1)}, s16[77,16,128]{2,1,0:T(8,128)(2,1)S(1)}, u32[]{:S(2)}, u32[]{:S(2)}) collective-permute-start(s16[77,16,128]{2,1,0:T(8,128)(2,1)S(1)} %get-tuple-element.42), channel_id=1, source_target_pairs={{4,0},{8,4},{12,8},{16,12},{20,16},{24,20},{28,24},{5,1},{9,5},{13... | collective-permute-start | bytes 946184 | tf_op jit(solution)/shard_map/ppermute | solution.py:559
  92.8 4.9 %collective-permute-start.10 = (s16[77,16,128]{2,1,0:T(8,128)(2,1)S(1)}, s16[77,16,128]{2,1,0:T(8,128)(2,1)S(1)}, u32[]{:S(2)}, u32[]{:S(2)}) collective-permute-start(s16[77,16,128]{2,1,0:T(8,128)(2,1)S(1)} %get-tuple-element.41.after_ref), channel_id=1, source_target_pairs={{0,4},{4,8},{8,12},{12,16},{16,20},{20,24},{24,28},{1,5},{5,9},{9,... | collective-permute-start | bytes 946184 | tf_op jit(solution)/shard_map/ppermute | solution.py:559
  97.8 0.8 table.1
  98.6 11.8 %all-to-all-start = ((f32[64,8,128]{2,1,0:T(8,128)}), f32[64,8,128]{2,1,0:T(8,128)S(1)}, u32[]{:S(2)}, u32[]{:S(2)}) async-start(f32[64,8,128]{2,1,0:T(8,128)} %bitcast.3), calls=%async_computation | async-start | bytes 524288 | tf_op jit(solution)/shard_map/all_to_all | solution.py:661
  110.4 6.8 %steps_second.1 = f32[3,8,16,128]{3,2,1,0:T(8,128)} custom-call(f32[3,8,16,128]{3,2,1,0:T(8,128)S(1)} %get-tuple-element.34.refs_2_.refs_0_, f32[3,8,16,128]{3,2,1,0:T(8,128)S(1)} %get-tuple-element.35.refs_3_.refs_1_, f32[8,16,128]{2,1,0:T(8,128)S(1)} %get-tuple-element.37.refs_2_, s16[50,16,128]{2,1,0:T(8,128)(2,1)S(1)} %collective-permute-done.8.refs_4_.refs_3_, ...), custom_call_target="tpu_custom_call" | custom-call | flops 74750001152 | tf_op jit(solution)/shard_map/steps_second/pallas_call | solution.py:543
  117.2 5.2 %all-to-all-done = f32[64,8,128]{2,1,0:T(8,128)S(1)} async-done(((f32[64,8,128]{2,1,0:T(8,128)}), f32[64,8,128]{2,1,0:T(8,128)S(1)}, u32[]{:S(2)}, u32[]{:S(2)}) %all-to-all-start) | async-done | bytes 262176 | tf_op jit(solution)/shard_map/all_to_all | solution.py:661
  122.4 0.7 copy-done.7
  123.1 1.0 fragility.1
  (39 shorter events, 1.6 us)
Async XLA Ops:
  0.6 14.9 %copy-start.4 = (f32[3,8,16,128]{3,2,1,0:T(8,128)S(1)}, f32[3,8,16,128]{3,2,1,0:T(8,128)}, u32[]{:S(2)}) copy-start(f32[3,8,16,128]{3,2,1,0:T(8,128)} %refs_1_.3) | copy-start | bytes 589828
  0.6 14.9 %copy-start.3 = (f32[3,8,16,128]{3,2,1,0:T(8,128)S(1)}, f32[3,8,16,128]{3,2,1,0:T(8,128)}, u32[]{:S(2)}) copy-start(f32[3,8,16,128]{3,2,1,0:T(8,128)} %refs_0_.3) | copy-start | bytes 589828
  3.1 10.7 %collective-permute-start.1 = (f32[8,16,128]{2,1,0:T(8,128)}, f32[8,16,128]{2,1,0:T(8,128)S(1)}, u32[]{:S(2)}, u32[]{:S(2)}) collective-permute-start(f32[8,16,128]{2,1,0:T(8,128)} %get-tuple-element.27), channel_id=1, source_target_pairs={{1,0},{2,1},{3,2},{5,4},{6,5},{7,6},{9,8},{10,9},{11,10},{13,12},{... | collective-permute-start | bytes 196616 | tf_op jit(solution)/shard_map/ppermute | solution.py:559
  11.9 3.6 %collective-permute-start = (f32[8,16,128]{2,1,0:T(8,128)}, f32[8,16,128]{2,1,0:T(8,128)S(1)}, u32[]{:S(2)}, u32[]{:S(2)}) collective-permute-start(f32[8,16,128]{2,1,0:T(8,128)} %get-tuple-element.27), channel_id=1, source_target_pairs={{0,1},{1,2},{2,3},{4,5},{5,6},{6,7},{8,9},{9,10},{10,11},{12,13},{... | collective-permute-start | bytes 196616 | tf_op jit(solution)/shard_map/ppermute | solution.py:559
  15.8 11.9 %collective-permute-start.2 = (s16[62,16,128]{2,1,0:T(8,128)(2,1)S(1)}, s16[62,16,128]{2,1,0:T(8,128)(2,1)S(1)}, u32[]{:S(2)}, u32[]{:S(2)}) collective-permute-start(s16[62,16,128]{2,1,0:T(8,128)(2,1)S(1)} %get-tuple-element.29), channel_id=1, source_target_pairs={{0,32},{32,64},{64,96},{96,128},{128,160},{160,192},{192,224},{224... | collective-permute-start | bytes 761864 | tf_op jit(solution)/shard_map/ppermute | solution.py:559
  17.1 15.3 %collective-permute-start.3 = (s16[62,16,128]{2,1,0:T(8,128)(2,1)S(1)}, s16[62,16,128]{2,1,0:T(8,128)(2,1)S(1)}, u32[]{:S(2)}, u32[]{:S(2)}) collective-permute-start(s16[62,16,128]{2,1,0:T(8,128)(2,1)S(1)} %get-tuple-element.30), channel_id=1, source_target_pairs={{32,0},{64,32},{96,64},{128,96},{160,128},{192,160},{224,192},{256... | collective-permute-start | bytes 761864 | tf_op jit(solution)/shard_map/ppermute | solution.py:559
  32.4 17.2 %copy-start.12 = (bf16[3,256,256]{2,1,0:T(8,128)(2,1)S(1)}, bf16[3,256,256]{2,1,0:T(8,128)(2,1)}, u32[]{:S(2)}) copy-start(bf16[3,256,256]{2,1,0:T(8,128)(2,1)} %constant.4.clone.refs_9_.refs_7_) | copy-start | bytes 1179652
  32.7 12.2 %collective-permute-start.4 = (s16[97,16,128]{2,1,0:T(8,128)(2,1)S(1)}, s16[97,16,128]{2,1,0:T(8,128)(2,1)S(1)}, u32[]{:S(2)}, u32[]{:S(2)}) collective-permute-start(s16[97,16,128]{2,1,0:T(8,128)(2,1)S(1)} %get-tuple-element.32), channel_id=1, source_target_pairs={{0,4},{4,8},{8,12},{12,16},{16,20},{20,24},{24,28},{1,5},{5,9},{9,... | collective-permute-start | bytes 1191944 | tf_op jit(solution)/shard_map/ppermute | solution.py:559
  36.7 12.9 %collective-permute-start.5 = (s16[97,16,128]{2,1,0:T(8,128)(2,1)S(1)}, s16[97,16,128]{2,1,0:T(8,128)(2,1)S(1)}, u32[]{:S(2)}, u32[]{:S(2)}) collective-permute-start(s16[97,16,128]{2,1,0:T(8,128)(2,1)S(1)} %get-tuple-element.33), channel_id=1, source_target_pairs={{4,0},{8,4},{12,8},{16,12},{20,16},{24,20},{28,24},{5,1},{9,5},{13... | collective-permute-start | bytes 1191944 | tf_op jit(solution)/shard_map/ppermute | solution.py:559
  56.3 12.1 %collective-permute-start.7 = (f32[8,16,128]{2,1,0:T(8,128)S(1)}, f32[8,16,128]{2,1,0:T(8,128)S(1)}, u32[]{:S(2)}, u32[]{:S(2)}) collective-permute-start(f32[8,16,128]{2,1,0:T(8,128)S(1)} %get-tuple-element.36), channel_id=1, source_target_pairs={{1,0},{2,1},{3,2},{5,4},{6,5},{7,6},{9,8},{10,9},{11,10},{13,12},{... | collective-permute-start | bytes 196616 | tf_op jit(solution)/shard_map/ppermute | solution.py:559
  59.4 9.0 %collective-permute-start.6 = (f32[8,16,128]{2,1,0:T(8,128)S(1)}, f32[8,16,128]{2,1,0:T(8,128)S(1)}, u32[]{:S(2)}, u32[]{:S(2)}) collective-permute-start(f32[8,16,128]{2,1,0:T(8,128)S(1)} %get-tuple-element.36), channel_id=1, source_target_pairs={{0,1},{1,2},{2,3},{4,5},{5,6},{6,7},{8,9},{9,10},{10,11},{12,13},{... | collective-permute-start | bytes 196616 | tf_op jit(solution)/shard_map/ppermute | solution.py:559
  61.9 13.6 %collective-permute-start.13 = (f32[8,16,128]{2,1,0:T(8,128)S(1)}, f32[8,16,128]{2,1,0:T(8,128)S(1)}, u32[]{:S(2)}, u32[]{:S(2)}) collective-permute-start(f32[8,16,128]{2,1,0:T(8,128)S(1)} %get-tuple-element.44.own_ref.own_in), channel_id=1, source_target_pairs={{32,0},{64,32},{96,64},{128,96},{160,128},{192,160},{224,192},{256... | collective-permute-start | bytes 196616 | tf_op jit(solution)/shard_map/ppermute | solution.py:559
  63.2 12.3 %collective-permute-start.12 = (f32[8,16,128]{2,1,0:T(8,128)S(1)}, f32[8,16,128]{2,1,0:T(8,128)S(1)}, u32[]{:S(2)}, u32[]{:S(2)}) collective-permute-start(f32[8,16,128]{2,1,0:T(8,128)S(1)} %get-tuple-element.44.own_ref.own_in), channel_id=1, source_target_pairs={{0,32},{32,64},{64,96},{96,128},{128,160},{160,192},{192,224},{224... | collective-permute-start | bytes 196616 | tf_op jit(solution)/shard_map/ppermute | solution.py:559
  68.7 22.5 %collective-permute-start.8 = (s16[50,16,128]{2,1,0:T(8,128)(2,1)S(1)}, s16[50,16,128]{2,1,0:T(8,128)(2,1)S(1)}, u32[]{:S(2)}, u32[]{:S(2)}) collective-permute-start(s16[50,16,128]{2,1,0:T(8,128)(2,1)S(1)} %get-tuple-element.38), channel_id=1, source_target_pairs={{0,32},{32,64},{64,96},{96,128},{128,160},{160,192},{192,224},{224... | collective-permute-start | bytes 614408 | tf_op jit(solution)/shard_map/ppermute | solution.py:559
  74.2 17.1 %collective-permute-start.9 = (s16[50,16,128]{2,1,0:T(8,128)(2,1)S(1)}, s16[50,16,128]{2,1,0:T(8,128)(2,1)S(1)}, u32[]{:S(2)}, u32[]{:S(2)}) collective-permute-start(s16[50,16,128]{2,1,0:T(8,128)(2,1)S(1)} %get-tuple-element.39), channel_id=1, source_target_pairs={{32,0},{64,32},{96,64},{128,96},{160,128},{192,160},{224,192},{256... | collective-permute-start | bytes 614408 | tf_op jit(solution)/shard_map/ppermute | solution.py:559
  75.5 11.3 %copy-start = (bf16[256,128]{1,0:T(8,128)(2,1)S(1)}, bf16[256,128]{1,0:T(8,128)(2,1)}, u32[]{:S(2)}) copy-start(bf16[256,128]{1,0:T(8,128)(2,1)} %constant.5.clone.weight_in) | copy-start | bytes 196612
  75.5 11.2 %copy-start.1 = (bf16[64,24]{0,1:T(8,128)(2,1)S(1)}, bf16[64,24]{0,1:T(8,128)(2,1)}, u32[]{:S(2)}) copy-start(bf16[64,24]{0,1:T(8,128)(2,1)} %param.24) | copy-start | bytes 9220
  75.6 5.6 %collective-permute-start.14 = (f32[24,8,128]{2,1,0:T(8,128)S(1)}, f32[24,8,128]{2,1,0:T(8,128)S(1)}, u32[]{:S(2)}, u32[]{:S(2)}) collective-permute-start(f32[24,8,128]{2,1,0:T(8,128)S(1)} %get-tuple-element.45), channel_id=1, source_target_pairs={{0,4},{4,8},{8,12},{12,16},{16,20},{20,24},{24,28},{1,5},{5,9},{9,... | collective-permute-start | bytes 294920 | tf_op jit(solution)/shard_map/ppermute | solution.py:559
  79.6 7.2 %collective-permute-start.15 = (f32[24,8,128]{2,1,0:T(8,128)S(1)}, f32[24,8,128]{2,1,0:T(8,128)S(1)}, u32[]{:S(2)}, u32[]{:S(2)}) collective-permute-start(f32[24,8,128]{2,1,0:T(8,128)S(1)} %get-tuple-element.46), channel_id=1, source_target_pairs={{4,0},{8,4},{12,8},{16,12},{20,16},{24,20},{28,24},{5,1},{9,5},{13... | collective-permute-start | bytes 294920 | tf_op jit(solution)/shard_map/ppermute | solution.py:559
  86.8 0.7 copy-start.2
  91.2 6.5 %copy-start.5 = (s32[16,1,128]{2,1,0:T(1,128)S(1)}, s32[16,1,128]{2,1,0:T(1,128)}, u32[]{:S(2)}) copy-start(s32[16,1,128]{2,1,0:T(1,128)} %param.19) | copy-start | bytes 24580
  91.5 18.8 %collective-permute-start.11 = (s16[77,16,128]{2,1,0:T(8,128)(2,1)S(1)}, s16[77,16,128]{2,1,0:T(8,128)(2,1)S(1)}, u32[]{:S(2)}, u32[]{:S(2)}) collective-permute-start(s16[77,16,128]{2,1,0:T(8,128)(2,1)S(1)} %get-tuple-element.42), channel_id=1, source_target_pairs={{4,0},{8,4},{12,8},{16,12},{20,16},{24,20},{28,24},{5,1},{9,5},{13... | collective-permute-start | bytes 946184 | tf_op jit(solution)/shard_map/ppermute | solution.py:559
  92.8 17.5 %collective-permute-start.10 = (s16[77,16,128]{2,1,0:T(8,128)(2,1)S(1)}, s16[77,16,128]{2,1,0:T(8,128)(2,1)S(1)}, u32[]{:S(2)}, u32[]{:S(2)}) collective-permute-start(s16[77,16,128]{2,1,0:T(8,128)(2,1)S(1)} %get-tuple-element.41.after_ref), channel_id=1, source_target_pairs={{0,4},{4,8},{8,12},{12,16},{16,20},{20,24},{24,28},{1,5},{5,9},{9,... | collective-permute-start | bytes 946184 | tf_op jit(solution)/shard_map/ppermute | solution.py:559
  98.6 23.8 %all-to-all-start = ((f32[64,8,128]{2,1,0:T(8,128)}), f32[64,8,128]{2,1,0:T(8,128)S(1)}, u32[]{:S(2)}, u32[]{:S(2)}) async-start(f32[64,8,128]{2,1,0:T(8,128)} %bitcast.3), calls=%async_computation | async-start | bytes 524288 | tf_op jit(solution)/shard_map/all_to_all | solution.py:661
  110.4 12.0 %copy-start.8 = (s32[1024]{0:T(1024)S(1)}, s32[1024]{0:T(1024)}, u32[]{:S(2)}) copy-start(s32[1024]{0:T(1024)} %param.22) | copy-start | bytes 12292
  110.4 12.0 %copy-start.9 = (f32[16,8]{0,1:T(8,128)S(1)}, f32[16,8]{0,1:T(8,128)}, u32[]{:S(2)}) copy-start(f32[16,8]{0,1:T(8,128)} %param.26) | copy-start | bytes 1540
  110.4 12.0 %copy-start.10 = (f32[16,8]{0,1:T(8,128)S(1)}, f32[16,8]{0,1:T(8,128)}, u32[]{:S(2)}) copy-start(f32[16,8]{0,1:T(8,128)} %param.27) | copy-start | bytes 1540
  122.4 0.7 copy-start.7
  122.4 0.7 copy-start.6
  122.4 0.7 copy-start.11

commit v10 on v9

--- a/solution.py
+++ b/solution.py
@@ -391,7 +391,7 @@
 
 
 def surface_kernel(
-    own_in, x_low, x_high, y_low, y_high, weight_in, code_in, seen_in, filter_in, count_in,
+    own_in, x_low, x_high, y_low, y_high, weight_in, code_in, seen_in, filter_in, count_in, after_in,
     demand_out, state_ref, rate_ref, sample_ref, seen_ref, filter_ref, count_ref,
 ):
     lane = lane_of()
@@ -490,7 +490,7 @@
     demand_out[...] = 0.5 * jnp.log1p(jnp.concatenate(energies, axis=0))
 
 
-def table_kernel(demand_ref, cells_ref, after_ref, table_out):
+def table_kernel(demand_ref, cells_ref, table_out):
     demand = demand_ref[...]
     for owner in range(table_out.shape[0]):
         cells = jnp.broadcast_to(cells_ref[owner : owner + 1, :], (CLASSES, 128))
@@ -534,7 +534,7 @@
 VM = pl.BlockSpec(memory_space=pltpu.VMEM)
 
 
-WEIGHTS = {"start": 1.4, "steps_first": 6.7, "steps_second": 6.5, "slab_message": 4.0, "surface": 0.02, "table": 4.0, "fragility": 1.0}
+WEIGHTS = {"start": 1.4, "steps_first": 6.7, "steps_second": 6.5, "surface": 4.0, "fragility": 1.0}
 UNIT_FLOPS = 1.15e10
 
 
@@ -632,12 +632,15 @@
     halo, powers, x_low, x_high = exchange_x(u, p, faces, ())
     slab_messages = call(slab_message_kernel, "slab_message", [(24, 8, 128)] * 2, [slab, near_low, near_high, powers])
     side_low, side_high = both_ways(*slab_messages, "gy")
+    messages = y_messages(u, p, (), halo, powers, x_low, x_high)
+    received = (halo, x_low, x_high, *both_ways(*messages, "gy"))
     (demand,) = call(
         surface_kernel,
         "surface",
         [(CLASSES, 128)],
         [slab, near_low, near_high, side_low, side_high, jnp.asarray(slab_weights(), jnp.bfloat16), codes, seen]
-        + [modal_filter.T, mode_count.reshape(1, CLASSES)],
+        + [modal_filter.T, mode_count.reshape(1, CLASSES), messages[0]],
+        specs=[VM] * 10 + [pl.BlockSpec(memory_space=pl.ANY)],
         scratch=[
             pltpu.VMEM((2, 24, 48, 128), F32),
             pltpu.VMEM((2, 24, 32, 128), F32),
@@ -647,15 +650,12 @@
             pltpu.VMEM((8, 128), jnp.int32),
         ],
     )
-    messages = y_messages(u, p, (), halo, powers, x_low, x_high)
-    received = (halo, x_low, x_high, *both_ways(*messages, "gy"))
     owners, levels = lax.axis_size("gx"), lax.axis_size("gz")
     (table,) = call(
         table_kernel,
         "table",
         [(owners, levels, CLASSES, 128)],
-        [demand, send_cells.reshape(owners, 128), messages[0]],
-        specs=[VM, VM, pl.BlockSpec(memory_space=pl.ANY)],
+        [demand, send_cells.reshape(owners, 128)],
     )
     table = table.reshape(owners * levels, CLASSES, 128)
     table = lax.all_to_all(table, ("gx", "gz"), split_axis=0, concat_axis=0, tiled=True)

time: 125 us -> 123 us (0.984); the launches traced: 124 us -> 120 us
  waiting for transfers between devices: 38.3 us -> 35.9 us
    ppermute x8, waiting for transfers between devices: 15.1 us -> 13 us  [both_ways(): lax.ppermute(to_down, axis, backward)]
  transfers between devices with their start and end apart: 17 -> 17, of which waited for: 8 -> 7; matrix products, arithmetic and copies ran while one was open for 0% -> 0% of each run, Pallas kernels for 9% -> 10%
where the time goes in v10:
time: 123 us; the launch traced here: 120 us
  starting transfers between devices  59.5 us (48%)
  waiting for transfers between devices  35.9 us (29%)
  Pallas kernels  22.7 us (18%)
  local copies, waits for them, and re-layouts  1.35 us (1%)
    ppermute x8, starting transfers between devices, both_ways(): lax.ppermute(to_up, axis, forward)  29 us
    pallas_call x11, Pallas kernels, call(): pl.pallas_call(kernel, out_shape=out, in_specs=specs or [VM] * len(args),...  22.7 us
    ppermute x8, starting transfers between devices, both_ways(): lax.ppermute(to_down, axis, backward)  19.7 us
    ppermute x8, waiting for transfers between devices, both_ways(): lax.ppermute(to_up, axis, forward)  17.7 us
    ppermute x8, waiting for transfers between devices, both_ways(): lax.ppermute(to_down, axis, backward)  13 us
    all_to_all x1, starting transfers between devices, body(): lax.all_to_all(table, ('gx', 'gz'), split_axis=0, concat_axis=0, tiled=True)  10.9 us
    all_to_all x1, waiting for transfers between devices, body(): lax.all_to_all(table, ('gx', 'gz'), split_axis=0, concat_axis=0, tiled=True)  5.16 us
  transfers between devices with their start and end apart: 17, of which 7 were waited for; matrix products, arithmetic and copies ran while one was open for 0% of the time, Pallas kernels for 10%

profile of v10, /device:TPU:1, one launch (start us, length us, event | category | flops | bytes accessed | tf_op | source)
XLA Modules:
  0.0 120.4 jit_solution(5466455175142921987)
XLA Ops:
  0.7 2.5 %start.1 = (f32[8,16,128]{2,1,0:T(8,128)S(1)}, f32[8,16,128]{2,1,0:T(8,128)S(1)}, f32[8,16,128]{2,1,0:T(8,128)}) custom-call(f32[3,8,16,128]{3,2,1,0:T(8,128)} %refs_0_.3, f32[3,8,16,128]{3,2,1,0:T(8,128)} %refs_1_.3, f32[8,16,128]{2,1,0:T(8,128)} %c_in.1, f32[8,16,128]{2,1,0:T(8,128)} %d_in.1), custom_call_target="tpu_custom_call" | custom-call | flops 16099999744 | tf_op jit(solution)/shard_map/start/pallas_call | solution.py:543
  3.1 8.8 %collective-permute-start.1 = (f32[8,16,128]{2,1,0:T(8,128)}, f32[8,16,128]{2,1,0:T(8,128)S(1)}, u32[]{:S(2)}, u32[]{:S(2)}) collective-permute-start(f32[8,16,128]{2,1,0:T(8,128)} %get-tuple-element.27), channel_id=1, source_target_pairs={{1,0},{2,1},{3,2},{5,4},{6,5},{7,6},{9,8},{10,9},{11,10},{13,12},{... | collective-permute-start | bytes 196616 | tf_op jit(solution)/shard_map/ppermute | solution.py:559
  11.9 1.9 %collective-permute-start = (f32[8,16,128]{2,1,0:T(8,128)}, f32[8,16,128]{2,1,0:T(8,128)S(1)}, u32[]{:S(2)}, u32[]{:S(2)}) collective-permute-start(f32[8,16,128]{2,1,0:T(8,128)} %get-tuple-element.27), channel_id=1, source_target_pairs={{0,1},{1,2},{2,3},{4,5},{5,6},{6,7},{8,9},{9,10},{10,11},{12,13},{... | collective-permute-start | bytes 196616 | tf_op jit(solution)/shard_map/ppermute | solution.py:559
  13.9 1.6 %collective-permute-done.refs_0_ = f32[8,16,128]{2,1,0:T(8,128)S(1)} collective-permute-done((f32[8,16,128]{2,1,0:T(8,128)}, f32[8,16,128]{2,1,0:T(8,128)S(1)}, u32[]{:S(2)}, u32[]{:S(2)}) %collective-permute-start) | collective-permute-done | bytes 65568 | tf_op jit(solution)/shard_map/ppermute | solution.py:559
  15.8 1.3 %collective-permute-start.2 = (s16[62,16,128]{2,1,0:T(8,128)(2,1)S(1)}, s16[62,16,128]{2,1,0:T(8,128)(2,1)S(1)}, u32[]{:S(2)}, u32[]{:S(2)}) collective-permute-start(s16[62,16,128]{2,1,0:T(8,128)(2,1)S(1)} %get-tuple-element.29), channel_id=1, source_target_pairs={{0,32},{32,64},{64,96},{96,128},{128,160},{160,192},{192,224},{224... | collective-permute-start | bytes 761864 | tf_op jit(solution)/shard_map/ppermute | solution.py:559
  17.1 1.3 %collective-permute-start.3 = (s16[62,16,128]{2,1,0:T(8,128)(2,1)S(1)}, s16[62,16,128]{2,1,0:T(8,128)(2,1)S(1)}, u32[]{:S(2)}, u32[]{:S(2)}) collective-permute-start(s16[62,16,128]{2,1,0:T(8,128)(2,1)S(1)} %get-tuple-element.30), channel_id=1, source_target_pairs={{32,0},{64,32},{96,64},{128,96},{160,128},{192,160},{224,192},{256... | collective-permute-start | bytes 761864 | tf_op jit(solution)/shard_map/ppermute | solution.py:559
  18.4 9.3 %collective-permute-done.2.refs_6_.refs_5_ = s16[62,16,128]{2,1,0:T(8,128)(2,1)S(1)} collective-permute-done((s16[62,16,128]{2,1,0:T(8,128)(2,1)S(1)}, s16[62,16,128]{2,1,0:T(8,128)(2,1)S(1)}, u32[]{:S(2)}, u32[]{:S(2)}) %collective-permute-start.2) | collective-permute-done | bytes 253984 | tf_op jit(solution)/shard_map/ppermute | solution.py:559
  27.7 4.7 %collective-permute-done.3.refs_7_.refs_6_ = s16[62,16,128]{2,1,0:T(8,128)(2,1)S(1)} collective-permute-done((s16[62,16,128]{2,1,0:T(8,128)(2,1)S(1)}, s16[62,16,128]{2,1,0:T(8,128)(2,1)S(1)}, u32[]{:S(2)}, u32[]{:S(2)}) %collective-permute-start.3) | collective-permute-done | bytes 253984 | tf_op jit(solution)/shard_map/ppermute | solution.py:559
  32.7 4.0 %collective-permute-start.4 = (s16[97,16,128]{2,1,0:T(8,128)(2,1)S(1)}, s16[97,16,128]{2,1,0:T(8,128)(2,1)S(1)}, u32[]{:S(2)}, u32[]{:S(2)}) collective-permute-start(s16[97,16,128]{2,1,0:T(8,128)(2,1)S(1)} %get-tuple-element.32), channel_id=1, source_target_pairs={{0,4},{4,8},{8,12},{12,16},{16,20},{20,24},{24,28},{1,5},{5,9},{9,... | collective-permute-start | bytes 1191944 | tf_op jit(solution)/shard_map/ppermute | solution.py:559
  36.7 1.3 %collective-permute-start.5 = (s16[97,16,128]{2,1,0:T(8,128)(2,1)S(1)}, s16[97,16,128]{2,1,0:T(8,128)(2,1)S(1)}, u32[]{:S(2)}, u32[]{:S(2)}) collective-permute-start(s16[97,16,128]{2,1,0:T(8,128)(2,1)S(1)} %get-tuple-element.33), channel_id=1, source_target_pairs={{4,0},{8,4},{12,8},{16,12},{20,16},{24,20},{28,24},{5,1},{9,5},{13... | collective-permute-start | bytes 1191944 | tf_op jit(solution)/shard_map/ppermute | solution.py:559
  38.0 6.8 %collective-permute-done.4.refs_7_ = s16[97,16,128]{2,1,0:T(8,128)(2,1)S(1)} collective-permute-done((s16[97,16,128]{2,1,0:T(8,128)(2,1)S(1)}, s16[97,16,128]{2,1,0:T(8,128)(2,1)S(1)}, u32[]{:S(2)}, u32[]{:S(2)}) %collective-permute-start.4) | collective-permute-done | bytes 397344 | tf_op jit(solution)/shard_map/ppermute | solution.py:559
  44.8 4.8 %collective-permute-done.5.refs_8_ = s16[97,16,128]{2,1,0:T(8,128)(2,1)S(1)} collective-permute-done((s16[97,16,128]{2,1,0:T(8,128)(2,1)S(1)}, s16[97,16,128]{2,1,0:T(8,128)(2,1)S(1)}, u32[]{:S(2)}, u32[]{:S(2)}) %collective-permute-start.5) | collective-permute-done | bytes 397344 | tf_op jit(solution)/shard_map/ppermute | solution.py:559
  49.6 6.7 %steps_first.1 = (f32[3,8,16,128]{3,2,1,0:T(8,128)S(1)}, f32[3,8,16,128]{3,2,1,0:T(8,128)S(1)}, f32[8,16,128]{2,1,0:T(8,128)S(1)}, f32[8,16,128]{2,1,0:T(8,128)S...) custom-call(f32[3,8,16,128]{3,2,1,0:T(8,128)S(1)} %copy-done, f32[3,8,16,128]{3,2,1,0:T(8,128)S(1)} %copy-done.1, ...), custom_call_target="tpu_custom_call" | custom-call | flops 77050003456 | tf_op jit(solution)/shard_map/steps_first/pallas_call | solution.py:543
  56.3 3.1 %collective-permute-start.7 = (f32[8,16,128]{2,1,0:T(8,128)S(1)}, f32[8,16,128]{2,1,0:T(8,128)S(1)}, u32[]{:S(2)}, u32[]{:S(2)}) collective-permute-start(f32[8,16,128]{2,1,0:T(8,128)S(1)} %get-tuple-element.36), channel_id=1, source_target_pairs={{1,0},{2,1},{3,2},{5,4},{6,5},{7,6},{9,8},{10,9},{11,10},{13,12},{... | collective-permute-start | bytes 196616 | tf_op jit(solution)/shard_map/ppermute | solution.py:559
  59.4 2.4 %collective-permute-start.6 = (f32[8,16,128]{2,1,0:T(8,128)S(1)}, f32[8,16,128]{2,1,0:T(8,128)S(1)}, u32[]{:S(2)}, u32[]{:S(2)}) collective-permute-start(f32[8,16,128]{2,1,0:T(8,128)S(1)} %get-tuple-element.36), channel_id=1, source_target_pairs={{0,1},{1,2},{2,3},{4,5},{5,6},{6,7},{8,9},{9,10},{10,11},{12,13},{... | collective-permute-start | bytes 196616 | tf_op jit(solution)/shard_map/ppermute | solution.py:559
  61.9 1.3 %collective-permute-start.13 = (f32[8,16,128]{2,1,0:T(8,128)S(1)}, f32[8,16,128]{2,1,0:T(8,128)S(1)}, u32[]{:S(2)}, u32[]{:S(2)}) collective-permute-start(f32[8,16,128]{2,1,0:T(8,128)S(1)} %get-tuple-element.44.own_ref.own_in), channel_id=1, source_target_pairs={{32,0},{64,32},{96,64},{128,96},{160,128},{192,160},{224,192},{256... | collective-permute-start | bytes 196616 | tf_op jit(solution)/shard_map/ppermute | solution.py:559
  63.2 5.2 %collective-permute-start.12 = (f32[8,16,128]{2,1,0:T(8,128)S(1)}, f32[8,16,128]{2,1,0:T(8,128)S(1)}, u32[]{:S(2)}, u32[]{:S(2)}) collective-permute-start(f32[8,16,128]{2,1,0:T(8,128)S(1)} %get-tuple-element.44.own_ref.own_in), channel_id=1, source_target_pairs={{0,32},{32,64},{64,96},{96,128},{128,160},{160,192},{192,224},{224... | collective-permute-start | bytes 196616 | tf_op jit(solution)/shard_map/ppermute | solution.py:559
  68.7 5.5 %collective-permute-start.8 = (s16[50,16,128]{2,1,0:T(8,128)(2,1)S(1)}, s16[50,16,128]{2,1,0:T(8,128)(2,1)S(1)}, u32[]{:S(2)}, u32[]{:S(2)}) collective-permute-start(s16[50,16,128]{2,1,0:T(8,128)(2,1)S(1)} %get-tuple-element.38), channel_id=1, source_target_pairs={{0,32},{32,64},{64,96},{96,128},{128,160},{160,192},{192,224},{224... | collective-permute-start | bytes 614408 | tf_op jit(solution)/shard_map/ppermute | solution.py:559
  74.2 1.3 %collective-permute-start.9 = (s16[50,16,128]{2,1,0:T(8,128)(2,1)S(1)}, s16[50,16,128]{2,1,0:T(8,128)(2,1)S(1)}, u32[]{:S(2)}, u32[]{:S(2)}) collective-permute-start(s16[50,16,128]{2,1,0:T(8,128)(2,1)S(1)} %get-tuple-element.39), channel_id=1, source_target_pairs={{32,0},{64,32},{96,64},{128,96},{160,128},{192,160},{224,192},{256... | collective-permute-start | bytes 614408 | tf_op jit(solution)/shard_map/ppermute | solution.py:559
  75.5 4.0 %collective-permute-start.14 = (f32[24,8,128]{2,1,0:T(8,128)S(1)}, f32[24,8,128]{2,1,0:T(8,128)S(1)}, u32[]{:S(2)}, u32[]{:S(2)}) collective-permute-start(f32[24,8,128]{2,1,0:T(8,128)S(1)} %get-tuple-element.45), channel_id=1, source_target_pairs={{0,4},{4,8},{8,12},{12,16},{16,20},{20,24},{24,28},{1,5},{5,9},{9,... | collective-permute-start | bytes 294920 | tf_op jit(solution)/shard_map/ppermute | solution.py:559
  79.5 1.3 %collective-permute-start.15 = (f32[24,8,128]{2,1,0:T(8,128)S(1)}, f32[24,8,128]{2,1,0:T(8,128)S(1)}, u32[]{:S(2)}, u32[]{:S(2)}) collective-permute-start(f32[24,8,128]{2,1,0:T(8,128)S(1)} %get-tuple-element.46), channel_id=1, source_target_pairs={{4,0},{8,4},{12,8},{16,12},{20,16},{24,20},{28,24},{5,1},{9,5},{13... | collective-permute-start | bytes 294920 | tf_op jit(solution)/shard_map/ppermute | solution.py:559
  80.8 3.5 %collective-permute-done.9.refs_5_.refs_4_ = s16[50,16,128]{2,1,0:T(8,128)(2,1)S(1)} collective-permute-done((s16[50,16,128]{2,1,0:T(8,128)(2,1)S(1)}, s16[50,16,128]{2,1,0:T(8,128)(2,1)S(1)}, u32[]{:S(2)}, u32[]{:S(2)}) %collective-permute-start.9) | collective-permute-done | bytes 204832 | tf_op jit(solution)/shard_map/ppermute | solution.py:559
  84.7 1.3 %collective-permute-start.11 = (s16[77,16,128]{2,1,0:T(8,128)(2,1)S(1)}, s16[77,16,128]{2,1,0:T(8,128)(2,1)S(1)}, u32[]{:S(2)}, u32[]{:S(2)}) collective-permute-start(s16[77,16,128]{2,1,0:T(8,128)(2,1)S(1)} %get-tuple-element.42), channel_id=1, source_target_pairs={{4,0},{8,4},{12,8},{16,12},{20,16},{24,20},{28,24},{5,1},{9,5},{13... | collective-permute-start | bytes 946184 | tf_op jit(solution)/shard_map/ppermute | solution.py:559
  86.0 4.6 %collective-permute-start.10 = (s16[77,16,128]{2,1,0:T(8,128)(2,1)S(1)}, s16[77,16,128]{2,1,0:T(8,128)(2,1)S(1)}, u32[]{:S(2)}, u32[]{:S(2)}) collective-permute-start(s16[77,16,128]{2,1,0:T(8,128)(2,1)S(1)} %get-tuple-element.41.after_in), channel_id=1, source_target_pairs={{0,4},{4,8},{8,12},{12,16},{16,20},{20,24},{24,28},{1,5},{5,9},{9,... | collective-permute-start | bytes 946184 | tf_op jit(solution)/shard_map/ppermute | solution.py:559
  90.7 0.6 copy-done.9
  91.3 3.8 %surface.1.demand_ref = f32[8,128]{1,0:T(8,128)S(1)} custom-call(f32[8,16,128]{2,1,0:T(8,128)S(1)} %get-tuple-element.44.own_ref.own_in, f32[8,16,128]{2,1,0:T(8,128)S(1)} %collective-permute-done.12.low_ref.x_low, f32[8,16,128]{2,1,0:T(8,128)S(1)} %collective-permute-done.13.high_ref.x_high, f32[24,8,128]{2,1,0:T(8,128)S(1)} %collective-permute-done.14.y_low, ...), custom_call_target="tpu_custom_call" | custom-call | flops 46000001024 | tf_op jit(solution)/shard_map/surface/pallas_call | solution.py:543
  95.1 0.8 table.1
  95.9 10.9 %all-to-all-start = ((f32[64,8,128]{2,1,0:T(8,128)}), f32[64,8,128]{2,1,0:T(8,128)S(1)}, u32[]{:S(2)}, u32[]{:S(2)}) async-start(f32[64,8,128]{2,1,0:T(8,128)} %bitcast.3), calls=%async_computation | async-start | bytes 524288 | tf_op jit(solution)/shard_map/all_to_all | solution.py:661
  106.8 6.8 %steps_second.1 = f32[3,8,16,128]{3,2,1,0:T(8,128)} custom-call(f32[3,8,16,128]{3,2,1,0:T(8,128)S(1)} %get-tuple-element.34.refs_2_.refs_0_, f32[3,8,16,128]{3,2,1,0:T(8,128)S(1)} %get-tuple-element.35.refs_3_.refs_1_, f32[8,16,128]{2,1,0:T(8,128)S(1)} %get-tuple-element.37.refs_2_, s16[50,16,128]{2,1,0:T(8,128)(2,1)S(1)} %collective-permute-done.8.refs_4_.refs_3_, ...), custom_call_target="tpu_custom_call" | custom-call | flops 74750001152 | tf_op jit(solution)/shard_map/steps_second/pallas_call | solution.py:543
  113.6 5.2 %all-to-all-done = f32[64,8,128]{2,1,0:T(8,128)S(1)} async-done(((f32[64,8,128]{2,1,0:T(8,128)}), f32[64,8,128]{2,1,0:T(8,128)S(1)}, u32[]{:S(2)}, u32[]{:S(2)}) %all-to-all-start) | async-done | bytes 262176 | tf_op jit(solution)/shard_map/all_to_all | solution.py:661
  118.8 0.7 copy-done.5
  119.5 1.0 fragility.1
  (39 shorter events, 1.3 us)
Async XLA Ops:
  0.6 14.9 %copy-start.1 = (f32[3,8,16,128]{3,2,1,0:T(8,128)S(1)}, f32[3,8,16,128]{3,2,1,0:T(8,128)}, u32[]{:S(2)}) copy-start(f32[3,8,16,128]{3,2,1,0:T(8,128)} %refs_1_.3) | copy-start | bytes 589828
  0.6 14.9 %copy-start = (f32[3,8,16,128]{3,2,1,0:T(8,128)S(1)}, f32[3,8,16,128]{3,2,1,0:T(8,128)}, u32[]{:S(2)}) copy-start(f32[3,8,16,128]{3,2,1,0:T(8,128)} %refs_0_.3) | copy-start | bytes 589828
  3.1 10.7 %collective-permute-start.1 = (f32[8,16,128]{2,1,0:T(8,128)}, f32[8,16,128]{2,1,0:T(8,128)S(1)}, u32[]{:S(2)}, u32[]{:S(2)}) collective-permute-start(f32[8,16,128]{2,1,0:T(8,128)} %get-tuple-element.27), channel_id=1, source_target_pairs={{1,0},{2,1},{3,2},{5,4},{6,5},{7,6},{9,8},{10,9},{11,10},{13,12},{... | collective-permute-start | bytes 196616 | tf_op jit(solution)/shard_map/ppermute | solution.py:559
  11.9 3.6 %collective-permute-start = (f32[8,16,128]{2,1,0:T(8,128)}, f32[8,16,128]{2,1,0:T(8,128)S(1)}, u32[]{:S(2)}, u32[]{:S(2)}) collective-permute-start(f32[8,16,128]{2,1,0:T(8,128)} %get-tuple-element.27), channel_id=1, source_target_pairs={{0,1},{1,2},{2,3},{4,5},{5,6},{6,7},{8,9},{9,10},{10,11},{12,13},{... | collective-permute-start | bytes 196616 | tf_op jit(solution)/shard_map/ppermute | solution.py:559
  15.8 11.9 %collective-permute-start.2 = (s16[62,16,128]{2,1,0:T(8,128)(2,1)S(1)}, s16[62,16,128]{2,1,0:T(8,128)(2,1)S(1)}, u32[]{:S(2)}, u32[]{:S(2)}) collective-permute-start(s16[62,16,128]{2,1,0:T(8,128)(2,1)S(1)} %get-tuple-element.29), channel_id=1, source_target_pairs={{0,32},{32,64},{64,96},{96,128},{128,160},{160,192},{192,224},{224... | collective-permute-start | bytes 761864 | tf_op jit(solution)/shard_map/ppermute | solution.py:559
  17.1 15.3 %collective-permute-start.3 = (s16[62,16,128]{2,1,0:T(8,128)(2,1)S(1)}, s16[62,16,128]{2,1,0:T(8,128)(2,1)S(1)}, u32[]{:S(2)}, u32[]{:S(2)}) collective-permute-start(s16[62,16,128]{2,1,0:T(8,128)(2,1)S(1)} %get-tuple-element.30), channel_id=1, source_target_pairs={{32,0},{64,32},{96,64},{128,96},{160,128},{192,160},{224,192},{256... | collective-permute-start | bytes 761864 | tf_op jit(solution)/shard_map/ppermute | solution.py:559
  32.4 17.2 %copy-start.11 = (bf16[3,256,256]{2,1,0:T(8,128)(2,1)S(1)}, bf16[3,256,256]{2,1,0:T(8,128)(2,1)}, u32[]{:S(2)}) copy-start(bf16[3,256,256]{2,1,0:T(8,128)(2,1)} %constant.4.clone.refs_9_.refs_7_) | copy-start | bytes 1179652
  32.7 12.2 %collective-permute-start.4 = (s16[97,16,128]{2,1,0:T(8,128)(2,1)S(1)}, s16[97,16,128]{2,1,0:T(8,128)(2,1)S(1)}, u32[]{:S(2)}, u32[]{:S(2)}) collective-permute-start(s16[97,16,128]{2,1,0:T(8,128)(2,1)S(1)} %get-tuple-element.32), channel_id=1, source_target_pairs={{0,4},{4,8},{8,12},{12,16},{16,20},{20,24},{24,28},{1,5},{5,9},{9,... | collective-permute-start | bytes 1191944 | tf_op jit(solution)/shard_map/ppermute | solution.py:559
  36.7 12.9 %collective-permute-start.5 = (s16[97,16,128]{2,1,0:T(8,128)(2,1)S(1)}, s16[97,16,128]{2,1,0:T(8,128)(2,1)S(1)}, u32[]{:S(2)}, u32[]{:S(2)}) collective-permute-start(s16[97,16,128]{2,1,0:T(8,128)(2,1)S(1)} %get-tuple-element.33), channel_id=1, source_target_pairs={{4,0},{8,4},{12,8},{16,12},{20,16},{24,20},{28,24},{5,1},{9,5},{13... | collective-permute-start | bytes 1191944 | tf_op jit(solution)/shard_map/ppermute | solution.py:559
  56.3 12.1 %collective-permute-start.7 = (f32[8,16,128]{2,1,0:T(8,128)S(1)}, f32[8,16,128]{2,1,0:T(8,128)S(1)}, u32[]{:S(2)}, u32[]{:S(2)}) collective-permute-start(f32[8,16,128]{2,1,0:T(8,128)S(1)} %get-tuple-element.36), channel_id=1, source_target_pairs={{1,0},{2,1},{3,2},{5,4},{6,5},{7,6},{9,8},{10,9},{11,10},{13,12},{... | collective-permute-start | bytes 196616 | tf_op jit(solution)/shard_map/ppermute | solution.py:559
  59.4 9.0 %collective-permute-start.6 = (f32[8,16,128]{2,1,0:T(8,128)S(1)}, f32[8,16,128]{2,1,0:T(8,128)S(1)}, u32[]{:S(2)}, u32[]{:S(2)}) collective-permute-start(f32[8,16,128]{2,1,0:T(8,128)S(1)} %get-tuple-element.36), channel_id=1, source_target_pairs={{0,1},{1,2},{2,3},{4,5},{5,6},{6,7},{8,9},{9,10},{10,11},{12,13},{... | collective-permute-start | bytes 196616 | tf_op jit(solution)/shard_map/ppermute | solution.py:559
  61.9 13.6 %collective-permute-start.13 = (f32[8,16,128]{2,1,0:T(8,128)S(1)}, f32[8,16,128]{2,1,0:T(8,128)S(1)}, u32[]{:S(2)}, u32[]{:S(2)}) collective-permute-start(f32[8,16,128]{2,1,0:T(8,128)S(1)} %get-tuple-element.44.own_ref.own_in), channel_id=1, source_target_pairs={{32,0},{64,32},{96,64},{128,96},{160,128},{192,160},{224,192},{256... | collective-permute-start | bytes 196616 | tf_op jit(solution)/shard_map/ppermute | solution.py:559
  63.2 12.3 %collective-permute-start.12 = (f32[8,16,128]{2,1,0:T(8,128)S(1)}, f32[8,16,128]{2,1,0:T(8,128)S(1)}, u32[]{:S(2)}, u32[]{:S(2)}) collective-permute-start(f32[8,16,128]{2,1,0:T(8,128)S(1)} %get-tuple-element.44.own_ref.own_in), channel_id=1, source_target_pairs={{0,32},{32,64},{64,96},{96,128},{128,160},{160,192},{192,224},{224... | collective-permute-start | bytes 196616 | tf_op jit(solution)/shard_map/ppermute | solution.py:559
  68.7 12.2 %collective-permute-start.8 = (s16[50,16,128]{2,1,0:T(8,128)(2,1)S(1)}, s16[50,16,128]{2,1,0:T(8,128)(2,1)S(1)}, u32[]{:S(2)}, u32[]{:S(2)}) collective-permute-start(s16[50,16,128]{2,1,0:T(8,128)(2,1)S(1)} %get-tuple-element.38), channel_id=1, source_target_pairs={{0,32},{32,64},{64,96},{96,128},{128,160},{160,192},{192,224},{224... | collective-permute-start | bytes 614408 | tf_op jit(solution)/shard_map/ppermute | solution.py:559
  74.2 10.2 %collective-permute-start.9 = (s16[50,16,128]{2,1,0:T(8,128)(2,1)S(1)}, s16[50,16,128]{2,1,0:T(8,128)(2,1)S(1)}, u32[]{:S(2)}, u32[]{:S(2)}) collective-permute-start(s16[50,16,128]{2,1,0:T(8,128)(2,1)S(1)} %get-tuple-element.39), channel_id=1, source_target_pairs={{32,0},{64,32},{96,64},{128,96},{160,128},{192,160},{224,192},{256... | collective-permute-start | bytes 614408 | tf_op jit(solution)/shard_map/ppermute | solution.py:559
  75.5 15.1 %collective-permute-start.14 = (f32[24,8,128]{2,1,0:T(8,128)S(1)}, f32[24,8,128]{2,1,0:T(8,128)S(1)}, u32[]{:S(2)}, u32[]{:S(2)}) collective-permute-start(f32[24,8,128]{2,1,0:T(8,128)S(1)} %get-tuple-element.45), channel_id=1, source_target_pairs={{0,4},{4,8},{8,12},{12,16},{16,20},{20,24},{24,28},{1,5},{5,9},{9,... | collective-permute-start | bytes 294920 | tf_op jit(solution)/shard_map/ppermute | solution.py:559
  79.5 11.1 %collective-permute-start.15 = (f32[24,8,128]{2,1,0:T(8,128)S(1)}, f32[24,8,128]{2,1,0:T(8,128)S(1)}, u32[]{:S(2)}, u32[]{:S(2)}) collective-permute-start(f32[24,8,128]{2,1,0:T(8,128)S(1)} %get-tuple-element.46), channel_id=1, source_target_pairs={{4,0},{8,4},{12,8},{16,12},{20,16},{24,20},{28,24},{5,1},{9,5},{13... | collective-permute-start | bytes 294920 | tf_op jit(solution)/shard_map/ppermute | solution.py:559
  84.4 6.3 %copy-start.12 = (bf16[256,128]{1,0:T(8,128)(2,1)S(1)}, bf16[256,128]{1,0:T(8,128)(2,1)}, u32[]{:S(2)}) copy-start(bf16[256,128]{1,0:T(8,128)(2,1)} %constant.5.clone.weight_in) | copy-start | bytes 196612
  84.7 6.0 %copy-start.3 = (bf16[64,24]{0,1:T(8,128)(2,1)S(1)}, bf16[64,24]{0,1:T(8,128)(2,1)}, u32[]{:S(2)}) copy-start(bf16[64,24]{0,1:T(8,128)(2,1)} %param.24) | copy-start | bytes 9220
  84.7 22.1 %collective-permute-start.11 = (s16[77,16,128]{2,1,0:T(8,128)(2,1)S(1)}, s16[77,16,128]{2,1,0:T(8,128)(2,1)S(1)}, u32[]{:S(2)}, u32[]{:S(2)}) collective-permute-start(s16[77,16,128]{2,1,0:T(8,128)(2,1)S(1)} %get-tuple-element.42), channel_id=1, source_target_pairs={{4,0},{8,4},{12,8},{16,12},{20,16},{24,20},{28,24},{5,1},{9,5},{13... | collective-permute-start | bytes 946184 | tf_op jit(solution)/shard_map/ppermute | solution.py:559
  86.0 20.8 %collective-permute-start.10 = (s16[77,16,128]{2,1,0:T(8,128)(2,1)S(1)}, s16[77,16,128]{2,1,0:T(8,128)(2,1)S(1)}, u32[]{:S(2)}, u32[]{:S(2)}) collective-permute-start(s16[77,16,128]{2,1,0:T(8,128)(2,1)S(1)} %get-tuple-element.41.after_in), channel_id=1, source_target_pairs={{0,4},{4,8},{8,12},{12,16},{16,20},{20,24},{24,28},{1,5},{5,9},{9,... | collective-permute-start | bytes 946184 | tf_op jit(solution)/shard_map/ppermute | solution.py:559
  90.6 0.7 copy-start.9
  91.3 3.8 %copy-start.2 = (s32[16,1,128]{2,1,0:T(1,128)S(1)}, s32[16,1,128]{2,1,0:T(1,128)}, u32[]{:S(2)}) copy-start(s32[16,1,128]{2,1,0:T(1,128)} %param.19) | copy-start | bytes 24580
  95.9 22.9 %all-to-all-start = ((f32[64,8,128]{2,1,0:T(8,128)}), f32[64,8,128]{2,1,0:T(8,128)S(1)}, u32[]{:S(2)}, u32[]{:S(2)}) async-start(f32[64,8,128]{2,1,0:T(8,128)} %bitcast.3), calls=%async_computation | async-start | bytes 524288 | tf_op jit(solution)/shard_map/all_to_all | solution.py:661
  106.8 12.0 %copy-start.6 = (s32[1024]{0:T(1024)S(1)}, s32[1024]{0:T(1024)}, u32[]{:S(2)}) copy-start(s32[1024]{0:T(1024)} %param.22) | copy-start | bytes 12292
  106.8 12.0 %copy-start.7 = (f32[16,8]{0,1:T(8,128)S(1)}, f32[16,8]{0,1:T(8,128)}, u32[]{:S(2)}) copy-start(f32[16,8]{0,1:T(8,128)} %param.26) | copy-start | bytes 1540
  106.8 12.0 %copy-start.8 = (f32[16,8]{0,1:T(8,128)S(1)}, f32[16,8]{0,1:T(8,128)}, u32[]{:S(2)}) copy-start(f32[16,8]{0,1:T(8,128)} %param.27) | copy-start | bytes 1540
  118.8 0.7 copy-start.5
  118.8 0.7 copy-start.4
  118.8 0.7 copy-start.10

commit v11 on v10

--- a/solution.py
+++ b/solution.py
@@ -118,17 +118,18 @@
 
 def x_message_kernel(coefficients, *refs):
     if coefficients:
-        z_low_ref, z_high_ref, u_ref, p_ref, a_ref, e_ref, halo_ref, up_ref, down_ref, power_ref = refs
+        z_second_ref, z_first_ref, u_ref, p_ref, a_ref, e_ref, halo_ref, up_ref, down_ref, power_ref = refs
     else:
-        z_low_ref, z_high_ref, u_ref, p_ref, halo_ref, up_ref, down_ref, power_ref = refs
+        z_second_ref, z_first_ref, u_ref, p_ref, halo_ref, up_ref, down_ref, power_ref = refs
     inner = lax.broadcasted_iota(jnp.int32, (16, 128), 1) % 16
+    from_first = (inner < 8) == is_odd("gz")
 
     def largest(x, carry):
         field, face = carry
         for k in range(3):
             both = jnp.maximum(jnp.abs(u_ref[k, x]), jnp.abs(p_ref[k, x]))
             field = jnp.maximum(field, jnp.maximum(both[0:8], both[8:16]))
-        halo = jnp.where(inner < 8, z_low_ref[x], z_high_ref[x])
+        halo = jnp.where(from_first, z_first_ref[x], z_second_ref[x])
         halo_ref[x] = halo
         halo = jnp.abs(halo)
         return field, jnp.maximum(face, jnp.maximum(halo[0:8], halo[8:16]))
@@ -172,14 +173,15 @@
 
 def y_message_kernel(coefficients, *refs):
     if coefficients:
-        u_ref, p_ref, a_ref, e_ref, halo_ref, power_ref, low_ref, high_ref, up_ref, down_ref = refs
+        u_ref, p_ref, a_ref, e_ref, halo_ref, power_ref, low_ref, high_ref, first_ref, second_ref = refs
     else:
-        u_ref, p_ref, halo_ref, power_ref, low_ref, high_ref, up_ref, down_ref = refs
+        u_ref, p_ref, halo_ref, power_ref, low_ref, high_ref, first_ref, second_ref = refs
+    odd = is_odd("gy")
     powers = power_ref[...]
     low_powers = jnp.concatenate(sent_exponents(low_ref), axis=0)
     high_powers = jnp.concatenate(sent_exponents(high_ref), axis=0)
     most = jnp.maximum(powers, jnp.maximum(low_powers, high_powers))
-    for out_ref in (up_ref, down_ref):
+    for out_ref in (first_ref, second_ref):
         out_ref[out_ref.shape[0] - 1] = coded(most + BIAS)
     own_scale = FULL * jnp.exp2(-most)
     low_scale = jnp.exp2(low_powers - most)
@@ -188,8 +190,10 @@
     face = [twice(scale[8:16]) for scale in (own_scale, low_scale, high_scale)]
 
     def put(at, pair):
-        up_ref[at] = coded(jnp.concatenate([pair[0][8:16], pair[1][8:16]], axis=0))
-        down_ref[at] = coded(jnp.concatenate([pair[0][0:8], pair[1][0:8]], axis=0))
+        up = jnp.concatenate([pair[0][8:16], pair[1][8:16]], axis=0)
+        down = jnp.concatenate([pair[0][0:8], pair[1][0:8]], axis=0)
+        first_ref[at] = coded(jnp.where(odd, down, up))
+        second_ref[at] = coded(jnp.where(odd, up, down))
 
     def group(parts, x_planes, y_planes, x_at, y_at):
         side = (y_planes - 8) // 4
@@ -221,9 +225,10 @@
     group([(halo_ref, face)], XH, YH, x_at, y_at)
 
 
-def fill(parts, x_low, x_high, y_low, y_high, x_at, x_planes, y_at, y_planes):
+def fill(parts, x_low, x_high, y_first, y_second, x_at, x_planes, y_at, y_planes):
     count = len(parts)
     side = (y_planes - 8) // 2
+    odd = is_odd("gy")
 
     def own(i, carry):
         for target, row, block, _ in parts:
@@ -240,8 +245,9 @@
     def y_side(i, carry):
         for at, (target, row, _, units) in enumerate(parts):
             here = y_at + at * y_planes // 2 + i
-            low = decoded(y_low[here]) * units[2]
-            high = decoded(y_high[here]) * units[3]
+            first, second = decoded(y_first[here]), decoded(y_second[here])
+            low = jnp.where(odd, first, second) * units[2]
+            high = jnp.where(odd, second, first) * units[3]
             for j in (0, 1):
                 target[8 - side + 2 * i + j, row : row + 8, :] = low[8 * j : 8 * j + 8]
                 target[8 - side + 2 * i + j, row + 24 : row + 32, :] = high[8 * j : 8 * j + 8]
@@ -255,18 +261,22 @@
 
 def steps_kernel(first, *refs):
     if first:
-        (u_in, p_in, a_in, e_in, halo_in, x_low, x_high, y_low, y_high, weight_in) = refs[:10]
+        (u_in, p_in, a_in, e_in, halo_in, x_low, x_high, y_first, y_second, weight_in) = refs[:10]
         (u_out, p_out, face_out, slab_out, seen_out, code_ref) = refs[10:16]
         state_ref, rate_ref, edge_ref = refs[16:]
     else:
-        (u_in, p_in, halo_in, x_low, x_high, y_low, y_high, weight_in, code_ref) = refs[:9]
+        (u_in, p_in, halo_in, x_low, x_high, y_second, y_first, weight_in, code_ref) = refs[:9]
         u_out, state_ref, rate_ref = refs[9:]
     a_ref, e_ref, ha_ref, he_ref = (rate_ref.at[at] for at in range(4))
     lane = lane_of()
     inner = lane % 16
 
-    sides = (x_low, x_high, y_low, y_high)
+    sides = (x_low, x_high, y_first, y_second)
     powers = [sent_exponents(message) for message in sides]
+    odd = is_odd("gy")
+    swapped = list(zip(powers[2], powers[3]))
+    powers[2] = [jnp.where(odd, one, other) for one, other in swapped]
+    powers[3] = [jnp.where(odd, other, one) for one, other in swapped]
     field = [twice(jnp.exp2(power[0]) * (1.0 / FULL)) for power in powers]
     face = [twice(jnp.exp2(power[1]) * (1.0 / FULL)) for power in powers]
     x_at, y_at = fill([(state_ref.at[0, k], 8, u_in.at[k], field) for k in range(3)], *sides, 0, XU, 0, YU)
@@ -559,16 +569,27 @@
     return lax.ppermute(to_up, axis, forward), lax.ppermute(to_down, axis, backward)
 
 
+def swaps(first, second, axis):
+    count = lax.axis_size(axis)
+    pairs = [[(i, i + 1) for i in range(begin, count - 1, 2)] for begin in (0, 1)]
+    pairs = [ways + [(b, a) for a, b in ways] for ways in pairs]
+    return lax.ppermute(first, axis, pairs[0]), lax.ppermute(second, axis, pairs[1])
+
+
+def is_odd(axis):
+    return lax.rem(lax.axis_index(axis), 2) == 1
+
+
 def exchange_x(u, p, faces, coefficients):
     extra = list(coefficients)
-    z_low, z_high = both_ways(faces, faces, "gz")
+    z_first, z_second = swaps(faces, faces, "gz")
     planes = 3 * XU + (3 + len(extra)) * XP + XH + 1
     message = jax.ShapeDtypeStruct((planes, 16, 128), jnp.int16)
     halo, up, down, powers = call(
         functools.partial(x_message_kernel, bool(extra)),
         "x_message",
         [(8, 16, 128), message, message, (16, 128)],
-        [z_low, z_high, u, p] + extra,
+        [z_second, z_first, u, p] + extra,
     )
     return halo, powers, *both_ways(up, down, "gx")
 
@@ -618,7 +639,7 @@
     )
     halo, powers, x_low, x_high = exchange_x(u, p, faces, (a, e))
     messages = y_messages(u, p, (a, e), halo, powers, x_low, x_high)
-    received = (halo, x_low, x_high, *both_ways(*messages, "gy"))
+    received = (halo, x_low, x_high, *swaps(*messages, "gy"))
     weights = jnp.asarray(depth_weights(), jnp.bfloat16)
     u, p, faces, slab, seen, codes = call(
         functools.partial(steps_kernel, True),
@@ -633,7 +654,7 @@
     slab_messages = call(slab_message_kernel, "slab_message", [(24, 8, 128)] * 2, [slab, near_low, near_high, powers])
     side_low, side_high = both_ways(*slab_messages, "gy")
     messages = y_messages(u, p, (), halo, powers, x_low, x_high)
-    received = (halo, x_low, x_high, *both_ways(*messages, "gy"))
+    received = (halo, x_low, x_high, *reversed(swaps(*messages, "gy")))
     (demand,) = call(
         surface_kernel,
         "surface",

time: 123 us -> 119 us (0.967)
  waiting for transfers between devices: 35.9 us -> 21.4 us
  starting transfers between devices: 59.5 us -> 71 us
    ppermute x0 -> x8, starting transfers between devices: none -> 37.2 us  [the longest x4 27.7 us: swaps(): lax.ppermute(first, axis, pairs[0])]
    ppermute x8 -> x4, waiting for transfers between devices: 17.7 us -> 2.34 us  [both_ways(): lax.ppermute(to_up, axis, forward)]
    ppermute x8 -> x4, starting transfers between devices: 19.7 us -> 5.17 us  [both_ways(): lax.ppermute(to_down, axis, backward)]
    ppermute x8 -> x4, starting transfers between devices: 29 us -> 18.1 us  [both_ways(): lax.ppermute(to_up, axis, forward)]
    ppermute x0 -> x8, waiting for transfers between devices: none -> 9.63 us  [the longest x4 5.21 us: swaps(): lax.ppermute(first, axis, pairs[0])]
    ppermute x8 -> x4, waiting for transfers between devices: 13 us -> 4.31 us  [both_ways(): lax.ppermute(to_down, axis, backward)]
  transfers between devices with their start and end apart: 17 -> 17, of which waited for: 7 -> 5; matrix products, arithmetic and copies ran while one was open for 0% -> 0% of each run, Pallas kernels for 10% -> 10%
where the time goes in v11:
time: 119 us; the launch traced here: 118 us
  starting transfers between devices  71 us (60%)
  Pallas kernels  22.9 us (19%)
  waiting for transfers between devices  21.4 us (18%)
  local copies, waits for them, and re-layouts  1.36 us (1%)
    ppermute x4, starting transfers between devices, swaps(): lax.ppermute(first, axis, pairs[0])  27.7 us
    pallas_call x11, Pallas kernels, call(): pl.pallas_call(kernel, out_shape=out, in_specs=specs or [VM] * len(args),...  22.9 us
    ppermute x4, starting transfers between devices, both_ways(): lax.ppermute(to_up, axis, forward)  18.1 us
    all_to_all x1, starting transfers between devices, body(): lax.all_to_all(table, ('gx', 'gz'), split_axis=0, concat_axis=0, tiled=True)  10.5 us
    ppermute x4, starting transfers between devices, swaps(): lax.ppermute(second, axis, pairs[1])  9.46 us
    ppermute x4, waiting for transfers between devices, swaps(): lax.ppermute(first, axis, pairs[0])  5.21 us
    ppermute x4, starting transfers between devices, both_ways(): lax.ppermute(to_down, axis, backward)  5.17 us
    all_to_all x1, waiting for transfers between devices, body(): lax.all_to_all(table, ('gx', 'gz'), split_axis=0, concat_axis=0, tiled=True)  5.12 us
  transfers between devices with their start and end apart: 17, of which 5 were waited for; matrix products, arithmetic and copies ran while one was open for 0% of the time, Pallas kernels for 10%

profile of v11, /device:TPU:1, one launch (start us, length us, event | category | flops | bytes accessed | tf_op | source)
XLA Modules:
  0.0 117.6 jit_solution(12992838911174541517)
XLA Ops:
  0.7 2.5 %start.1 = (f32[8,16,128]{2,1,0:T(8,128)S(1)}, f32[8,16,128]{2,1,0:T(8,128)S(1)}, f32[8,16,128]{2,1,0:T(8,128)}) custom-call(f32[3,8,16,128]{3,2,1,0:T(8,128)} %refs_0_.3, f32[3,8,16,128]{3,2,1,0:T(8,128)} %refs_1_.3, f32[8,16,128]{2,1,0:T(8,128)} %c_in.1, f32[8,16,128]{2,1,0:T(8,128)} %d_in.1), custom_call_target="tpu_custom_call" | custom-call | flops 16099999744 | tf_op jit(solution)/shard_map/start/pallas_call | solution.py:553
  3.1 8.8 %collective-permute-start.1 = (f32[8,16,128]{2,1,0:T(8,128)}, f32[8,16,128]{2,1,0:T(8,128)S(1)}, u32[]{:S(2)}, u32[]{:S(2)}) collective-permute-start(f32[8,16,128]{2,1,0:T(8,128)} %get-tuple-element.27), channel_id=1, source_target_pairs={{0,1},{2,3},{1,0},{3,2},{4,5},{6,7},{5,4},{7,6},{8,9},{10,11},{9,8... | collective-permute-start | bytes 196616 | tf_op jit(solution)/shard_map/ppermute | solution.py:576
  11.9 1.9 %collective-permute-start = (f32[8,16,128]{2,1,0:T(8,128)}, f32[8,16,128]{2,1,0:T(8,128)S(1)}, u32[]{:S(2)}, u32[]{:S(2)}) collective-permute-start(f32[8,16,128]{2,1,0:T(8,128)} %get-tuple-element.27), channel_id=1, source_target_pairs={{1,2},{2,1},{5,6},{6,5},{9,10},{10,9},{13,14},{14,13},{17,18},{18,... | collective-permute-start | bytes 196616 | tf_op jit(solution)/shard_map/ppermute | solution.py:576
  13.9 4.4 %collective-permute-done.refs_0_ = f32[8,16,128]{2,1,0:T(8,128)S(1)} collective-permute-done((f32[8,16,128]{2,1,0:T(8,128)}, f32[8,16,128]{2,1,0:T(8,128)S(1)}, u32[]{:S(2)}, u32[]{:S(2)}) %collective-permute-start) | collective-permute-done | bytes 65568 | tf_op jit(solution)/shard_map/ppermute | solution.py:576
  18.6 1.3 %collective-permute-start.2 = (s16[62,16,128]{2,1,0:T(8,128)(2,1)S(1)}, s16[62,16,128]{2,1,0:T(8,128)(2,1)S(1)}, u32[]{:S(2)}, u32[]{:S(2)}) collective-permute-start(s16[62,16,128]{2,1,0:T(8,128)(2,1)S(1)} %get-tuple-element.29), channel_id=1, source_target_pairs={{0,32},{32,64},{64,96},{96,128},{128,160},{160,192},{192,224},{224... | collective-permute-start | bytes 761864 | tf_op jit(solution)/shard_map/ppermute | solution.py:569
  19.9 1.3 %collective-permute-start.3 = (s16[62,16,128]{2,1,0:T(8,128)(2,1)S(1)}, s16[62,16,128]{2,1,0:T(8,128)(2,1)S(1)}, u32[]{:S(2)}, u32[]{:S(2)}) collective-permute-start(s16[62,16,128]{2,1,0:T(8,128)(2,1)S(1)} %get-tuple-element.30), channel_id=1, source_target_pairs={{32,0},{64,32},{96,64},{128,96},{160,128},{192,160},{224,192},{256... | collective-permute-start | bytes 761864 | tf_op jit(solution)/shard_map/ppermute | solution.py:569
  21.2 2.3 %collective-permute-done.2.refs_6_.refs_5_ = s16[62,16,128]{2,1,0:T(8,128)(2,1)S(1)} collective-permute-done((s16[62,16,128]{2,1,0:T(8,128)(2,1)S(1)}, s16[62,16,128]{2,1,0:T(8,128)(2,1)S(1)}, u32[]{:S(2)}, u32[]{:S(2)}) %collective-permute-start.2) | collective-permute-done | bytes 253984 | tf_op jit(solution)/shard_map/ppermute | solution.py:569
  23.5 4.3 %collective-permute-done.3.refs_7_.refs_6_ = s16[62,16,128]{2,1,0:T(8,128)(2,1)S(1)} collective-permute-done((s16[62,16,128]{2,1,0:T(8,128)(2,1)S(1)}, s16[62,16,128]{2,1,0:T(8,128)(2,1)S(1)}, u32[]{:S(2)}, u32[]{:S(2)}) %collective-permute-start.3) | collective-permute-done | bytes 253984 | tf_op jit(solution)/shard_map/ppermute | solution.py:569
  27.8 0.4 y_message.2
  28.2 5.7 %collective-permute-start.4 = (s16[97,16,128]{2,1,0:T(8,128)(2,1)S(1)}, s16[97,16,128]{2,1,0:T(8,128)(2,1)S(1)}, u32[]{:S(2)}, u32[]{:S(2)}) collective-permute-start(s16[97,16,128]{2,1,0:T(8,128)(2,1)S(1)} %get-tuple-element.32), channel_id=1, source_target_pairs={{0,4},{8,12},{16,20},{24,28},{4,0},{12,8},{20,16},{28,24},{1,5},{9... | collective-permute-start | bytes 1191944 | tf_op jit(solution)/shard_map/ppermute | solution.py:576
  33.9 0.7 collective-permute-start.5
  34.6 5.2 %collective-permute-done.4.refs_7_ = s16[97,16,128]{2,1,0:T(8,128)(2,1)S(1)} collective-permute-done((s16[97,16,128]{2,1,0:T(8,128)(2,1)S(1)}, s16[97,16,128]{2,1,0:T(8,128)(2,1)S(1)}, u32[]{:S(2)}, u32[]{:S(2)}) %collective-permute-start.4) | collective-permute-done | bytes 397344 | tf_op jit(solution)/shard_map/ppermute | solution.py:576
  39.8 6.8 %steps_first.1 = (f32[3,8,16,128]{3,2,1,0:T(8,128)S(1)}, f32[3,8,16,128]{3,2,1,0:T(8,128)S(1)}, f32[8,16,128]{2,1,0:T(8,128)S(1)}, f32[8,16,128]{2,1,0:T(8,128)S...) custom-call(f32[3,8,16,128]{3,2,1,0:T(8,128)S(1)} %copy-done, f32[3,8,16,128]{3,2,1,0:T(8,128)S(1)} %copy-done.1, ...), custom_call_target="tpu_custom_call" | custom-call | flops 77050003456 | tf_op jit(solution)/shard_map/steps_first/pallas_call | solution.py:553
  46.6 1.9 %collective-permute-start.7 = (f32[8,16,128]{2,1,0:T(8,128)S(1)}, f32[8,16,128]{2,1,0:T(8,128)S(1)}, u32[]{:S(2)}, u32[]{:S(2)}) collective-permute-start(f32[8,16,128]{2,1,0:T(8,128)S(1)} %get-tuple-element.36), channel_id=1, source_target_pairs={{0,1},{2,3},{1,0},{3,2},{4,5},{6,7},{5,4},{7,6},{8,9},{10,11},{9,8... | collective-permute-start | bytes 196616 | tf_op jit(solution)/shard_map/ppermute | solution.py:576
  48.5 6.2 %collective-permute-start.6 = (f32[8,16,128]{2,1,0:T(8,128)S(1)}, f32[8,16,128]{2,1,0:T(8,128)S(1)}, u32[]{:S(2)}, u32[]{:S(2)}) collective-permute-start(f32[8,16,128]{2,1,0:T(8,128)S(1)} %get-tuple-element.36), channel_id=1, source_target_pairs={{1,2},{2,1},{5,6},{6,5},{9,10},{10,9},{13,14},{14,13},{17,18},{18,... | collective-permute-start | bytes 196616 | tf_op jit(solution)/shard_map/ppermute | solution.py:576
  54.7 1.3 %collective-permute-start.13 = (f32[8,16,128]{2,1,0:T(8,128)S(1)}, f32[8,16,128]{2,1,0:T(8,128)S(1)}, u32[]{:S(2)}, u32[]{:S(2)}) collective-permute-start(f32[8,16,128]{2,1,0:T(8,128)S(1)} %get-tuple-element.44.own_ref.own_in), channel_id=1, source_target_pairs={{32,0},{64,32},{96,64},{128,96},{160,128},{192,160},{224,192},{256... | collective-permute-start | bytes 196616 | tf_op jit(solution)/shard_map/ppermute | solution.py:569
  56.0 4.9 %collective-permute-start.12 = (f32[8,16,128]{2,1,0:T(8,128)S(1)}, f32[8,16,128]{2,1,0:T(8,128)S(1)}, u32[]{:S(2)}, u32[]{:S(2)}) collective-permute-start(f32[8,16,128]{2,1,0:T(8,128)S(1)} %get-tuple-element.44.own_ref.own_in), channel_id=1, source_target_pairs={{0,32},{32,64},{64,96},{96,128},{128,160},{160,192},{192,224},{224... | collective-permute-start | bytes 196616 | tf_op jit(solution)/shard_map/ppermute | solution.py:569
  61.2 3.6 %collective-permute-start.8 = (s16[50,16,128]{2,1,0:T(8,128)(2,1)S(1)}, s16[50,16,128]{2,1,0:T(8,128)(2,1)S(1)}, u32[]{:S(2)}, u32[]{:S(2)}) collective-permute-start(s16[50,16,128]{2,1,0:T(8,128)(2,1)S(1)} %get-tuple-element.38), channel_id=1, source_target_pairs={{0,32},{32,64},{64,96},{96,128},{128,160},{160,192},{192,224},{224... | collective-permute-start | bytes 614408 | tf_op jit(solution)/shard_map/ppermute | solution.py:569
  64.8 1.3 %collective-permute-start.9 = (s16[50,16,128]{2,1,0:T(8,128)(2,1)S(1)}, s16[50,16,128]{2,1,0:T(8,128)(2,1)S(1)}, u32[]{:S(2)}, u32[]{:S(2)}) collective-permute-start(s16[50,16,128]{2,1,0:T(8,128)(2,1)S(1)} %get-tuple-element.39), channel_id=1, source_target_pairs={{32,0},{64,32},{96,64},{128,96},{160,128},{192,160},{224,192},{256... | collective-permute-start | bytes 614408 | tf_op jit(solution)/shard_map/ppermute | solution.py:569
  66.2 8.3 %collective-permute-start.14 = (f32[24,8,128]{2,1,0:T(8,128)S(1)}, f32[24,8,128]{2,1,0:T(8,128)S(1)}, u32[]{:S(2)}, u32[]{:S(2)}) collective-permute-start(f32[24,8,128]{2,1,0:T(8,128)S(1)} %get-tuple-element.45), channel_id=1, source_target_pairs={{0,4},{4,8},{8,12},{12,16},{16,20},{20,24},{24,28},{1,5},{5,9},{9,... | collective-permute-start | bytes 294920 | tf_op jit(solution)/shard_map/ppermute | solution.py:569
  74.5 1.3 %collective-permute-start.15 = (f32[24,8,128]{2,1,0:T(8,128)S(1)}, f32[24,8,128]{2,1,0:T(8,128)S(1)}, u32[]{:S(2)}, u32[]{:S(2)}) collective-permute-start(f32[24,8,128]{2,1,0:T(8,128)S(1)} %get-tuple-element.46), channel_id=1, source_target_pairs={{4,0},{8,4},{12,8},{16,12},{20,16},{24,20},{28,24},{5,1},{9,5},{13... | collective-permute-start | bytes 294920 | tf_op jit(solution)/shard_map/ppermute | solution.py:569
  75.8 0.3 y_message.3
  76.1 0.7 collective-permute-start.10
  76.8 11.3 %collective-permute-start.11 = (s16[77,16,128]{2,1,0:T(8,128)(2,1)S(1)}, s16[77,16,128]{2,1,0:T(8,128)(2,1)S(1)}, u32[]{:S(2)}, u32[]{:S(2)}) collective-permute-start(s16[77,16,128]{2,1,0:T(8,128)(2,1)S(1)} %get-tuple-element.42.after_in), channel_id=1, source_target_pairs={{0,4},{8,12},{16,20},{24,28},{4,0},{12,8},{20,16},{28,24},{1,5},{9... | collective-permute-start | bytes 946184 | tf_op jit(solution)/shard_map/ppermute | solution.py:576
  88.2 0.6 copy-done.9
  88.8 3.8 %surface.1.demand_ref = f32[8,128]{1,0:T(8,128)S(1)} custom-call(f32[8,16,128]{2,1,0:T(8,128)S(1)} %get-tuple-element.44.own_ref.own_in, f32[8,16,128]{2,1,0:T(8,128)S(1)} %collective-permute-done.12.low_ref.x_low, f32[8,16,128]{2,1,0:T(8,128)S(1)} %collective-permute-done.13.high_ref.x_high, f32[24,8,128]{2,1,0:T(8,128)S(1)} %collective-permute-done.14.y_low, ...), custom_call_target="tpu_custom_call" | custom-call | flops 46000001024 | tf_op jit(solution)/shard_map/surface/pallas_call | solution.py:553
  92.6 0.8 table.1
  93.4 10.5 %all-to-all-start = ((f32[64,8,128]{2,1,0:T(8,128)}), f32[64,8,128]{2,1,0:T(8,128)S(1)}, u32[]{:S(2)}, u32[]{:S(2)}) async-start(f32[64,8,128]{2,1,0:T(8,128)} %bitcast.3), calls=%async_computation | async-start | bytes 524288 | tf_op jit(solution)/shard_map/all_to_all | solution.py:682
  104.0 6.8 %steps_second.1 = f32[3,8,16,128]{3,2,1,0:T(8,128)} custom-call(f32[3,8,16,128]{3,2,1,0:T(8,128)S(1)} %get-tuple-element.34.refs_2_.refs_0_, f32[3,8,16,128]{3,2,1,0:T(8,128)S(1)} %get-tuple-element.35.refs_3_.refs_1_, f32[8,16,128]{2,1,0:T(8,128)S(1)} %get-tuple-element.37.refs_2_, s16[50,16,128]{2,1,0:T(8,128)(2,1)S(1)} %collective-permute-done.8.refs_4_.refs_3_, ...), custom_call_target="tpu_custom_call" | custom-call | flops 74750001152 | tf_op jit(solution)/shard_map/steps_second/pallas_call | solution.py:553
  110.9 5.1 %all-to-all-done = f32[64,8,128]{2,1,0:T(8,128)S(1)} async-done(((f32[64,8,128]{2,1,0:T(8,128)}), f32[64,8,128]{2,1,0:T(8,128)S(1)}, u32[]{:S(2)}, u32[]{:S(2)}) %all-to-all-start) | async-done | bytes 262176 | tf_op jit(solution)/shard_map/all_to_all | solution.py:682
  116.0 0.7 copy-done.5
  116.7 1.0 fragility.1
  (39 shorter events, 0.7 us)
Async XLA Ops:
  0.6 17.7 %copy-start.1 = (f32[3,8,16,128]{3,2,1,0:T(8,128)S(1)}, f32[3,8,16,128]{3,2,1,0:T(8,128)}, u32[]{:S(2)}) copy-start(f32[3,8,16,128]{3,2,1,0:T(8,128)} %refs_1_.3) | copy-start | bytes 589828
  0.6 17.7 %copy-start = (f32[3,8,16,128]{3,2,1,0:T(8,128)S(1)}, f32[3,8,16,128]{3,2,1,0:T(8,128)}, u32[]{:S(2)}) copy-start(f32[3,8,16,128]{3,2,1,0:T(8,128)} %refs_0_.3) | copy-start | bytes 589828
  3.1 10.7 %collective-permute-start.1 = (f32[8,16,128]{2,1,0:T(8,128)}, f32[8,16,128]{2,1,0:T(8,128)S(1)}, u32[]{:S(2)}, u32[]{:S(2)}) collective-permute-start(f32[8,16,128]{2,1,0:T(8,128)} %get-tuple-element.27), channel_id=1, source_target_pairs={{0,1},{2,3},{1,0},{3,2},{4,5},{6,7},{5,4},{7,6},{8,9},{10,11},{9,8... | collective-permute-start | bytes 196616 | tf_op jit(solution)/shard_map/ppermute | solution.py:576
  11.9 6.4 %collective-permute-start = (f32[8,16,128]{2,1,0:T(8,128)}, f32[8,16,128]{2,1,0:T(8,128)S(1)}, u32[]{:S(2)}, u32[]{:S(2)}) collective-permute-start(f32[8,16,128]{2,1,0:T(8,128)} %get-tuple-element.27), channel_id=1, source_target_pairs={{1,2},{2,1},{5,6},{6,5},{9,10},{10,9},{13,14},{14,13},{17,18},{18,... | collective-permute-start | bytes 196616 | tf_op jit(solution)/shard_map/ppermute | solution.py:576
  18.6 4.9 %collective-permute-start.2 = (s16[62,16,128]{2,1,0:T(8,128)(2,1)S(1)}, s16[62,16,128]{2,1,0:T(8,128)(2,1)S(1)}, u32[]{:S(2)}, u32[]{:S(2)}) collective-permute-start(s16[62,16,128]{2,1,0:T(8,128)(2,1)S(1)} %get-tuple-element.29), channel_id=1, source_target_pairs={{0,32},{32,64},{64,96},{96,128},{128,160},{160,192},{192,224},{224... | collective-permute-start | bytes 761864 | tf_op jit(solution)/shard_map/ppermute | solution.py:569
  19.9 7.9 %collective-permute-start.3 = (s16[62,16,128]{2,1,0:T(8,128)(2,1)S(1)}, s16[62,16,128]{2,1,0:T(8,128)(2,1)S(1)}, u32[]{:S(2)}, u32[]{:S(2)}) collective-permute-start(s16[62,16,128]{2,1,0:T(8,128)(2,1)S(1)} %get-tuple-element.30), channel_id=1, source_target_pairs={{32,0},{64,32},{96,64},{128,96},{160,128},{192,160},{224,192},{256... | collective-permute-start | bytes 761864 | tf_op jit(solution)/shard_map/ppermute | solution.py:569
  27.8 12.0 %copy-start.11 = (bf16[3,256,256]{2,1,0:T(8,128)(2,1)S(1)}, bf16[3,256,256]{2,1,0:T(8,128)(2,1)}, u32[]{:S(2)}) copy-start(bf16[3,256,256]{2,1,0:T(8,128)(2,1)} %constant.4.clone.refs_9_.refs_7_) | copy-start | bytes 1179652
  28.2 11.6 %collective-permute-start.4 = (s16[97,16,128]{2,1,0:T(8,128)(2,1)S(1)}, s16[97,16,128]{2,1,0:T(8,128)(2,1)S(1)}, u32[]{:S(2)}, u32[]{:S(2)}) collective-permute-start(s16[97,16,128]{2,1,0:T(8,128)(2,1)S(1)} %get-tuple-element.32), channel_id=1, source_target_pairs={{0,4},{8,12},{16,20},{24,28},{4,0},{12,8},{20,16},{28,24},{1,5},{9... | collective-permute-start | bytes 1191944 | tf_op jit(solution)/shard_map/ppermute | solution.py:576
  33.9 5.9 %collective-permute-start.5 = (s16[97,16,128]{2,1,0:T(8,128)(2,1)S(1)}, s16[97,16,128]{2,1,0:T(8,128)(2,1)S(1)}, u32[]{:S(2)}, u32[]{:S(2)}) collective-permute-start(s16[97,16,128]{2,1,0:T(8,128)(2,1)S(1)} %get-tuple-element.33), channel_id=1, source_target_pairs={{4,8},{12,16},{20,24},{8,4},{16,12},{24,20},{5,9},{13,17},{21,25},... | collective-permute-start | bytes 1191944 | tf_op jit(solution)/shard_map/ppermute | solution.py:576
  46.6 14.3 %collective-permute-start.7 = (f32[8,16,128]{2,1,0:T(8,128)S(1)}, f32[8,16,128]{2,1,0:T(8,128)S(1)}, u32[]{:S(2)}, u32[]{:S(2)}) collective-permute-start(f32[8,16,128]{2,1,0:T(8,128)S(1)} %get-tuple-element.36), channel_id=1, source_target_pairs={{0,1},{2,3},{1,0},{3,2},{4,5},{6,7},{5,4},{7,6},{8,9},{10,11},{9,8... | collective-permute-start | bytes 196616 | tf_op jit(solution)/shard_map/ppermute | solution.py:576
  48.5 12.4 %collective-permute-start.6 = (f32[8,16,128]{2,1,0:T(8,128)S(1)}, f32[8,16,128]{2,1,0:T(8,128)S(1)}, u32[]{:S(2)}, u32[]{:S(2)}) collective-permute-start(f32[8,16,128]{2,1,0:T(8,128)S(1)} %get-tuple-element.36), channel_id=1, source_target_pairs={{1,2},{2,1},{5,6},{6,5},{9,10},{10,9},{13,14},{14,13},{17,18},{18,... | collective-permute-start | bytes 196616 | tf_op jit(solution)/shard_map/ppermute | solution.py:576
  54.7 11.4 %collective-permute-start.13 = (f32[8,16,128]{2,1,0:T(8,128)S(1)}, f32[8,16,128]{2,1,0:T(8,128)S(1)}, u32[]{:S(2)}, u32[]{:S(2)}) collective-permute-start(f32[8,16,128]{2,1,0:T(8,128)S(1)} %get-tuple-element.44.own_ref.own_in), channel_id=1, source_target_pairs={{32,0},{64,32},{96,64},{128,96},{160,128},{192,160},{224,192},{256... | collective-permute-start | bytes 196616 | tf_op jit(solution)/shard_map/ppermute | solution.py:569
  56.0 10.1 %collective-permute-start.12 = (f32[8,16,128]{2,1,0:T(8,128)S(1)}, f32[8,16,128]{2,1,0:T(8,128)S(1)}, u32[]{:S(2)}, u32[]{:S(2)}) collective-permute-start(f32[8,16,128]{2,1,0:T(8,128)S(1)} %get-tuple-element.44.own_ref.own_in), channel_id=1, source_target_pairs={{0,32},{32,64},{64,96},{96,128},{128,160},{160,192},{192,224},{224... | collective-permute-start | bytes 196616 | tf_op jit(solution)/shard_map/ppermute | solution.py:569
  61.2 14.6 %collective-permute-start.8 = (s16[50,16,128]{2,1,0:T(8,128)(2,1)S(1)}, s16[50,16,128]{2,1,0:T(8,128)(2,1)S(1)}, u32[]{:S(2)}, u32[]{:S(2)}) collective-permute-start(s16[50,16,128]{2,1,0:T(8,128)(2,1)S(1)} %get-tuple-element.38), channel_id=1, source_target_pairs={{0,32},{32,64},{64,96},{96,128},{128,160},{160,192},{192,224},{224... | collective-permute-start | bytes 614408 | tf_op jit(solution)/shard_map/ppermute | solution.py:569
  64.8 11.0 %collective-permute-start.9 = (s16[50,16,128]{2,1,0:T(8,128)(2,1)S(1)}, s16[50,16,128]{2,1,0:T(8,128)(2,1)S(1)}, u32[]{:S(2)}, u32[]{:S(2)}) collective-permute-start(s16[50,16,128]{2,1,0:T(8,128)(2,1)S(1)} %get-tuple-element.39), channel_id=1, source_target_pairs={{32,0},{64,32},{96,64},{128,96},{160,128},{192,160},{224,192},{256... | collective-permute-start | bytes 614408 | tf_op jit(solution)/shard_map/ppermute | solution.py:569
  66.2 22.0 %collective-permute-start.14 = (f32[24,8,128]{2,1,0:T(8,128)S(1)}, f32[24,8,128]{2,1,0:T(8,128)S(1)}, u32[]{:S(2)}, u32[]{:S(2)}) collective-permute-start(f32[24,8,128]{2,1,0:T(8,128)S(1)} %get-tuple-element.45), channel_id=1, source_target_pairs={{0,4},{4,8},{8,12},{12,16},{16,20},{20,24},{24,28},{1,5},{5,9},{9,... | collective-permute-start | bytes 294920 | tf_op jit(solution)/shard_map/ppermute | solution.py:569
  74.5 13.7 %collective-permute-start.15 = (f32[24,8,128]{2,1,0:T(8,128)S(1)}, f32[24,8,128]{2,1,0:T(8,128)S(1)}, u32[]{:S(2)}, u32[]{:S(2)}) collective-permute-start(f32[24,8,128]{2,1,0:T(8,128)S(1)} %get-tuple-element.46), channel_id=1, source_target_pairs={{4,0},{8,4},{12,8},{16,12},{20,16},{24,20},{28,24},{5,1},{9,5},{13... | collective-permute-start | bytes 294920 | tf_op jit(solution)/shard_map/ppermute | solution.py:569
  75.8 12.4 %copy-start.12 = (bf16[256,128]{1,0:T(8,128)(2,1)S(1)}, bf16[256,128]{1,0:T(8,128)(2,1)}, u32[]{:S(2)}) copy-start(bf16[256,128]{1,0:T(8,128)(2,1)} %constant.5.clone.weight_in) | copy-start | bytes 196612
  76.1 12.1 %copy-start.3 = (bf16[64,24]{0,1:T(8,128)(2,1)S(1)}, bf16[64,24]{0,1:T(8,128)(2,1)}, u32[]{:S(2)}) copy-start(bf16[64,24]{0,1:T(8,128)(2,1)} %param.24) | copy-start | bytes 9220
  76.1 27.8 %collective-permute-start.10 = (s16[77,16,128]{2,1,0:T(8,128)(2,1)S(1)}, s16[77,16,128]{2,1,0:T(8,128)(2,1)S(1)}, u32[]{:S(2)}, u32[]{:S(2)}) collective-permute-start(s16[77,16,128]{2,1,0:T(8,128)(2,1)S(1)} %get-tuple-element.41), channel_id=1, source_target_pairs={{4,8},{12,16},{20,24},{8,4},{16,12},{24,20},{5,9},{13,17},{21,25},... | collective-permute-start | bytes 946184 | tf_op jit(solution)/shard_map/ppermute | solution.py:576
  76.8 27.2 %collective-permute-start.11 = (s16[77,16,128]{2,1,0:T(8,128)(2,1)S(1)}, s16[77,16,128]{2,1,0:T(8,128)(2,1)S(1)}, u32[]{:S(2)}, u32[]{:S(2)}) collective-permute-start(s16[77,16,128]{2,1,0:T(8,128)(2,1)S(1)} %get-tuple-element.42.after_in), channel_id=1, source_target_pairs={{0,4},{8,12},{16,20},{24,28},{4,0},{12,8},{20,16},{28,24},{1,5},{9... | collective-permute-start | bytes 946184 | tf_op jit(solution)/shard_map/ppermute | solution.py:576
  88.2 0.7 copy-start.9
  88.8 3.8 %copy-start.2 = (s32[16,1,128]{2,1,0:T(1,128)S(1)}, s32[16,1,128]{2,1,0:T(1,128)}, u32[]{:S(2)}) copy-start(s32[16,1,128]{2,1,0:T(1,128)} %param.19) | copy-start | bytes 24580
  93.4 22.5 %all-to-all-start = ((f32[64,8,128]{2,1,0:T(8,128)}), f32[64,8,128]{2,1,0:T(8,128)S(1)}, u32[]{:S(2)}, u32[]{:S(2)}) async-start(f32[64,8,128]{2,1,0:T(8,128)} %bitcast.3), calls=%async_computation | async-start | bytes 524288 | tf_op jit(solution)/shard_map/all_to_all | solution.py:682
  104.0 12.0 %copy-start.6 = (s32[1024]{0:T(1024)S(1)}, s32[1024]{0:T(1024)}, u32[]{:S(2)}) copy-start(s32[1024]{0:T(1024)} %param.22) | copy-start | bytes 12292
  104.0 12.0 %copy-start.7 = (f32[16,8]{0,1:T(8,128)S(1)}, f32[16,8]{0,1:T(8,128)}, u32[]{:S(2)}) copy-start(f32[16,8]{0,1:T(8,128)} %param.26) | copy-start | bytes 1540
  104.0 12.0 %copy-start.8 = (f32[16,8]{0,1:T(8,128)S(1)}, f32[16,8]{0,1:T(8,128)}, u32[]{:S(2)}) copy-start(f32[16,8]{0,1:T(8,128)} %param.27) | copy-start | bytes 1540
  116.0 0.7 copy-start.5
  116.0 0.7 copy-start.4
  116.0 0.7 copy-start.10

commit v12 on v11

--- a/solution.py
+++ b/solution.py
@@ -175,7 +175,7 @@
     if coefficients:
         u_ref, p_ref, a_ref, e_ref, halo_ref, power_ref, low_ref, high_ref, first_ref, second_ref = refs
     else:
-        u_ref, p_ref, halo_ref, power_ref, low_ref, high_ref, first_ref, second_ref = refs
+        u_ref, p_ref, halo_ref, power_ref, low_ref, high_ref, second_ref, first_ref = refs
     odd = is_odd("gy")
     powers = power_ref[...]
     low_powers = jnp.concatenate(sent_exponents(low_ref), axis=0)
@@ -265,7 +265,7 @@
         (u_out, p_out, face_out, slab_out, seen_out, code_ref) = refs[10:16]
         state_ref, rate_ref, edge_ref = refs[16:]
     else:
-        (u_in, p_in, halo_in, x_low, x_high, y_second, y_first, weight_in, code_ref) = refs[:9]
+        (u_in, p_in, halo_in, x_low, x_high, y_first, y_second, weight_in, code_ref) = refs[:9]
         u_out, state_ref, rate_ref = refs[9:]
     a_ref, e_ref, ha_ref, he_ref = (rate_ref.at[at] for at in range(4))
     lane = lane_of()
@@ -390,30 +390,36 @@
     lax.fori_loop(0, 8, finish, 0, unroll=4)
 
 
-def slab_message_kernel(own_ref, low_ref, high_ref, after_ref, up_ref, down_ref):
+def slab_message_kernel(own_ref, low_ref, high_ref, after_ref, first_ref, second_ref):
+    odd = is_odd("gy")
+
     def plane(i, carry):
         for at, source in ((0, low_ref), (8, own_ref), (16, high_ref)):
-            up_ref[at + i] = source[i, 8:16, :]
-            down_ref[at + i] = source[i, 0:8, :]
+            up, down = source[i, 8:16, :], source[i, 0:8, :]
+            first_ref[at + i] = jnp.where(odd, down, up)
+            second_ref[at + i] = jnp.where(odd, up, down)
         return carry
 
     lax.fori_loop(0, 8, plane, 0, unroll=2)
 
 
 def surface_kernel(
-    own_in, x_low, x_high, y_low, y_high, weight_in, code_in, seen_in, filter_in, count_in, after_in,
+    own_in, x_low, x_high, y_first, y_second, weight_in, code_in, seen_in, filter_in, count_in, after_in,
     demand_out, state_ref, rate_ref, sample_ref, seen_ref, filter_ref, count_ref,
 ):
     lane = lane_of()
     inner = lane % 16
+
+    odd = is_odd("gy")
 
     def near_side(i, carry):
         state_ref[0, i, 16:32, :] = x_low[i]
         state_ref[0, 8 + i, 16:32, :] = own_in[i]
         state_ref[0, 16 + i, 16:32, :] = x_high[i]
         for part in range(3):
-            state_ref[0, 8 * part + i, 8:16, :] = y_low[8 * part + i]
-            state_ref[0, 8 * part + i, 32:40, :] = y_high[8 * part + i]
+            one, other = y_first[8 * part + i], y_second[8 * part + i]
+            state_ref[0, 8 * part + i, 8:16, :] = jnp.where(odd, one, other)
+            state_ref[0, 8 * part + i, 32:40, :] = jnp.where(odd, other, one)
         return carry
 
     lax.fori_loop(0, 8, near_side, 0, unroll=2)
@@ -598,12 +604,13 @@
     extra = list(coefficients)
     planes = (3 * YU + (3 + len(extra)) * YP + YH) // 2 + 1
     message = jax.ShapeDtypeStruct((planes, 16, 128), jnp.int16)
-    return call(
+    messages = call(
         functools.partial(y_message_kernel, bool(extra)),
         "y_message",
         [message, message],
         [u, p] + extra + [halo, powers, x_low, x_high],
     )
+    return messages if extra else messages[::-1]
 
 
 def body(
@@ -652,14 +659,14 @@
     near_low, near_high = both_ways(slab, slab, "gx")
     halo, powers, x_low, x_high = exchange_x(u, p, faces, ())
     slab_messages = call(slab_message_kernel, "slab_message", [(24, 8, 128)] * 2, [slab, near_low, near_high, powers])
-    side_low, side_high = both_ways(*slab_messages, "gy")
+    side_first, side_second = swaps(*slab_messages, "gy")
     messages = y_messages(u, p, (), halo, powers, x_low, x_high)
-    received = (halo, x_low, x_high, *reversed(swaps(*messages, "gy")))
+    received = (halo, x_low, x_high, *swaps(*messages, "gy"))
     (demand,) = call(
         surface_kernel,
         "surface",
         [(CLASSES, 128)],
-        [slab, near_low, near_high, side_low, side_high, jnp.asarray(slab_weights(), jnp.bfloat16), codes, seen]
+        [slab, near_low, near_high, side_first, side_second, jnp.asarray(slab_weights(), jnp.bfloat16), codes, seen]
         + [modal_filter.T, mode_count.reshape(1, CLASSES), messages[0]],
         specs=[VM] * 10 + [pl.BlockSpec(memory_space=pl.ANY)],
         scratch=[

time: 119 us -> 119 us (level)
    ppermute x4 -> x5, starting transfers between devices: 27.7 us -> 36.2 us  [swaps(): lax.ppermute(first, axis, pairs[0])]
    ppermute x4 -> x3, starting transfers between devices: 18.1 us -> 9.79 us  [both_ways(): lax.ppermute(to_up, axis, forward)]
    ppermute x4 -> x3, starting transfers between devices: 5.17 us -> 3.88 us  [both_ways(): lax.ppermute(to_down, axis, backward)]
    ppermute x4 -> x5, starting transfers between devices: 9.46 us -> 10.1 us  [swaps(): lax.ppermute(second, axis, pairs[1])]
    ppermute x4 -> x3, waiting for transfers between devices: 4.31 us -> 4.78 us  [both_ways(): lax.ppermute(to_down, axis, backward)]
    ppermute x4 -> x5, waiting for transfers between devices: 5.21 us -> 5.21 us  [swaps(): lax.ppermute(first, axis, pairs[0])]
    ppermute x4 -> x5, waiting for transfers between devices: 4.43 us -> 4.43 us  [swaps(): lax.ppermute(second, axis, pairs[1])]
  transfers between devices with their start and end apart: 17 -> 17, of which waited for: 5 -> 6; matrix products, arithmetic and copies ran while one was open for 0% -> 0% of each run, Pallas kernels for 10% -> 10%
where the time goes in v12:
time: 119 us; the launch traced here: 118 us
  starting transfers between devices  70.5 us (59%)
  Pallas kernels  22.9 us (19%)
  waiting for transfers between devices  21.9 us (18%)
  local copies, waits for them, and re-layouts  1.35 us (1%)
    ppermute x5, starting transfers between devices, swaps(): lax.ppermute(first, axis, pairs[0])  36.2 us
    pallas_call x11, Pallas kernels, call(): pl.pallas_call(kernel, out_shape=out, in_specs=specs or [VM] * len(args),...  22.9 us
    all_to_all x1, starting transfers between devices, body(): lax.all_to_all(table, ('gx', 'gz'), split_axis=0, concat_axis=0, tiled=True)  10.5 us
    ppermute x5, starting transfers between devices, swaps(): lax.ppermute(second, axis, pairs[1])  10.1 us
    ppermute x3, starting transfers between devices, both_ways(): lax.ppermute(to_up, axis, forward)  9.79 us
    ppermute x5, waiting for transfers between devices, swaps(): lax.ppermute(first, axis, pairs[0])  5.21 us
    all_to_all x1, waiting for transfers between devices, body(): lax.all_to_all(table, ('gx', 'gz'), split_axis=0, concat_axis=0, tiled=True)  5.12 us
    ppermute x3, waiting for transfers between devices, both_ways(): lax.ppermute(to_down, axis, backward)  4.78 us
  transfers between devices with their start and end apart: 17, of which 6 were waited for; matrix products, arithmetic and copies ran while one was open for 0% of the time, Pallas kernels for 10%

profile of v12, /device:TPU:1, one launch (start us, length us, event | category | flops | bytes accessed | tf_op | source)
XLA Modules:
  0.0 117.6 jit_solution(1232477415806207790)
XLA Ops:
  0.7 2.5 %start.1 = (f32[8,16,128]{2,1,0:T(8,128)S(1)}, f32[8,16,128]{2,1,0:T(8,128)S(1)}, f32[8,16,128]{2,1,0:T(8,128)}) custom-call(f32[3,8,16,128]{3,2,1,0:T(8,128)} %refs_0_.3, f32[3,8,16,128]{3,2,1,0:T(8,128)} %refs_1_.3, f32[8,16,128]{2,1,0:T(8,128)} %c_in.1, f32[8,16,128]{2,1,0:T(8,128)} %d_in.1), custom_call_target="tpu_custom_call" | custom-call | flops 16099999744 | tf_op jit(solution)/shard_map/start/pallas_call | solution.py:559
  3.1 8.8 %collective-permute-start.1 = (f32[8,16,128]{2,1,0:T(8,128)}, f32[8,16,128]{2,1,0:T(8,128)S(1)}, u32[]{:S(2)}, u32[]{:S(2)}) collective-permute-start(f32[8,16,128]{2,1,0:T(8,128)} %get-tuple-element.27), channel_id=1, source_target_pairs={{0,1},{2,3},{1,0},{3,2},{4,5},{6,7},{5,4},{7,6},{8,9},{10,11},{9,8... | collective-permute-start | bytes 196616 | tf_op jit(solution)/shard_map/ppermute | solution.py:582
  11.9 1.9 %collective-permute-start = (f32[8,16,128]{2,1,0:T(8,128)}, f32[8,16,128]{2,1,0:T(8,128)S(1)}, u32[]{:S(2)}, u32[]{:S(2)}) collective-permute-start(f32[8,16,128]{2,1,0:T(8,128)} %get-tuple-element.27), channel_id=1, source_target_pairs={{1,2},{2,1},{5,6},{6,5},{9,10},{10,9},{13,14},{14,13},{17,18},{18,... | collective-permute-start | bytes 196616 | tf_op jit(solution)/shard_map/ppermute | solution.py:582
  13.9 4.4 %collective-permute-done.refs_0_ = f32[8,16,128]{2,1,0:T(8,128)S(1)} collective-permute-done((f32[8,16,128]{2,1,0:T(8,128)}, f32[8,16,128]{2,1,0:T(8,128)S(1)}, u32[]{:S(2)}, u32[]{:S(2)}) %collective-permute-start) | collective-permute-done | bytes 65568 | tf_op jit(solution)/shard_map/ppermute | solution.py:582
  18.6 1.3 %collective-permute-start.2 = (s16[62,16,128]{2,1,0:T(8,128)(2,1)S(1)}, s16[62,16,128]{2,1,0:T(8,128)(2,1)S(1)}, u32[]{:S(2)}, u32[]{:S(2)}) collective-permute-start(s16[62,16,128]{2,1,0:T(8,128)(2,1)S(1)} %get-tuple-element.29), channel_id=1, source_target_pairs={{0,32},{32,64},{64,96},{96,128},{128,160},{160,192},{192,224},{224... | collective-permute-start | bytes 761864 | tf_op jit(solution)/shard_map/ppermute | solution.py:575
  19.9 1.3 %collective-permute-start.3 = (s16[62,16,128]{2,1,0:T(8,128)(2,1)S(1)}, s16[62,16,128]{2,1,0:T(8,128)(2,1)S(1)}, u32[]{:S(2)}, u32[]{:S(2)}) collective-permute-start(s16[62,16,128]{2,1,0:T(8,128)(2,1)S(1)} %get-tuple-element.30), channel_id=1, source_target_pairs={{32,0},{64,32},{96,64},{128,96},{160,128},{192,160},{224,192},{256... | collective-permute-start | bytes 761864 | tf_op jit(solution)/shard_map/ppermute | solution.py:575
  21.2 2.3 %collective-permute-done.2.refs_6_.refs_5_ = s16[62,16,128]{2,1,0:T(8,128)(2,1)S(1)} collective-permute-done((s16[62,16,128]{2,1,0:T(8,128)(2,1)S(1)}, s16[62,16,128]{2,1,0:T(8,128)(2,1)S(1)}, u32[]{:S(2)}, u32[]{:S(2)}) %collective-permute-start.2) | collective-permute-done | bytes 253984 | tf_op jit(solution)/shard_map/ppermute | solution.py:575
  23.5 4.3 %collective-permute-done.3.refs_7_.refs_6_ = s16[62,16,128]{2,1,0:T(8,128)(2,1)S(1)} collective-permute-done((s16[62,16,128]{2,1,0:T(8,128)(2,1)S(1)}, s16[62,16,128]{2,1,0:T(8,128)(2,1)S(1)}, u32[]{:S(2)}, u32[]{:S(2)}) %collective-permute-start.3) | collective-permute-done | bytes 253984 | tf_op jit(solution)/shard_map/ppermute | solution.py:575
  27.8 0.4 y_message.2
  28.2 5.7 %collective-permute-start.4 = (s16[97,16,128]{2,1,0:T(8,128)(2,1)S(1)}, s16[97,16,128]{2,1,0:T(8,128)(2,1)S(1)}, u32[]{:S(2)}, u32[]{:S(2)}) collective-permute-start(s16[97,16,128]{2,1,0:T(8,128)(2,1)S(1)} %get-tuple-element.32), channel_id=1, source_target_pairs={{0,4},{8,12},{16,20},{24,28},{4,0},{12,8},{20,16},{28,24},{1,5},{9... | collective-permute-start | bytes 1191944 | tf_op jit(solution)/shard_map/ppermute | solution.py:582
  33.9 0.7 collective-permute-start.5
  34.6 5.2 %collective-permute-done.4.refs_7_ = s16[97,16,128]{2,1,0:T(8,128)(2,1)S(1)} collective-permute-done((s16[97,16,128]{2,1,0:T(8,128)(2,1)S(1)}, s16[97,16,128]{2,1,0:T(8,128)(2,1)S(1)}, u32[]{:S(2)}, u32[]{:S(2)}) %collective-permute-start.4) | collective-permute-done | bytes 397344 | tf_op jit(solution)/shard_map/ppermute | solution.py:582
  39.8 6.8 %steps_first.1 = (f32[3,8,16,128]{3,2,1,0:T(8,128)S(1)}, f32[3,8,16,128]{3,2,1,0:T(8,128)S(1)}, f32[8,16,128]{2,1,0:T(8,128)S(1)}, f32[8,16,128]{2,1,0:T(8,128)S...) custom-call(f32[3,8,16,128]{3,2,1,0:T(8,128)S(1)} %copy-done, f32[3,8,16,128]{3,2,1,0:T(8,128)S(1)} %copy-done.1, ...), custom_call_target="tpu_custom_call" | custom-call | flops 77050003456 | tf_op jit(solution)/shard_map/steps_first/pallas_call | solution.py:559
  46.6 1.9 %collective-permute-start.7 = (f32[8,16,128]{2,1,0:T(8,128)S(1)}, f32[8,16,128]{2,1,0:T(8,128)S(1)}, u32[]{:S(2)}, u32[]{:S(2)}) collective-permute-start(f32[8,16,128]{2,1,0:T(8,128)S(1)} %get-tuple-element.36), channel_id=1, source_target_pairs={{0,1},{2,3},{1,0},{3,2},{4,5},{6,7},{5,4},{7,6},{8,9},{10,11},{9,8... | collective-permute-start | bytes 196616 | tf_op jit(solution)/shard_map/ppermute | solution.py:582
  48.5 6.2 %collective-permute-start.6 = (f32[8,16,128]{2,1,0:T(8,128)S(1)}, f32[8,16,128]{2,1,0:T(8,128)S(1)}, u32[]{:S(2)}, u32[]{:S(2)}) collective-permute-start(f32[8,16,128]{2,1,0:T(8,128)S(1)} %get-tuple-element.36), channel_id=1, source_target_pairs={{1,2},{2,1},{5,6},{6,5},{9,10},{10,9},{13,14},{14,13},{17,18},{18,... | collective-permute-start | bytes 196616 | tf_op jit(solution)/shard_map/ppermute | solution.py:582
  54.7 1.3 %collective-permute-start.13 = (f32[8,16,128]{2,1,0:T(8,128)S(1)}, f32[8,16,128]{2,1,0:T(8,128)S(1)}, u32[]{:S(2)}, u32[]{:S(2)}) collective-permute-start(f32[8,16,128]{2,1,0:T(8,128)S(1)} %get-tuple-element.44.own_ref.own_in), channel_id=1, source_target_pairs={{32,0},{64,32},{96,64},{128,96},{160,128},{192,160},{224,192},{256... | collective-permute-start | bytes 196616 | tf_op jit(solution)/shard_map/ppermute | solution.py:575
  56.0 4.9 %collective-permute-start.12 = (f32[8,16,128]{2,1,0:T(8,128)S(1)}, f32[8,16,128]{2,1,0:T(8,128)S(1)}, u32[]{:S(2)}, u32[]{:S(2)}) collective-permute-start(f32[8,16,128]{2,1,0:T(8,128)S(1)} %get-tuple-element.44.own_ref.own_in), channel_id=1, source_target_pairs={{0,32},{32,64},{64,96},{96,128},{128,160},{160,192},{192,224},{224... | collective-permute-start | bytes 196616 | tf_op jit(solution)/shard_map/ppermute | solution.py:575
  61.2 3.6 %collective-permute-start.8 = (s16[50,16,128]{2,1,0:T(8,128)(2,1)S(1)}, s16[50,16,128]{2,1,0:T(8,128)(2,1)S(1)}, u32[]{:S(2)}, u32[]{:S(2)}) collective-permute-start(s16[50,16,128]{2,1,0:T(8,128)(2,1)S(1)} %get-tuple-element.38), channel_id=1, source_target_pairs={{0,32},{32,64},{64,96},{96,128},{128,160},{160,192},{192,224},{224... | collective-permute-start | bytes 614408 | tf_op jit(solution)/shard_map/ppermute | solution.py:575
  64.8 1.3 %collective-permute-start.9 = (s16[50,16,128]{2,1,0:T(8,128)(2,1)S(1)}, s16[50,16,128]{2,1,0:T(8,128)(2,1)S(1)}, u32[]{:S(2)}, u32[]{:S(2)}) collective-permute-start(s16[50,16,128]{2,1,0:T(8,128)(2,1)S(1)} %get-tuple-element.39), channel_id=1, source_target_pairs={{32,0},{64,32},{96,64},{128,96},{160,128},{192,160},{224,192},{256... | collective-permute-start | bytes 614408 | tf_op jit(solution)/shard_map/ppermute | solution.py:575
  66.2 8.3 %collective-permute-start.14 = (f32[24,8,128]{2,1,0:T(8,128)S(1)}, f32[24,8,128]{2,1,0:T(8,128)S(1)}, u32[]{:S(2)}, u32[]{:S(2)}) collective-permute-start(f32[24,8,128]{2,1,0:T(8,128)S(1)} %get-tuple-element.45), channel_id=1, source_target_pairs={{0,4},{8,12},{16,20},{24,28},{4,0},{12,8},{20,16},{28,24},{1,5},{9... | collective-permute-start | bytes 294920 | tf_op jit(solution)/shard_map/ppermute | solution.py:582
  74.5 0.7 collective-permute-start.15
  75.2 0.5 collective-permute-done.9.refs_5_.refs_4_
  76.0 0.7 collective-permute-start.11
  76.7 11.5 %collective-permute-start.10 = (s16[77,16,128]{2,1,0:T(8,128)(2,1)S(1)}, s16[77,16,128]{2,1,0:T(8,128)(2,1)S(1)}, u32[]{:S(2)}, u32[]{:S(2)}) collective-permute-start(s16[77,16,128]{2,1,0:T(8,128)(2,1)S(1)} %get-tuple-element.41.after_in), channel_id=1, source_target_pairs={{0,4},{8,12},{16,20},{24,28},{4,0},{12,8},{20,16},{28,24},{1,5},{9... | collective-permute-start | bytes 946184 | tf_op jit(solution)/shard_map/ppermute | solution.py:582
  88.2 0.6 copy-done.9
  88.8 3.8 %surface.1.demand_ref = f32[8,128]{1,0:T(8,128)S(1)} custom-call(f32[8,16,128]{2,1,0:T(8,128)S(1)} %get-tuple-element.44.own_ref.own_in, f32[8,16,128]{2,1,0:T(8,128)S(1)} %collective-permute-done.12.low_ref.x_low, f32[8,16,128]{2,1,0:T(8,128)S(1)} %collective-permute-done.13.high_ref.x_high, f32[24,8,128]{2,1,0:T(8,128)S(1)} %collective-permute-done.14.y_first, ...), custom_call_target="tpu_custom_call" | custom-call | flops 46000001024 | tf_op jit(solution)/shard_map/surface/pallas_call | solution.py:559
  92.6 0.8 table.1
  93.4 10.5 %all-to-all-start = ((f32[64,8,128]{2,1,0:T(8,128)}), f32[64,8,128]{2,1,0:T(8,128)S(1)}, u32[]{:S(2)}, u32[]{:S(2)}) async-start(f32[64,8,128]{2,1,0:T(8,128)} %bitcast.3), calls=%async_computation | async-start | bytes 524288 | tf_op jit(solution)/shard_map/all_to_all | solution.py:689
  104.0 6.8 %steps_second.1 = f32[3,8,16,128]{3,2,1,0:T(8,128)} custom-call(f32[3,8,16,128]{3,2,1,0:T(8,128)S(1)} %get-tuple-element.34.refs_2_.refs_0_, f32[3,8,16,128]{3,2,1,0:T(8,128)S(1)} %get-tuple-element.35.refs_3_.refs_1_, f32[8,16,128]{2,1,0:T(8,128)S(1)} %get-tuple-element.37.refs_2_, s16[50,16,128]{2,1,0:T(8,128)(2,1)S(1)} %collective-permute-done.8.refs_4_.refs_3_, ...), custom_call_target="tpu_custom_call" | custom-call | flops 74750001152 | tf_op jit(solution)/shard_map/steps_second/pallas_call | solution.py:559
  110.9 5.1 %all-to-all-done = f32[64,8,128]{2,1,0:T(8,128)S(1)} async-done(((f32[64,8,128]{2,1,0:T(8,128)}), f32[64,8,128]{2,1,0:T(8,128)S(1)}, u32[]{:S(2)}, u32[]{:S(2)}) %all-to-all-start) | async-done | bytes 262176 | tf_op jit(solution)/shard_map/all_to_all | solution.py:689
  116.0 0.7 copy-done.5
  116.7 1.0 fragility.1
  (39 shorter events, 1.0 us)
Async XLA Ops:
  0.6 17.7 %copy-start.1 = (f32[3,8,16,128]{3,2,1,0:T(8,128)S(1)}, f32[3,8,16,128]{3,2,1,0:T(8,128)}, u32[]{:S(2)}) copy-start(f32[3,8,16,128]{3,2,1,0:T(8,128)} %refs_1_.3) | copy-start | bytes 589828
  0.6 17.7 %copy-start = (f32[3,8,16,128]{3,2,1,0:T(8,128)S(1)}, f32[3,8,16,128]{3,2,1,0:T(8,128)}, u32[]{:S(2)}) copy-start(f32[3,8,16,128]{3,2,1,0:T(8,128)} %refs_0_.3) | copy-start | bytes 589828
  3.1 10.7 %collective-permute-start.1 = (f32[8,16,128]{2,1,0:T(8,128)}, f32[8,16,128]{2,1,0:T(8,128)S(1)}, u32[]{:S(2)}, u32[]{:S(2)}) collective-permute-start(f32[8,16,128]{2,1,0:T(8,128)} %get-tuple-element.27), channel_id=1, source_target_pairs={{0,1},{2,3},{1,0},{3,2},{4,5},{6,7},{5,4},{7,6},{8,9},{10,11},{9,8... | collective-permute-start | bytes 196616 | tf_op jit(solution)/shard_map/ppermute | solution.py:582
  11.9 6.4 %collective-permute-start = (f32[8,16,128]{2,1,0:T(8,128)}, f32[8,16,128]{2,1,0:T(8,128)S(1)}, u32[]{:S(2)}, u32[]{:S(2)}) collective-permute-start(f32[8,16,128]{2,1,0:T(8,128)} %get-tuple-element.27), channel_id=1, source_target_pairs={{1,2},{2,1},{5,6},{6,5},{9,10},{10,9},{13,14},{14,13},{17,18},{18,... | collective-permute-start | bytes 196616 | tf_op jit(solution)/shard_map/ppermute | solution.py:582
  18.6 4.9 %collective-permute-start.2 = (s16[62,16,128]{2,1,0:T(8,128)(2,1)S(1)}, s16[62,16,128]{2,1,0:T(8,128)(2,1)S(1)}, u32[]{:S(2)}, u32[]{:S(2)}) collective-permute-start(s16[62,16,128]{2,1,0:T(8,128)(2,1)S(1)} %get-tuple-element.29), channel_id=1, source_target_pairs={{0,32},{32,64},{64,96},{96,128},{128,160},{160,192},{192,224},{224... | collective-permute-start | bytes 761864 | tf_op jit(solution)/shard_map/ppermute | solution.py:575
  19.9 7.9 %collective-permute-start.3 = (s16[62,16,128]{2,1,0:T(8,128)(2,1)S(1)}, s16[62,16,128]{2,1,0:T(8,128)(2,1)S(1)}, u32[]{:S(2)}, u32[]{:S(2)}) collective-permute-start(s16[62,16,128]{2,1,0:T(8,128)(2,1)S(1)} %get-tuple-element.30), channel_id=1, source_target_pairs={{32,0},{64,32},{96,64},{128,96},{160,128},{192,160},{224,192},{256... | collective-permute-start | bytes 761864 | tf_op jit(solution)/shard_map/ppermute | solution.py:575
  27.8 12.0 %copy-start.11 = (bf16[3,256,256]{2,1,0:T(8,128)(2,1)S(1)}, bf16[3,256,256]{2,1,0:T(8,128)(2,1)}, u32[]{:S(2)}) copy-start(bf16[3,256,256]{2,1,0:T(8,128)(2,1)} %constant.4.clone.refs_9_.refs_7_) | copy-start | bytes 1179652
  28.2 11.6 %collective-permute-start.4 = (s16[97,16,128]{2,1,0:T(8,128)(2,1)S(1)}, s16[97,16,128]{2,1,0:T(8,128)(2,1)S(1)}, u32[]{:S(2)}, u32[]{:S(2)}) collective-permute-start(s16[97,16,128]{2,1,0:T(8,128)(2,1)S(1)} %get-tuple-element.32), channel_id=1, source_target_pairs={{0,4},{8,12},{16,20},{24,28},{4,0},{12,8},{20,16},{28,24},{1,5},{9... | collective-permute-start | bytes 1191944 | tf_op jit(solution)/shard_map/ppermute | solution.py:582
  33.9 5.9 %collective-permute-start.5 = (s16[97,16,128]{2,1,0:T(8,128)(2,1)S(1)}, s16[97,16,128]{2,1,0:T(8,128)(2,1)S(1)}, u32[]{:S(2)}, u32[]{:S(2)}) collective-permute-start(s16[97,16,128]{2,1,0:T(8,128)(2,1)S(1)} %get-tuple-element.33), channel_id=1, source_target_pairs={{4,8},{12,16},{20,24},{8,4},{16,12},{24,20},{5,9},{13,17},{21,25},... | collective-permute-start | bytes 1191944 | tf_op jit(solution)/shard_map/ppermute | solution.py:582
  46.6 14.3 %collective-permute-start.7 = (f32[8,16,128]{2,1,0:T(8,128)S(1)}, f32[8,16,128]{2,1,0:T(8,128)S(1)}, u32[]{:S(2)}, u32[]{:S(2)}) collective-permute-start(f32[8,16,128]{2,1,0:T(8,128)S(1)} %get-tuple-element.36), channel_id=1, source_target_pairs={{0,1},{2,3},{1,0},{3,2},{4,5},{6,7},{5,4},{7,6},{8,9},{10,11},{9,8... | collective-permute-start | bytes 196616 | tf_op jit(solution)/shard_map/ppermute | solution.py:582
  48.5 12.4 %collective-permute-start.6 = (f32[8,16,128]{2,1,0:T(8,128)S(1)}, f32[8,16,128]{2,1,0:T(8,128)S(1)}, u32[]{:S(2)}, u32[]{:S(2)}) collective-permute-start(f32[8,16,128]{2,1,0:T(8,128)S(1)} %get-tuple-element.36), channel_id=1, source_target_pairs={{1,2},{2,1},{5,6},{6,5},{9,10},{10,9},{13,14},{14,13},{17,18},{18,... | collective-permute-start | bytes 196616 | tf_op jit(solution)/shard_map/ppermute | solution.py:582
  54.7 11.4 %collective-permute-start.13 = (f32[8,16,128]{2,1,0:T(8,128)S(1)}, f32[8,16,128]{2,1,0:T(8,128)S(1)}, u32[]{:S(2)}, u32[]{:S(2)}) collective-permute-start(f32[8,16,128]{2,1,0:T(8,128)S(1)} %get-tuple-element.44.own_ref.own_in), channel_id=1, source_target_pairs={{32,0},{64,32},{96,64},{128,96},{160,128},{192,160},{224,192},{256... | collective-permute-start | bytes 196616 | tf_op jit(solution)/shard_map/ppermute | solution.py:575
  56.0 10.1 %collective-permute-start.12 = (f32[8,16,128]{2,1,0:T(8,128)S(1)}, f32[8,16,128]{2,1,0:T(8,128)S(1)}, u32[]{:S(2)}, u32[]{:S(2)}) collective-permute-start(f32[8,16,128]{2,1,0:T(8,128)S(1)} %get-tuple-element.44.own_ref.own_in), channel_id=1, source_target_pairs={{0,32},{32,64},{64,96},{96,128},{128,160},{160,192},{192,224},{224... | collective-permute-start | bytes 196616 | tf_op jit(solution)/shard_map/ppermute | solution.py:575
  61.2 14.0 %collective-permute-start.8 = (s16[50,16,128]{2,1,0:T(8,128)(2,1)S(1)}, s16[50,16,128]{2,1,0:T(8,128)(2,1)S(1)}, u32[]{:S(2)}, u32[]{:S(2)}) collective-permute-start(s16[50,16,128]{2,1,0:T(8,128)(2,1)S(1)} %get-tuple-element.38), channel_id=1, source_target_pairs={{0,32},{32,64},{64,96},{96,128},{128,160},{160,192},{192,224},{224... | collective-permute-start | bytes 614408 | tf_op jit(solution)/shard_map/ppermute | solution.py:575
  64.8 10.8 %collective-permute-start.9 = (s16[50,16,128]{2,1,0:T(8,128)(2,1)S(1)}, s16[50,16,128]{2,1,0:T(8,128)(2,1)S(1)}, u32[]{:S(2)}, u32[]{:S(2)}) collective-permute-start(s16[50,16,128]{2,1,0:T(8,128)(2,1)S(1)} %get-tuple-element.39), channel_id=1, source_target_pairs={{32,0},{64,32},{96,64},{128,96},{160,128},{192,160},{224,192},{256... | collective-permute-start | bytes 614408 | tf_op jit(solution)/shard_map/ppermute | solution.py:575
  66.2 22.0 %collective-permute-start.14 = (f32[24,8,128]{2,1,0:T(8,128)S(1)}, f32[24,8,128]{2,1,0:T(8,128)S(1)}, u32[]{:S(2)}, u32[]{:S(2)}) collective-permute-start(f32[24,8,128]{2,1,0:T(8,128)S(1)} %get-tuple-element.45), channel_id=1, source_target_pairs={{0,4},{8,12},{16,20},{24,28},{4,0},{12,8},{20,16},{28,24},{1,5},{9... | collective-permute-start | bytes 294920 | tf_op jit(solution)/shard_map/ppermute | solution.py:582
  74.5 13.7 %collective-permute-start.15 = (f32[24,8,128]{2,1,0:T(8,128)S(1)}, f32[24,8,128]{2,1,0:T(8,128)S(1)}, u32[]{:S(2)}, u32[]{:S(2)}) collective-permute-start(f32[24,8,128]{2,1,0:T(8,128)S(1)} %get-tuple-element.46), channel_id=1, source_target_pairs={{4,8},{12,16},{20,24},{8,4},{16,12},{24,20},{5,9},{13,17},{21,25},... | collective-permute-start | bytes 294920 | tf_op jit(solution)/shard_map/ppermute | solution.py:582
  75.6 12.5 %copy-start.12 = (bf16[256,128]{1,0:T(8,128)(2,1)S(1)}, bf16[256,128]{1,0:T(8,128)(2,1)}, u32[]{:S(2)}) copy-start(bf16[256,128]{1,0:T(8,128)(2,1)} %constant.5.clone.weight_in) | copy-start | bytes 196612
  76.0 12.2 %copy-start.3 = (bf16[64,24]{0,1:T(8,128)(2,1)S(1)}, bf16[64,24]{0,1:T(8,128)(2,1)}, u32[]{:S(2)}) copy-start(bf16[64,24]{0,1:T(8,128)(2,1)} %param.24) | copy-start | bytes 9220
  76.0 28.0 %collective-permute-start.11 = (s16[77,16,128]{2,1,0:T(8,128)(2,1)S(1)}, s16[77,16,128]{2,1,0:T(8,128)(2,1)S(1)}, u32[]{:S(2)}, u32[]{:S(2)}) collective-permute-start(s16[77,16,128]{2,1,0:T(8,128)(2,1)S(1)} %get-tuple-element.42), channel_id=1, source_target_pairs={{4,8},{12,16},{20,24},{8,4},{16,12},{24,20},{5,9},{13,17},{21,25},... | collective-permute-start | bytes 946184 | tf_op jit(solution)/shard_map/ppermute | solution.py:582
  76.7 27.3 %collective-permute-start.10 = (s16[77,16,128]{2,1,0:T(8,128)(2,1)S(1)}, s16[77,16,128]{2,1,0:T(8,128)(2,1)S(1)}, u32[]{:S(2)}, u32[]{:S(2)}) collective-permute-start(s16[77,16,128]{2,1,0:T(8,128)(2,1)S(1)} %get-tuple-element.41.after_in), channel_id=1, source_target_pairs={{0,4},{8,12},{16,20},{24,28},{4,0},{12,8},{20,16},{28,24},{1,5},{9... | collective-permute-start | bytes 946184 | tf_op jit(solution)/shard_map/ppermute | solution.py:582
  88.2 0.7 copy-start.9
  88.8 3.8 %copy-start.2 = (s32[16,1,128]{2,1,0:T(1,128)S(1)}, s32[16,1,128]{2,1,0:T(1,128)}, u32[]{:S(2)}) copy-start(s32[16,1,128]{2,1,0:T(1,128)} %param.19) | copy-start | bytes 24580
  93.4 22.5 %all-to-all-start = ((f32[64,8,128]{2,1,0:T(8,128)}), f32[64,8,128]{2,1,0:T(8,128)S(1)}, u32[]{:S(2)}, u32[]{:S(2)}) async-start(f32[64,8,128]{2,1,0:T(8,128)} %bitcast.3), calls=%async_computation | async-start | bytes 524288 | tf_op jit(solution)/shard_map/all_to_all | solution.py:689
  104.0 12.0 %copy-start.6 = (s32[1024]{0:T(1024)S(1)}, s32[1024]{0:T(1024)}, u32[]{:S(2)}) copy-start(s32[1024]{0:T(1024)} %param.22) | copy-start | bytes 12292
  104.0 12.0 %copy-start.7 = (f32[16,8]{0,1:T(8,128)S(1)}, f32[16,8]{0,1:T(8,128)}, u32[]{:S(2)}) copy-start(f32[16,8]{0,1:T(8,128)} %param.26) | copy-start | bytes 1540
  104.0 12.0 %copy-start.8 = (f32[16,8]{0,1:T(8,128)S(1)}, f32[16,8]{0,1:T(8,128)}, u32[]{:S(2)}) copy-start(f32[16,8]{0,1:T(8,128)} %param.27) | copy-start | bytes 1540
  116.0 0.7 copy-start.5
  116.0 0.7 copy-start.4
  116.0 0.7 copy-start.10

commit v13 on v12

--- a/solution.py
+++ b/solution.py
@@ -404,7 +404,7 @@
 
 
 def surface_kernel(
-    own_in, x_low, x_high, y_first, y_second, weight_in, code_in, seen_in, filter_in, count_in, after_in,
+    own_in, x_low, x_high, y_first, y_second, weight_in, code_in, seen_in, filter_in, count_in,
     demand_out, state_ref, rate_ref, sample_ref, seen_ref, filter_ref, count_ref,
 ):
     lane = lane_of()
@@ -506,7 +506,7 @@
     demand_out[...] = 0.5 * jnp.log1p(jnp.concatenate(energies, axis=0))
 
 
-def table_kernel(demand_ref, cells_ref, table_out):
+def table_kernel(demand_ref, cells_ref, after_ref, table_out):
     demand = demand_ref[...]
     for owner in range(table_out.shape[0]):
         cells = jnp.broadcast_to(cells_ref[owner : owner + 1, :], (CLASSES, 128))
@@ -550,7 +550,7 @@
 VM = pl.BlockSpec(memory_space=pltpu.VMEM)
 
 
-WEIGHTS = {"start": 1.4, "steps_first": 6.7, "steps_second": 6.5, "surface": 4.0, "fragility": 1.0}
+WEIGHTS = {"start": 1.4, "steps_first": 6.7, "steps_second": 6.5, "slab_message": 4.0, "surface": 0.02, "table": 4.0, "fragility": 1.0}
 UNIT_FLOPS = 1.15e10
 
 
@@ -660,15 +660,12 @@
     halo, powers, x_low, x_high = exchange_x(u, p, faces, ())
     slab_messages = call(slab_message_kernel, "slab_message", [(24, 8, 128)] * 2, [slab, near_low, near_high, powers])
     side_first, side_second = swaps(*slab_messages, "gy")
-    messages = y_messages(u, p, (), halo, powers, x_low, x_high)
-    received = (halo, x_low, x_high, *swaps(*messages, "gy"))
     (demand,) = call(
         surface_kernel,
         "surface",
         [(CLASSES, 128)],
         [slab, near_low, near_high, side_first, side_second, jnp.asarray(slab_weights(), jnp.bfloat16), codes, seen]
-        + [modal_filter.T, mode_count.reshape(1, CLASSES), messages[0]],
-        specs=[VM] * 10 + [pl.BlockSpec(memory_space=pl.ANY)],
+        + [modal_filter.T, mode_count.reshape(1, CLASSES)],
         scratch=[
             pltpu.VMEM((2, 24, 48, 128), F32),
             pltpu.VMEM((2, 24, 32, 128), F32),
@@ -678,12 +675,15 @@
             pltpu.VMEM((8, 128), jnp.int32),
         ],
     )
+    messages = y_messages(u, p, (), halo, powers, x_low, x_high)
+    received = (halo, x_low, x_high, *swaps(*messages, "gy"))
     owners, levels = lax.axis_size("gx"), lax.axis_size("gz")
     (table,) = call(
         table_kernel,
         "table",
         [(owners, levels, CLASSES, 128)],
-        [demand, send_cells.reshape(owners, 128)],
+        [demand, send_cells.reshape(owners, 128), messages[0]],
+        specs=[VM, VM, pl.BlockSpec(memory_space=pl.ANY)],
     )
     table = table.reshape(owners * levels, CLASSES, 128)
     table = lax.all_to_all(table, ("gx", "gz"), split_axis=0, concat_axis=0, tiled=True)

time: 119 us -> 122 us (1.025)
  waiting for transfers between devices: 21.9 us -> 24 us
    ppermute x5, waiting for transfers between devices: 5.21 us -> 7.77 us  [swaps(): lax.ppermute(first, axis, pairs[0])]
    all_to_all x1, starting transfers between devices: 10.5 us -> 12.6 us  [body(): lax.all_to_all(table, ('gx', 'gz'), split_axis=0, concat_axis=0, tiled=True)]
where the time goes in v13:
time: 122 us; the launch traced here: 121 us
  starting transfers between devices  71.6 us (59%)
  waiting for transfers between devices  24 us (20%)
  Pallas kernels  22.9 us (19%)
  local copies, waits for them, and re-layouts  1.37 us (1%)
    ppermute x5, starting transfers between devices, swaps(): lax.ppermute(first, axis, pairs[0])  35.2 us
    pallas_call x11, Pallas kernels, call(): pl.pallas_call(kernel, out_shape=out, in_specs=specs or [VM] * len(args),...  22.9 us
    all_to_all x1, starting transfers between devices, body(): lax.all_to_all(table, ('gx', 'gz'), split_axis=0, concat_axis=0, tiled=True)  12.6 us
    ppermute x5, starting transfers between devices, swaps(): lax.ppermute(second, axis, pairs[1])  10.1 us
    ppermute x3, starting transfers between devices, both_ways(): lax.ppermute(to_up, axis, forward)  9.79 us
    ppermute x5, waiting for transfers between devices, swaps(): lax.ppermute(first, axis, pairs[0])  7.77 us
    all_to_all x1, waiting for transfers between devices, body(): lax.all_to_all(table, ('gx', 'gz'), split_axis=0, concat_axis=0, tiled=True)  5.12 us
    ppermute x5, waiting for transfers between devices, swaps(): lax.ppermute(second, axis, pairs[1])  4.43 us
  transfers between devices with their start and end apart: 17, of which 6 were waited for; matrix products, arithmetic and copies ran while one was open for 0% of the time, Pallas kernels for 10%

profile of v13, /device:TPU:1, one launch (start us, length us, event | category | flops | bytes accessed | tf_op | source)
XLA Modules:
  0.0 120.8 jit_solution(1490436248519160574)
XLA Ops:
  0.7 2.5 %start.1 = (f32[8,16,128]{2,1,0:T(8,128)S(1)}, f32[8,16,128]{2,1,0:T(8,128)S(1)}, f32[8,16,128]{2,1,0:T(8,128)}) custom-call(f32[3,8,16,128]{3,2,1,0:T(8,128)} %refs_0_.3, f32[3,8,16,128]{3,2,1,0:T(8,128)} %refs_1_.3, f32[8,16,128]{2,1,0:T(8,128)} %c_in.1, f32[8,16,128]{2,1,0:T(8,128)} %d_in.1), custom_call_target="tpu_custom_call" | custom-call | flops 16099999744 | tf_op jit(solution)/shard_map/start/pallas_call | solution.py:559
  3.1 8.8 %collective-permute-start.1 = (f32[8,16,128]{2,1,0:T(8,128)}, f32[8,16,128]{2,1,0:T(8,128)S(1)}, u32[]{:S(2)}, u32[]{:S(2)}) collective-permute-start(f32[8,16,128]{2,1,0:T(8,128)} %get-tuple-element.27), channel_id=1, source_target_pairs={{0,1},{2,3},{1,0},{3,2},{4,5},{6,7},{5,4},{7,6},{8,9},{10,11},{9,8... | collective-permute-start | bytes 196616 | tf_op jit(solution)/shard_map/ppermute | solution.py:582
  11.9 1.9 %collective-permute-start = (f32[8,16,128]{2,1,0:T(8,128)}, f32[8,16,128]{2,1,0:T(8,128)S(1)}, u32[]{:S(2)}, u32[]{:S(2)}) collective-permute-start(f32[8,16,128]{2,1,0:T(8,128)} %get-tuple-element.27), channel_id=1, source_target_pairs={{1,2},{2,1},{5,6},{6,5},{9,10},{10,9},{13,14},{14,13},{17,18},{18,... | collective-permute-start | bytes 196616 | tf_op jit(solution)/shard_map/ppermute | solution.py:582
  13.9 4.4 %collective-permute-done.refs_0_ = f32[8,16,128]{2,1,0:T(8,128)S(1)} collective-permute-done((f32[8,16,128]{2,1,0:T(8,128)}, f32[8,16,128]{2,1,0:T(8,128)S(1)}, u32[]{:S(2)}, u32[]{:S(2)}) %collective-permute-start) | collective-permute-done | bytes 65568 | tf_op jit(solution)/shard_map/ppermute | solution.py:582
  18.6 1.3 %collective-permute-start.2 = (s16[62,16,128]{2,1,0:T(8,128)(2,1)S(1)}, s16[62,16,128]{2,1,0:T(8,128)(2,1)S(1)}, u32[]{:S(2)}, u32[]{:S(2)}) collective-permute-start(s16[62,16,128]{2,1,0:T(8,128)(2,1)S(1)} %get-tuple-element.29), channel_id=1, source_target_pairs={{0,32},{32,64},{64,96},{96,128},{128,160},{160,192},{192,224},{224... | collective-permute-start | bytes 761864 | tf_op jit(solution)/shard_map/ppermute | solution.py:575
  19.9 1.3 %collective-permute-start.3 = (s16[62,16,128]{2,1,0:T(8,128)(2,1)S(1)}, s16[62,16,128]{2,1,0:T(8,128)(2,1)S(1)}, u32[]{:S(2)}, u32[]{:S(2)}) collective-permute-start(s16[62,16,128]{2,1,0:T(8,128)(2,1)S(1)} %get-tuple-element.30), channel_id=1, source_target_pairs={{32,0},{64,32},{96,64},{128,96},{160,128},{192,160},{224,192},{256... | collective-permute-start | bytes 761864 | tf_op jit(solution)/shard_map/ppermute | solution.py:575
  21.2 2.3 %collective-permute-done.2.refs_6_.refs_5_ = s16[62,16,128]{2,1,0:T(8,128)(2,1)S(1)} collective-permute-done((s16[62,16,128]{2,1,0:T(8,128)(2,1)S(1)}, s16[62,16,128]{2,1,0:T(8,128)(2,1)S(1)}, u32[]{:S(2)}, u32[]{:S(2)}) %collective-permute-start.2) | collective-permute-done | bytes 253984 | tf_op jit(solution)/shard_map/ppermute | solution.py:575
  23.5 4.3 %collective-permute-done.3.refs_7_.refs_6_ = s16[62,16,128]{2,1,0:T(8,128)(2,1)S(1)} collective-permute-done((s16[62,16,128]{2,1,0:T(8,128)(2,1)S(1)}, s16[62,16,128]{2,1,0:T(8,128)(2,1)S(1)}, u32[]{:S(2)}, u32[]{:S(2)}) %collective-permute-start.3) | collective-permute-done | bytes 253984 | tf_op jit(solution)/shard_map/ppermute | solution.py:575
  27.8 0.4 y_message.2
  28.2 5.7 %collective-permute-start.4 = (s16[97,16,128]{2,1,0:T(8,128)(2,1)S(1)}, s16[97,16,128]{2,1,0:T(8,128)(2,1)S(1)}, u32[]{:S(2)}, u32[]{:S(2)}) collective-permute-start(s16[97,16,128]{2,1,0:T(8,128)(2,1)S(1)} %get-tuple-element.32), channel_id=1, source_target_pairs={{0,4},{8,12},{16,20},{24,28},{4,0},{12,8},{20,16},{28,24},{1,5},{9... | collective-permute-start | bytes 1191944 | tf_op jit(solution)/shard_map/ppermute | solution.py:582
  33.9 0.7 collective-permute-start.5
  34.6 5.2 %collective-permute-done.4.refs_7_ = s16[97,16,128]{2,1,0:T(8,128)(2,1)S(1)} collective-permute-done((s16[97,16,128]{2,1,0:T(8,128)(2,1)S(1)}, s16[97,16,128]{2,1,0:T(8,128)(2,1)S(1)}, u32[]{:S(2)}, u32[]{:S(2)}) %collective-permute-start.4) | collective-permute-done | bytes 397344 | tf_op jit(solution)/shard_map/ppermute | solution.py:582
  39.8 6.8 %steps_first.1 = (f32[3,8,16,128]{3,2,1,0:T(8,128)S(1)}, f32[3,8,16,128]{3,2,1,0:T(8,128)S(1)}, f32[8,16,128]{2,1,0:T(8,128)S(1)}, f32[8,16,128]{2,1,0:T(8,128)S...) custom-call(f32[3,8,16,128]{3,2,1,0:T(8,128)S(1)} %copy-done.3, f32[3,8,16,128]{3,2,1,0:T(8,128)S(1)} %copy-done.4, ...), custom_call_target="tpu_custom_call" | custom-call | flops 77050003456 | tf_op jit(solution)/shard_map/steps_first/pallas_call | solution.py:559
  46.6 1.9 %collective-permute-start.7 = (f32[8,16,128]{2,1,0:T(8,128)S(1)}, f32[8,16,128]{2,1,0:T(8,128)S(1)}, u32[]{:S(2)}, u32[]{:S(2)}) collective-permute-start(f32[8,16,128]{2,1,0:T(8,128)S(1)} %get-tuple-element.36), channel_id=1, source_target_pairs={{0,1},{2,3},{1,0},{3,2},{4,5},{6,7},{5,4},{7,6},{8,9},{10,11},{9,8... | collective-permute-start | bytes 196616 | tf_op jit(solution)/shard_map/ppermute | solution.py:582
  48.5 6.2 %collective-permute-start.6 = (f32[8,16,128]{2,1,0:T(8,128)S(1)}, f32[8,16,128]{2,1,0:T(8,128)S(1)}, u32[]{:S(2)}, u32[]{:S(2)}) collective-permute-start(f32[8,16,128]{2,1,0:T(8,128)S(1)} %get-tuple-element.36), channel_id=1, source_target_pairs={{1,2},{2,1},{5,6},{6,5},{9,10},{10,9},{13,14},{14,13},{17,18},{18,... | collective-permute-start | bytes 196616 | tf_op jit(solution)/shard_map/ppermute | solution.py:582
  54.7 1.3 %collective-permute-start.13 = (f32[8,16,128]{2,1,0:T(8,128)S(1)}, f32[8,16,128]{2,1,0:T(8,128)S(1)}, u32[]{:S(2)}, u32[]{:S(2)}) collective-permute-start(f32[8,16,128]{2,1,0:T(8,128)S(1)} %get-tuple-element.44.own_ref.own_in), channel_id=1, source_target_pairs={{32,0},{64,32},{96,64},{128,96},{160,128},{192,160},{224,192},{256... | collective-permute-start | bytes 196616 | tf_op jit(solution)/shard_map/ppermute | solution.py:575
  56.0 4.9 %collective-permute-start.12 = (f32[8,16,128]{2,1,0:T(8,128)S(1)}, f32[8,16,128]{2,1,0:T(8,128)S(1)}, u32[]{:S(2)}, u32[]{:S(2)}) collective-permute-start(f32[8,16,128]{2,1,0:T(8,128)S(1)} %get-tuple-element.44.own_ref.own_in), channel_id=1, source_target_pairs={{0,32},{32,64},{64,96},{96,128},{128,160},{160,192},{192,224},{224... | collective-permute-start | bytes 196616 | tf_op jit(solution)/shard_map/ppermute | solution.py:575
  61.2 3.6 %collective-permute-start.8 = (s16[50,16,128]{2,1,0:T(8,128)(2,1)S(1)}, s16[50,16,128]{2,1,0:T(8,128)(2,1)S(1)}, u32[]{:S(2)}, u32[]{:S(2)}) collective-permute-start(s16[50,16,128]{2,1,0:T(8,128)(2,1)S(1)} %get-tuple-element.38), channel_id=1, source_target_pairs={{0,32},{32,64},{64,96},{96,128},{128,160},{160,192},{192,224},{224... | collective-permute-start | bytes 614408 | tf_op jit(solution)/shard_map/ppermute | solution.py:575
  64.8 1.3 %collective-permute-start.9 = (s16[50,16,128]{2,1,0:T(8,128)(2,1)S(1)}, s16[50,16,128]{2,1,0:T(8,128)(2,1)S(1)}, u32[]{:S(2)}, u32[]{:S(2)}) collective-permute-start(s16[50,16,128]{2,1,0:T(8,128)(2,1)S(1)} %get-tuple-element.39), channel_id=1, source_target_pairs={{32,0},{64,32},{96,64},{128,96},{160,128},{192,160},{224,192},{256... | collective-permute-start | bytes 614408 | tf_op jit(solution)/shard_map/ppermute | solution.py:575
  66.2 8.3 %collective-permute-start.14 = (f32[24,8,128]{2,1,0:T(8,128)S(1)}, f32[24,8,128]{2,1,0:T(8,128)S(1)}, u32[]{:S(2)}, u32[]{:S(2)}) collective-permute-start(f32[24,8,128]{2,1,0:T(8,128)S(1)} %get-tuple-element.45), channel_id=1, source_target_pairs={{0,4},{8,12},{16,20},{24,28},{4,0},{12,8},{20,16},{28,24},{1,5},{9... | collective-permute-start | bytes 294920 | tf_op jit(solution)/shard_map/ppermute | solution.py:582
  74.5 0.7 collective-permute-start.15
  75.2 2.6 %collective-permute-done.14.y_first = f32[24,8,128]{2,1,0:T(8,128)S(1)} collective-permute-done((f32[24,8,128]{2,1,0:T(8,128)S(1)}, f32[24,8,128]{2,1,0:T(8,128)S(1)}, u32[]{:S(2)}, u32[]{:S(2)}) %collective-permute-start.14) | collective-permute-done | bytes 98336 | tf_op jit(solution)/shard_map/ppermute | solution.py:582
  77.8 0.6 copy-done.2
  78.4 3.8 %surface.1.demand_ref = f32[8,128]{1,0:T(8,128)S(1)} custom-call(f32[8,16,128]{2,1,0:T(8,128)S(1)} %get-tuple-element.44.own_ref.own_in, f32[8,16,128]{2,1,0:T(8,128)S(1)} %collective-permute-done.12.low_ref.x_low, f32[8,16,128]{2,1,0:T(8,128)S(1)} %collective-permute-done.13.high_ref.x_high, f32[24,8,128]{2,1,0:T(8,128)S(1)} %collective-permute-done.14.y_first, ...), custom_call_target="tpu_custom_call" | custom-call | flops 230000000 | tf_op jit(solution)/shard_map/surface/pallas_call | solution.py:559
  82.6 0.7 collective-permute-start.11
  83.2 10.5 %collective-permute-start.10 = (s16[77,16,128]{2,1,0:T(8,128)(2,1)S(1)}, s16[77,16,128]{2,1,0:T(8,128)(2,1)S(1)}, u32[]{:S(2)}, u32[]{:S(2)}) collective-permute-start(s16[77,16,128]{2,1,0:T(8,128)(2,1)S(1)} %get-tuple-element.41.after_ref), channel_id=1, source_target_pairs={{0,4},{8,12},{16,20},{24,28},{4,0},{12,8},{20,16},{28,24},{1,5},{9... | collective-permute-start | bytes 946184 | tf_op jit(solution)/shard_map/ppermute | solution.py:582
  93.7 0.8 table.1
  94.5 12.6 %all-to-all-start = ((f32[64,8,128]{2,1,0:T(8,128)}), f32[64,8,128]{2,1,0:T(8,128)S(1)}, u32[]{:S(2)}, u32[]{:S(2)}) async-start(f32[64,8,128]{2,1,0:T(8,128)} %bitcast.3), calls=%async_computation | async-start | bytes 524288 | tf_op jit(solution)/shard_map/all_to_all | solution.py:689
  107.2 6.8 %steps_second.1 = f32[3,8,16,128]{3,2,1,0:T(8,128)} custom-call(f32[3,8,16,128]{3,2,1,0:T(8,128)S(1)} %get-tuple-element.34.refs_2_.refs_0_, f32[3,8,16,128]{3,2,1,0:T(8,128)S(1)} %get-tuple-element.35.refs_3_.refs_1_, f32[8,16,128]{2,1,0:T(8,128)S(1)} %get-tuple-element.37.refs_2_, s16[50,16,128]{2,1,0:T(8,128)(2,1)S(1)} %collective-permute-done.8.refs_4_.refs_3_, ...), custom_call_target="tpu_custom_call" | custom-call | flops 74750001152 | tf_op jit(solution)/shard_map/steps_second/pallas_call | solution.py:559
  114.0 5.1 %all-to-all-done = f32[64,8,128]{2,1,0:T(8,128)S(1)} async-done(((f32[64,8,128]{2,1,0:T(8,128)}), f32[64,8,128]{2,1,0:T(8,128)S(1)}, u32[]{:S(2)}, u32[]{:S(2)}) %all-to-all-start) | async-done | bytes 262176 | tf_op jit(solution)/shard_map/all_to_all | solution.py:689
  119.2 0.7 copy-done.7
  119.9 1.0 fragility.1
  (39 shorter events, 1.0 us)
Async XLA Ops:
  0.6 17.7 %copy-start.4 = (f32[3,8,16,128]{3,2,1,0:T(8,128)S(1)}, f32[3,8,16,128]{3,2,1,0:T(8,128)}, u32[]{:S(2)}) copy-start(f32[3,8,16,128]{3,2,1,0:T(8,128)} %refs_1_.3) | copy-start | bytes 589828
  0.6 17.7 %copy-start.3 = (f32[3,8,16,128]{3,2,1,0:T(8,128)S(1)}, f32[3,8,16,128]{3,2,1,0:T(8,128)}, u32[]{:S(2)}) copy-start(f32[3,8,16,128]{3,2,1,0:T(8,128)} %refs_0_.3) | copy-start | bytes 589828
  3.1 10.7 %collective-permute-start.1 = (f32[8,16,128]{2,1,0:T(8,128)}, f32[8,16,128]{2,1,0:T(8,128)S(1)}, u32[]{:S(2)}, u32[]{:S(2)}) collective-permute-start(f32[8,16,128]{2,1,0:T(8,128)} %get-tuple-element.27), channel_id=1, source_target_pairs={{0,1},{2,3},{1,0},{3,2},{4,5},{6,7},{5,4},{7,6},{8,9},{10,11},{9,8... | collective-permute-start | bytes 196616 | tf_op jit(solution)/shard_map/ppermute | solution.py:582
  11.9 6.4 %collective-permute-start = (f32[8,16,128]{2,1,0:T(8,128)}, f32[8,16,128]{2,1,0:T(8,128)S(1)}, u32[]{:S(2)}, u32[]{:S(2)}) collective-permute-start(f32[8,16,128]{2,1,0:T(8,128)} %get-tuple-element.27), channel_id=1, source_target_pairs={{1,2},{2,1},{5,6},{6,5},{9,10},{10,9},{13,14},{14,13},{17,18},{18,... | collective-permute-start | bytes 196616 | tf_op jit(solution)/shard_map/ppermute | solution.py:582
  18.6 4.9 %collective-permute-start.2 = (s16[62,16,128]{2,1,0:T(8,128)(2,1)S(1)}, s16[62,16,128]{2,1,0:T(8,128)(2,1)S(1)}, u32[]{:S(2)}, u32[]{:S(2)}) collective-permute-start(s16[62,16,128]{2,1,0:T(8,128)(2,1)S(1)} %get-tuple-element.29), channel_id=1, source_target_pairs={{0,32},{32,64},{64,96},{96,128},{128,160},{160,192},{192,224},{224... | collective-permute-start | bytes 761864 | tf_op jit(solution)/shard_map/ppermute | solution.py:575
  19.9 7.9 %collective-permute-start.3 = (s16[62,16,128]{2,1,0:T(8,128)(2,1)S(1)}, s16[62,16,128]{2,1,0:T(8,128)(2,1)S(1)}, u32[]{:S(2)}, u32[]{:S(2)}) collective-permute-start(s16[62,16,128]{2,1,0:T(8,128)(2,1)S(1)} %get-tuple-element.30), channel_id=1, source_target_pairs={{32,0},{64,32},{96,64},{128,96},{160,128},{192,160},{224,192},{256... | collective-permute-start | bytes 761864 | tf_op jit(solution)/shard_map/ppermute | solution.py:575
  27.8 12.0 %copy-start.12 = (bf16[3,256,256]{2,1,0:T(8,128)(2,1)S(1)}, bf16[3,256,256]{2,1,0:T(8,128)(2,1)}, u32[]{:S(2)}) copy-start(bf16[3,256,256]{2,1,0:T(8,128)(2,1)} %constant.4.clone.refs_9_.refs_7_) | copy-start | bytes 1179652
  28.2 11.6 %collective-permute-start.4 = (s16[97,16,128]{2,1,0:T(8,128)(2,1)S(1)}, s16[97,16,128]{2,1,0:T(8,128)(2,1)S(1)}, u32[]{:S(2)}, u32[]{:S(2)}) collective-permute-start(s16[97,16,128]{2,1,0:T(8,128)(2,1)S(1)} %get-tuple-element.32), channel_id=1, source_target_pairs={{0,4},{8,12},{16,20},{24,28},{4,0},{12,8},{20,16},{28,24},{1,5},{9... | collective-permute-start | bytes 1191944 | tf_op jit(solution)/shard_map/ppermute | solution.py:582
  33.9 5.9 %collective-permute-start.5 = (s16[97,16,128]{2,1,0:T(8,128)(2,1)S(1)}, s16[97,16,128]{2,1,0:T(8,128)(2,1)S(1)}, u32[]{:S(2)}, u32[]{:S(2)}) collective-permute-start(s16[97,16,128]{2,1,0:T(8,128)(2,1)S(1)} %get-tuple-element.33), channel_id=1, source_target_pairs={{4,8},{12,16},{20,24},{8,4},{16,12},{24,20},{5,9},{13,17},{21,25},... | collective-permute-start | bytes 1191944 | tf_op jit(solution)/shard_map/ppermute | solution.py:582
  46.6 14.3 %collective-permute-start.7 = (f32[8,16,128]{2,1,0:T(8,128)S(1)}, f32[8,16,128]{2,1,0:T(8,128)S(1)}, u32[]{:S(2)}, u32[]{:S(2)}) collective-permute-start(f32[8,16,128]{2,1,0:T(8,128)S(1)} %get-tuple-element.36), channel_id=1, source_target_pairs={{0,1},{2,3},{1,0},{3,2},{4,5},{6,7},{5,4},{7,6},{8,9},{10,11},{9,8... | collective-permute-start | bytes 196616 | tf_op jit(solution)/shard_map/ppermute | solution.py:582
  48.5 12.4 %collective-permute-start.6 = (f32[8,16,128]{2,1,0:T(8,128)S(1)}, f32[8,16,128]{2,1,0:T(8,128)S(1)}, u32[]{:S(2)}, u32[]{:S(2)}) collective-permute-start(f32[8,16,128]{2,1,0:T(8,128)S(1)} %get-tuple-element.36), channel_id=1, source_target_pairs={{1,2},{2,1},{5,6},{6,5},{9,10},{10,9},{13,14},{14,13},{17,18},{18,... | collective-permute-start | bytes 196616 | tf_op jit(solution)/shard_map/ppermute | solution.py:582
  54.7 11.4 %collective-permute-start.13 = (f32[8,16,128]{2,1,0:T(8,128)S(1)}, f32[8,16,128]{2,1,0:T(8,128)S(1)}, u32[]{:S(2)}, u32[]{:S(2)}) collective-permute-start(f32[8,16,128]{2,1,0:T(8,128)S(1)} %get-tuple-element.44.own_ref.own_in), channel_id=1, source_target_pairs={{32,0},{64,32},{96,64},{128,96},{160,128},{192,160},{224,192},{256... | collective-permute-start | bytes 196616 | tf_op jit(solution)/shard_map/ppermute | solution.py:575
  56.0 10.1 %collective-permute-start.12 = (f32[8,16,128]{2,1,0:T(8,128)S(1)}, f32[8,16,128]{2,1,0:T(8,128)S(1)}, u32[]{:S(2)}, u32[]{:S(2)}) collective-permute-start(f32[8,16,128]{2,1,0:T(8,128)S(1)} %get-tuple-element.44.own_ref.own_in), channel_id=1, source_target_pairs={{0,32},{32,64},{64,96},{96,128},{128,160},{160,192},{192,224},{224... | collective-permute-start | bytes 196616 | tf_op jit(solution)/shard_map/ppermute | solution.py:575
  61.2 21.0 %collective-permute-start.8 = (s16[50,16,128]{2,1,0:T(8,128)(2,1)S(1)}, s16[50,16,128]{2,1,0:T(8,128)(2,1)S(1)}, u32[]{:S(2)}, u32[]{:S(2)}) collective-permute-start(s16[50,16,128]{2,1,0:T(8,128)(2,1)S(1)} %get-tuple-element.38), channel_id=1, source_target_pairs={{0,32},{32,64},{64,96},{96,128},{128,160},{160,192},{192,224},{224... | collective-permute-start | bytes 614408 | tf_op jit(solution)/shard_map/ppermute | solution.py:575
  64.8 17.4 %collective-permute-start.9 = (s16[50,16,128]{2,1,0:T(8,128)(2,1)S(1)}, s16[50,16,128]{2,1,0:T(8,128)(2,1)S(1)}, u32[]{:S(2)}, u32[]{:S(2)}) collective-permute-start(s16[50,16,128]{2,1,0:T(8,128)(2,1)S(1)} %get-tuple-element.39), channel_id=1, source_target_pairs={{32,0},{64,32},{96,64},{128,96},{160,128},{192,160},{224,192},{256... | collective-permute-start | bytes 614408 | tf_op jit(solution)/shard_map/ppermute | solution.py:575
  66.1 11.6 %copy-start = (bf16[256,128]{1,0:T(8,128)(2,1)S(1)}, bf16[256,128]{1,0:T(8,128)(2,1)}, u32[]{:S(2)}) copy-start(bf16[256,128]{1,0:T(8,128)(2,1)} %constant.5.clone.weight_in) | copy-start | bytes 196612
  66.2 11.6 %copy-start.1 = (bf16[64,24]{0,1:T(8,128)(2,1)S(1)}, bf16[64,24]{0,1:T(8,128)(2,1)}, u32[]{:S(2)}) copy-start(bf16[64,24]{0,1:T(8,128)(2,1)} %param.24) | copy-start | bytes 9220
  66.2 11.5 %collective-permute-start.14 = (f32[24,8,128]{2,1,0:T(8,128)S(1)}, f32[24,8,128]{2,1,0:T(8,128)S(1)}, u32[]{:S(2)}, u32[]{:S(2)}) collective-permute-start(f32[24,8,128]{2,1,0:T(8,128)S(1)} %get-tuple-element.45), channel_id=1, source_target_pairs={{0,4},{8,12},{16,20},{24,28},{4,0},{12,8},{20,16},{28,24},{1,5},{9... | collective-permute-start | bytes 294920 | tf_op jit(solution)/shard_map/ppermute | solution.py:582
  74.5 3.2 %collective-permute-start.15 = (f32[24,8,128]{2,1,0:T(8,128)S(1)}, f32[24,8,128]{2,1,0:T(8,128)S(1)}, u32[]{:S(2)}, u32[]{:S(2)}) collective-permute-start(f32[24,8,128]{2,1,0:T(8,128)S(1)} %get-tuple-element.46), channel_id=1, source_target_pairs={{4,8},{12,16},{20,24},{8,4},{16,12},{24,20},{5,9},{13,17},{21,25},... | collective-permute-start | bytes 294920 | tf_op jit(solution)/shard_map/ppermute | solution.py:582
  77.7 0.7 copy-start.2
  82.2 11.5 %copy-start.5 = (s32[16,1,128]{2,1,0:T(1,128)S(1)}, s32[16,1,128]{2,1,0:T(1,128)}, u32[]{:S(2)}) copy-start(s32[16,1,128]{2,1,0:T(1,128)} %param.19) | copy-start | bytes 24580
  82.6 24.6 %collective-permute-start.11 = (s16[77,16,128]{2,1,0:T(8,128)(2,1)S(1)}, s16[77,16,128]{2,1,0:T(8,128)(2,1)S(1)}, u32[]{:S(2)}, u32[]{:S(2)}) collective-permute-start(s16[77,16,128]{2,1,0:T(8,128)(2,1)S(1)} %get-tuple-element.42), channel_id=1, source_target_pairs={{4,8},{12,16},{20,24},{8,4},{16,12},{24,20},{5,9},{13,17},{21,25},... | collective-permute-start | bytes 946184 | tf_op jit(solution)/shard_map/ppermute | solution.py:582
  83.2 23.9 %collective-permute-start.10 = (s16[77,16,128]{2,1,0:T(8,128)(2,1)S(1)}, s16[77,16,128]{2,1,0:T(8,128)(2,1)S(1)}, u32[]{:S(2)}, u32[]{:S(2)}) collective-permute-start(s16[77,16,128]{2,1,0:T(8,128)(2,1)S(1)} %get-tuple-element.41.after_ref), channel_id=1, source_target_pairs={{0,4},{8,12},{16,20},{24,28},{4,0},{12,8},{20,16},{28,24},{1,5},{9... | collective-permute-start | bytes 946184 | tf_op jit(solution)/shard_map/ppermute | solution.py:582
  94.5 24.6 %all-to-all-start = ((f32[64,8,128]{2,1,0:T(8,128)}), f32[64,8,128]{2,1,0:T(8,128)S(1)}, u32[]{:S(2)}, u32[]{:S(2)}) async-start(f32[64,8,128]{2,1,0:T(8,128)} %bitcast.3), calls=%async_computation | async-start | bytes 524288 | tf_op jit(solution)/shard_map/all_to_all | solution.py:689
  107.2 12.0 %copy-start.8 = (s32[1024]{0:T(1024)S(1)}, s32[1024]{0:T(1024)}, u32[]{:S(2)}) copy-start(s32[1024]{0:T(1024)} %param.22) | copy-start | bytes 12292
  107.2 12.0 %copy-start.9 = (f32[16,8]{0,1:T(8,128)S(1)}, f32[16,8]{0,1:T(8,128)}, u32[]{:S(2)}) copy-start(f32[16,8]{0,1:T(8,128)} %param.26) | copy-start | bytes 1540
  107.2 12.0 %copy-start.10 = (f32[16,8]{0,1:T(8,128)S(1)}, f32[16,8]{0,1:T(8,128)}, u32[]{:S(2)}) copy-start(f32[16,8]{0,1:T(8,128)} %param.27) | copy-start | bytes 1540
  119.2 0.7 copy-start.7
  119.2 0.7 copy-start.6
  119.2 0.7 copy-start.11

commit v14 on v12

--- a/solution.py
+++ b/solution.py
@@ -25,9 +25,6 @@
 BIAS = 200
 UNIT_A = 2.0 / FULL
 UNIT_E = 0.2 / 12.0 / FULL
-
-
-PLANES = 4
 
 
 def depth_weights():
@@ -315,18 +312,18 @@
 
     lax.fori_loop(2, 22, prepare, 0, unroll=4)
 
-    def advance(src, dst, x):
+    def advance(src, dst, x, count):
         rows = pl.ds(8, 32)
-        fields = [[src[k, 2 + j, rows, :] for j in range(PLANES)] for k in range(4)]
+        fields = [[src[k, 2 + j, rows, :] for j in range(count)] for k in range(4)]
         parts = [[split(v) for v in field] for field in fields]
         depth = []
         for k in range(3):
-            pieces = [jnp.concatenate([parts[k][j][part], parts[3][j][part]], axis=1) for part in (0, 1) for j in range(PLANES)]
+            pieces = [jnp.concatenate([parts[k][j][part], parts[3][j][part]], axis=1) for part in (0, 1) for j in range(count)]
             both = jnp.dot(jnp.concatenate(pieces, axis=0), weight_in[k], preferred_element_type=F32)
-            depth.append(both[0 : 32 * PLANES] + both[32 * PLANES :])
+            depth.append(both[0 : 32 * count] + both[32 * count :])
         side = depth[0][:, 128:] + depth[1][:, 128:] + depth[2][:, 128:]
         fresh = []
-        for j in range(PLANES):
+        for j in range(count):
             for k in range(4):
                 v = fields[k][j]
                 near = (src[k, 1 + j, rows, :] + src[k, 3 + j, rows, :]) + (
@@ -342,23 +339,19 @@
                 fresh.append((k, j, old + a_each[x + j] * (v - old) + e_each[x + j] * laplace))
         return fresh, side
 
-    def one_step(step, carry):
+    def block_of(step, x, count):
         dst = state_ref.at[(step + 1) % 2]
-
-        def planes(at, inside):
-            x = 2 * step + 2 + PLANES * at
-            fresh, side = advance(state_ref.at[step % 2, :, pl.ds(x - 2, 4 + PLANES)], dst, x)
-            for k, j, value in fresh:
-                dst[k, x + j, 8:40, :] = value
-            if first:
-                for j in range(PLANES):
-                    edge_ref[step, x + j, :, :] = side[32 * j + 8 : 32 * j + 24]
-            return inside
-
-        lax.fori_loop(0, (20 - 4 * step) // PLANES, planes, 0)
-        return carry
-
-    lax.fori_loop(0, HALF, one_step, 0)
+        fresh, side = advance(state_ref.at[step % 2, :, pl.ds(x - 2, 4 + count)], dst, x, count)
+        for k, j, value in fresh:
+            dst[k, x + j, 8:40, :] = value
+        if first:
+            for j in range(count):
+                edge_ref[step, x + j, :, :] = side[32 * j + 8 : 32 * j + 24]
+
+    for step in range(HALF):
+        count = (20 - 4 * step) // 2
+        block_of(step, 2 * step + 2, count)
+        block_of(step, 2 * step + 2 + count, count)
 
     block = pl.ds(16, 16)
 
@@ -446,32 +439,27 @@
     lax.fori_loop(0, 24, prepare, 0, unroll=4)
     lax.fori_loop(2, 22, rates, 0, unroll=4)
 
-    def one_step(step, carry):
-        dst = state_ref.at[(step + 1) % 2]
-
-        def planes(at, inside):
-            x = 2 * step + 2 + PLANES * at
-            src = state_ref.at[step % 2, pl.ds(x - 2, 4 + PLANES)]
-            rows = pl.ds(8, 32)
-            fields = [src[2 + j, rows, :] for j in range(PLANES)]
-            halves = jnp.concatenate([jnp.concatenate(split(v), axis=1) for v in fields], axis=0)
-            depth = jnp.dot(halves, weight_in[...], preferred_element_type=F32)
-            fresh = []
-            for j, v in enumerate(fields):
-                near = (src[1 + j, rows, :] + src[3 + j, rows, :]) + (src[2 + j, pl.ds(7, 32), :] + src[2 + j, pl.ds(9, 32), :])
-                far = (src[j, rows, :] + src[4 + j, rows, :]) + (src[2 + j, pl.ds(6, 32), :] + src[2 + j, pl.ds(10, 32), :])
-                laplace = depth[32 * j : 32 * j + 32] + (16.0 * near - far)
-                old = dst[x + j, rows, :]
-                fresh.append(old + rate_ref[0, x + j] * (v - old) + rate_ref[1, x + j] * laplace)
-            for j, value in enumerate(fresh):
-                dst[x + j, 8:40, :] = value
-                sample_ref[step, x + j, :, :] = value[8:24]
-            return inside
-
-        lax.fori_loop(0, (20 - 4 * step) // PLANES, planes, 0)
-        return carry
-
-    lax.fori_loop(0, HALF, one_step, 0)
+    def advance(step, x, count):
+        src, dst = state_ref.at[step % 2, pl.ds(x - 2, 4 + count)], state_ref.at[(step + 1) % 2]
+        rows = pl.ds(8, 32)
+        fields = [src[2 + j, rows, :] for j in range(count)]
+        halves = jnp.concatenate([jnp.concatenate(split(v), axis=1) for v in fields], axis=0)
+        depth = jnp.dot(halves, weight_in[...], preferred_element_type=F32)
+        fresh = []
+        for j, v in enumerate(fields):
+            near = (src[1 + j, rows, :] + src[3 + j, rows, :]) + (src[2 + j, pl.ds(7, 32), :] + src[2 + j, pl.ds(9, 32), :])
+            far = (src[j, rows, :] + src[4 + j, rows, :]) + (src[2 + j, pl.ds(6, 32), :] + src[2 + j, pl.ds(10, 32), :])
+            laplace = depth[32 * j : 32 * j + 32] + (16.0 * near - far)
+            old = dst[x + j, rows, :]
+            fresh.append(old + rate_ref[0, x + j] * (v - old) + rate_ref[1, x + j] * laplace)
+        for j, value in enumerate(fresh):
+            dst[x + j, 8:40, :] = value
+            sample_ref[step, x + j, :, :] = value[8:24]
+
+    for step in range(HALF):
+        count = (20 - 4 * step) // 2
+        advance(step, 2 * step + 2, count)
+        advance(step, 2 * step + 2 + count, count)
 
     def finish(x, carry):
         for row in (0, 8):

time: 119 us -> 116 us (0.975)
  Pallas kernels: 22.9 us -> 18.5 us
  waiting for transfers between devices: 21.9 us -> 23.4 us
    pallas_call x11, Pallas kernels: 22.9 us -> 18.5 us  [call(): pl.pallas_call(kernel, out_shape=out, in_specs=specs or [VM] * len(args),...]
    all_to_all x1, waiting for transfers between devices: 5.12 us -> 6.63 us  [body(): lax.all_to_all(table, ('gx', 'gz'), split_axis=0, concat_axis=0, tiled=True)]
  transfers between devices with their start and end apart: 17 -> 17, of which waited for: 6 -> 6; matrix products, arithmetic and copies ran while one was open for 0% -> 0% of each run, Pallas kernels for 10% -> 8%
where the time goes in v14:
time: 116 us; the launch traced here: 115 us
  starting transfers between devices  70.5 us (61%)
  waiting for transfers between devices  23.4 us (20%)
  Pallas kernels  18.5 us (16%)
  local copies, waits for them, and re-layouts  1.35 us (1%)
    ppermute x5, starting transfers between devices, swaps(): lax.ppermute(first, axis, pairs[0])  36.2 us
    pallas_call x11, Pallas kernels, call(): pl.pallas_call(kernel, out_shape=out, in_specs=specs or [VM] * len(args),...  18.5 us
    all_to_all x1, starting transfers between devices, body(): lax.all_to_all(table, ('gx', 'gz'), split_axis=0, concat_axis=0, tiled=True)  10.5 us
    ppermute x5, starting transfers between devices, swaps(): lax.ppermute(second, axis, pairs[1])  10.1 us
    ppermute x3, starting transfers between devices, both_ways(): lax.ppermute(to_up, axis, forward)  9.8 us
    all_to_all x1, waiting for transfers between devices, body(): lax.all_to_all(table, ('gx', 'gz'), split_axis=0, concat_axis=0, tiled=True)  6.63 us
    ppermute x5, waiting for transfers between devices, swaps(): lax.ppermute(first, axis, pairs[0])  5.21 us
    ppermute x3, waiting for transfers between devices, both_ways(): lax.ppermute(to_down, axis, backward)  4.78 us
  transfers between devices with their start and end apart: 17, of which 6 were waited for; matrix products, arithmetic and copies ran while one was open for 0% of the time, Pallas kernels for 8%

profile of v14, /device:TPU:1, one launch (start us, length us, event | category | flops | bytes accessed | tf_op | source)
XLA Modules:
  0.0 114.7 jit_solution(1518086467727887815)
XLA Ops:
  0.7 2.5 %start.1 = (f32[8,16,128]{2,1,0:T(8,128)S(1)}, f32[8,16,128]{2,1,0:T(8,128)S(1)}, f32[8,16,128]{2,1,0:T(8,128)}) custom-call(f32[3,8,16,128]{3,2,1,0:T(8,128)} %refs_0_.3, f32[3,8,16,128]{3,2,1,0:T(8,128)} %refs_1_.3, f32[8,16,128]{2,1,0:T(8,128)} %c_in.1, f32[8,16,128]{2,1,0:T(8,128)} %d_in.1), custom_call_target="tpu_custom_call" | custom-call | flops 16099999744 | tf_op jit(solution)/shard_map/start/pallas_call | solution.py:547
  3.1 8.8 %collective-permute-start.1 = (f32[8,16,128]{2,1,0:T(8,128)}, f32[8,16,128]{2,1,0:T(8,128)S(1)}, u32[]{:S(2)}, u32[]{:S(2)}) collective-permute-start(f32[8,16,128]{2,1,0:T(8,128)} %get-tuple-element.27), channel_id=1, source_target_pairs={{0,1},{2,3},{1,0},{3,2},{4,5},{6,7},{5,4},{7,6},{8,9},{10,11},{9,8... | collective-permute-start | bytes 196616 | tf_op jit(solution)/shard_map/ppermute | solution.py:570
  11.9 1.9 %collective-permute-start = (f32[8,16,128]{2,1,0:T(8,128)}, f32[8,16,128]{2,1,0:T(8,128)S(1)}, u32[]{:S(2)}, u32[]{:S(2)}) collective-permute-start(f32[8,16,128]{2,1,0:T(8,128)} %get-tuple-element.27), channel_id=1, source_target_pairs={{1,2},{2,1},{5,6},{6,5},{9,10},{10,9},{13,14},{14,13},{17,18},{18,... | collective-permute-start | bytes 196616 | tf_op jit(solution)/shard_map/ppermute | solution.py:570
  13.9 4.4 %collective-permute-done.refs_0_ = f32[8,16,128]{2,1,0:T(8,128)S(1)} collective-permute-done((f32[8,16,128]{2,1,0:T(8,128)}, f32[8,16,128]{2,1,0:T(8,128)S(1)}, u32[]{:S(2)}, u32[]{:S(2)}) %collective-permute-start) | collective-permute-done | bytes 65568 | tf_op jit(solution)/shard_map/ppermute | solution.py:570
  18.6 1.3 %collective-permute-start.2 = (s16[62,16,128]{2,1,0:T(8,128)(2,1)S(1)}, s16[62,16,128]{2,1,0:T(8,128)(2,1)S(1)}, u32[]{:S(2)}, u32[]{:S(2)}) collective-permute-start(s16[62,16,128]{2,1,0:T(8,128)(2,1)S(1)} %get-tuple-element.29), channel_id=1, source_target_pairs={{0,32},{32,64},{64,96},{96,128},{128,160},{160,192},{192,224},{224... | collective-permute-start | bytes 761864 | tf_op jit(solution)/shard_map/ppermute | solution.py:563
  19.9 1.3 %collective-permute-start.3 = (s16[62,16,128]{2,1,0:T(8,128)(2,1)S(1)}, s16[62,16,128]{2,1,0:T(8,128)(2,1)S(1)}, u32[]{:S(2)}, u32[]{:S(2)}) collective-permute-start(s16[62,16,128]{2,1,0:T(8,128)(2,1)S(1)} %get-tuple-element.30), channel_id=1, source_target_pairs={{32,0},{64,32},{96,64},{128,96},{160,128},{192,160},{224,192},{256... | collective-permute-start | bytes 761864 | tf_op jit(solution)/shard_map/ppermute | solution.py:563
  21.2 2.3 %collective-permute-done.2.refs_6_.refs_5_ = s16[62,16,128]{2,1,0:T(8,128)(2,1)S(1)} collective-permute-done((s16[62,16,128]{2,1,0:T(8,128)(2,1)S(1)}, s16[62,16,128]{2,1,0:T(8,128)(2,1)S(1)}, u32[]{:S(2)}, u32[]{:S(2)}) %collective-permute-start.2) | collective-permute-done | bytes 253984 | tf_op jit(solution)/shard_map/ppermute | solution.py:563
  23.5 4.3 %collective-permute-done.3.refs_7_.refs_6_ = s16[62,16,128]{2,1,0:T(8,128)(2,1)S(1)} collective-permute-done((s16[62,16,128]{2,1,0:T(8,128)(2,1)S(1)}, s16[62,16,128]{2,1,0:T(8,128)(2,1)S(1)}, u32[]{:S(2)}, u32[]{:S(2)}) %collective-permute-start.3) | collective-permute-done | bytes 253984 | tf_op jit(solution)/shard_map/ppermute | solution.py:563
  27.8 0.4 y_message.2
  28.2 5.7 %collective-permute-start.4 = (s16[97,16,128]{2,1,0:T(8,128)(2,1)S(1)}, s16[97,16,128]{2,1,0:T(8,128)(2,1)S(1)}, u32[]{:S(2)}, u32[]{:S(2)}) collective-permute-start(s16[97,16,128]{2,1,0:T(8,128)(2,1)S(1)} %get-tuple-element.32), channel_id=1, source_target_pairs={{0,4},{8,12},{16,20},{24,28},{4,0},{12,8},{20,16},{28,24},{1,5},{9... | collective-permute-start | bytes 1191944 | tf_op jit(solution)/shard_map/ppermute | solution.py:570
  33.9 0.7 collective-permute-start.5
  34.6 5.2 %collective-permute-done.4.refs_7_ = s16[97,16,128]{2,1,0:T(8,128)(2,1)S(1)} collective-permute-done((s16[97,16,128]{2,1,0:T(8,128)(2,1)S(1)}, s16[97,16,128]{2,1,0:T(8,128)(2,1)S(1)}, u32[]{:S(2)}, u32[]{:S(2)}) %collective-permute-start.4) | collective-permute-done | bytes 397344 | tf_op jit(solution)/shard_map/ppermute | solution.py:570
  39.8 5.2 %steps_first.1 = (f32[3,8,16,128]{3,2,1,0:T(8,128)S(1)}, f32[3,8,16,128]{3,2,1,0:T(8,128)S(1)}, f32[8,16,128]{2,1,0:T(8,128)S(1)}, f32[8,16,128]{2,1,0:T(8,128)S...) custom-call(f32[3,8,16,128]{3,2,1,0:T(8,128)S(1)} %copy-done, f32[3,8,16,128]{3,2,1,0:T(8,128)S(1)} %copy-done.1, ...), custom_call_target="tpu_custom_call" | custom-call | flops 77050003456 | tf_op jit(solution)/shard_map/steps_first/pallas_call | solution.py:547
  45.1 1.9 %collective-permute-start.7 = (f32[8,16,128]{2,1,0:T(8,128)S(1)}, f32[8,16,128]{2,1,0:T(8,128)S(1)}, u32[]{:S(2)}, u32[]{:S(2)}) collective-permute-start(f32[8,16,128]{2,1,0:T(8,128)S(1)} %get-tuple-element.36), channel_id=1, source_target_pairs={{0,1},{2,3},{1,0},{3,2},{4,5},{6,7},{5,4},{7,6},{8,9},{10,11},{9,8... | collective-permute-start | bytes 196616 | tf_op jit(solution)/shard_map/ppermute | solution.py:570
  47.0 6.2 %collective-permute-start.6 = (f32[8,16,128]{2,1,0:T(8,128)S(1)}, f32[8,16,128]{2,1,0:T(8,128)S(1)}, u32[]{:S(2)}, u32[]{:S(2)}) collective-permute-start(f32[8,16,128]{2,1,0:T(8,128)S(1)} %get-tuple-element.36), channel_id=1, source_target_pairs={{1,2},{2,1},{5,6},{6,5},{9,10},{10,9},{13,14},{14,13},{17,18},{18,... | collective-permute-start | bytes 196616 | tf_op jit(solution)/shard_map/ppermute | solution.py:570
  53.2 1.3 %collective-permute-start.13 = (f32[8,16,128]{2,1,0:T(8,128)S(1)}, f32[8,16,128]{2,1,0:T(8,128)S(1)}, u32[]{:S(2)}, u32[]{:S(2)}) collective-permute-start(f32[8,16,128]{2,1,0:T(8,128)S(1)} %get-tuple-element.44.own_ref.own_in), channel_id=1, source_target_pairs={{32,0},{64,32},{96,64},{128,96},{160,128},{192,160},{224,192},{256... | collective-permute-start | bytes 196616 | tf_op jit(solution)/shard_map/ppermute | solution.py:563
  54.5 4.9 %collective-permute-start.12 = (f32[8,16,128]{2,1,0:T(8,128)S(1)}, f32[8,16,128]{2,1,0:T(8,128)S(1)}, u32[]{:S(2)}, u32[]{:S(2)}) collective-permute-start(f32[8,16,128]{2,1,0:T(8,128)S(1)} %get-tuple-element.44.own_ref.own_in), channel_id=1, source_target_pairs={{0,32},{32,64},{64,96},{96,128},{128,160},{160,192},{192,224},{224... | collective-permute-start | bytes 196616 | tf_op jit(solution)/shard_map/ppermute | solution.py:563
  59.7 3.6 %collective-permute-start.8 = (s16[50,16,128]{2,1,0:T(8,128)(2,1)S(1)}, s16[50,16,128]{2,1,0:T(8,128)(2,1)S(1)}, u32[]{:S(2)}, u32[]{:S(2)}) collective-permute-start(s16[50,16,128]{2,1,0:T(8,128)(2,1)S(1)} %get-tuple-element.38), channel_id=1, source_target_pairs={{0,32},{32,64},{64,96},{96,128},{128,160},{160,192},{192,224},{224... | collective-permute-start | bytes 614408 | tf_op jit(solution)/shard_map/ppermute | solution.py:563
  63.3 1.3 %collective-permute-start.9 = (s16[50,16,128]{2,1,0:T(8,128)(2,1)S(1)}, s16[50,16,128]{2,1,0:T(8,128)(2,1)S(1)}, u32[]{:S(2)}, u32[]{:S(2)}) collective-permute-start(s16[50,16,128]{2,1,0:T(8,128)(2,1)S(1)} %get-tuple-element.39), channel_id=1, source_target_pairs={{32,0},{64,32},{96,64},{128,96},{160,128},{192,160},{224,192},{256... | collective-permute-start | bytes 614408 | tf_op jit(solution)/shard_map/ppermute | solution.py:563
  64.6 8.3 %collective-permute-start.14 = (f32[24,8,128]{2,1,0:T(8,128)S(1)}, f32[24,8,128]{2,1,0:T(8,128)S(1)}, u32[]{:S(2)}, u32[]{:S(2)}) collective-permute-start(f32[24,8,128]{2,1,0:T(8,128)S(1)} %get-tuple-element.45), channel_id=1, source_target_pairs={{0,4},{8,12},{16,20},{24,28},{4,0},{12,8},{20,16},{28,24},{1,5},{9... | collective-permute-start | bytes 294920 | tf_op jit(solution)/shard_map/ppermute | solution.py:570
  72.9 0.7 collective-permute-start.15
  73.6 0.5 collective-permute-done.9.refs_5_.refs_4_
  74.4 0.7 collective-permute-start.11
  75.1 11.5 %collective-permute-start.10 = (s16[77,16,128]{2,1,0:T(8,128)(2,1)S(1)}, s16[77,16,128]{2,1,0:T(8,128)(2,1)S(1)}, u32[]{:S(2)}, u32[]{:S(2)}) collective-permute-start(s16[77,16,128]{2,1,0:T(8,128)(2,1)S(1)} %get-tuple-element.41.after_in), channel_id=1, source_target_pairs={{0,4},{8,12},{16,20},{24,28},{4,0},{12,8},{20,16},{28,24},{1,5},{9... | collective-permute-start | bytes 946184 | tf_op jit(solution)/shard_map/ppermute | solution.py:570
  86.7 0.6 copy-done.9
  87.3 2.4 %surface.1.demand_ref = f32[8,128]{1,0:T(8,128)S(1)} custom-call(f32[8,16,128]{2,1,0:T(8,128)S(1)} %get-tuple-element.44.own_ref.own_in, f32[8,16,128]{2,1,0:T(8,128)S(1)} %collective-permute-done.12.low_ref.x_low, f32[8,16,128]{2,1,0:T(8,128)S(1)} %collective-permute-done.13.high_ref.x_high, f32[24,8,128]{2,1,0:T(8,128)S(1)} %collective-permute-done.14.y_first, ...), custom_call_target="tpu_custom_call" | custom-call | flops 46000001024 | tf_op jit(solution)/shard_map/surface/pallas_call | solution.py:547
  89.7 0.8 table.1
  90.5 10.5 %all-to-all-start = ((f32[64,8,128]{2,1,0:T(8,128)}), f32[64,8,128]{2,1,0:T(8,128)S(1)}, u32[]{:S(2)}, u32[]{:S(2)}) async-start(f32[64,8,128]{2,1,0:T(8,128)} %bitcast.3), calls=%async_computation | async-start | bytes 524288 | tf_op jit(solution)/shard_map/all_to_all | solution.py:677
  101.1 5.3 %steps_second.1 = f32[3,8,16,128]{3,2,1,0:T(8,128)} custom-call(f32[3,8,16,128]{3,2,1,0:T(8,128)S(1)} %get-tuple-element.34.refs_2_.refs_0_, f32[3,8,16,128]{3,2,1,0:T(8,128)S(1)} %get-tuple-element.35.refs_3_.refs_1_, f32[8,16,128]{2,1,0:T(8,128)S(1)} %get-tuple-element.37.refs_2_, s16[50,16,128]{2,1,0:T(8,128)(2,1)S(1)} %collective-permute-done.8.refs_4_.refs_3_, ...), custom_call_target="tpu_custom_call" | custom-call | flops 74750001152 | tf_op jit(solution)/shard_map/steps_second/pallas_call | solution.py:547
  106.4 6.6 %all-to-all-done = f32[64,8,128]{2,1,0:T(8,128)S(1)} async-done(((f32[64,8,128]{2,1,0:T(8,128)}), f32[64,8,128]{2,1,0:T(8,128)S(1)}, u32[]{:S(2)}, u32[]{:S(2)}) %all-to-all-start) | async-done | bytes 262176 | tf_op jit(solution)/shard_map/all_to_all | solution.py:677
  113.1 0.7 copy-done.5
  113.8 1.0 fragility.1
  (39 shorter events, 1.0 us)
Async XLA Ops:
  0.6 17.7 %copy-start.1 = (f32[3,8,16,128]{3,2,1,0:T(8,128)S(1)}, f32[3,8,16,128]{3,2,1,0:T(8,128)}, u32[]{:S(2)}) copy-start(f32[3,8,16,128]{3,2,1,0:T(8,128)} %refs_1_.3) | copy-start | bytes 589828
  0.6 17.7 %copy-start = (f32[3,8,16,128]{3,2,1,0:T(8,128)S(1)}, f32[3,8,16,128]{3,2,1,0:T(8,128)}, u32[]{:S(2)}) copy-start(f32[3,8,16,128]{3,2,1,0:T(8,128)} %refs_0_.3) | copy-start | bytes 589828
  3.1 10.7 %collective-permute-start.1 = (f32[8,16,128]{2,1,0:T(8,128)}, f32[8,16,128]{2,1,0:T(8,128)S(1)}, u32[]{:S(2)}, u32[]{:S(2)}) collective-permute-start(f32[8,16,128]{2,1,0:T(8,128)} %get-tuple-element.27), channel_id=1, source_target_pairs={{0,1},{2,3},{1,0},{3,2},{4,5},{6,7},{5,4},{7,6},{8,9},{10,11},{9,8... | collective-permute-start | bytes 196616 | tf_op jit(solution)/shard_map/ppermute | solution.py:570
  11.9 6.4 %collective-permute-start = (f32[8,16,128]{2,1,0:T(8,128)}, f32[8,16,128]{2,1,0:T(8,128)S(1)}, u32[]{:S(2)}, u32[]{:S(2)}) collective-permute-start(f32[8,16,128]{2,1,0:T(8,128)} %get-tuple-element.27), channel_id=1, source_target_pairs={{1,2},{2,1},{5,6},{6,5},{9,10},{10,9},{13,14},{14,13},{17,18},{18,... | collective-permute-start | bytes 196616 | tf_op jit(solution)/shard_map/ppermute | solution.py:570
  18.6 4.9 %collective-permute-start.2 = (s16[62,16,128]{2,1,0:T(8,128)(2,1)S(1)}, s16[62,16,128]{2,1,0:T(8,128)(2,1)S(1)}, u32[]{:S(2)}, u32[]{:S(2)}) collective-permute-start(s16[62,16,128]{2,1,0:T(8,128)(2,1)S(1)} %get-tuple-element.29), channel_id=1, source_target_pairs={{0,32},{32,64},{64,96},{96,128},{128,160},{160,192},{192,224},{224... | collective-permute-start | bytes 761864 | tf_op jit(solution)/shard_map/ppermute | solution.py:563
  19.9 7.9 %collective-permute-start.3 = (s16[62,16,128]{2,1,0:T(8,128)(2,1)S(1)}, s16[62,16,128]{2,1,0:T(8,128)(2,1)S(1)}, u32[]{:S(2)}, u32[]{:S(2)}) collective-permute-start(s16[62,16,128]{2,1,0:T(8,128)(2,1)S(1)} %get-tuple-element.30), channel_id=1, source_target_pairs={{32,0},{64,32},{96,64},{128,96},{160,128},{192,160},{224,192},{256... | collective-permute-start | bytes 761864 | tf_op jit(solution)/shard_map/ppermute | solution.py:563
  27.8 12.0 %copy-start.11 = (bf16[3,256,256]{2,1,0:T(8,128)(2,1)S(1)}, bf16[3,256,256]{2,1,0:T(8,128)(2,1)}, u32[]{:S(2)}) copy-start(bf16[3,256,256]{2,1,0:T(8,128)(2,1)} %constant.4.clone.refs_9_.refs_7_) | copy-start | bytes 1179652
  28.2 11.6 %collective-permute-start.4 = (s16[97,16,128]{2,1,0:T(8,128)(2,1)S(1)}, s16[97,16,128]{2,1,0:T(8,128)(2,1)S(1)}, u32[]{:S(2)}, u32[]{:S(2)}) collective-permute-start(s16[97,16,128]{2,1,0:T(8,128)(2,1)S(1)} %get-tuple-element.32), channel_id=1, source_target_pairs={{0,4},{8,12},{16,20},{24,28},{4,0},{12,8},{20,16},{28,24},{1,5},{9... | collective-permute-start | bytes 1191944 | tf_op jit(solution)/shard_map/ppermute | solution.py:570
  33.9 5.9 %collective-permute-start.5 = (s16[97,16,128]{2,1,0:T(8,128)(2,1)S(1)}, s16[97,16,128]{2,1,0:T(8,128)(2,1)S(1)}, u32[]{:S(2)}, u32[]{:S(2)}) collective-permute-start(s16[97,16,128]{2,1,0:T(8,128)(2,1)S(1)} %get-tuple-element.33), channel_id=1, source_target_pairs={{4,8},{12,16},{20,24},{8,4},{16,12},{24,20},{5,9},{13,17},{21,25},... | collective-permute-start | bytes 1191944 | tf_op jit(solution)/shard_map/ppermute | solution.py:570
  45.1 14.3 %collective-permute-start.7 = (f32[8,16,128]{2,1,0:T(8,128)S(1)}, f32[8,16,128]{2,1,0:T(8,128)S(1)}, u32[]{:S(2)}, u32[]{:S(2)}) collective-permute-start(f32[8,16,128]{2,1,0:T(8,128)S(1)} %get-tuple-element.36), channel_id=1, source_target_pairs={{0,1},{2,3},{1,0},{3,2},{4,5},{6,7},{5,4},{7,6},{8,9},{10,11},{9,8... | collective-permute-start | bytes 196616 | tf_op jit(solution)/shard_map/ppermute | solution.py:570
  47.0 12.4 %collective-permute-start.6 = (f32[8,16,128]{2,1,0:T(8,128)S(1)}, f32[8,16,128]{2,1,0:T(8,128)S(1)}, u32[]{:S(2)}, u32[]{:S(2)}) collective-permute-start(f32[8,16,128]{2,1,0:T(8,128)S(1)} %get-tuple-element.36), channel_id=1, source_target_pairs={{1,2},{2,1},{5,6},{6,5},{9,10},{10,9},{13,14},{14,13},{17,18},{18,... | collective-permute-start | bytes 196616 | tf_op jit(solution)/shard_map/ppermute | solution.py:570
  53.2 11.4 %collective-permute-start.13 = (f32[8,16,128]{2,1,0:T(8,128)S(1)}, f32[8,16,128]{2,1,0:T(8,128)S(1)}, u32[]{:S(2)}, u32[]{:S(2)}) collective-permute-start(f32[8,16,128]{2,1,0:T(8,128)S(1)} %get-tuple-element.44.own_ref.own_in), channel_id=1, source_target_pairs={{32,0},{64,32},{96,64},{128,96},{160,128},{192,160},{224,192},{256... | collective-permute-start | bytes 196616 | tf_op jit(solution)/shard_map/ppermute | solution.py:563
  54.5 10.1 %collective-permute-start.12 = (f32[8,16,128]{2,1,0:T(8,128)S(1)}, f32[8,16,128]{2,1,0:T(8,128)S(1)}, u32[]{:S(2)}, u32[]{:S(2)}) collective-permute-start(f32[8,16,128]{2,1,0:T(8,128)S(1)} %get-tuple-element.44.own_ref.own_in), channel_id=1, source_target_pairs={{0,32},{32,64},{64,96},{96,128},{128,160},{160,192},{192,224},{224... | collective-permute-start | bytes 196616 | tf_op jit(solution)/shard_map/ppermute | solution.py:563
  59.7 13.9 %collective-permute-start.8 = (s16[50,16,128]{2,1,0:T(8,128)(2,1)S(1)}, s16[50,16,128]{2,1,0:T(8,128)(2,1)S(1)}, u32[]{:S(2)}, u32[]{:S(2)}) collective-permute-start(s16[50,16,128]{2,1,0:T(8,128)(2,1)S(1)} %get-tuple-element.38), channel_id=1, source_target_pairs={{0,32},{32,64},{64,96},{96,128},{128,160},{160,192},{192,224},{224... | collective-permute-start | bytes 614408 | tf_op jit(solution)/shard_map/ppermute | solution.py:563
  63.3 10.8 %collective-permute-start.9 = (s16[50,16,128]{2,1,0:T(8,128)(2,1)S(1)}, s16[50,16,128]{2,1,0:T(8,128)(2,1)S(1)}, u32[]{:S(2)}, u32[]{:S(2)}) collective-permute-start(s16[50,16,128]{2,1,0:T(8,128)(2,1)S(1)} %get-tuple-element.39), channel_id=1, source_target_pairs={{32,0},{64,32},{96,64},{128,96},{160,128},{192,160},{224,192},{256... | collective-permute-start | bytes 614408 | tf_op jit(solution)/shard_map/ppermute | solution.py:563
  64.6 22.0 %collective-permute-start.14 = (f32[24,8,128]{2,1,0:T(8,128)S(1)}, f32[24,8,128]{2,1,0:T(8,128)S(1)}, u32[]{:S(2)}, u32[]{:S(2)}) collective-permute-start(f32[24,8,128]{2,1,0:T(8,128)S(1)} %get-tuple-element.45), channel_id=1, source_target_pairs={{0,4},{8,12},{16,20},{24,28},{4,0},{12,8},{20,16},{28,24},{1,5},{9... | collective-permute-start | bytes 294920 | tf_op jit(solution)/shard_map/ppermute | solution.py:570
  72.9 13.7 %collective-permute-start.15 = (f32[24,8,128]{2,1,0:T(8,128)S(1)}, f32[24,8,128]{2,1,0:T(8,128)S(1)}, u32[]{:S(2)}, u32[]{:S(2)}) collective-permute-start(f32[24,8,128]{2,1,0:T(8,128)S(1)} %get-tuple-element.46), channel_id=1, source_target_pairs={{4,8},{12,16},{20,24},{8,4},{16,12},{24,20},{5,9},{13,17},{21,25},... | collective-permute-start | bytes 294920 | tf_op jit(solution)/shard_map/ppermute | solution.py:570
  74.1 12.6 %copy-start.12 = (bf16[256,128]{1,0:T(8,128)(2,1)S(1)}, bf16[256,128]{1,0:T(8,128)(2,1)}, u32[]{:S(2)}) copy-start(bf16[256,128]{1,0:T(8,128)(2,1)} %constant.5.clone.weight_in) | copy-start | bytes 196612
  74.4 12.2 %copy-start.3 = (bf16[64,24]{0,1:T(8,128)(2,1)S(1)}, bf16[64,24]{0,1:T(8,128)(2,1)}, u32[]{:S(2)}) copy-start(bf16[64,24]{0,1:T(8,128)(2,1)} %param.24) | copy-start | bytes 9220
  74.4 26.6 %collective-permute-start.11 = (s16[77,16,128]{2,1,0:T(8,128)(2,1)S(1)}, s16[77,16,128]{2,1,0:T(8,128)(2,1)S(1)}, u32[]{:S(2)}, u32[]{:S(2)}) collective-permute-start(s16[77,16,128]{2,1,0:T(8,128)(2,1)S(1)} %get-tuple-element.42), channel_id=1, source_target_pairs={{4,8},{12,16},{20,24},{8,4},{16,12},{24,20},{5,9},{13,17},{21,25},... | collective-permute-start | bytes 946184 | tf_op jit(solution)/shard_map/ppermute | solution.py:570
  75.1 26.0 %collective-permute-start.10 = (s16[77,16,128]{2,1,0:T(8,128)(2,1)S(1)}, s16[77,16,128]{2,1,0:T(8,128)(2,1)S(1)}, u32[]{:S(2)}, u32[]{:S(2)}) collective-permute-start(s16[77,16,128]{2,1,0:T(8,128)(2,1)S(1)} %get-tuple-element.41.after_in), channel_id=1, source_target_pairs={{0,4},{8,12},{16,20},{24,28},{4,0},{12,8},{20,16},{28,24},{1,5},{9... | collective-permute-start | bytes 946184 | tf_op jit(solution)/shard_map/ppermute | solution.py:570
  86.6 0.7 copy-start.9
  87.3 2.4 %copy-start.2 = (s32[16,1,128]{2,1,0:T(1,128)S(1)}, s32[16,1,128]{2,1,0:T(1,128)}, u32[]{:S(2)}) copy-start(s32[16,1,128]{2,1,0:T(1,128)} %param.19) | copy-start | bytes 24580
  90.5 22.6 %all-to-all-start = ((f32[64,8,128]{2,1,0:T(8,128)}), f32[64,8,128]{2,1,0:T(8,128)S(1)}, u32[]{:S(2)}, u32[]{:S(2)}) async-start(f32[64,8,128]{2,1,0:T(8,128)} %bitcast.3), calls=%async_computation | async-start | bytes 524288 | tf_op jit(solution)/shard_map/all_to_all | solution.py:677
  101.1 12.0 %copy-start.6 = (s32[1024]{0:T(1024)S(1)}, s32[1024]{0:T(1024)}, u32[]{:S(2)}) copy-start(s32[1024]{0:T(1024)} %param.22) | copy-start | bytes 12292
  101.1 12.0 %copy-start.7 = (f32[16,8]{0,1:T(8,128)S(1)}, f32[16,8]{0,1:T(8,128)}, u32[]{:S(2)}) copy-start(f32[16,8]{0,1:T(8,128)} %param.26) | copy-start | bytes 1540
  101.1 12.0 %copy-start.8 = (f32[16,8]{0,1:T(8,128)S(1)}, f32[16,8]{0,1:T(8,128)}, u32[]{:S(2)}) copy-start(f32[16,8]{0,1:T(8,128)} %param.27) | copy-start | bytes 1540
  113.1 0.7 copy-start.5
  113.1 0.7 copy-start.4
  113.1 0.7 copy-start.10

commit v15 on v14

--- a/solution.py
+++ b/solution.py
@@ -263,7 +263,7 @@
         state_ref, rate_ref, edge_ref = refs[16:]
     else:
         (u_in, p_in, halo_in, x_low, x_high, y_first, y_second, weight_in, code_ref) = refs[:9]
-        u_out, state_ref, rate_ref = refs[9:]
+        u_out, state_ref, rate_ref = refs[-3:]
     a_ref, e_ref, ha_ref, he_ref = (rate_ref.at[at] for at in range(4))
     lane = lane_of()
     inner = lane % 16
@@ -383,7 +383,8 @@
     lax.fori_loop(0, 8, finish, 0, unroll=4)
 
 
-def slab_message_kernel(own_ref, low_ref, high_ref, after_ref, first_ref, second_ref):
+def slab_message_kernel(own_ref, low_ref, high_ref, *refs):
+    first_ref, second_ref = refs[-2:]
     odd = is_odd("gy")
 
     def plane(i, carry):
@@ -646,7 +647,15 @@
 
     near_low, near_high = both_ways(slab, slab, "gx")
     halo, powers, x_low, x_high = exchange_x(u, p, faces, ())
-    slab_messages = call(slab_message_kernel, "slab_message", [(24, 8, 128)] * 2, [slab, near_low, near_high, powers])
+    owners, levels = lax.axis_size("gx"), lax.axis_size("gz")
+    slab_inputs = [jnp.asarray(slab_weights(), jnp.bfloat16), modal_filter.T, mode_count.reshape(1, CLASSES)]
+    cells = send_cells.reshape(owners, 128)
+    slab_messages = call(
+        slab_message_kernel,
+        "slab_message",
+        [(24, 8, 128)] * 2,
+        [slab, near_low, near_high, powers, cells] + slab_inputs,
+    )
     side_first, side_second = swaps(*slab_messages, "gy")
     messages = y_messages(u, p, (), halo, powers, x_low, x_high)
     received = (halo, x_low, x_high, *swaps(*messages, "gy"))
@@ -654,8 +663,7 @@
         surface_kernel,
         "surface",
         [(CLASSES, 128)],
-        [slab, near_low, near_high, side_first, side_second, jnp.asarray(slab_weights(), jnp.bfloat16), codes, seen]
-        + [modal_filter.T, mode_count.reshape(1, CLASSES), messages[0]],
+        [slab, near_low, near_high, side_first, side_second, slab_inputs[0], codes, seen] + slab_inputs[1:] + [messages[0]],
         specs=[VM] * 10 + [pl.BlockSpec(memory_space=pl.ANY)],
         scratch=[
             pltpu.VMEM((2, 24, 48, 128), F32),
@@ -666,31 +674,34 @@
             pltpu.VMEM((8, 128), jnp.int32),
         ],
     )
-    owners, levels = lax.axis_size("gx"), lax.axis_size("gz")
     (table,) = call(
         table_kernel,
         "table",
         [(owners, levels, CLASSES, 128)],
-        [demand, send_cells.reshape(owners, 128)],
+        [demand, cells],
     )
     table = table.reshape(owners * levels, CLASSES, 128)
     table = lax.all_to_all(table, ("gx", "gz"), split_axis=0, concat_axis=0, tiled=True)
+    building_inputs = [
+        building_slot.reshape(8, 128),
+        building_class.reshape(8, 128),
+        city.reshape(8, 128),
+        amplify.reshape(1, CITIES),
+        median.T,
+        spread.T,
+    ]
     (field,) = call(
-        functools.partial(steps_kernel, False), "steps_second", [own], [u, p, *received, weights, codes], scratch=[wide, rates]
+        functools.partial(steps_kernel, False),
+        "steps_second",
+        [own],
+        [u, p, *received, weights, codes] + building_inputs,
+        scratch=[wide, rates],
     )
     (probability,) = call(
         fragility_kernel,
         "fragility",
         [(16, 1024)],
-        [
-            table.reshape(owners, levels, CLASSES, 128),
-            building_slot.reshape(8, 128),
-            building_class.reshape(8, 128),
-            city.reshape(8, 128),
-            amplify.reshape(1, CITIES),
-            median.T,
-            spread.T,
-        ],
+        [table.reshape(owners, levels, CLASSES, 128)] + building_inputs,
         scratch=[pltpu.VMEM((8, 128), F32), pltpu.VMEM((128, 128), F32)],
     )
     return (field, probability)

time: 116 us -> 115 us (level)
  waiting for transfers between devices: 23.4 us -> 22.1 us
  transfers between devices with their start and end apart: 17 -> 17, of which waited for: 6 -> 5; matrix products, arithmetic and copies ran while one was open for 0% -> 0% of each run, Pallas kernels for 8% -> 8%
where the time goes in v15:
time: 115 us; the launch traced here: 114 us
  starting transfers between devices  70.3 us (61%)
  waiting for transfers between devices  22.1 us (19%)
  Pallas kernels  18.8 us (16%)
  local copies, waits for them, and re-layouts  1.32 us (1%)
    ppermute x5, starting transfers between devices, swaps(): lax.ppermute(first, axis, pairs[0])  36 us
    pallas_call x11, Pallas kernels, call(): pl.pallas_call(kernel, out_shape=out, in_specs=specs or [VM] * len(args),...  18.8 us
    all_to_all x1, starting transfers between devices, body(): lax.all_to_all(table, ('gx', 'gz'), split_axis=0, concat_axis=0, tiled=True)  10.5 us
    ppermute x5, starting transfers between devices, swaps(): lax.ppermute(second, axis, pairs[1])  10.1 us
    ppermute x3, starting transfers between devices, both_ways(): lax.ppermute(to_up, axis, forward)  9.79 us
    all_to_all x1, waiting for transfers between devices, body(): lax.all_to_all(table, ('gx', 'gz'), split_axis=0, concat_axis=0, tiled=True)  5.81 us
    ppermute x5, waiting for transfers between devices, swaps(): lax.ppermute(first, axis, pairs[0])  5.21 us
    ppermute x5, waiting for transfers between devices, swaps(): lax.ppermute(second, axis, pairs[1])  4.43 us
  transfers between devices with their start and end apart: 17, of which 5 were waited for; matrix products, arithmetic and copies ran while one was open for 0% of the time, Pallas kernels for 8%

profile of v15, /device:TPU:1, one launch (start us, length us, event | category | flops | bytes accessed | tf_op | source)
XLA Modules:
  0.0 113.6 jit_solution(1254843734853580022)
XLA Ops:
  0.7 2.5 %start.1 = (f32[8,16,128]{2,1,0:T(8,128)S(1)}, f32[8,16,128]{2,1,0:T(8,128)S(1)}, f32[8,16,128]{2,1,0:T(8,128)}) custom-call(f32[3,8,16,128]{3,2,1,0:T(8,128)} %refs_0_.3, f32[3,8,16,128]{3,2,1,0:T(8,128)} %refs_1_.3, f32[8,16,128]{2,1,0:T(8,128)} %c_in.1, f32[8,16,128]{2,1,0:T(8,128)} %d_in.1), custom_call_target="tpu_custom_call" | custom-call | flops 16099999744 | tf_op jit(solution)/shard_map/start/pallas_call | solution.py:548
  3.1 8.8 %collective-permute-start.1 = (f32[8,16,128]{2,1,0:T(8,128)}, f32[8,16,128]{2,1,0:T(8,128)S(1)}, u32[]{:S(2)}, u32[]{:S(2)}) collective-permute-start(f32[8,16,128]{2,1,0:T(8,128)} %get-tuple-element.27), channel_id=1, source_target_pairs={{0,1},{2,3},{1,0},{3,2},{4,5},{6,7},{5,4},{7,6},{8,9},{10,11},{9,8... | collective-permute-start | bytes 196616 | tf_op jit(solution)/shard_map/ppermute | solution.py:571
  11.9 1.9 %collective-permute-start = (f32[8,16,128]{2,1,0:T(8,128)}, f32[8,16,128]{2,1,0:T(8,128)S(1)}, u32[]{:S(2)}, u32[]{:S(2)}) collective-permute-start(f32[8,16,128]{2,1,0:T(8,128)} %get-tuple-element.27), channel_id=1, source_target_pairs={{1,2},{2,1},{5,6},{6,5},{9,10},{10,9},{13,14},{14,13},{17,18},{18,... | collective-permute-start | bytes 196616 | tf_op jit(solution)/shard_map/ppermute | solution.py:571
  13.9 4.4 %collective-permute-done.refs_0_ = f32[8,16,128]{2,1,0:T(8,128)S(1)} collective-permute-done((f32[8,16,128]{2,1,0:T(8,128)}, f32[8,16,128]{2,1,0:T(8,128)S(1)}, u32[]{:S(2)}, u32[]{:S(2)}) %collective-permute-start) | collective-permute-done | bytes 65568 | tf_op jit(solution)/shard_map/ppermute | solution.py:571
  18.6 1.3 %collective-permute-start.2 = (s16[62,16,128]{2,1,0:T(8,128)(2,1)S(1)}, s16[62,16,128]{2,1,0:T(8,128)(2,1)S(1)}, u32[]{:S(2)}, u32[]{:S(2)}) collective-permute-start(s16[62,16,128]{2,1,0:T(8,128)(2,1)S(1)} %get-tuple-element.29), channel_id=1, source_target_pairs={{0,32},{32,64},{64,96},{96,128},{128,160},{160,192},{192,224},{224... | collective-permute-start | bytes 761864 | tf_op jit(solution)/shard_map/ppermute | solution.py:564
  19.9 1.3 %collective-permute-start.3 = (s16[62,16,128]{2,1,0:T(8,128)(2,1)S(1)}, s16[62,16,128]{2,1,0:T(8,128)(2,1)S(1)}, u32[]{:S(2)}, u32[]{:S(2)}) collective-permute-start(s16[62,16,128]{2,1,0:T(8,128)(2,1)S(1)} %get-tuple-element.30), channel_id=1, source_target_pairs={{32,0},{64,32},{96,64},{128,96},{160,128},{192,160},{224,192},{256... | collective-permute-start | bytes 761864 | tf_op jit(solution)/shard_map/ppermute | solution.py:564
  21.2 2.3 %collective-permute-done.2.refs_6_.refs_5_ = s16[62,16,128]{2,1,0:T(8,128)(2,1)S(1)} collective-permute-done((s16[62,16,128]{2,1,0:T(8,128)(2,1)S(1)}, s16[62,16,128]{2,1,0:T(8,128)(2,1)S(1)}, u32[]{:S(2)}, u32[]{:S(2)}) %collective-permute-start.2) | collective-permute-done | bytes 253984 | tf_op jit(solution)/shard_map/ppermute | solution.py:564
  23.5 4.3 %collective-permute-done.3.refs_7_.refs_6_ = s16[62,16,128]{2,1,0:T(8,128)(2,1)S(1)} collective-permute-done((s16[62,16,128]{2,1,0:T(8,128)(2,1)S(1)}, s16[62,16,128]{2,1,0:T(8,128)(2,1)S(1)}, u32[]{:S(2)}, u32[]{:S(2)}) %collective-permute-start.3) | collective-permute-done | bytes 253984 | tf_op jit(solution)/shard_map/ppermute | solution.py:564
  27.8 0.4 y_message.2
  28.2 5.7 %collective-permute-start.4 = (s16[97,16,128]{2,1,0:T(8,128)(2,1)S(1)}, s16[97,16,128]{2,1,0:T(8,128)(2,1)S(1)}, u32[]{:S(2)}, u32[]{:S(2)}) collective-permute-start(s16[97,16,128]{2,1,0:T(8,128)(2,1)S(1)} %get-tuple-element.32), channel_id=1, source_target_pairs={{0,4},{8,12},{16,20},{24,28},{4,0},{12,8},{20,16},{28,24},{1,5},{9... | collective-permute-start | bytes 1191944 | tf_op jit(solution)/shard_map/ppermute | solution.py:571
  33.9 0.7 collective-permute-start.5
  34.6 5.2 %collective-permute-done.4.refs_7_ = s16[97,16,128]{2,1,0:T(8,128)(2,1)S(1)} collective-permute-done((s16[97,16,128]{2,1,0:T(8,128)(2,1)S(1)}, s16[97,16,128]{2,1,0:T(8,128)(2,1)S(1)}, u32[]{:S(2)}, u32[]{:S(2)}) %collective-permute-start.4) | collective-permute-done | bytes 397344 | tf_op jit(solution)/shard_map/ppermute | solution.py:571
  39.8 5.4 %steps_first.1 = (f32[3,8,16,128]{3,2,1,0:T(8,128)S(1)}, f32[3,8,16,128]{3,2,1,0:T(8,128)S(1)}, f32[8,16,128]{2,1,0:T(8,128)S(1)}, f32[8,16,128]{2,1,0:T(8,128)S...) custom-call(f32[3,8,16,128]{3,2,1,0:T(8,128)S(1)} %copy-done, f32[3,8,16,128]{3,2,1,0:T(8,128)S(1)} %copy-done.1, ...), custom_call_target="tpu_custom_call" | custom-call | flops 77050003456 | tf_op jit(solution)/shard_map/steps_first/pallas_call | solution.py:548
  45.2 1.9 %collective-permute-start.7 = (f32[8,16,128]{2,1,0:T(8,128)S(1)}, f32[8,16,128]{2,1,0:T(8,128)S(1)}, u32[]{:S(2)}, u32[]{:S(2)}) collective-permute-start(f32[8,16,128]{2,1,0:T(8,128)S(1)} %get-tuple-element.36), channel_id=1, source_target_pairs={{0,1},{2,3},{1,0},{3,2},{4,5},{6,7},{5,4},{7,6},{8,9},{10,11},{9,8... | collective-permute-start | bytes 196616 | tf_op jit(solution)/shard_map/ppermute | solution.py:571
  47.1 6.2 %collective-permute-start.6 = (f32[8,16,128]{2,1,0:T(8,128)S(1)}, f32[8,16,128]{2,1,0:T(8,128)S(1)}, u32[]{:S(2)}, u32[]{:S(2)}) collective-permute-start(f32[8,16,128]{2,1,0:T(8,128)S(1)} %get-tuple-element.36), channel_id=1, source_target_pairs={{1,2},{2,1},{5,6},{6,5},{9,10},{10,9},{13,14},{14,13},{17,18},{18,... | collective-permute-start | bytes 196616 | tf_op jit(solution)/shard_map/ppermute | solution.py:571
  53.3 1.3 %collective-permute-start.13 = (f32[8,16,128]{2,1,0:T(8,128)S(1)}, f32[8,16,128]{2,1,0:T(8,128)S(1)}, u32[]{:S(2)}, u32[]{:S(2)}) collective-permute-start(f32[8,16,128]{2,1,0:T(8,128)S(1)} %get-tuple-element.44.own_ref.own_in), channel_id=1, source_target_pairs={{32,0},{64,32},{96,64},{128,96},{160,128},{192,160},{224,192},{256... | collective-permute-start | bytes 196616 | tf_op jit(solution)/shard_map/ppermute | solution.py:564
  54.6 4.9 %collective-permute-start.12 = (f32[8,16,128]{2,1,0:T(8,128)S(1)}, f32[8,16,128]{2,1,0:T(8,128)S(1)}, u32[]{:S(2)}, u32[]{:S(2)}) collective-permute-start(f32[8,16,128]{2,1,0:T(8,128)S(1)} %get-tuple-element.44.own_ref.own_in), channel_id=1, source_target_pairs={{0,32},{32,64},{64,96},{96,128},{128,160},{160,192},{192,224},{224... | collective-permute-start | bytes 196616 | tf_op jit(solution)/shard_map/ppermute | solution.py:564
  59.8 3.6 %collective-permute-start.8 = (s16[50,16,128]{2,1,0:T(8,128)(2,1)S(1)}, s16[50,16,128]{2,1,0:T(8,128)(2,1)S(1)}, u32[]{:S(2)}, u32[]{:S(2)}) collective-permute-start(s16[50,16,128]{2,1,0:T(8,128)(2,1)S(1)} %get-tuple-element.38), channel_id=1, source_target_pairs={{0,32},{32,64},{64,96},{96,128},{128,160},{160,192},{192,224},{224... | collective-permute-start | bytes 614408 | tf_op jit(solution)/shard_map/ppermute | solution.py:564
  63.4 1.3 %collective-permute-start.9 = (s16[50,16,128]{2,1,0:T(8,128)(2,1)S(1)}, s16[50,16,128]{2,1,0:T(8,128)(2,1)S(1)}, u32[]{:S(2)}, u32[]{:S(2)}) collective-permute-start(s16[50,16,128]{2,1,0:T(8,128)(2,1)S(1)} %get-tuple-element.39), channel_id=1, source_target_pairs={{32,0},{64,32},{96,64},{128,96},{160,128},{192,160},{224,192},{256... | collective-permute-start | bytes 614408 | tf_op jit(solution)/shard_map/ppermute | solution.py:564
  64.8 0.6 copy-done.9
  65.5 8.3 %collective-permute-start.14 = (f32[24,8,128]{2,1,0:T(8,128)S(1)}, f32[24,8,128]{2,1,0:T(8,128)S(1)}, u32[]{:S(2)}, u32[]{:S(2)}) collective-permute-start(f32[24,8,128]{2,1,0:T(8,128)S(1)} %get-tuple-element.45), channel_id=1, source_target_pairs={{0,4},{8,12},{16,20},{24,28},{4,0},{12,8},{20,16},{28,24},{1,5},{9... | collective-permute-start | bytes 294920 | tf_op jit(solution)/shard_map/ppermute | solution.py:571
  73.7 0.7 collective-permute-start.15
  74.4 0.3 y_message.3
  74.8 0.7 collective-permute-start.11
  75.5 11.3 %collective-permute-start.10 = (s16[77,16,128]{2,1,0:T(8,128)(2,1)S(1)}, s16[77,16,128]{2,1,0:T(8,128)(2,1)S(1)}, u32[]{:S(2)}, u32[]{:S(2)}) collective-permute-start(s16[77,16,128]{2,1,0:T(8,128)(2,1)S(1)} %get-tuple-element.41.after_in), channel_id=1, source_target_pairs={{0,4},{8,12},{16,20},{24,28},{4,0},{12,8},{20,16},{28,24},{1,5},{9... | collective-permute-start | bytes 946184 | tf_op jit(solution)/shard_map/ppermute | solution.py:571
  86.8 2.4 %surface.1.demand_ref = f32[8,128]{1,0:T(8,128)S(1)} custom-call(f32[8,16,128]{2,1,0:T(8,128)S(1)} %get-tuple-element.44.own_ref.own_in, f32[8,16,128]{2,1,0:T(8,128)S(1)} %collective-permute-done.12.low_ref.x_low, f32[8,16,128]{2,1,0:T(8,128)S(1)} %collective-permute-done.13.high_ref.x_high, f32[24,8,128]{2,1,0:T(8,128)S(1)} %collective-permute-done.14.y_first, ...), custom_call_target="tpu_custom_call" | custom-call | flops 46000001024 | tf_op jit(solution)/shard_map/surface/pallas_call | solution.py:548
  89.3 0.8 table.1
  90.1 10.5 %all-to-all-start = ((f32[64,8,128]{2,1,0:T(8,128)}), f32[64,8,128]{2,1,0:T(8,128)S(1)}, u32[]{:S(2)}, u32[]{:S(2)}) async-start(f32[64,8,128]{2,1,0:T(8,128)} %bitcast.9), calls=%async_computation | async-start | bytes 524288 | tf_op jit(solution)/shard_map/all_to_all | solution.py:684
  100.7 0.6 copy-done.5
  101.3 5.5 %steps_second.1 = f32[3,8,16,128]{3,2,1,0:T(8,128)} custom-call(f32[3,8,16,128]{3,2,1,0:T(8,128)S(1)} %get-tuple-element.34.refs_2_.refs_0_, f32[3,8,16,128]{3,2,1,0:T(8,128)S(1)} %get-tuple-element.35.refs_3_.refs_1_, f32[8,16,128]{2,1,0:T(8,128)S(1)} %get-tuple-element.37.refs_2_, s16[50,16,128]{2,1,0:T(8,128)(2,1)S(1)} %collective-permute-done.8.refs_4_.refs_3_, ...), custom_call_target="tpu_custom_call" | custom-call | flops 74750001152 | tf_op jit(solution)/shard_map/steps_second/pallas_call | solution.py:548
  106.8 5.8 %all-to-all-done = f32[64,8,128]{2,1,0:T(8,128)S(1)} async-done(((f32[64,8,128]{2,1,0:T(8,128)}), f32[64,8,128]{2,1,0:T(8,128)S(1)}, u32[]{:S(2)}, u32[]{:S(2)}) %all-to-all-start) | async-done | bytes 262176 | tf_op jit(solution)/shard_map/all_to_all | solution.py:684
  112.6 1.0 fragility.1
  (39 shorter events, 0.7 us)
Async XLA Ops:
  0.6 17.7 %copy-start.1 = (f32[3,8,16,128]{3,2,1,0:T(8,128)S(1)}, f32[3,8,16,128]{3,2,1,0:T(8,128)}, u32[]{:S(2)}) copy-start(f32[3,8,16,128]{3,2,1,0:T(8,128)} %refs_1_.3) | copy-start | bytes 589828
  0.6 17.7 %copy-start = (f32[3,8,16,128]{3,2,1,0:T(8,128)S(1)}, f32[3,8,16,128]{3,2,1,0:T(8,128)}, u32[]{:S(2)}) copy-start(f32[3,8,16,128]{3,2,1,0:T(8,128)} %refs_0_.3) | copy-start | bytes 589828
  3.1 10.7 %collective-permute-start.1 = (f32[8,16,128]{2,1,0:T(8,128)}, f32[8,16,128]{2,1,0:T(8,128)S(1)}, u32[]{:S(2)}, u32[]{:S(2)}) collective-permute-start(f32[8,16,128]{2,1,0:T(8,128)} %get-tuple-element.27), channel_id=1, source_target_pairs={{0,1},{2,3},{1,0},{3,2},{4,5},{6,7},{5,4},{7,6},{8,9},{10,11},{9,8... | collective-permute-start | bytes 196616 | tf_op jit(solution)/shard_map/ppermute | solution.py:571
  11.9 6.4 %collective-permute-start = (f32[8,16,128]{2,1,0:T(8,128)}, f32[8,16,128]{2,1,0:T(8,128)S(1)}, u32[]{:S(2)}, u32[]{:S(2)}) collective-permute-start(f32[8,16,128]{2,1,0:T(8,128)} %get-tuple-element.27), channel_id=1, source_target_pairs={{1,2},{2,1},{5,6},{6,5},{9,10},{10,9},{13,14},{14,13},{17,18},{18,... | collective-permute-start | bytes 196616 | tf_op jit(solution)/shard_map/ppermute | solution.py:571
  18.6 4.9 %collective-permute-start.2 = (s16[62,16,128]{2,1,0:T(8,128)(2,1)S(1)}, s16[62,16,128]{2,1,0:T(8,128)(2,1)S(1)}, u32[]{:S(2)}, u32[]{:S(2)}) collective-permute-start(s16[62,16,128]{2,1,0:T(8,128)(2,1)S(1)} %get-tuple-element.29), channel_id=1, source_target_pairs={{0,32},{32,64},{64,96},{96,128},{128,160},{160,192},{192,224},{224... | collective-permute-start | bytes 761864 | tf_op jit(solution)/shard_map/ppermute | solution.py:564
  19.9 7.9 %collective-permute-start.3 = (s16[62,16,128]{2,1,0:T(8,128)(2,1)S(1)}, s16[62,16,128]{2,1,0:T(8,128)(2,1)S(1)}, u32[]{:S(2)}, u32[]{:S(2)}) collective-permute-start(s16[62,16,128]{2,1,0:T(8,128)(2,1)S(1)} %get-tuple-element.30), channel_id=1, source_target_pairs={{32,0},{64,32},{96,64},{128,96},{160,128},{192,160},{224,192},{256... | collective-permute-start | bytes 761864 | tf_op jit(solution)/shard_map/ppermute | solution.py:564
  27.8 12.0 %copy-start.11 = (bf16[3,256,256]{2,1,0:T(8,128)(2,1)S(1)}, bf16[3,256,256]{2,1,0:T(8,128)(2,1)}, u32[]{:S(2)}) copy-start(bf16[3,256,256]{2,1,0:T(8,128)(2,1)} %constant.4.clone.refs_9_.refs_7_) | copy-start | bytes 1179652
  28.2 11.6 %collective-permute-start.4 = (s16[97,16,128]{2,1,0:T(8,128)(2,1)S(1)}, s16[97,16,128]{2,1,0:T(8,128)(2,1)S(1)}, u32[]{:S(2)}, u32[]{:S(2)}) collective-permute-start(s16[97,16,128]{2,1,0:T(8,128)(2,1)S(1)} %get-tuple-element.32), channel_id=1, source_target_pairs={{0,4},{8,12},{16,20},{24,28},{4,0},{12,8},{20,16},{28,24},{1,5},{9... | collective-permute-start | bytes 1191944 | tf_op jit(solution)/shard_map/ppermute | solution.py:571
  33.9 5.9 %collective-permute-start.5 = (s16[97,16,128]{2,1,0:T(8,128)(2,1)S(1)}, s16[97,16,128]{2,1,0:T(8,128)(2,1)S(1)}, u32[]{:S(2)}, u32[]{:S(2)}) collective-permute-start(s16[97,16,128]{2,1,0:T(8,128)(2,1)S(1)} %get-tuple-element.33), channel_id=1, source_target_pairs={{4,8},{12,16},{20,24},{8,4},{16,12},{24,20},{5,9},{13,17},{21,25},... | collective-permute-start | bytes 1191944 | tf_op jit(solution)/shard_map/ppermute | solution.py:571
  45.2 14.3 %collective-permute-start.7 = (f32[8,16,128]{2,1,0:T(8,128)S(1)}, f32[8,16,128]{2,1,0:T(8,128)S(1)}, u32[]{:S(2)}, u32[]{:S(2)}) collective-permute-start(f32[8,16,128]{2,1,0:T(8,128)S(1)} %get-tuple-element.36), channel_id=1, source_target_pairs={{0,1},{2,3},{1,0},{3,2},{4,5},{6,7},{5,4},{7,6},{8,9},{10,11},{9,8... | collective-permute-start | bytes 196616 | tf_op jit(solution)/shard_map/ppermute | solution.py:571
  47.1 12.4 %collective-permute-start.6 = (f32[8,16,128]{2,1,0:T(8,128)S(1)}, f32[8,16,128]{2,1,0:T(8,128)S(1)}, u32[]{:S(2)}, u32[]{:S(2)}) collective-permute-start(f32[8,16,128]{2,1,0:T(8,128)S(1)} %get-tuple-element.36), channel_id=1, source_target_pairs={{1,2},{2,1},{5,6},{6,5},{9,10},{10,9},{13,14},{14,13},{17,18},{18,... | collective-permute-start | bytes 196616 | tf_op jit(solution)/shard_map/ppermute | solution.py:571
  53.3 11.4 %collective-permute-start.13 = (f32[8,16,128]{2,1,0:T(8,128)S(1)}, f32[8,16,128]{2,1,0:T(8,128)S(1)}, u32[]{:S(2)}, u32[]{:S(2)}) collective-permute-start(f32[8,16,128]{2,1,0:T(8,128)S(1)} %get-tuple-element.44.own_ref.own_in), channel_id=1, source_target_pairs={{32,0},{64,32},{96,64},{128,96},{160,128},{192,160},{224,192},{256... | collective-permute-start | bytes 196616 | tf_op jit(solution)/shard_map/ppermute | solution.py:564
  54.6 10.2 %collective-permute-start.12 = (f32[8,16,128]{2,1,0:T(8,128)S(1)}, f32[8,16,128]{2,1,0:T(8,128)S(1)}, u32[]{:S(2)}, u32[]{:S(2)}) collective-permute-start(f32[8,16,128]{2,1,0:T(8,128)S(1)} %get-tuple-element.44.own_ref.own_in), channel_id=1, source_target_pairs={{0,32},{32,64},{64,96},{96,128},{128,160},{160,192},{192,224},{224... | collective-permute-start | bytes 196616 | tf_op jit(solution)/shard_map/ppermute | solution.py:564
  59.5 5.3 %copy-start.3 = (bf16[64,24]{0,1:T(8,128)(2,1)S(1)}, bf16[64,24]{0,1:T(8,128)(2,1)}, u32[]{:S(2)}) copy-start(bf16[64,24]{0,1:T(8,128)(2,1)} %param.24) | copy-start | bytes 9220
  59.5 5.3 %copy-start.12 = (bf16[256,128]{1,0:T(8,128)(2,1)S(1)}, bf16[256,128]{1,0:T(8,128)(2,1)}, u32[]{:S(2)}) copy-start(bf16[256,128]{1,0:T(8,128)(2,1)} %constant.5.clone.refs_2_.weight_in) | copy-start | bytes 196612
  59.8 5.0 %copy-start.2 = (s32[16,1,128]{2,1,0:T(1,128)S(1)}, s32[16,1,128]{2,1,0:T(1,128)}, u32[]{:S(2)}) copy-start(s32[16,1,128]{2,1,0:T(1,128)} %param.19) | copy-start | bytes 24580
  59.8 14.6 %collective-permute-start.8 = (s16[50,16,128]{2,1,0:T(8,128)(2,1)S(1)}, s16[50,16,128]{2,1,0:T(8,128)(2,1)S(1)}, u32[]{:S(2)}, u32[]{:S(2)}) collective-permute-start(s16[50,16,128]{2,1,0:T(8,128)(2,1)S(1)} %get-tuple-element.38), channel_id=1, source_target_pairs={{0,32},{32,64},{64,96},{96,128},{128,160},{160,192},{192,224},{224... | collective-permute-start | bytes 614408 | tf_op jit(solution)/shard_map/ppermute | solution.py:564
  63.4 11.0 %collective-permute-start.9 = (s16[50,16,128]{2,1,0:T(8,128)(2,1)S(1)}, s16[50,16,128]{2,1,0:T(8,128)(2,1)S(1)}, u32[]{:S(2)}, u32[]{:S(2)}) collective-permute-start(s16[50,16,128]{2,1,0:T(8,128)(2,1)S(1)} %get-tuple-element.39), channel_id=1, source_target_pairs={{32,0},{64,32},{96,64},{128,96},{160,128},{192,160},{224,192},{256... | collective-permute-start | bytes 614408 | tf_op jit(solution)/shard_map/ppermute | solution.py:564
  64.8 0.7 copy-start.9
  65.5 21.3 %collective-permute-start.14 = (f32[24,8,128]{2,1,0:T(8,128)S(1)}, f32[24,8,128]{2,1,0:T(8,128)S(1)}, u32[]{:S(2)}, u32[]{:S(2)}) collective-permute-start(f32[24,8,128]{2,1,0:T(8,128)S(1)} %get-tuple-element.45), channel_id=1, source_target_pairs={{0,4},{8,12},{16,20},{24,28},{4,0},{12,8},{20,16},{28,24},{1,5},{9... | collective-permute-start | bytes 294920 | tf_op jit(solution)/shard_map/ppermute | solution.py:571
  73.7 13.0 %collective-permute-start.15 = (f32[24,8,128]{2,1,0:T(8,128)S(1)}, f32[24,8,128]{2,1,0:T(8,128)S(1)}, u32[]{:S(2)}, u32[]{:S(2)}) collective-permute-start(f32[24,8,128]{2,1,0:T(8,128)S(1)} %get-tuple-element.46), channel_id=1, source_target_pairs={{4,8},{12,16},{20,24},{8,4},{16,12},{24,20},{5,9},{13,17},{21,25},... | collective-permute-start | bytes 294920 | tf_op jit(solution)/shard_map/ppermute | solution.py:571
  74.8 25.8 %collective-permute-start.11 = (s16[77,16,128]{2,1,0:T(8,128)(2,1)S(1)}, s16[77,16,128]{2,1,0:T(8,128)(2,1)S(1)}, u32[]{:S(2)}, u32[]{:S(2)}) collective-permute-start(s16[77,16,128]{2,1,0:T(8,128)(2,1)S(1)} %get-tuple-element.42), channel_id=1, source_target_pairs={{4,8},{12,16},{20,24},{8,4},{16,12},{24,20},{5,9},{13,17},{21,25},... | collective-permute-start | bytes 946184 | tf_op jit(solution)/shard_map/ppermute | solution.py:571
  75.5 25.2 %collective-permute-start.10 = (s16[77,16,128]{2,1,0:T(8,128)(2,1)S(1)}, s16[77,16,128]{2,1,0:T(8,128)(2,1)S(1)}, u32[]{:S(2)}, u32[]{:S(2)}) collective-permute-start(s16[77,16,128]{2,1,0:T(8,128)(2,1)S(1)} %get-tuple-element.41.after_in), channel_id=1, source_target_pairs={{0,4},{8,12},{16,20},{24,28},{4,0},{12,8},{20,16},{28,24},{1,5},{9... | collective-permute-start | bytes 946184 | tf_op jit(solution)/shard_map/ppermute | solution.py:571
  89.2 11.5 %copy-start.6 = (s32[1024]{0:T(1024)S(1)}, s32[1024]{0:T(1024)}, u32[]{:S(2)}) copy-start(s32[1024]{0:T(1024)} %param.22) | copy-start | bytes 12292
  89.2 11.4 %copy-start.7 = (f32[16,8]{0,1:T(8,128)S(1)}, f32[16,8]{0,1:T(8,128)}, u32[]{:S(2)}) copy-start(f32[16,8]{0,1:T(8,128)} %param.26) | copy-start | bytes 1540
  89.2 11.4 %copy-start.8 = (f32[16,8]{0,1:T(8,128)S(1)}, f32[16,8]{0,1:T(8,128)}, u32[]{:S(2)}) copy-start(f32[16,8]{0,1:T(8,128)} %param.27) | copy-start | bytes 1540
  90.1 22.6 %all-to-all-start = ((f32[64,8,128]{2,1,0:T(8,128)}), f32[64,8,128]{2,1,0:T(8,128)S(1)}, u32[]{:S(2)}, u32[]{:S(2)}) async-start(f32[64,8,128]{2,1,0:T(8,128)} %bitcast.9), calls=%async_computation | async-start | bytes 524288 | tf_op jit(solution)/shard_map/all_to_all | solution.py:684
  100.6 0.7 copy-start.5
  100.6 0.7 copy-start.4
  100.7 0.7 copy-start.10

commit v16 on v15

--- a/solution.py
+++ b/solution.py
@@ -398,8 +398,8 @@
 
 
 def surface_kernel(
-    own_in, x_low, x_high, y_first, y_second, weight_in, code_in, seen_in, filter_in, count_in, after_in,
-    demand_out, state_ref, rate_ref, sample_ref, seen_ref, filter_ref, count_ref,
+    own_in, x_low, x_high, y_first, y_second, weight_in, code_in, seen_in, filter_in, count_in, cells_in, after_in,
+    table_out, state_ref, rate_ref, sample_ref, seen_ref, filter_ref, count_ref,
 ):
     lane = lane_of()
     inner = lane % 16
@@ -492,13 +492,9 @@
         part = modal[MODES * kind : MODES * (kind + 1), :]
         part = jnp.where(modes < counts[kind : kind + 1, :], part * part, 0.0)
         energies.append(jnp.sum(part, axis=0, keepdims=True))
-    demand_out[...] = 0.5 * jnp.log1p(jnp.concatenate(energies, axis=0))
-
-
-def table_kernel(demand_ref, cells_ref, table_out):
-    demand = demand_ref[...]
+    demand = 0.5 * jnp.log1p(jnp.concatenate(energies, axis=0))
     for owner in range(table_out.shape[0]):
-        cells = jnp.broadcast_to(cells_ref[owner : owner + 1, :], (CLASSES, 128))
+        cells = jnp.broadcast_to(cells_in[owner : owner + 1, :], (CLASSES, 128))
         chosen = jnp.take_along_axis(demand, cells, axis=1)
         for level in range(table_out.shape[1]):
             table_out[owner, level] = chosen
@@ -659,12 +655,12 @@
     side_first, side_second = swaps(*slab_messages, "gy")
     messages = y_messages(u, p, (), halo, powers, x_low, x_high)
     received = (halo, x_low, x_high, *swaps(*messages, "gy"))
-    (demand,) = call(
+    (table,) = call(
         surface_kernel,
         "surface",
-        [(CLASSES, 128)],
-        [slab, near_low, near_high, side_first, side_second, slab_inputs[0], codes, seen] + slab_inputs[1:] + [messages[0]],
-        specs=[VM] * 10 + [pl.BlockSpec(memory_space=pl.ANY)],
+        [(owners, levels, CLASSES, 128)],
+        [slab, near_low, near_high, side_first, side_second, slab_inputs[0], codes, seen] + slab_inputs[1:] + [cells, messages[0]],
+        specs=[VM] * 11 + [pl.BlockSpec(memory_space=pl.ANY)],
         scratch=[
             pltpu.VMEM((2, 24, 48, 128), F32),
             pltpu.VMEM((2, 24, 32, 128), F32),
@@ -673,12 +669,6 @@
             pltpu.VMEM((3 * STEPS, CLASSES * MODES), F32),
             pltpu.VMEM((8, 128), jnp.int32),
         ],
-    )
-    (table,) = call(
-        table_kernel,
-        "table",
-        [(owners, levels, CLASSES, 128)],
-        [demand, cells],
     )
     table = table.reshape(owners * levels, CLASSES, 128)
     table = lax.all_to_all(table, ("gx", "gz"), split_axis=0, concat_axis=0, tiled=True)

time: 115 us -> 115 us (level)
    pallas_call x11 -> x10, Pallas kernels: 18.8 us -> 18.8 us  [call(): pl.pallas_call(kernel, out_shape=out, in_specs=specs or [VM] * len(args),...]
where the time goes in v16:
time: 115 us; the launch traced here: 114 us
  starting transfers between devices  70.3 us (61%)
  waiting for transfers between devices  22.1 us (19%)
  Pallas kernels  18.8 us (16%)
  local copies, waits for them, and re-layouts  1.32 us (1%)
    ppermute x5, starting transfers between devices, swaps(): lax.ppermute(first, axis, pairs[0])  36 us
    pallas_call x10, Pallas kernels, call(): pl.pallas_call(kernel, out_shape=out, in_specs=specs or [VM] * len(args),...  18.8 us
    all_to_all x1, starting transfers between devices, body(): lax.all_to_all(table, ('gx', 'gz'), split_axis=0, concat_axis=0, tiled=True)  10.5 us
    ppermute x5, starting transfers between devices, swaps(): lax.ppermute(second, axis, pairs[1])  10.1 us
    ppermute x3, starting transfers between devices, both_ways(): lax.ppermute(to_up, axis, forward)  9.79 us
    all_to_all x1, waiting for transfers between devices, body(): lax.all_to_all(table, ('gx', 'gz'), split_axis=0, concat_axis=0, tiled=True)  5.81 us
    ppermute x5, waiting for transfers between devices, swaps(): lax.ppermute(first, axis, pairs[0])  5.21 us
    ppermute x5, waiting for transfers between devices, swaps(): lax.ppermute(second, axis, pairs[1])  4.43 us
  transfers between devices with their start and end apart: 17, of which 5 were waited for; matrix products, arithmetic and copies ran while one was open for 0% of the time, Pallas kernels for 8%

profile of v16, /device:TPU:1, one launch (start us, length us, event | category | flops | bytes accessed | tf_op | source)
XLA Modules:
  0.0 113.6 jit_solution(11483843392721319522)
XLA Ops:
  0.7 2.5 %start.1 = (f32[8,16,128]{2,1,0:T(8,128)S(1)}, f32[8,16,128]{2,1,0:T(8,128)S(1)}, f32[8,16,128]{2,1,0:T(8,128)}) custom-call(f32[3,8,16,128]{3,2,1,0:T(8,128)} %refs_0_.3, f32[3,8,16,128]{3,2,1,0:T(8,128)} %refs_1_.3, f32[8,16,128]{2,1,0:T(8,128)} %c_in.1, f32[8,16,128]{2,1,0:T(8,128)} %d_in.1), custom_call_target="tpu_custom_call" | custom-call | flops 16099999744 | tf_op jit(solution)/shard_map/start/pallas_call | solution.py:544
  3.1 8.8 %collective-permute-start.1 = (f32[8,16,128]{2,1,0:T(8,128)}, f32[8,16,128]{2,1,0:T(8,128)S(1)}, u32[]{:S(2)}, u32[]{:S(2)}) collective-permute-start(f32[8,16,128]{2,1,0:T(8,128)} %get-tuple-element.27), channel_id=1, source_target_pairs={{0,1},{2,3},{1,0},{3,2},{4,5},{6,7},{5,4},{7,6},{8,9},{10,11},{9,8... | collective-permute-start | bytes 196616 | tf_op jit(solution)/shard_map/ppermute | solution.py:567
  11.9 1.9 %collective-permute-start = (f32[8,16,128]{2,1,0:T(8,128)}, f32[8,16,128]{2,1,0:T(8,128)S(1)}, u32[]{:S(2)}, u32[]{:S(2)}) collective-permute-start(f32[8,16,128]{2,1,0:T(8,128)} %get-tuple-element.27), channel_id=1, source_target_pairs={{1,2},{2,1},{5,6},{6,5},{9,10},{10,9},{13,14},{14,13},{17,18},{18,... | collective-permute-start | bytes 196616 | tf_op jit(solution)/shard_map/ppermute | solution.py:567
  13.9 4.4 %collective-permute-done.refs_0_ = f32[8,16,128]{2,1,0:T(8,128)S(1)} collective-permute-done((f32[8,16,128]{2,1,0:T(8,128)}, f32[8,16,128]{2,1,0:T(8,128)S(1)}, u32[]{:S(2)}, u32[]{:S(2)}) %collective-permute-start) | collective-permute-done | bytes 65568 | tf_op jit(solution)/shard_map/ppermute | solution.py:567
  18.3 0.3 x_message.2
  18.6 1.3 %collective-permute-start.2 = (s16[62,16,128]{2,1,0:T(8,128)(2,1)S(1)}, s16[62,16,128]{2,1,0:T(8,128)(2,1)S(1)}, u32[]{:S(2)}, u32[]{:S(2)}) collective-permute-start(s16[62,16,128]{2,1,0:T(8,128)(2,1)S(1)} %get-tuple-element.29), channel_id=1, source_target_pairs={{0,32},{32,64},{64,96},{96,128},{128,160},{160,192},{192,224},{224... | collective-permute-start | bytes 761864 | tf_op jit(solution)/shard_map/ppermute | solution.py:560
  19.9 1.3 %collective-permute-start.3 = (s16[62,16,128]{2,1,0:T(8,128)(2,1)S(1)}, s16[62,16,128]{2,1,0:T(8,128)(2,1)S(1)}, u32[]{:S(2)}, u32[]{:S(2)}) collective-permute-start(s16[62,16,128]{2,1,0:T(8,128)(2,1)S(1)} %get-tuple-element.30), channel_id=1, source_target_pairs={{32,0},{64,32},{96,64},{128,96},{160,128},{192,160},{224,192},{256... | collective-permute-start | bytes 761864 | tf_op jit(solution)/shard_map/ppermute | solution.py:560
  21.2 2.3 %collective-permute-done.2.refs_6_.refs_5_ = s16[62,16,128]{2,1,0:T(8,128)(2,1)S(1)} collective-permute-done((s16[62,16,128]{2,1,0:T(8,128)(2,1)S(1)}, s16[62,16,128]{2,1,0:T(8,128)(2,1)S(1)}, u32[]{:S(2)}, u32[]{:S(2)}) %collective-permute-start.2) | collective-permute-done | bytes 253984 | tf_op jit(solution)/shard_map/ppermute | solution.py:560
  23.5 4.3 %collective-permute-done.3.refs_7_.refs_6_ = s16[62,16,128]{2,1,0:T(8,128)(2,1)S(1)} collective-permute-done((s16[62,16,128]{2,1,0:T(8,128)(2,1)S(1)}, s16[62,16,128]{2,1,0:T(8,128)(2,1)S(1)}, u32[]{:S(2)}, u32[]{:S(2)}) %collective-permute-start.3) | collective-permute-done | bytes 253984 | tf_op jit(solution)/shard_map/ppermute | solution.py:560
  27.8 0.4 y_message.2
  28.2 5.7 %collective-permute-start.4 = (s16[97,16,128]{2,1,0:T(8,128)(2,1)S(1)}, s16[97,16,128]{2,1,0:T(8,128)(2,1)S(1)}, u32[]{:S(2)}, u32[]{:S(2)}) collective-permute-start(s16[97,16,128]{2,1,0:T(8,128)(2,1)S(1)} %get-tuple-element.32), channel_id=1, source_target_pairs={{0,4},{8,12},{16,20},{24,28},{4,0},{12,8},{20,16},{28,24},{1,5},{9... | collective-permute-start | bytes 1191944 | tf_op jit(solution)/shard_map/ppermute | solution.py:567
  33.9 0.7 collective-permute-start.5
  34.6 5.2 %collective-permute-done.4.refs_7_ = s16[97,16,128]{2,1,0:T(8,128)(2,1)S(1)} collective-permute-done((s16[97,16,128]{2,1,0:T(8,128)(2,1)S(1)}, s16[97,16,128]{2,1,0:T(8,128)(2,1)S(1)}, u32[]{:S(2)}, u32[]{:S(2)}) %collective-permute-start.4) | collective-permute-done | bytes 397344 | tf_op jit(solution)/shard_map/ppermute | solution.py:567
  39.8 5.4 %steps_first.1 = (f32[3,8,16,128]{3,2,1,0:T(8,128)S(1)}, f32[3,8,16,128]{3,2,1,0:T(8,128)S(1)}, f32[8,16,128]{2,1,0:T(8,128)S(1)}, f32[8,16,128]{2,1,0:T(8,128)S...) custom-call(f32[3,8,16,128]{3,2,1,0:T(8,128)S(1)} %copy-done, f32[3,8,16,128]{3,2,1,0:T(8,128)S(1)} %copy-done.1, ...), custom_call_target="tpu_custom_call" | custom-call | flops 77050003456 | tf_op jit(solution)/shard_map/steps_first/pallas_call | solution.py:544
  45.2 1.9 %collective-permute-start.7 = (f32[8,16,128]{2,1,0:T(8,128)S(1)}, f32[8,16,128]{2,1,0:T(8,128)S(1)}, u32[]{:S(2)}, u32[]{:S(2)}) collective-permute-start(f32[8,16,128]{2,1,0:T(8,128)S(1)} %get-tuple-element.36), channel_id=1, source_target_pairs={{0,1},{2,3},{1,0},{3,2},{4,5},{6,7},{5,4},{7,6},{8,9},{10,11},{9,8... | collective-permute-start | bytes 196616 | tf_op jit(solution)/shard_map/ppermute | solution.py:567
  47.1 6.2 %collective-permute-start.6 = (f32[8,16,128]{2,1,0:T(8,128)S(1)}, f32[8,16,128]{2,1,0:T(8,128)S(1)}, u32[]{:S(2)}, u32[]{:S(2)}) collective-permute-start(f32[8,16,128]{2,1,0:T(8,128)S(1)} %get-tuple-element.36), channel_id=1, source_target_pairs={{1,2},{2,1},{5,6},{6,5},{9,10},{10,9},{13,14},{14,13},{17,18},{18,... | collective-permute-start | bytes 196616 | tf_op jit(solution)/shard_map/ppermute | solution.py:567
  53.3 1.3 %collective-permute-start.13 = (f32[8,16,128]{2,1,0:T(8,128)S(1)}, f32[8,16,128]{2,1,0:T(8,128)S(1)}, u32[]{:S(2)}, u32[]{:S(2)}) collective-permute-start(f32[8,16,128]{2,1,0:T(8,128)S(1)} %get-tuple-element.44.own_ref.own_in), channel_id=1, source_target_pairs={{32,0},{64,32},{96,64},{128,96},{160,128},{192,160},{224,192},{256... | collective-permute-start | bytes 196616 | tf_op jit(solution)/shard_map/ppermute | solution.py:560
  54.6 4.9 %collective-permute-start.12 = (f32[8,16,128]{2,1,0:T(8,128)S(1)}, f32[8,16,128]{2,1,0:T(8,128)S(1)}, u32[]{:S(2)}, u32[]{:S(2)}) collective-permute-start(f32[8,16,128]{2,1,0:T(8,128)S(1)} %get-tuple-element.44.own_ref.own_in), channel_id=1, source_target_pairs={{0,32},{32,64},{64,96},{96,128},{128,160},{160,192},{192,224},{224... | collective-permute-start | bytes 196616 | tf_op jit(solution)/shard_map/ppermute | solution.py:560
  59.8 3.6 %collective-permute-start.8 = (s16[50,16,128]{2,1,0:T(8,128)(2,1)S(1)}, s16[50,16,128]{2,1,0:T(8,128)(2,1)S(1)}, u32[]{:S(2)}, u32[]{:S(2)}) collective-permute-start(s16[50,16,128]{2,1,0:T(8,128)(2,1)S(1)} %get-tuple-element.38), channel_id=1, source_target_pairs={{0,32},{32,64},{64,96},{96,128},{128,160},{160,192},{192,224},{224... | collective-permute-start | bytes 614408 | tf_op jit(solution)/shard_map/ppermute | solution.py:560
  63.4 1.3 %collective-permute-start.9 = (s16[50,16,128]{2,1,0:T(8,128)(2,1)S(1)}, s16[50,16,128]{2,1,0:T(8,128)(2,1)S(1)}, u32[]{:S(2)}, u32[]{:S(2)}) collective-permute-start(s16[50,16,128]{2,1,0:T(8,128)(2,1)S(1)} %get-tuple-element.39), channel_id=1, source_target_pairs={{32,0},{64,32},{96,64},{128,96},{160,128},{192,160},{224,192},{256... | collective-permute-start | bytes 614408 | tf_op jit(solution)/shard_map/ppermute | solution.py:560
  64.8 0.6 copy-done.9
  65.5 8.3 %collective-permute-start.14 = (f32[24,8,128]{2,1,0:T(8,128)S(1)}, f32[24,8,128]{2,1,0:T(8,128)S(1)}, u32[]{:S(2)}, u32[]{:S(2)}) collective-permute-start(f32[24,8,128]{2,1,0:T(8,128)S(1)} %get-tuple-element.45), channel_id=1, source_target_pairs={{0,4},{8,12},{16,20},{24,28},{4,0},{12,8},{20,16},{28,24},{1,5},{9... | collective-permute-start | bytes 294920 | tf_op jit(solution)/shard_map/ppermute | solution.py:567
  73.7 0.7 collective-permute-start.15
  74.4 0.3 y_message.3
  74.8 0.7 collective-permute-start.11
  75.5 11.3 %collective-permute-start.10 = (s16[77,16,128]{2,1,0:T(8,128)(2,1)S(1)}, s16[77,16,128]{2,1,0:T(8,128)(2,1)S(1)}, u32[]{:S(2)}, u32[]{:S(2)}) collective-permute-start(s16[77,16,128]{2,1,0:T(8,128)(2,1)S(1)} %get-tuple-element.41.after_in), channel_id=1, source_target_pairs={{0,4},{8,12},{16,20},{24,28},{4,0},{12,8},{20,16},{28,24},{1,5},{9... | collective-permute-start | bytes 946184 | tf_op jit(solution)/shard_map/ppermute | solution.py:567
  86.8 3.2 %surface.1 = f32[16,4,8,128]{3,2,1,0:T(8,128)} custom-call(f32[8,16,128]{2,1,0:T(8,128)S(1)} %get-tuple-element.44.own_ref.own_in, f32[8,16,128]{2,1,0:T(8,128)S(1)} %collective-permute-done.12.low_ref.x_low, f32[8,16,128]{2,1,0:T(8,128)S(1)} %collective-permute-done.13.high_ref.x_high, f32[24,8,128]{2,1,0:T(8,128)S(1)} %collective-permute-done.14.y_first, ...), custom_call_target="tpu_custom_call" | custom-call | flops 46000001024 | tf_op jit(solution)/shard_map/surface/pallas_call | solution.py:544
  90.1 10.5 %all-to-all-start = ((f32[64,8,128]{2,1,0:T(8,128)}), f32[64,8,128]{2,1,0:T(8,128)S(1)}, u32[]{:S(2)}, u32[]{:S(2)}) async-start(f32[64,8,128]{2,1,0:T(8,128)} %bitcast.9), calls=%async_computation | async-start | bytes 524288 | tf_op jit(solution)/shard_map/all_to_all | solution.py:674
  100.7 0.6 copy-done.5
  101.3 5.5 %steps_second.1 = f32[3,8,16,128]{3,2,1,0:T(8,128)} custom-call(f32[3,8,16,128]{3,2,1,0:T(8,128)S(1)} %get-tuple-element.34.refs_2_.refs_0_, f32[3,8,16,128]{3,2,1,0:T(8,128)S(1)} %get-tuple-element.35.refs_3_.refs_1_, f32[8,16,128]{2,1,0:T(8,128)S(1)} %get-tuple-element.37.refs_2_, s16[50,16,128]{2,1,0:T(8,128)(2,1)S(1)} %collective-permute-done.8.refs_4_.refs_3_, ...), custom_call_target="tpu_custom_call" | custom-call | flops 74750001152 | tf_op jit(solution)/shard_map/steps_second/pallas_call | solution.py:544
  106.8 5.8 %all-to-all-done = f32[64,8,128]{2,1,0:T(8,128)S(1)} async-done(((f32[64,8,128]{2,1,0:T(8,128)}), f32[64,8,128]{2,1,0:T(8,128)S(1)}, u32[]{:S(2)}, u32[]{:S(2)}) %all-to-all-start) | async-done | bytes 262176 | tf_op jit(solution)/shard_map/all_to_all | solution.py:674
  112.6 1.0 fragility.1
  (38 shorter events, 0.4 us)
Async XLA Ops:
  0.6 17.7 %copy-start.1 = (f32[3,8,16,128]{3,2,1,0:T(8,128)S(1)}, f32[3,8,16,128]{3,2,1,0:T(8,128)}, u32[]{:S(2)}) copy-start(f32[3,8,16,128]{3,2,1,0:T(8,128)} %refs_1_.3) | copy-start | bytes 589828
  0.6 17.7 %copy-start = (f32[3,8,16,128]{3,2,1,0:T(8,128)S(1)}, f32[3,8,16,128]{3,2,1,0:T(8,128)}, u32[]{:S(2)}) copy-start(f32[3,8,16,128]{3,2,1,0:T(8,128)} %refs_0_.3) | copy-start | bytes 589828
  3.1 10.7 %collective-permute-start.1 = (f32[8,16,128]{2,1,0:T(8,128)}, f32[8,16,128]{2,1,0:T(8,128)S(1)}, u32[]{:S(2)}, u32[]{:S(2)}) collective-permute-start(f32[8,16,128]{2,1,0:T(8,128)} %get-tuple-element.27), channel_id=1, source_target_pairs={{0,1},{2,3},{1,0},{3,2},{4,5},{6,7},{5,4},{7,6},{8,9},{10,11},{9,8... | collective-permute-start | bytes 196616 | tf_op jit(solution)/shard_map/ppermute | solution.py:567
  11.9 6.4 %collective-permute-start = (f32[8,16,128]{2,1,0:T(8,128)}, f32[8,16,128]{2,1,0:T(8,128)S(1)}, u32[]{:S(2)}, u32[]{:S(2)}) collective-permute-start(f32[8,16,128]{2,1,0:T(8,128)} %get-tuple-element.27), channel_id=1, source_target_pairs={{1,2},{2,1},{5,6},{6,5},{9,10},{10,9},{13,14},{14,13},{17,18},{18,... | collective-permute-start | bytes 196616 | tf_op jit(solution)/shard_map/ppermute | solution.py:567
  18.6 4.9 %collective-permute-start.2 = (s16[62,16,128]{2,1,0:T(8,128)(2,1)S(1)}, s16[62,16,128]{2,1,0:T(8,128)(2,1)S(1)}, u32[]{:S(2)}, u32[]{:S(2)}) collective-permute-start(s16[62,16,128]{2,1,0:T(8,128)(2,1)S(1)} %get-tuple-element.29), channel_id=1, source_target_pairs={{0,32},{32,64},{64,96},{96,128},{128,160},{160,192},{192,224},{224... | collective-permute-start | bytes 761864 | tf_op jit(solution)/shard_map/ppermute | solution.py:560
  19.9 7.9 %collective-permute-start.3 = (s16[62,16,128]{2,1,0:T(8,128)(2,1)S(1)}, s16[62,16,128]{2,1,0:T(8,128)(2,1)S(1)}, u32[]{:S(2)}, u32[]{:S(2)}) collective-permute-start(s16[62,16,128]{2,1,0:T(8,128)(2,1)S(1)} %get-tuple-element.30), channel_id=1, source_target_pairs={{32,0},{64,32},{96,64},{128,96},{160,128},{192,160},{224,192},{256... | collective-permute-start | bytes 761864 | tf_op jit(solution)/shard_map/ppermute | solution.py:560
  27.8 12.0 %copy-start.11 = (bf16[3,256,256]{2,1,0:T(8,128)(2,1)S(1)}, bf16[3,256,256]{2,1,0:T(8,128)(2,1)}, u32[]{:S(2)}) copy-start(bf16[3,256,256]{2,1,0:T(8,128)(2,1)} %constant.4.clone.refs_9_.refs_7_) | copy-start | bytes 1179652
  28.2 11.6 %collective-permute-start.4 = (s16[97,16,128]{2,1,0:T(8,128)(2,1)S(1)}, s16[97,16,128]{2,1,0:T(8,128)(2,1)S(1)}, u32[]{:S(2)}, u32[]{:S(2)}) collective-permute-start(s16[97,16,128]{2,1,0:T(8,128)(2,1)S(1)} %get-tuple-element.32), channel_id=1, source_target_pairs={{0,4},{8,12},{16,20},{24,28},{4,0},{12,8},{20,16},{28,24},{1,5},{9... | collective-permute-start | bytes 1191944 | tf_op jit(solution)/shard_map/ppermute | solution.py:567
  33.9 5.9 %collective-permute-start.5 = (s16[97,16,128]{2,1,0:T(8,128)(2,1)S(1)}, s16[97,16,128]{2,1,0:T(8,128)(2,1)S(1)}, u32[]{:S(2)}, u32[]{:S(2)}) collective-permute-start(s16[97,16,128]{2,1,0:T(8,128)(2,1)S(1)} %get-tuple-element.33), channel_id=1, source_target_pairs={{4,8},{12,16},{20,24},{8,4},{16,12},{24,20},{5,9},{13,17},{21,25},... | collective-permute-start | bytes 1191944 | tf_op jit(solution)/shard_map/ppermute | solution.py:567
  45.2 14.3 %collective-permute-start.7 = (f32[8,16,128]{2,1,0:T(8,128)S(1)}, f32[8,16,128]{2,1,0:T(8,128)S(1)}, u32[]{:S(2)}, u32[]{:S(2)}) collective-permute-start(f32[8,16,128]{2,1,0:T(8,128)S(1)} %get-tuple-element.36), channel_id=1, source_target_pairs={{0,1},{2,3},{1,0},{3,2},{4,5},{6,7},{5,4},{7,6},{8,9},{10,11},{9,8... | collective-permute-start | bytes 196616 | tf_op jit(solution)/shard_map/ppermute | solution.py:567
  47.1 12.4 %collective-permute-start.6 = (f32[8,16,128]{2,1,0:T(8,128)S(1)}, f32[8,16,128]{2,1,0:T(8,128)S(1)}, u32[]{:S(2)}, u32[]{:S(2)}) collective-permute-start(f32[8,16,128]{2,1,0:T(8,128)S(1)} %get-tuple-element.36), channel_id=1, source_target_pairs={{1,2},{2,1},{5,6},{6,5},{9,10},{10,9},{13,14},{14,13},{17,18},{18,... | collective-permute-start | bytes 196616 | tf_op jit(solution)/shard_map/ppermute | solution.py:567
  53.3 11.4 %collective-permute-start.13 = (f32[8,16,128]{2,1,0:T(8,128)S(1)}, f32[8,16,128]{2,1,0:T(8,128)S(1)}, u32[]{:S(2)}, u32[]{:S(2)}) collective-permute-start(f32[8,16,128]{2,1,0:T(8,128)S(1)} %get-tuple-element.44.own_ref.own_in), channel_id=1, source_target_pairs={{32,0},{64,32},{96,64},{128,96},{160,128},{192,160},{224,192},{256... | collective-permute-start | bytes 196616 | tf_op jit(solution)/shard_map/ppermute | solution.py:560
  54.6 10.2 %collective-permute-start.12 = (f32[8,16,128]{2,1,0:T(8,128)S(1)}, f32[8,16,128]{2,1,0:T(8,128)S(1)}, u32[]{:S(2)}, u32[]{:S(2)}) collective-permute-start(f32[8,16,128]{2,1,0:T(8,128)S(1)} %get-tuple-element.44.own_ref.own_in), channel_id=1, source_target_pairs={{0,32},{32,64},{64,96},{96,128},{128,160},{160,192},{192,224},{224... | collective-permute-start | bytes 196616 | tf_op jit(solution)/shard_map/ppermute | solution.py:560
  59.5 5.3 %copy-start.3 = (bf16[64,24]{0,1:T(8,128)(2,1)S(1)}, bf16[64,24]{0,1:T(8,128)(2,1)}, u32[]{:S(2)}) copy-start(bf16[64,24]{0,1:T(8,128)(2,1)} %param.24) | copy-start | bytes 9220
  59.5 5.3 %copy-start.12 = (bf16[256,128]{1,0:T(8,128)(2,1)S(1)}, bf16[256,128]{1,0:T(8,128)(2,1)}, u32[]{:S(2)}) copy-start(bf16[256,128]{1,0:T(8,128)(2,1)} %constant.5.clone.refs_2_.weight_in) | copy-start | bytes 196612
  59.8 5.0 %copy-start.2 = (s32[16,1,128]{2,1,0:T(1,128)S(1)}, s32[16,1,128]{2,1,0:T(1,128)}, u32[]{:S(2)}) copy-start(s32[16,1,128]{2,1,0:T(1,128)} %param.19) | copy-start | bytes 24580
  59.8 14.6 %collective-permute-start.8 = (s16[50,16,128]{2,1,0:T(8,128)(2,1)S(1)}, s16[50,16,128]{2,1,0:T(8,128)(2,1)S(1)}, u32[]{:S(2)}, u32[]{:S(2)}) collective-permute-start(s16[50,16,128]{2,1,0:T(8,128)(2,1)S(1)} %get-tuple-element.38), channel_id=1, source_target_pairs={{0,32},{32,64},{64,96},{96,128},{128,160},{160,192},{192,224},{224... | collective-permute-start | bytes 614408 | tf_op jit(solution)/shard_map/ppermute | solution.py:560
  63.4 11.0 %collective-permute-start.9 = (s16[50,16,128]{2,1,0:T(8,128)(2,1)S(1)}, s16[50,16,128]{2,1,0:T(8,128)(2,1)S(1)}, u32[]{:S(2)}, u32[]{:S(2)}) collective-permute-start(s16[50,16,128]{2,1,0:T(8,128)(2,1)S(1)} %get-tuple-element.39), channel_id=1, source_target_pairs={{32,0},{64,32},{96,64},{128,96},{160,128},{192,160},{224,192},{256... | collective-permute-start | bytes 614408 | tf_op jit(solution)/shard_map/ppermute | solution.py:560
  64.8 0.7 copy-start.9
  65.5 21.3 %collective-permute-start.14 = (f32[24,8,128]{2,1,0:T(8,128)S(1)}, f32[24,8,128]{2,1,0:T(8,128)S(1)}, u32[]{:S(2)}, u32[]{:S(2)}) collective-permute-start(f32[24,8,128]{2,1,0:T(8,128)S(1)} %get-tuple-element.45), channel_id=1, source_target_pairs={{0,4},{8,12},{16,20},{24,28},{4,0},{12,8},{20,16},{28,24},{1,5},{9... | collective-permute-start | bytes 294920 | tf_op jit(solution)/shard_map/ppermute | solution.py:567
  73.7 13.0 %collective-permute-start.15 = (f32[24,8,128]{2,1,0:T(8,128)S(1)}, f32[24,8,128]{2,1,0:T(8,128)S(1)}, u32[]{:S(2)}, u32[]{:S(2)}) collective-permute-start(f32[24,8,128]{2,1,0:T(8,128)S(1)} %get-tuple-element.46), channel_id=1, source_target_pairs={{4,8},{12,16},{20,24},{8,4},{16,12},{24,20},{5,9},{13,17},{21,25},... | collective-permute-start | bytes 294920 | tf_op jit(solution)/shard_map/ppermute | solution.py:567
  74.8 25.8 %collective-permute-start.11 = (s16[77,16,128]{2,1,0:T(8,128)(2,1)S(1)}, s16[77,16,128]{2,1,0:T(8,128)(2,1)S(1)}, u32[]{:S(2)}, u32[]{:S(2)}) collective-permute-start(s16[77,16,128]{2,1,0:T(8,128)(2,1)S(1)} %get-tuple-element.42), channel_id=1, source_target_pairs={{4,8},{12,16},{20,24},{8,4},{16,12},{24,20},{5,9},{13,17},{21,25},... | collective-permute-start | bytes 946184 | tf_op jit(solution)/shard_map/ppermute | solution.py:567
  75.5 25.2 %collective-permute-start.10 = (s16[77,16,128]{2,1,0:T(8,128)(2,1)S(1)}, s16[77,16,128]{2,1,0:T(8,128)(2,1)S(1)}, u32[]{:S(2)}, u32[]{:S(2)}) collective-permute-start(s16[77,16,128]{2,1,0:T(8,128)(2,1)S(1)} %get-tuple-element.41.after_in), channel_id=1, source_target_pairs={{0,4},{8,12},{16,20},{24,28},{4,0},{12,8},{20,16},{28,24},{1,5},{9... | collective-permute-start | bytes 946184 | tf_op jit(solution)/shard_map/ppermute | solution.py:567
  86.8 13.9 %copy-start.6 = (s32[1024]{0:T(1024)S(1)}, s32[1024]{0:T(1024)}, u32[]{:S(2)}) copy-start(s32[1024]{0:T(1024)} %param.22) | copy-start | bytes 12292
  86.8 13.9 %copy-start.7 = (f32[16,8]{0,1:T(8,128)S(1)}, f32[16,8]{0,1:T(8,128)}, u32[]{:S(2)}) copy-start(f32[16,8]{0,1:T(8,128)} %param.26) | copy-start | bytes 1540
  86.8 13.9 %copy-start.8 = (f32[16,8]{0,1:T(8,128)S(1)}, f32[16,8]{0,1:T(8,128)}, u32[]{:S(2)}) copy-start(f32[16,8]{0,1:T(8,128)} %param.27) | copy-start | bytes 1540
  90.1 22.6 %all-to-all-start = ((f32[64,8,128]{2,1,0:T(8,128)}), f32[64,8,128]{2,1,0:T(8,128)S(1)}, u32[]{:S(2)}, u32[]{:S(2)}) async-start(f32[64,8,128]{2,1,0:T(8,128)} %bitcast.9), calls=%async_computation | async-start | bytes 524288 | tf_op jit(solution)/shard_map/all_to_all | solution.py:674
  100.6 0.7 copy-start.5
  100.6 0.7 copy-start.4
  100.7 0.7 copy-start.10
